TPU v7x, 32 devices: a whole 2x2x4 slice. The times are simulated.
32 devices in a mesh: replica: 2 (over y), tensor: 2 (over x), group: 8 (over z, core).
Axes of the slice: x: 2, y: 2, z: 4, core: 2. Of those that a mesh axis runs over, the one named last changes fastest.
Arguments:
- hidden_in: bfloat16 [16, 512, 5120], P(('replica', 'group'), None, 'tensor'), parts along dimension 0, may hold values from -6 to 6
- ln_gain: bfloat16 [5120], P('tensor'), may hold values from 0.25 to 1.75
- wq: bfloat16 [5120, 4096], P(None, 'tensor'), may hold values from -0.078125 to 0.078125
- wk: bfloat16 [5120, 1024], P(None, 'tensor'), may hold values from -0.078125 to 0.078125
- wv: bfloat16 [5120, 1024], P(None, 'tensor'), may hold values from -0.078125 to 0.078125
- q_gain: bfloat16 [128], replicated, may hold values from 0.7 to 6
- key_norm_gain: bfloat16 [128], replicated, may hold values from 0.7 to 6
- wo: bfloat16 [4096, 5120], P('tensor'), may hold values from -0.5 to 0.5
- prompt_spans: int32 [6], P('replica'), parts along dimension 0, may hold values from 1 to 4, 8 in all
- span_source: int32 [16], P('replica'), parts along dimension 0, may hold values from 0 to 7, each once
- span_target: int32 [16], P('replica'), parts along dimension 0, may hold values from 0 to 7, each once
- page_slot: int32 [64], P('replica'), parts along dimension 0, may hold values from 0 to 31, each once
Outputs:
- mixed: bfloat16 [16, 512, 5120], P(('replica', 'group'), None, 'tensor'), parts along dimension 0
- kv_pages: bfloat16 [64, 2, 128, 1024], P(('replica', 'group')), parts along dimension 0
There are 2 independent parts, one for each index of `replica`. A program takes and returns all parts, laid end to end along the dimension named above; an argument that names none is the same for every part. Nothing has to cross between parts.
Inputs may be any that keep to these rules, and one draw needn't show every extreme that they name: `prompt_spans`: the lengths sum to 8; the longest prompt has exactly 4 spans. `span_source`: a permutation of the slots. `span_target`: a permutation of the slots. `page_slot`: a permutation of the page slots.
All inputs are finite; a program needn't handle non-finite values.
Results may differ from a plain program's by a relative error of at most 0.011.
The roundings to bfloat16 on the way count: a program that leaves them out, or rounds other values in their place, can miss the bound.
Values may be sent and summed in bfloat16 or wider, within the bound.
No kernel may reach another device: no remote copies, remote signals or barrier semaphores. Data moves between devices by JAX's collectives and lax.ppermute only.
A program may use at most 576 MiB of HBM per device.

v0:
```python
import math

import jax
import jax.numpy as jnp
from jax import lax
from jax.sharding import PartitionSpec as P

PAGE_ROWS = 128


epsilon = 1e-06
rope_base = 1000000.0
very_negative = -1e30


def norm_per_head(values, gain):
    mean_sq = jnp.mean(values * values, axis=-1, keepdims=True)
    return values * lax.rsqrt(mean_sq + epsilon) * gain.astype(jnp.float32)


def apply_rotary(values, token_positions):
    half_width = values.shape[-1] // 2
    freqs = jnp.power(
        jnp.float32(rope_base), -jnp.arange(half_width, dtype=jnp.float32) * 2.0 / values.shape[-1]
    )
    angles = token_positions[:, None] * freqs[None, :]
    cosine = jnp.cos(angles)[:, None, :]
    sine = jnp.sin(angles)[:, None, :]
    first_half = values[..., :half_width]
    second_half = values[..., half_width:]
    return jnp.concatenate(
        [first_half * cosine - second_half * sine, second_half * cosine + first_half * sine],
        axis=-1,
    )


def span_tables(prompt_spans, span_ids):
    ends = jnp.cumsum(prompt_spans, dtype=jnp.int32)
    prompt_of = jnp.sum(
        (span_ids[:, None] >= ends[None, :]).astype(jnp.int32), axis=1, dtype=jnp.int32
    )
    starts = ends - prompt_spans
    onehot_table = (
        prompt_of[:, None] == jnp.arange(prompt_spans.shape[0], dtype=jnp.int32)[None, :]
    ).astype(jnp.int32)
    start_of = jnp.sum(onehot_table * starts[None, :], axis=1, dtype=jnp.int32)
    return (prompt_of, start_of)


def lookup(table, chosen):
    onehot_table = (chosen[:, None] == jnp.arange(table.shape[0], dtype=jnp.int32)[None, :]).astype(
        jnp.int32
    )
    return jnp.sum(onehot_table * table[None, :], axis=1, dtype=jnp.int32)


def inverse_of(permuted, slot_list):
    onehot_table = (permuted[None, :] == slot_list[:, None]).astype(jnp.int32)
    return jnp.sum(
        onehot_table * jnp.arange(permuted.shape[0], dtype=jnp.int32)[None, :],
        axis=1,
        dtype=jnp.int32,
    )


def pack_for(blocks, targets, owners):
    slots_each = blocks.shape[0]
    routing = (
        targets[None, :] == jnp.arange(owners * slots_each, dtype=jnp.int32)[:, None]
    ).astype(jnp.bfloat16)
    flat_blocks = blocks.reshape(slots_each, -1)
    packed = jnp.dot(routing, flat_blocks, preferred_element_type=jnp.float32).astype(jnp.bfloat16)
    return packed.reshape((owners, slots_each) + blocks.shape[1:])


def process(
    local_rows, span_ids, ln_gain, wq, wk, wv, q_gain, key_norm_gain, wo, prompt_spans, page_slot
):
    slots_each, span_len, cols_each = local_rows.shape
    tensor_size = lax.axis_size("tensor")
    group_size = lax.axis_size("group")
    tensor_rank = lax.axis_index("tensor")
    head_dim = q_gain.shape[0]
    local_heads = wq.shape[1] // head_dim
    kv_cols = wk.shape[1]
    kv_heads = kv_cols * tensor_size // head_dim
    query_heads = local_heads * tensor_size
    group_ratio = query_heads // kv_heads
    own_kv = max(1, local_heads // group_ratio)
    per_kv = local_heads // own_kv
    first_kv = tensor_rank * local_heads // group_ratio
    prompt_of, start_of = span_tables(prompt_spans, span_ids)
    whole, gain_all = (
        lax.all_gather(local_rows, "tensor", axis=2, tiled=True),
        lax.all_gather(ln_gain, "tensor", axis=0, tiled=True),
    )
    widened = whole.astype(jnp.float32)
    mean_sq = jnp.mean(widened * widened, axis=-1, keepdims=True)
    normed = (widened * lax.rsqrt(mean_sq + epsilon) * gain_all.astype(jnp.float32)).astype(
        jnp.bfloat16
    )
    flattened_rows = normed.reshape(-1, whole.shape[2])
    row_total = flattened_rows.shape[0]
    row_offsets = jnp.arange(span_len, dtype=jnp.int32)
    token_positions = (
        ((span_ids - start_of)[:, None] * span_len + row_offsets[None, :])
        .reshape(-1)
        .astype(jnp.float32)
    )
    query_lin = jnp.dot(flattened_rows, wq, preferred_element_type=jnp.float32).reshape(
        row_total, local_heads, head_dim
    )
    key_part = (
        jnp.dot(flattened_rows, wk, preferred_element_type=jnp.float32)
        .astype(jnp.bfloat16)
        .reshape(slots_each, span_len, kv_cols)
    )
    value_part = (
        jnp.dot(flattened_rows, wv, preferred_element_type=jnp.float32)
        .astype(jnp.bfloat16)
        .reshape(slots_each, span_len, kv_cols)
    )
    key_full, value_full = (
        lax.all_gather(key_part, "tensor", axis=2, tiled=True),
        lax.all_gather(value_part, "tensor", axis=2, tiled=True),
    )
    queries = apply_rotary(norm_per_head(query_lin, q_gain), token_positions).astype(jnp.bfloat16)
    key_tensor = apply_rotary(
        norm_per_head(
            key_full.reshape(row_total, kv_heads, head_dim).astype(jnp.float32), key_norm_gain
        ),
        token_positions,
    ).astype(jnp.bfloat16)
    own_keys = lax.dynamic_slice_in_dim(key_tensor, first_kv, own_kv, 1).reshape(
        slots_each, span_len, own_kv * head_dim
    )
    own_values = lax.dynamic_slice_in_dim(
        value_full.reshape(row_total, kv_heads, head_dim), first_kv, own_kv, 1
    ).reshape(slots_each, span_len, own_kv * head_dim)
    query_rows = span_ids[:, None] * span_len + row_offsets[None, :]
    grouped = queries.reshape(slots_each, span_len, own_kv, per_kv, head_dim)
    score_scale = 1.0 / math.sqrt(head_dim)
    start_best = jnp.full((slots_each, own_kv, per_kv, span_len), very_negative, jnp.float32)
    best = start_best
    part_keys = lax.all_gather(own_keys, "group", axis=0, tiled=True)
    part_values = lax.all_gather(own_values, "group", axis=0, tiled=True)
    part_ids = lax.all_gather(span_ids, "group", axis=0, tiled=True)
    count = part_keys.shape[0]
    part_prompt, part_start = span_tables(prompt_spans, part_ids)
    key_rows = part_ids[:, None] * span_len + row_offsets[None, :]
    allowed = (prompt_of[:, None, None, None] == part_prompt[None, None, :, None]) & (
        key_rows[None, None, :, :] <= query_rows[:, :, None, None]
    )
    allowed = allowed[:, None, None]
    scores = (
        jnp.einsum(
            "sikgd,pjkd->skgipj",
            grouped,
            part_keys.reshape(count, span_len, own_kv, head_dim),
            preferred_element_type=jnp.float32,
        )
        * score_scale
    )
    scores = jnp.where(allowed, scores, very_negative)
    newest = jnp.maximum(best, jnp.max(scores, axis=(4, 5)))
    weights = jnp.where(allowed, jnp.exp(scores - newest[..., None, None]), 0.0)
    totals = jnp.sum(weights, axis=(4, 5))
    gathered_values = jnp.einsum(
        "skgipj,pjkd->skgid",
        weights.astype(jnp.bfloat16),
        part_values.reshape(count, span_len, own_kv, head_dim),
        preferred_element_type=jnp.float32,
    )
    weighted = gathered_values
    best, totals, weighted = (newest, totals, weighted)
    attended = weighted / totals[..., None]
    attended = (
        jnp.transpose(attended, (0, 3, 1, 2, 4))
        .reshape(row_total, local_heads * head_dim)
        .astype(jnp.bfloat16)
    )
    own_sum = (
        lax.psum_scatter(
            lax.dot_general(
                wo, attended, (((0,), (1,)), ((), ())), preferred_element_type=jnp.float32
            ).astype(jnp.bfloat16),
            "tensor",
            scatter_dimension=0,
            tiled=True,
        )
        .astype(jnp.float32)
        .T
    )
    result = (
        (local_rows.reshape(row_total, cols_each).astype(jnp.float32) + own_sum)
        .astype(jnp.bfloat16)
        .reshape(local_rows.shape)
    )
    pages_each = span_len // PAGE_ROWS
    all_cols = kv_heads * head_dim
    key_rows_all = key_tensor.reshape(-1, PAGE_ROWS, all_cols)
    value_rows_all = value_full.reshape(-1, PAGE_ROWS, all_cols)
    page_blocks = jnp.stack([key_rows_all, value_rows_all], axis=1)
    page_ids = (
        span_ids[:, None] * pages_each + jnp.arange(pages_each, dtype=jnp.int32)[None, :]
    ).reshape(-1)
    page_targets = lookup(page_slot, page_ids)
    packed_pages = pack_for(page_blocks, page_targets, group_size)
    arrived_pages = lax.all_to_all(packed_pages, "group", split_axis=0, concat_axis=0, tiled=True)
    cache = jnp.sum(arrived_pages, axis=0, dtype=jnp.float32).astype(jnp.bfloat16)
    return (result, cache)


def local(
    hidden_in,
    ln_gain,
    wq,
    wk,
    wv,
    q_gain,
    key_norm_gain,
    wo,
    prompt_spans,
    span_source,
    span_target,
    page_slot,
):
    slots_each = hidden_in.shape[0]
    group_size = lax.axis_size("group")
    group_rank = lax.axis_index("group")
    own_slots = group_rank * slots_each + jnp.arange(slots_each, dtype=jnp.int32)
    source_ids = inverse_of(span_source, own_slots)
    moved_to = lookup(span_target, source_ids)
    packed = pack_for(hidden_in, moved_to, group_size)
    arrived = lax.all_to_all(packed, "group", split_axis=0, concat_axis=0, tiled=True)
    moved_rows = jnp.sum(arrived, axis=0, dtype=jnp.float32).astype(jnp.bfloat16)
    target_ids = inverse_of(span_target, own_slots)
    mixed, cache = process(
        moved_rows,
        target_ids,
        ln_gain,
        wq,
        wk,
        wv,
        q_gain,
        key_norm_gain,
        wo,
        prompt_spans,
        page_slot,
    )
    return (mixed, cache)


def solution(mesh):
    in_specs = (
        P(("replica", "group"), None, "tensor"),
        P("tensor"),
        P(None, "tensor"),
        P(None, "tensor"),
        P(None, "tensor"),
        P(),
        P(),
        P("tensor", None),
        P("replica"),
        P("replica"),
        P("replica"),
        P("replica"),
    )
    out_specs = (P(("replica", "group"), None, "tensor"), P(("replica", "group"), None, None, None))
    return jax.shard_map(local, mesh=mesh, in_specs=in_specs, out_specs=out_specs, check_vma=False)
```

profile of v0, /device:TPU:0, one launch (start us, length us, event | category | flops | bytes accessed | tf_op | source)
XLA Modules:
  0.0 1128.4 jit_solution(16540823720318435564)
XLA Ops:
  7.2 1.3 fusion.38
  8.5 2.0 fusion.41
  10.5 0.6 fusion.40
  11.2 6.7 reshape.363
  17.9 7.2 multiply_convert_fusion
  25.1 27.1 %copy.108 = bf16[1,8,512,2560]{3,2,1,0:T(8,128)(2,1)S(1)} copy(bf16[1,8,512,2560]{3,1,2,0:T(8,128)(2,1)S(1)} %bitcast.121) | data formatting | bytes 41943040
  52.1 460.7 %all_to_all.10 = bf16[8,1,512,2560]{3,2,1,0:T(8,128)(2,1)} all-to-all(bf16[8,1,512,2560]{3,2,1,0:T(8,128)(2,1)S(1)} %bitcast.122), channel_id=1, replica_groups=mesh['replica'=2,'tensor'=2,'group'=8] {'group'}, dimensions={0} | all-to-all | bytes 41943040 | tf_op jit(solution)/shard_map/all_to_all | solution.py:235
  512.9 13.1 %reduce_sum.131 = bf16[512,2560]{1,0:T(8,128)(2,1)} reduce(bf16[8,1,512,2560]{3,2,1,0:T(8,128)(2,1)} %all_to_all.10, bf16[]{:T(256)} %constant.58.clone.1), dimensions={0,1}, to_apply=%region_2.0 | reduce | flops 9175040 | bytes 23592962 | tf_op jit(solution)/shard_map/reduce_sum | solution.py:236
  526.2 4.4 all-gather.3
  530.7 1.4 fusion.42
  532.0 1.3 fusion.43
  534.7 58.2 %all-gather.14.cloned.1.call-done = bf16[512,5120]{1,0:T(8,128)(2,1)} async-done(((bf16[512,2560]{1,0:T(8,128)(2,1)}), bf16[512,5120]{1,0:T(8,128)(2,1)}) %all-gather.14.cloned.1.call-update) | async-done | bytes 5242896 | tf_op jit(solution)/shard_map/all_gather | solution.py:94
  592.9 3.7 fusion.6
  597.0 6.2 fusion.31
  604.1 7.8 fusion.28
  612.1 12.5 %all-gather.18.cloned.1.call-done = bf16[512,1024]{1,0:T(8,128)(2,1)} async-done(((bf16[512,512]{1,0:T(8,128)(2,1)}), bf16[512,1024]{1,0:T(8,128)(2,1)}) %all-gather.18.cloned.1.call-update) | async-done | bytes 1048592 | tf_op jit(solution)/shard_map/all_gather | solution.py:124
  624.7 1.5 convert_bitcast_fusion
  627.5 0.9 multiply_multiply_fusion.1
  628.3 0.9 multiply_subtract_fusion
  630.1 1.0 reshape.356
  631.8 1.4 dynamic-update-slice
  633.2 8.9 all-reduce
  643.6 26.3 %copy.87 = bf16[2048,5120]{1,0:T(8,128)(2,1)} copy(bf16[2048,5120]{0,1:T(8,128)(2,1)} %bitcast.125) | data formatting | bytes 41943040 | tf_op jit(solution)/shard_map/dot_general | solution.py:110
  670.8 1.6 compare_and_fusion
  672.5 16.2 %multiply_reduce_fusion = (f32[512,16]{0,1:T(8,128)S(1)}, f32[512,16,128]{0,2,1:T(8,128)S(1)}) fusion(bf16[16,128,5120]{2,1,0:T(8,128)(2,1)} %bitcast.126, f32[5120]{0:T(1024)S(1)} %bitcast.140, f32[512]{0:T(512)S(1)} %add_rsqrt_fusion.2, bf16[512,5120]{1,0:T(8,128)(2,1)} %all-gather.14.cloned.1.call-done), kind=kOutput, calls=%fused_computation.33 | convolution fusion | flops 10749992960 | bytes 30464000 | tf_op jit(solution)/shard_map/dot_general | solution.py:110
  688.7 0.8 multiply_multiply_fusion
  689.4 2.1 subtract_convert_fusion
  691.5 2.7 copy.73
  694.2 2.8 copy.72
  697.0 1.3 convert_element_type.129
  698.3 1.6 copy.90
  699.9 1.1 constant_dynamic-slice_fusion.1
  701.0 2.1 reshape.352
  703.0 1.4 pad_maximum_fusion
  704.4 2.9 copy.92
  707.4 9.8 convolution_convert_fusion
  717.2 18.9 %copy.93 = bf16[4,8,256,1024]{3,2,1,0:T(8,128)(2,1)} copy(bf16[4,8,256,1024]{3,1,2,0:T(8,128)(2,1)} %bitcast.124) | data formatting | bytes 33554432
  736.1 5.7 all-to-all-start.1
  741.9 6.5 copy.70
  748.4 48.8 %fusion = (f32[4,4,512]{2,1,0:T(4,128)S(1)}, f32[4,8,512,512,4]{3,2,4,1,0:T(8,128)}) fusion(pred[512,8,512]{0,2,1:T(8,128)(4,1)S(1)} %compare_and_fusion, bf16[512,4,4,64]{3,0,2,1:T(8,128)(2,1)} %copy.73, bf16[512,4,4,64]{3,0,2,1:T(8,128)(2,1)} %copy.72, bf16[8,512,4,128,1]{1,3,2,0,4:T(8,128)(2,1)} %bitcast.127), kind=kOutput, calls=%fused_computation.3 | convolution fusion | flops 8694784000 | bytes 142639104 | tf_op jit(solution)/shard_map/sikgd,pjkd->skgipj/dot_general | solution.py:156
  797.2 6.5 copy.65
  803.7 65.3 %fusion.1 = (f32[4,4,512]{2,1,0:T(4,128)S(1)}, bf16[4,4,512,8,512]{2,4,1,3,0:T(8,128)(2,1)}) fusion(f32[4,8,512,512,4]{3,2,4,1,0:T(8,128)} %get-tuple-element.15, f32[4,4,512]{2,1,0:T(4,128)S(1)} %broadcast_maximum_fusion, pred[512,8,512]{0,2,1:T(8,128)(4,1)S(1)} %compare_and_fusion), kind=kLoop, calls=%fused_computation.4 | loop fusion | flops 201318400 | bytes 203489280 | tf_op jit(solution)/shard_map/reduce_sum | solution.py:167
  869.0 24.1 %fusion.17 = bf16[1,512,4,4,128]{1,4,3,2,0:T(8,128)(2,1)S(1)} fusion(bf16[4,4,512,8,512]{2,4,1,3,0:T(8,128)(2,1)} %get-tuple-element.5, bf16[8,512,4,128,1]{1,3,2,0,4:T(8,128)(2,1)} %bitcast.133, f32[512,4,4]{0,2,1:T(4,128)S(1)} %bitcast.137), kind=kOutput, calls=%fused_computation.28 | convolution fusion | flops 8592031744 | bytes 73433088 | tf_op jit(solution)/shard_map/skgipj,pjkd->skgid/dot_general | solution.py:168
  893.1 17.1 %fusion.9 = bf16[5120,512]{0,1:T(8,128)(2,1)} fusion(bf16[512,2048]{0,1:T(8,128)(2,1)S(1)} %bitcast.143, bf16[2048,5120]{1,0:T(8,128)(2,1)} %param.19), kind=kOutput, calls=%fused_computation.18 | convolution fusion | flops 10740039680 | bytes 28311552 | tf_op jit(solution)/shard_map/dot_general | solution.py:184
  910.2 70.8 %reduce-scatter.2.cloned.1.call-done = bf16[2560,512]{0,1:T(8,128)(2,1)} async-done(((bf16[5120,512]{0,1:T(8,128)(2,1)}), bf16[2560,512]{0,1:T(8,128)(2,1)}) %reduce-scatter.2.cloned.1.call-update) | async-done | bytes 2621456 | tf_op jit(solution)/shard_map/reduce_scatter | solution.py:183
  981.1 3.9 fusion.25
  984.9 125.3 %all-to-all-done.1 = bf16[8,4,2,128,1024]{4,3,2,1,0:T(8,128)(2,1)} async-done(((bf16[8,4,2,128,1024]{4,3,2,1,0:T(8,128)(2,1)}), bf16[8,4,2,128,1024]{4,3,2,1,0:T(8,128)(2,1)}, u32[]{:S(2)}, u32[]{:S(2)}) %all-to-all-start.1) | async-done | bytes 16777248 | tf_op jit(solution)/shard_map/all_to_all | solution.py:209
  1110.3 10.8 reduce_sum.144
  (62 shorter events, 5.7 us)
Async XLA Ops:
  7.2 585.7 %all-gather.14.cloned.1.call-start = ((), (), s32[]{:S(2)}) async-start(), calls=%async_computation.6 | async-start | bytes 7864320 | tf_op jit(solution)/shard_map/all_gather | solution.py:94
  512.9 13.2 %copy-start.4 = (s32[3]{0:T(128)S(1)}, s32[3]{0:T(128)}, u32[]{:S(2)}) copy-start(s32[3]{0:T(128)} %param.20) | copy-start | bytes 40
  512.9 13.4 %copy-start.5 = (bf16[128]{0:T(256)(128)(2,1)S(1)}, bf16[128]{0:T(256)(128)(2,1)}, u32[]{:S(2)}) copy-start(bf16[128]{0:T(256)(128)(2,1)} %param.18) | copy-start | bytes 772
  512.9 13.4 %copy-start.3 = (bf16[2560]{0:T(1024)(128)(2,1)S(1)}, bf16[2560]{0:T(1024)(128)(2,1)}, u32[]{:S(2)}) copy-start(bf16[2560]{0:T(1024)(128)(2,1)} %param.13) | copy-start | bytes 15364
  526.0 98.7 %all-gather.18.cloned.1.call-start = ((), (), s32[]{:S(2)}) async-start(), calls=%async_computation.8 | async-start | bytes 1572864 | tf_op jit(solution)/shard_map/all_gather | solution.py:124
  592.9 4.0 copy-start.1
  603.2 95.0 %all-gather.16.cloned.1.call-start = ((), (), s32[]{:S(2)}) async-start(), calls=%async_computation.7 | async-start | bytes 1572864 | tf_op jit(solution)/shard_map/all_gather | solution.py:125
  611.9 130.0 %all-gather.12.cloned.1.call-start = ((), (), s32[]{:S(2)}) async-start(), calls=%async_computation.4 | async-start | bytes 4718592 | tf_op jit(solution)/shard_map/all_gather | solution.py:145
  629.2 2.0 copy-start.8
  629.2 14.3 %copy-start.6 = (bf16[128]{0:T(256)(128)(2,1)S(1)}, bf16[128]{0:T(256)(128)(2,1)}, u32[]{:S(2)}) copy-start(bf16[128]{0:T(256)(128)(2,1)} %param.17) | copy-start | bytes 772
  631.1 166.1 %all-gather.10.cloned.1.call-start = ((), (), s32[]{:S(2)}) async-start(), calls=%async_computation.3 | async-start | bytes 4718592 | tf_op jit(solution)/shard_map/all_gather | solution.py:146
  643.5 26.3 %copy-start.7 = (s32[32]{0:T(128)S(1)}, s32[32]{0:T(128)}, u32[]{:S(2)}) copy-start(s32[32]{0:T(128)} %param.23) | copy-start | bytes 388
  698.3 4.7 copy-start.2
  736.1 374.2 %all-to-all-start.1 = ((bf16[8,4,2,128,1024]{4,3,2,1,0:T(8,128)(2,1)}), bf16[8,4,2,128,1024]{4,3,2,1,0:T(8,128)(2,1)}, u32[]{:S(2)}, u32[]{:S(2)}) async-start(bf16[8,4,2,128,1024]{4,3,2,1,0:T(8,128)(2,1)} %bitcast.123), calls=%async_computation.2 | async-start | bytes 33554432 | tf_op jit(solution)/shard_map/all_to_all | solution.py:209
  741.9 239.2 %reduce-scatter.2.cloned.1.call-start = ((), (), s32[]{:S(2)}) async-start(), calls=%async_computation.5 | async-start | bytes 7864320 | tf_op jit(solution)/shard_map/reduce_scatter | solution.py:183
  910.2 70.9 %copy-start = (bf16[512,2560]{1,0:T(8,128)(2,1)S(1)}, bf16[512,2560]{1,0:T(8,128)(2,1)}, u32[]{:S(2)}) copy-start(bf16[512,2560]{1,0:T(8,128)(2,1)} %reduce_sum.131) | copy-start | bytes 7864324
Sparse Core Ops, SparseCore 0:
  526.1 66.7 all-gather.13
  603.3 21.2 all-gather.17
  626.2 21.2 all-gather.15
  649.0 47.1 all-gather.11
  707.5 49.6 all-gather.9
  910.3 70.6 reduce-scatter.1
where the time goes:
time: 1140 us; the launch traced here: 1130 us
  blocking collectives  474 us (42%)
  waiting for transfers between devices  267 us (23%)
  matrix products  130 us (11%)
  other arithmetic  123 us (11%)
  local copies, waits for them, and re-layouts  111 us (10%)
  between operations  17.6 us (2%)
    all_to_all x1, blocking collectives, local(): lax.all_to_all(packed, 'group', split_axis=0, concat_axis=0, tiled=True)  461 us
    all_to_all x1, waiting for transfers between devices, process(): lax.all_to_all(packed_pages, 'group', split_axis=0, concat_axis=0, tiled=...  125 us
    reduce_scatter x1, waiting for transfers between devices, process(): lax.psum_scatter(lax.dot_general(wo, attended, (((0,), (1,)), ((), ())),...  70.8 us
    reduce_sum x1, other arithmetic, process(): totals = jnp.sum(weights, axis=(4, 5))  65.3 us
    all_gather x1, waiting for transfers between devices, process(): lax.all_gather(local_rows, 'tensor', axis=2, tiled=True)  58.2 us
    unnamed x26, local copies, waits for them, and re-layouts  53.3 us
    dot_general x1, matrix products, process(): jnp.einsum('sikgd,pjkd->skgipj', grouped, part_keys.reshape(count, span_l...  48.8 us
    dot_general x1, local copies, waits for them, and re-layouts, process(): jnp.dot(flattened_rows, wq, preferred_element_type=jnp.float32)  26.3 us
  transfers between devices with their start and end apart: 7, of which 4 were waited for; matrix products, arithmetic and copies ran while one was open for 25% of the time, Pallas kernels for 0%

commit v1 on v0

v1 whole, which is shorter than its diff:
```python
import functools
import math

import jax
import jax.numpy as jnp
from jax import lax
from jax.experimental import pallas as pl
from jax.experimental.pallas import tpu as pltpu
from jax.sharding import PartitionSpec as P

PAGE_ROWS = 128
epsilon = 1e-06
rope_base = 1000000.0
very_negative = -1e30
VMEM_BYTES = 48 * 1024 * 1024
PARTS = 2


def params():
    return pltpu.CompilerParams(vmem_limit_bytes=VMEM_BYTES)


def cost(flops, moved, transcendentals=0):
    return pl.CostEstimate(
        flops=int(flops), bytes_accessed=int(moved), transcendentals=int(transcendentals)
    )


class Layout:
    def __init__(self, spans, pages):
        self.start = 0
        self.slot = self.start + spans
        self.offset = self.slot + spans
        self.from_slot = self.offset + spans
        self.page = self.from_slot + spans
        self.group_rank = self.page + pages
        self.tensor_rank = self.group_rank + 1
        self.length = self.tensor_rank + 1


def tables_kernel(lay, spans, pages, ranks, prompt_spans, source, target, page_slot, out):
    out[lay.group_rank] = ranks[0]
    out[lay.tensor_rank] = ranks[1]
    for k in range(spans):
        start = jnp.int32(0)
        begin = jnp.int32(0)
        for p in range(prompt_spans.shape[0]):
            start = jnp.where(begin <= k, begin, start)
            begin = begin + prompt_spans[p]
        slot = source[k]
        out[lay.start + k] = start
        out[lay.slot + k] = slot
        out[lay.offset + slot] = k - start
        out[lay.from_slot + target[k]] = slot
    for p in range(pages):
        out[lay.page + page_slot[p]] = jnp.int32(p)


def make_tables(lay, spans, pages, ranks, prompt_spans, source, target, page_slot):
    smem = pl.BlockSpec(memory_space=pltpu.SMEM)
    return pl.pallas_call(
        functools.partial(tables_kernel, lay, spans, pages),
        out_shape=jax.ShapeDtypeStruct((lay.length,), jnp.int32),
        in_specs=[smem] * 5,
        out_specs=smem,
        name="tables",
    )(ranks, prompt_spans, source, target, page_slot)


def head_norm_rope(u, gain, cosine, sine):
    mean_sq = jnp.mean(u * u, axis=-1, keepdims=True)
    u = u * lax.rsqrt(mean_sq + epsilon) * gain
    half = u.shape[-1] // 2
    return u * cosine + pltpu.roll(u, half, 1) * sine


def kv_kernel(x, gain, wk, wv, kgain, cosine, sine, normed, kv):
    head = kgain.shape[1]

    @pl.when(pl.program_id(0) == 0)
    def _():
        wide = x[...].astype(jnp.float32)
        mean_sq = jnp.mean(wide * wide, axis=-1, keepdims=True)
        normed[...] = (
            wide * lax.rsqrt(mean_sq + epsilon) * gain[...].astype(jnp.float32)
        ).astype(jnp.bfloat16)

    rows = normed[...]
    keys = jnp.dot(rows, wk[...], preferred_element_type=jnp.float32).astype(jnp.bfloat16)
    gains = kgain[...].astype(jnp.float32)
    for h in range(wk.shape[1] // head):
        u = keys[:, h * head : (h + 1) * head].astype(jnp.float32)
        kv[0, :, h * head : (h + 1) * head] = head_norm_rope(
            u, gains, cosine[...], sine[...]
        ).astype(jnp.bfloat16)
    kv[1] = jnp.dot(rows, wv[...], preferred_element_type=jnp.float32).astype(jnp.bfloat16)


def make_kv(x, gain, wk, wv, kgain, cosine, sine):
    rows, width = x.shape
    cols = wk.shape[1]
    tile = 256 if cols % 256 == 0 else cols
    head = kgain.shape[1]
    fixed = lambda n: (0, 0)
    return pl.pallas_call(
        kv_kernel,
        grid=(cols // tile,),
        in_specs=[
            pl.BlockSpec((rows, width), fixed),
            pl.BlockSpec((1, width), fixed),
            pl.BlockSpec((width, tile), lambda n: (0, n)),
            pl.BlockSpec((width, tile), lambda n: (0, n)),
            pl.BlockSpec((1, head), fixed),
            pl.BlockSpec((rows, head), fixed),
            pl.BlockSpec((rows, head), fixed),
        ],
        out_specs=[
            pl.BlockSpec((rows, width), fixed),
            pl.BlockSpec((2, rows, tile), lambda n: (0, 0, n)),
        ],
        out_shape=[
            jax.ShapeDtypeStruct((rows, width), jnp.bfloat16),
            jax.ShapeDtypeStruct((2, rows, cols), jnp.bfloat16),
        ],
        compiler_params=params(),
        cost_estimate=cost(4 * rows * width * cols, 4 * width * cols + 4 * rows * width),
        name="keys_values",
    )(x, gain, wk, wv, kgain, cosine, sine)


def q_kernel(normed, wq, qgain, cosine, sine, out):
    head = qgain.shape[1]
    lin = jnp.dot(normed[...], wq[...], preferred_element_type=jnp.float32)
    gains = qgain[...].astype(jnp.float32)
    for h in range(wq.shape[1] // head):
        out[:, h * head : (h + 1) * head] = head_norm_rope(
            lin[:, h * head : (h + 1) * head], gains, cosine[...], sine[...]
        ).astype(jnp.bfloat16)


def make_q(normed, wq, qgain, cosine, sine):
    rows, width = normed.shape
    cols = wq.shape[1]
    tile = 256 if cols % 256 == 0 else cols
    head = qgain.shape[1]
    fixed = lambda n: (0, 0)
    return pl.pallas_call(
        q_kernel,
        grid=(cols // tile,),
        in_specs=[
            pl.BlockSpec((rows, width), fixed),
            pl.BlockSpec((width, tile), lambda n: (0, n)),
            pl.BlockSpec((1, head), fixed),
            pl.BlockSpec((rows, head), fixed),
            pl.BlockSpec((rows, head), fixed),
        ],
        out_specs=pl.BlockSpec((rows, tile), lambda n: (0, n)),
        out_shape=jax.ShapeDtypeStruct((rows, cols), jnp.bfloat16),
        compiler_params=params(),
        cost_estimate=cost(2 * rows * width * cols, 2 * width * cols + 2 * rows * (width + cols)),
        name="queries",
    )(normed, wq, qgain, cosine, sine)


def attention_kernel(lay, spans, most, per_kv, head, table, *refs):
    q_refs, k_refs, v_refs, out = refs[:PARTS], refs[PARTS : 2 * PARTS], refs[2 * PARTS : -1], refs[-1]
    owners, rows = k_refs[0].shape[0], k_refs[0].shape[3]
    group_rank = table[lay.group_rank]
    scale = (1.0 / math.sqrt(head)) * math.log2(math.e)
    q_rows, k_rows = PARTS * per_kv * rows, owners * rows
    row = lax.broadcasted_iota(jnp.int32, (q_rows, k_rows), 0)
    col = lax.broadcasted_iota(jnp.int32, (q_rows, k_rows), 1)
    q_at = group_rank * PARTS * rows + (row // (per_kv * rows)) * rows + row % rows
    k_at = (col // rows) * PARTS * rows + col % rows
    allowed = [k_at + c * rows <= q_at for c in range(PARTS)]

    def one_span(k, carry):
        slot = table[lay.slot + k]
        earlier = k - table[lay.start + k]
        queries = jnp.concatenate(
            [
                ref[slot, :, g * head : (g + 1) * head]
                for ref in q_refs
                for g in range(per_kv)
            ],
            axis=0,
        )

        def with_earlier(count):
            scores, blocks = [], []
            for back in range(count + 1):
                at = table[lay.slot + k - back]
                for c in range(PARTS):
                    block = k_refs[c][:, 0, at].reshape(k_rows, head)
                    s = lax.dot_general(
                        queries, block, (((1,), (1,)), ((), ())),
                        preferred_element_type=jnp.float32,
                    )
                    if back == 0:
                        s = jnp.where(allowed[c], s, very_negative)
                    scores.append(s)
                    blocks.append((c, at))
            best = scores[0]
            for s in scores[1:]:
                best = jnp.maximum(best, s)
            best = jnp.max(best, axis=-1, keepdims=True)
            total = None
            summed = None
            for s, (c, at) in zip(scores, blocks):
                w = jnp.exp2((s - best) * scale)
                part = jnp.sum(w, axis=-1, keepdims=True)
                value = v_refs[c][:, 0, at].reshape(k_rows, head)
                term = jnp.dot(
                    w.astype(jnp.bfloat16), value, preferred_element_type=jnp.float32
                )
                total = part if total is None else total + part
                summed = term if summed is None else summed + term
            result = (summed / total).astype(jnp.bfloat16)
            for c in range(PARTS):
                for g in range(per_kv):
                    at_row = (c * per_kv + g) * rows
                    out[slot, c * rows : (c + 1) * rows, g * head : (g + 1) * head] = result[
                        at_row : at_row + rows
                    ]

        for count in range(most):
            pl.when(earlier == count)(functools.partial(with_earlier, count))
        return carry

    lax.fori_loop(0, spans, one_span, 0)


def make_attention(lay, most, table, queries, gathered, per_kv, head):
    spans, rows, cols = queries[0].shape
    owners = gathered[0].shape[0]
    own_kv = cols // (per_kv * head)
    q_spec = pl.BlockSpec((spans, rows, per_kv * head), lambda h, t: (0, 0, h))
    k_spec = pl.BlockSpec((owners, 1, spans, rows, head), lambda h, t: (0, 0, 0, 0, h))
    v_spec = pl.BlockSpec((owners, 1, spans, rows, head), lambda h, t: (0, 1, 0, 0, h))
    all_rows = spans * rows * PARTS
    pairs = 2.2 * all_rows * owners * rows * PARTS * per_kv * own_kv
    return pl.pallas_call(
        functools.partial(attention_kernel, lay, spans, most, per_kv, head),
        grid_spec=pltpu.PrefetchScalarGridSpec(
            num_scalar_prefetch=1,
            grid=(own_kv,),
            in_specs=[q_spec] * PARTS + [k_spec] * PARTS + [v_spec] * PARTS,
            out_specs=pl.BlockSpec((spans, rows * PARTS, per_kv * head), lambda h, t: (0, 0, h)),
        ),
        out_shape=jax.ShapeDtypeStruct((spans, rows * PARTS, cols), jnp.bfloat16),
        compiler_params=params(),
        cost_estimate=cost(4 * pairs * head, 4 * all_rows * cols + 4 * PARTS * gathered[0].size, pairs),
        name="attention",
    )(table, *queries, *gathered, *gathered)


def project_kernel(table, attended, wo, out):
    out[...] = jnp.dot(
        attended[...], wo[...], preferred_element_type=jnp.float32
    ).astype(jnp.bfloat16)


def make_projection(lay, table, attended, wo, first, count, tile, name):
    rows, depth = attended.shape
    return pl.pallas_call(
        project_kernel,
        grid_spec=pltpu.PrefetchScalarGridSpec(
            num_scalar_prefetch=1,
            grid=(count,),
            in_specs=[
                pl.BlockSpec((rows, depth), lambda n, t: (0, 0)),
                pl.BlockSpec((depth, tile), lambda n, t: (0, first(t[lay.tensor_rank]) + n)),
            ],
            out_specs=pl.BlockSpec((rows, tile), lambda n, t: (0, n)),
        ),
        out_shape=jax.ShapeDtypeStruct((rows, count * tile), jnp.bfloat16),
        compiler_params=params(),
        cost_estimate=cost(
            2 * rows * depth * count * tile, 2 * (rows * depth + (rows + depth) * count * tile)
        ),
        name=name,
    )(table, attended, wo)


def add_kernel(table, *refs):
    x_refs, own, received, out = refs[:PARTS], refs[PARTS], refs[PARTS + 1], refs[PARTS + 2]
    rows = x_refs[0].shape[1]
    for c in range(PARTS):
        at = slice(c * rows, (c + 1) * rows)
        summed = own[0, at].astype(jnp.float32) + received[0, at].astype(jnp.float32)
        out[0, at] = (x_refs[c][0].astype(jnp.float32) + summed).astype(jnp.bfloat16)


def make_sum(lay, table, arrived, own, received, first, tile):
    spans, rows, cols = received.shape
    part = rows // PARTS
    tiles = cols // tile
    slot_of = lambda t, table: table[lay.from_slot + t]
    return pl.pallas_call(
        add_kernel,
        grid_spec=pltpu.PrefetchScalarGridSpec(
            num_scalar_prefetch=1,
            grid=(spans, tiles),
            in_specs=[
                pl.BlockSpec((1, part, tile), lambda t, n, s: (slot_of(t, s), 0, first + n))
            ] * PARTS
            + [
                pl.BlockSpec((1, rows, tile), lambda t, n, s: (slot_of(t, s), 0, first + n)),
                pl.BlockSpec((1, rows, tile), lambda t, n, s: (slot_of(t, s), 0, n)),
            ],
            out_specs=pl.BlockSpec((1, rows, tile), lambda t, n, s: (t, 0, n)),
        ),
        out_shape=jax.ShapeDtypeStruct((spans, rows, cols), jnp.bfloat16),
        compiler_params=params(),
        cost_estimate=cost(3 * spans * rows * cols, 8 * spans * rows * cols),
        name="residual",
    )(table, *arrived, own, received)


def pages_kernel(table, *refs):
    sources, out = refs[:PARTS], refs[PARTS]
    rows = sources[0].shape[3]
    for d in range(sources[0].shape[0]):
        for c in range(PARTS):
            at = (d * PARTS + c) * rows
            out[0, :, at : at + rows] = sources[c][d, :, 0]


def make_pages(lay, table, gathered, pages_each):
    owners, _, spans, rows, cols = gathered[0].shape
    per_page = PAGE_ROWS // (rows * PARTS)

    def source(i, t):
        page = t[lay.page + t[lay.group_rank] * pages_each + i]
        return (lax.rem(page, pages_each), 0, t[lay.slot + lax.div(page, pages_each)], 0, 0)

    return pl.pallas_call(
        pages_kernel,
        grid_spec=pltpu.PrefetchScalarGridSpec(
            num_scalar_prefetch=1,
            grid=(pages_each,),
            in_specs=[pl.BlockSpec((per_page, 2, 1, rows, cols), source)] * PARTS,
            out_specs=pl.BlockSpec((1, 2, PAGE_ROWS, cols), lambda i, t: (i, 0, 0, 0)),
        ),
        out_shape=jax.ShapeDtypeStruct((pages_each, 2, PAGE_ROWS, cols), jnp.bfloat16),
        compiler_params=params(),
        cost_estimate=cost(0, 8 * pages_each * PAGE_ROWS * cols),
        name="pages",
    )(table, *gathered)


def rope_tables(offsets, span_len, first_row, rows, head):
    half = head // 2
    freqs = jnp.power(
        jnp.float32(rope_base), -jnp.arange(half, dtype=jnp.float32) * 2.0 / head
    )
    at = offsets[:, None] * span_len + first_row + jnp.arange(rows, dtype=jnp.int32)[None, :]
    angles = at.reshape(-1).astype(jnp.float32)[:, None] * freqs[None, :]
    cosine, sine = jnp.cos(angles), jnp.sin(angles)
    return (
        jnp.concatenate([cosine, cosine], axis=1),
        jnp.concatenate([-sine, sine], axis=1),
    )


def widths_of(cols, tile):
    tiles = cols // tile
    if tiles == 10:
        return [2, 3, 3, 2]
    return [tiles]


def local(
    hidden_in, ln_gain, wq, wk, wv, q_gain, key_norm_gain, wo,
    prompt_spans, span_source, span_target, page_slot,
):
    _, span_len, cols = hidden_in.shape
    tensor_size = lax.axis_size("tensor")
    owners = lax.axis_size("group")
    tensor_rank = lax.axis_index("tensor")
    group_rank = lax.axis_index("group")
    head = q_gain.shape[0]
    own_rows = span_len // owners
    rows = own_rows // PARTS
    pages_each = span_len // PAGE_ROWS
    spans = span_source.shape[0]
    most = spans - (prompt_spans.shape[0] - 1)
    most = min(most, spans // 2)
    local_heads = wq.shape[1] // head
    kv_cols = wk.shape[1]
    kv_heads = kv_cols * tensor_size // head
    lay = Layout(spans, spans * pages_each)

    if kv_cols < head:
        share = head // kv_cols
        sets = [list(range(i, i + share)) for i in range(0, tensor_size, share)]
        wk, wv = [
            lax.all_gather(w, "tensor", axis=1, tiled=True, axis_index_groups=sets)
            for w in (wk, wv)
        ]
    per_kv = local_heads // max(1, wk.shape[1] // head)

    ranks = jnp.stack([group_rank, tensor_rank]).astype(jnp.int32)
    table = make_tables(
        lay, spans, spans * pages_each, ranks, prompt_spans, span_source, span_target, page_slot
    )
    gain = lax.all_gather(ln_gain, "tensor", axis=0, tiled=True)[None]
    offsets = table[lay.offset : lay.offset + spans]

    split = hidden_in.reshape(owners, PARTS, rows, cols)
    arrived, queries, gathered, normed = [], [], [], []
    ropes = []
    for c in range(PARTS):
        arrived.append(
            lax.all_to_all(split[:, c], "group", split_axis=0, concat_axis=0, tiled=True)
        )
        ropes.append(
            rope_tables(offsets, span_len, group_rank * own_rows + c * rows, rows, head)
        )
    for c in range(PARTS):
        whole = lax.all_gather(
            arrived[c].reshape(spans * rows, cols), "tensor", axis=1, tiled=True
        )
        rows_normed, kv = make_kv(
            whole, gain, wk, wv, key_norm_gain[None], *ropes[c]
        )
        normed.append(rows_normed)
        kv = kv.reshape(2, spans, rows, kv.shape[2])
        gathered.append(lax.all_gather(kv, "group", axis=0, tiled=False))
    for c in range(PARTS):
        made = make_q(normed[c], wq, q_gain[None], *ropes[c])
        queries.append(made.reshape(spans, rows, made.shape[1]))

    attended = make_attention(lay, most, table, queries, gathered, per_kv, head)
    attended = attended.reshape(spans * own_rows, -1)

    pages = make_pages(lay, table, gathered, pages_each)
    if kv_cols < head:
        pages = lax.dynamic_slice_in_dim(
            pages, lax.rem(tensor_rank, head // kv_cols) * kv_cols, kv_cols, 3
        )
    cache = lax.all_gather(pages, "tensor", axis=3, tiled=True)

    if tensor_size == 2:
        tile = 256
        half_tiles = cols // tile
        widths = widths_of(cols, tile)
        received, first = [], 0
        for width in widths:
            partial = make_projection(
                lay, table, attended, wo,
                lambda r, first=first: (1 - r) * half_tiles + first, width, tile, "send_part",
            )
            received.append(
                lax.ppermute(partial, "tensor", [(0, 1), (1, 0)]).reshape(spans, own_rows, -1)
            )
            first += width
        own = make_projection(
            lay, table, attended, wo, lambda r: r * half_tiles, half_tiles, tile, "own_part"
        ).reshape(spans, own_rows, cols)
        pieces, first = [], 0
        for width, got in zip(widths, received):
            moved = make_sum(lay, table, arrived, own, got, first, tile)
            pieces.append(
                lax.all_to_all(moved, "group", split_axis=0, concat_axis=0, tiled=True)
            )
            first += width
        mixed = jnp.concatenate(pieces, axis=2).reshape(1, span_len, cols)
    else:
        partial = jnp.dot(attended, wo, preferred_element_type=jnp.float32)
        summed = lax.psum_scatter(
            partial.astype(jnp.bfloat16), "tensor", scatter_dimension=1, tiled=True
        )
        x = jnp.concatenate(arrived, axis=1).astype(jnp.float32)
        moved = (x + summed.reshape(x.shape).astype(jnp.float32)).astype(jnp.bfloat16)
        moved = jnp.take(moved, table[lay.from_slot : lay.from_slot + spans], axis=0)
        moved = lax.all_to_all(moved, "group", split_axis=0, concat_axis=0, tiled=True)
        mixed = moved.reshape(1, span_len, cols)
    return (mixed, cache)


def solution(mesh):
    in_specs = (
        P(("replica", "group"), None, "tensor"),
        P("tensor"),
        P(None, "tensor"),
        P(None, "tensor"),
        P(None, "tensor"),
        P(),
        P(),
        P("tensor", None),
        P("replica"),
        P("replica"),
        P("replica"),
        P("replica"),
    )
    out_specs = (P(("replica", "group"), None, "tensor"), P(("replica", "group"), None, None, None))
    return jax.shard_map(local, mesh=mesh, in_specs=in_specs, out_specs=out_specs, check_vma=False)
```

time: 1140 us -> 433 us (0.38)
  blocking collectives: 474 us -> 78.2 us
  Pallas kernels: 0 us -> 136 us
  matrix products: 130 us -> 0 us
  other arithmetic: 123 us -> 5.57 us
  waiting for transfers between devices: 267 us -> 150 us
  local copies, waits for them, and re-layouts: 111 us -> 18.8 us
  starting transfers between devices: 6.17 us -> 24.6 us
    all_to_all x1 -> x2, blocking collectives: 461 us -> 73.8 us  [local(): lax.all_to_all(split[:, c], 'group', split_axis=0, concat_axis=0, tiled=T...]
    pallas_call x0 -> x16, Pallas kernels: none -> 136 us  [the longest x4 38 us: make_sum(): pl.pallas_call(add_kernel, grid_spec=pltpu.PrefetchScalarGridSpec(num_sca...]
    dot_general x7 -> x0, matrix products: 130 us -> none  [the longest x1 48.8 us: process(): jnp.einsum('sikgd,pjkd->skgipj', grouped, part_keys.reshape(count, span_l...]
    all_to_all x1 -> x4, waiting for transfers between devices: 125 us -> 19.7 us  [local(): lax.all_to_all(moved, 'group', split_axis=0, concat_axis=0, tiled=True)]
    reduce_sum x11 -> x0, other arithmetic: 99.7 us -> none  [the longest x1 65.3 us: process(): totals = jnp.sum(weights, axis=(4, 5))]
    reduce_scatter x1 -> x0, waiting for transfers between devices: 70.8 us -> none  [process(): lax.psum_scatter(lax.dot_general(wo, attended, (((0,), (1,)), ((), ())),...]
    ppermute x0 -> x4, waiting for transfers between devices: none -> 50.5 us  [local(): lax.ppermute(partial, 'tensor', [(0, 1), (1, 0)])]
    unnamed x26 -> x50, local copies, waits for them, and re-layouts: 53.3 us -> 16.8 us
  transfers between devices with their start and end apart: 7 -> 13, of which waited for: 4 -> 8; matrix products, arithmetic and copies ran while one was open for 25% -> 1% of each run, Pallas kernels for 0% -> 24%
where the time goes in v1:
time: 433 us; the launch traced here: 427 us
  waiting for transfers between devices  150 us (35%)
  Pallas kernels  136 us (31%)
  blocking collectives  78.2 us (18%)
  starting transfers between devices  24.6 us (6%)
  local copies, waits for them, and re-layouts  18.8 us (4%)
  between operations  14.1 us (3%)
  other arithmetic  5.57 us (1%)
    all_to_all x2, blocking collectives, local(): lax.all_to_all(split[:, c], 'group', split_axis=0, concat_axis=0, tiled=T...  73.8 us
    all_gather x2, waiting for transfers between devices, local(): gathered.append(lax.all_gather(kv, 'group', axis=0, tiled=False))  56.6 us
    ppermute x4, waiting for transfers between devices, local(): lax.ppermute(partial, 'tensor', [(0, 1), (1, 0)])  50.5 us
    pallas_call x4, Pallas kernels, make_sum(): pl.pallas_call(add_kernel, grid_spec=pltpu.PrefetchScalarGridSpec(num_sca...  38 us
    pallas_call x5, Pallas kernels, make_projection(): pl.pallas_call(project_kernel, grid_spec=pltpu.PrefetchScalarGridSpec(num...  27.9 us
    pallas_call x2, Pallas kernels, make_q(): pl.pallas_call(q_kernel, grid=(cols // tile,), in_specs=[pl.BlockSpec((ro...  25.4 us
    pallas_call x1, Pallas kernels, make_attention(): pl.pallas_call(functools.partial(attention_kernel, lay, spans, most, per_...  23.7 us
    all_gather x2, waiting for transfers between devices, local(): lax.all_gather(arrived[c].reshape(spans * rows, cols), 'tensor', axis=1,...  22.2 us
  transfers between devices with their start and end apart: 13, of which 8 were waited for; matrix products, arithmetic and copies ran while one was open for 1% of the time, Pallas kernels for 24%

profile of v1, /device:TPU:0, one launch (start us, length us, event | category | flops | bytes accessed | tf_op | source)
XLA Modules:
  0.0 427.4 jit_solution(8074975518646711450)
XLA Ops:
  7.2 1.9 slice_bitcast_fusion
  9.1 38.4 %all_to_all.30.refs_0_ = bf16[8,32,2560]{2,1,0:T(8,128)(2,1)} all-to-all(bf16[8,32,2560]{2,1,0:T(8,128)(2,1)S(1)} %get-tuple-element.11), channel_id=1, replica_groups=mesh['replica'=2,'tensor'=2,'group'=8] {'group'}, dimensions={0} | all-to-all | bytes 2621440 | tf_op jit(solution)/shard_map/all_to_all | solution.py:415
  47.7 35.3 %all_to_all.31.refs_1_ = bf16[8,32,2560]{2,1,0:T(8,128)(2,1)} all-to-all(bf16[8,32,2560]{2,1,0:T(8,128)(2,1)S(1)} %get-tuple-element.10), channel_id=1, replica_groups=mesh['replica'=2,'tensor'=2,'group'=8] {'group'}, dimensions={0} | all-to-all | bytes 2621440 | tf_op jit(solution)/shard_map/all_to_all | solution.py:415
  83.8 1.3 tables.1.table
  86.0 4.4 %all-gather = bf16[2,1,2560]{2,1,0:T(2,128)(2,1)S(1)} all-gather(bf16[1,1,2560]{2,1,0:T(2,128)(2,1)S(1)} %reshape.93), channel_id=1, replica_groups=mesh['replica'=2,'tensor'=2,'group'=8] {'tensor'}, dimensions={0}, use_global_device_ids=true | all-gather | bytes 15360 | tf_op jit(solution)/shard_map/all_gather | solution.py:407
  90.4 1.0 fusion.1
  91.7 1.9 copy-done.12
  93.5 8.6 %keys_values.2 = (bf16[256,5120]{1,0:T(8,128)(2,1)S(1)}, bf16[2,256,512]{2,1,0:T(8,128)(2,1)}) custom-call(bf16[256,5120]{1,0:T(8,128)(2,1)S(1)} %copy-done.12, bf16[1,5120]{1,0:T(2,128)(2,1)S(1)} %bitcast.44, bf16[5120,512]{1,0:T(8,128)(2,1)} %wk.3, bf16[5120,512]{1,0:T(8,128)(2,1)} %wv.3, bf16[1,128]{1,0:T(2,128)(2,1)S(1)} %bitcast.46, ...), custom_call_target="tpu_custom_call" | custom-call | flops 2684354560 | bytes 15728640 | tf_op jit(solution)/shard_map/keys_values/pallas_call | solution.py:105
  102.2 1.5 copy-done.13
  104.1 22.2 %all-gather.9.cloned.1.call-done.x = bf16[256,5120]{1,0:T(8,128)(2,1)} async-done(((bf16[256,2560]{1,0:T(8,128)(2,1)}), bf16[256,5120]{1,0:T(8,128)(2,1)}) %all-gather.9.cloned.1.call-update) | async-done | bytes 2621456 | tf_op jit(solution)/shard_map/all_gather | solution.py:421
  126.3 1.7 copy-done.11
  128.0 8.1 %keys_values.3 = (bf16[256,5120]{1,0:T(8,128)(2,1)S(1)}, bf16[2,256,512]{2,1,0:T(8,128)(2,1)}) custom-call(bf16[256,5120]{1,0:T(8,128)(2,1)S(1)} %copy-done.11, bf16[1,5120]{1,0:T(2,128)(2,1)S(1)} %bitcast.45, bf16[5120,512]{1,0:T(8,128)(2,1)} %wk.3, bf16[5120,512]{1,0:T(8,128)(2,1)} %wv.3, bf16[1,128]{1,0:T(2,128)(2,1)S(1)} %bitcast.47, ...), custom_call_target="tpu_custom_call" | custom-call | flops 2684354560 | bytes 15728640 | tf_op jit(solution)/shard_map/keys_values/pallas_call | solution.py:105
  136.2 1.5 copy-done.15
  137.7 1.7 copy-done.14
  139.4 12.8 %queries.2 = bf16[256,2048]{1,0:T(8,128)(2,1)S(1)} custom-call(bf16[256,5120]{1,0:T(8,128)(2,1)S(1)} %copy-done.14, bf16[5120,2048]{1,0:T(8,128)(2,1)} %wq.3, bf16[1,128]{1,0:T(2,128)(2,1)S(1)} %bitcast.48, f32[256,128]{1,0:T(8,128)S(1)} %pad_maximum_fusion.1.cosine, f32[256,128]{1,0:T(8,128)S(1)} %pad_maximum_fusion.2.sine), custom_call_target="tpu_custom_call" | custom-call | flops 5368709120 | bytes 24641536 | tf_op jit(solution)/shard_map/queries/pallas_call | solution.py:147
  152.2 12.6 %queries.3 = bf16[256,2048]{1,0:T(8,128)(2,1)S(1)} custom-call(bf16[256,5120]{1,0:T(8,128)(2,1)S(1)} %copy-done.16, bf16[5120,2048]{1,0:T(8,128)(2,1)} %wq.3, bf16[1,128]{1,0:T(2,128)(2,1)S(1)} %bitcast.49, f32[256,128]{1,0:T(8,128)S(1)} %pad_maximum_fusion.3.cosine, f32[256,128]{1,0:T(8,128)S(1)} %pad_maximum_fusion.4.sine), custom_call_target="tpu_custom_call" | custom-call | flops 5368709120 | bytes 24641536 | tf_op jit(solution)/shard_map/queries/pallas_call | solution.py:147
  164.9 1.0 copy-done.8
  165.8 9.2 %all-gather.11.cloned.1.call-done.refs_2_.refs_4_.refs_0_ = bf16[8,2,8,32,512]{4,3,2,1,0:T(8,128)(2,1)} async-done(((bf16[1,2,8,32,512]{4,3,2,1,0:T(8,128)(2,1)}), bf16[8,2,8,32,512]{4,3,2,1,0:T(8,128)(2,1)}) %all-gather.11.cloned.1.call-update) | async-done | bytes 4194320 | tf_op jit(solution)/shard_map/all_gather | solution.py:429
  175.0 47.5 %all-gather.13.cloned.1.call-done.refs_3_.refs_5_.refs_1_ = bf16[8,2,8,32,512]{4,3,2,1,0:T(8,128)(2,1)} async-done(((bf16[1,2,8,32,512]{4,3,2,1,0:T(8,128)(2,1)}), bf16[8,2,8,32,512]{4,3,2,1,0:T(8,128)(2,1)}) %all-gather.13.cloned.1.call-update) | async-done | bytes 4194320 | tf_op jit(solution)/shard_map/all_gather | solution.py:429
  222.5 1.2 copy-done.9
  223.7 23.7 %attention.1 = bf16[8,64,2048]{2,1,0:T(8,128)(2,1)S(1)} custom-call(s32[66]{0:T(128)S(1)} %copy-done.19, bf16[8,32,2048]{2,1,0:T(8,128)(2,1)S(1)} %bitcast.38, bf16[8,32,2048]{2,1,0:T(8,128)(2,1)S(1)} %bitcast.39, bf16[8,2,8,32,512]{4,3,2,1,0:T(8,128)(2,1)} %all-gather.11.cloned.1.call-done.refs_2_.refs_4_.refs_0_, ...), custom_call_target="tpu_custom_call" | custom-call | flops 4724464128 | bytes 20971520 | tf_op jit(solution)/shard_map/attention/pallas_call | solution.py:242
  247.4 3.2 send_part.4
  250.7 1.5 collective-permute-start
  252.2 11.4 %own_part.1 = bf16[512,2560]{1,0:T(8,128)(2,1)S(1)} custom-call(s32[66]{0:T(128)S(1)} %copy-done.19, bf16[512,2048]{1,0:T(8,128)(2,1)S(1)} %bitcast.28, bf16[2048,5120]{1,0:T(8,128)(2,1)} %wo.9), custom_call_target="tpu_custom_call" | custom-call | flops 5368709120 | bytes 15204352 | tf_op jit(solution)/shard_map/own_part/pallas_call | solution.py:265
  263.6 1.5 copy-done
  265.1 7.3 %residual.4 = bf16[8,64,512]{2,1,0:T(8,128)(2,1)S(1)} custom-call(s32[66]{0:T(128)S(1)} %copy-done.19, bf16[8,32,2560]{2,1,0:T(8,128)(2,1)S(1)} %copy-done.1, bf16[8,32,2560]{2,1,0:T(8,128)(2,1)S(1)} %copy-done.2, bf16[8,64,2560]{2,1,0:T(8,128)(2,1)} %bitcast.32, bf16[8,64,512]{2,1,0:T(8,128)(2,1)S(1)} %bitcast.42), custom_call_target="tpu_custom_call" | custom-call | flops 786432 | bytes 2097152 | tf_op jit(solution)/shard_map/residual/pallas_call | solution.py:299
  273.2 4.1 all-to-all-start.2
  277.3 3.3 send_part.7
  280.6 1.3 collective-permute-start.3
  281.9 13.0 %collective-permute-done.3 = bf16[512,512]{1,0:T(8,128)(2,1)S(1)} collective-permute-done((bf16[512,512]{1,0:T(8,128)(2,1)S(1)}, bf16[512,512]{1,0:T(8,128)(2,1)S(1)}, u32[]{:S(2)}, u32[]{:S(2)}) %collective-permute-start.3) | collective-permute-done | bytes 524320 | tf_op jit(solution)/shard_map/ppermute | solution.py:455
  294.9 7.4 %residual.7 = bf16[8,64,512]{2,1,0:T(8,128)(2,1)S(1)} custom-call(s32[66]{0:T(128)S(1)} %copy-done.19, bf16[8,32,2560]{2,1,0:T(8,128)(2,1)S(1)} %copy-done.1, bf16[8,32,2560]{2,1,0:T(8,128)(2,1)S(1)} %copy-done.3, bf16[8,64,2560]{2,1,0:T(8,128)(2,1)} %bitcast.33, bf16[8,64,512]{2,1,0:T(8,128)(2,1)S(1)} %bitcast.43), custom_call_target="tpu_custom_call" | custom-call | flops 786432 | bytes 2097152 | tf_op jit(solution)/shard_map/residual/pallas_call | solution.py:299
  303.1 4.8 %all-to-all-start.5 = ((bf16[8,64,512]{2,1,0:T(8,128)(2,1)}), bf16[8,64,512]{2,1,0:T(8,128)(2,1)}, u32[]{:S(2)}, u32[]{:S(2)}) async-start(bf16[8,64,512]{2,1,0:T(8,128)(2,1)} %copy-done.17), calls=%async_computation.5 | async-start | bytes 1048576 | tf_op jit(solution)/shard_map/all_to_all | solution.py:465
  307.8 4.5 %send_part.5 = bf16[512,768]{1,0:T(8,128)(2,1)S(1)} custom-call(s32[66]{0:T(128)S(1)} %copy-done.19, bf16[512,2048]{1,0:T(8,128)(2,1)S(1)} %bitcast.30, bf16[2048,5120]{1,0:T(8,128)(2,1)} %wo.9), custom_call_target="tpu_custom_call" | custom-call | flops 1610612736 | bytes 6029312 | tf_op jit(solution)/shard_map/send_part/pallas_call | solution.py:265
  312.3 1.3 collective-permute-start.1
  313.6 18.7 %collective-permute-done.1 = bf16[512,768]{1,0:T(8,128)(2,1)S(1)} collective-permute-done((bf16[512,768]{1,0:T(8,128)(2,1)S(1)}, bf16[512,768]{1,0:T(8,128)(2,1)S(1)}, u32[]{:S(2)}, u32[]{:S(2)}) %collective-permute-start.1) | collective-permute-done | bytes 786464 | tf_op jit(solution)/shard_map/ppermute | solution.py:455
  332.3 10.7 %residual.5 = bf16[8,64,768]{2,1,0:T(8,128)(2,1)S(1)} custom-call(s32[66]{0:T(128)S(1)} %copy-done.19, bf16[8,32,2560]{2,1,0:T(8,128)(2,1)S(1)} %copy-done.1, bf16[8,32,2560]{2,1,0:T(8,128)(2,1)S(1)} %copy-done.4, bf16[8,64,2560]{2,1,0:T(8,128)(2,1)} %bitcast.34, bf16[8,64,768]{2,1,0:T(8,128)(2,1)S(1)} %bitcast.41), custom_call_target="tpu_custom_call" | custom-call | flops 1179648 | bytes 3145728 | tf_op jit(solution)/shard_map/residual/pallas_call | solution.py:299
  344.0 4.7 %all-to-all-start.3 = ((bf16[8,64,768]{2,1,0:T(8,128)(2,1)}), bf16[8,64,768]{2,1,0:T(8,128)(2,1)}, u32[]{:S(2)}, u32[]{:S(2)}) async-start(bf16[8,64,768]{2,1,0:T(8,128)(2,1)} %copy-done.10), calls=%async_computation.3 | async-start | bytes 1572864 | tf_op jit(solution)/shard_map/all_to_all | solution.py:465
  348.8 5.6 %send_part.6 = bf16[512,768]{1,0:T(8,128)(2,1)} custom-call(s32[66]{0:T(128)S(1)} %copy-done.19, bf16[512,2048]{1,0:T(8,128)(2,1)S(1)} %bitcast.31, bf16[2048,5120]{1,0:T(8,128)(2,1)} %wo.9), custom_call_target="tpu_custom_call" | custom-call | flops 1610612736 | bytes 6029312 | tf_op jit(solution)/shard_map/send_part/pallas_call | solution.py:265
  354.3 1.2 collective-permute-start.2
  355.5 2.7 pages.1
  358.2 1.0 copy-done.7
  359.2 18.8 %collective-permute-done.2 = bf16[512,768]{1,0:T(8,128)(2,1)S(1)} collective-permute-done((bf16[512,768]{1,0:T(8,128)(2,1)}, bf16[512,768]{1,0:T(8,128)(2,1)S(1)}, u32[]{:S(2)}, u32[]{:S(2)}) %collective-permute-start.2) | collective-permute-done | bytes 786464 | tf_op jit(solution)/shard_map/ppermute | solution.py:455
  378.0 12.6 %residual.6 = bf16[8,64,768]{2,1,0:T(8,128)(2,1)} custom-call(s32[66]{0:T(128)S(1)} %copy-done.19, bf16[8,32,2560]{2,1,0:T(8,128)(2,1)S(1)} %copy-done.1, bf16[8,32,2560]{2,1,0:T(8,128)(2,1)S(1)} %copy-done.5, bf16[8,64,2560]{2,1,0:T(8,128)(2,1)} %bitcast.35, bf16[8,64,768]{2,1,0:T(8,128)(2,1)S(1)} %bitcast.40), custom_call_target="tpu_custom_call" | custom-call | flops 1179648 | bytes 3145728 | tf_op jit(solution)/shard_map/residual/pallas_call | solution.py:299
  390.6 5.2 %all-to-all-start.4 = ((bf16[8,64,768]{2,1,0:T(8,128)(2,1)}), bf16[8,64,768]{2,1,0:T(8,128)(2,1)S(1)}, u32[]{:S(2)}, u32[]{:S(2)}) async-start(bf16[8,64,768]{2,1,0:T(8,128)(2,1)} %residual.6), calls=%async_computation.4 | async-start | bytes 1572864 | tf_op jit(solution)/shard_map/all_to_all | solution.py:465
  395.9 1.3 all-gather.15.cloned.1.call-done
  397.1 19.7 %all-to-all-done.4 = bf16[8,64,768]{2,1,0:T(8,128)(2,1)S(1)} async-done(((bf16[8,64,768]{2,1,0:T(8,128)(2,1)}), bf16[8,64,768]{2,1,0:T(8,128)(2,1)S(1)}, u32[]{:S(2)}, u32[]{:S(2)}) %all-to-all-start.4) | async-done | bytes 786464 | tf_op jit(solution)/shard_map/all_to_all | solution.py:465
  416.8 2.7 pad_maximum_fusion
  419.6 1.3 copy.21
  (65 shorter events, 5.0 us)
Async XLA Ops:
  7.2 84.5 %all-gather.7.cloned.1.call-start = ((), (), s32[]{:S(2)}) async-start(), calls=%async_computation.6 | async-start | bytes 3932160 | tf_op jit(solution)/shard_map/all_gather | solution.py:421
  47.6 38.4 %copy-start.23 = (bf16[2560]{0:T(1024)(128)(2,1)S(1)}, bf16[2560]{0:T(1024)(128)(2,1)}, u32[]{:S(2)}) copy-start(bf16[2560]{0:T(1024)(128)(2,1)} %param.13) | copy-start | bytes 15364
  47.6 78.7 %all-gather.9.cloned.1.call-start = ((), (), s32[]{:S(2)}) async-start(), calls=%async_computation.7 | async-start | bytes 3932160 | tf_op jit(solution)/shard_map/all_gather | solution.py:421
  47.7 44.0 %copy-start.20 = (bf16[128]{0:T(256)(128)(2,1)S(1)}, bf16[128]{0:T(256)(128)(2,1)}, u32[]{:S(2)}) copy-start(bf16[128]{0:T(256)(128)(2,1)} %param.18) | copy-start | bytes 772
  83.0 92.0 %all-gather.11.cloned.1.call-start = ((), (), s32[]{:S(2)}) async-start(), calls=%async_computation.8 | async-start | bytes 4718592 | tf_op jit(solution)/shard_map/all_gather | solution.py:429
  91.6 1.9 copy-start.12
  102.2 1.5 copy-start.13
  103.7 118.8 %all-gather.13.cloned.1.call-start = ((), (), s32[]{:S(2)}) async-start(), calls=%async_computation.9 | async-start | bytes 4718592 | tf_op jit(solution)/shard_map/all_gather | solution.py:429
  126.3 1.7 copy-start.11
  128.0 9.6 %copy-start.21 = (bf16[128]{0:T(256)(128)(2,1)S(1)}, bf16[128]{0:T(256)(128)(2,1)}, u32[]{:S(2)}) copy-start(bf16[128]{0:T(256)(128)(2,1)} %param.17) | copy-start | bytes 772
  136.2 1.5 copy-start.15
  137.7 1.7 copy-start.14
  139.4 12.8 %copy-start.16 = (bf16[256,5120]{1,0:T(8,128)(2,1)S(1)}, bf16[256,5120]{1,0:T(8,128)(2,1)}, u32[]{:S(2)}) copy-start(bf16[256,5120]{1,0:T(8,128)(2,1)} %copy-done.15) | copy-start | bytes 7864324
  152.2 70.2 %copy-start.19 = (s32[66]{0:T(128)S(1)}, s32[66]{0:T(128)}, u32[]{:S(2)}) copy-start(s32[66]{0:T(128)} %tables.1.table) | copy-start | bytes 796
  164.9 1.0 copy-start.8
  222.5 1.2 copy-start.9
  250.6 14.4 %copy-start.1 = (bf16[8,32,2560]{2,1,0:T(8,128)(2,1)S(1)}, bf16[8,32,2560]{2,1,0:T(8,128)(2,1)}, u32[]{:S(2)}) copy-start(bf16[8,32,2560]{2,1,0:T(8,128)(2,1)} %all_to_all.30.refs_0_) | copy-start | bytes 3932164
  250.6 14.4 %copy-start.2 = (bf16[8,32,2560]{2,1,0:T(8,128)(2,1)S(1)}, bf16[8,32,2560]{2,1,0:T(8,128)(2,1)}, u32[]{:S(2)}) copy-start(bf16[8,32,2560]{2,1,0:T(8,128)(2,1)} %all_to_all.31.refs_1_) | copy-start | bytes 3932164
  250.7 14.4 %collective-permute-start = (bf16[512,512]{1,0:T(8,128)(2,1)S(1)}, bf16[512,512]{1,0:T(8,128)(2,1)S(1)}, u32[]{:S(2)}, u32[]{:S(2)}) collective-permute-start(bf16[512,512]{1,0:T(8,128)(2,1)S(1)} %send_part.4), channel_id=1, source_target_pairs={{0,8},{8,0},{1,9},{9,1},{2,10},{10,2},{3,11},{11,3},{4,12},{12,4},... | collective-permute-start | bytes 1572872 | tf_op jit(solution)/shard_map/ppermute | solution.py:455
  263.6 1.5 copy-start
  272.4 0.8 copy-start.18
  273.2 29.9 %all-to-all-start.2 = ((bf16[8,64,512]{2,1,0:T(8,128)(2,1)}), bf16[8,64,512]{2,1,0:T(8,128)(2,1)}, u32[]{:S(2)}, u32[]{:S(2)}) async-start(bf16[8,64,512]{2,1,0:T(8,128)(2,1)} %copy-done.18), calls=%async_computation.2 | async-start | bytes 1048576 | tf_op jit(solution)/shard_map/all_to_all | solution.py:465
  277.3 17.5 %copy-start.3 = (bf16[8,32,2560]{2,1,0:T(8,128)(2,1)S(1)}, bf16[8,32,2560]{2,1,0:T(8,128)(2,1)}, u32[]{:S(2)}) copy-start(bf16[8,32,2560]{2,1,0:T(8,128)(2,1)} %all_to_all.31.refs_1_) | copy-start | bytes 3932164
  280.6 14.3 %collective-permute-start.3 = (bf16[512,512]{1,0:T(8,128)(2,1)S(1)}, bf16[512,512]{1,0:T(8,128)(2,1)S(1)}, u32[]{:S(2)}, u32[]{:S(2)}) collective-permute-start(bf16[512,512]{1,0:T(8,128)(2,1)S(1)} %send_part.7), channel_id=1, source_target_pairs={{0,8},{8,0},{1,9},{9,1},{2,10},{10,2},{3,11},{11,3},{4,12},{12,4},... | collective-permute-start | bytes 1572872 | tf_op jit(solution)/shard_map/ppermute | solution.py:455
  302.3 0.8 copy-start.17
  303.1 40.9 %all-to-all-start.5 = ((bf16[8,64,512]{2,1,0:T(8,128)(2,1)}), bf16[8,64,512]{2,1,0:T(8,128)(2,1)}, u32[]{:S(2)}, u32[]{:S(2)}) async-start(bf16[8,64,512]{2,1,0:T(8,128)(2,1)} %copy-done.17), calls=%async_computation.5 | async-start | bytes 1048576 | tf_op jit(solution)/shard_map/all_to_all | solution.py:465
  307.8 24.5 %copy-start.4 = (bf16[8,32,2560]{2,1,0:T(8,128)(2,1)S(1)}, bf16[8,32,2560]{2,1,0:T(8,128)(2,1)}, u32[]{:S(2)}) copy-start(bf16[8,32,2560]{2,1,0:T(8,128)(2,1)} %all_to_all.31.refs_1_) | copy-start | bytes 3932164
  312.3 20.0 %collective-permute-start.1 = (bf16[512,768]{1,0:T(8,128)(2,1)S(1)}, bf16[512,768]{1,0:T(8,128)(2,1)S(1)}, u32[]{:S(2)}, u32[]{:S(2)}) collective-permute-start(bf16[512,768]{1,0:T(8,128)(2,1)S(1)} %send_part.5), channel_id=1, source_target_pairs={{0,8},{8,0},{1,9},{9,1},{2,10},{10,2},{3,11},{11,3},{4,12},{12,4},... | collective-permute-start | bytes 2359304 | tf_op jit(solution)/shard_map/ppermute | solution.py:455
  343.1 0.9 copy-start.10
  344.0 46.7 %all-to-all-start.3 = ((bf16[8,64,768]{2,1,0:T(8,128)(2,1)}), bf16[8,64,768]{2,1,0:T(8,128)(2,1)}, u32[]{:S(2)}, u32[]{:S(2)}) async-start(bf16[8,64,768]{2,1,0:T(8,128)(2,1)} %copy-done.10), calls=%async_computation.3 | async-start | bytes 1572864 | tf_op jit(solution)/shard_map/all_to_all | solution.py:465
  348.7 48.4 %all-gather.15.cloned.1.call-start = ((), (), s32[]{:S(2)}) async-start(), calls=%async_computation.10 | async-start | bytes 3145728 | tf_op jit(solution)/shard_map/all_gather | solution.py:442
  348.7 6.8 %copy-start.6 = (bf16[8,2,8,32,512]{4,3,2,1,0:T(8,128)(2,1)S(1)}, bf16[8,2,8,32,512]{4,3,2,1,0:T(8,128)(2,1)}, u32[]{:S(2)}) copy-start(bf16[8,2,8,32,512]{4,3,2,1,0:T(8,128)(2,1)} %all-gather.11.cloned.1.call-done.refs_2_.refs_4_.refs_0_) | copy-start | bytes 12582916
  354.3 23.7 %copy-start.5 = (bf16[8,32,2560]{2,1,0:T(8,128)(2,1)S(1)}, bf16[8,32,2560]{2,1,0:T(8,128)(2,1)}, u32[]{:S(2)}) copy-start(bf16[8,32,2560]{2,1,0:T(8,128)(2,1)} %all_to_all.31.refs_1_) | copy-start | bytes 3932164
  354.3 23.7 %collective-permute-start.2 = (bf16[512,768]{1,0:T(8,128)(2,1)}, bf16[512,768]{1,0:T(8,128)(2,1)S(1)}, u32[]{:S(2)}, u32[]{:S(2)}) collective-permute-start(bf16[512,768]{1,0:T(8,128)(2,1)} %send_part.6), channel_id=1, source_target_pairs={{0,8},{8,0},{1,9},{9,1},{2,10},{10,2},{3,11},{11,3},{4,12},{12,4},... | collective-permute-start | bytes 2359304 | tf_op jit(solution)/shard_map/ppermute | solution.py:455
  358.2 1.0 copy-start.7
  390.6 26.2 %all-to-all-start.4 = ((bf16[8,64,768]{2,1,0:T(8,128)(2,1)}), bf16[8,64,768]{2,1,0:T(8,128)(2,1)S(1)}, u32[]{:S(2)}, u32[]{:S(2)}) async-start(bf16[8,64,768]{2,1,0:T(8,128)(2,1)} %residual.6), calls=%async_computation.4 | async-start | bytes 1572864 | tf_op jit(solution)/shard_map/all_to_all | solution.py:465
  397.1 22.4 %copy-start.22 = (bf16[4,2,128,1024]{3,2,1,0:T(8,128)(2,1)S(1)}, bf16[4,2,128,1024]{3,2,1,0:T(8,128)(2,1)}, u32[]{:S(2)}) copy-start(bf16[4,2,128,1024]{3,2,1,0:T(8,128)(2,1)} %all-gather.15.cloned.1.call-done) | copy-start | bytes 6291460
Sparse Core Ops, SparseCore 0:
  47.7 37.9 all-gather.6
  87.2 39.0 all-gather.8
  127.9 47.0 all-gather.10
  176.4 45.9 all-gather.12
  359.3 37.7 all-gather.14

commit v2 on v1

v2 whole, which is shorter than its diff:
```python
import functools
import math

import jax
import jax.numpy as jnp
from jax import lax
from jax.experimental import pallas as pl
from jax.experimental.pallas import tpu as pltpu
from jax.sharding import PartitionSpec as P

PAGE_ROWS = 128
epsilon = 1e-06
rope_base = 1000000.0
very_negative = -1e30
VMEM_BYTES = 48 * 1024 * 1024
PARTS = 2
CORES = 2


def params():
    return pltpu.CompilerParams(vmem_limit_bytes=VMEM_BYTES)


def cost(flops, moved, transcendentals=0):
    return pl.CostEstimate(
        flops=int(flops), bytes_accessed=int(moved), transcendentals=int(transcendentals)
    )


def hop_order(chips):
    return [0, 1, chips - 1] + list(range(2, chips - 1)) if chips > 2 else list(range(chips))


class Layout:
    def __init__(self, spans, pages, owners):
        self.chips = owners // CORES
        self.span_at = 0
        self.earlier_at = self.span_at + spans
        self.target_at = self.earlier_at + spans
        self.page = self.target_at + spans
        self.origin = self.page + pages
        self.group_rank = self.origin + owners * spans
        self.tensor_rank = self.group_rank + 1
        self.length = self.tensor_rank + 1


def tables_kernel(lay, spans, pages, ranks, prompt_spans, source, target, page_slot, out, span_of, start_of):
    chips = lay.chips
    group_rank = ranks[0]
    out[lay.group_rank] = group_rank
    out[lay.tensor_rank] = ranks[1]
    for k in range(spans):
        start = jnp.int32(0)
        begin = jnp.int32(0)
        for p in range(prompt_spans.shape[0]):
            start = jnp.where(begin <= k, begin, start)
            begin = begin + prompt_spans[p]
        start_of[k] = start
        span_of[source[k]] = jnp.int32(k)
    for p in range(pages):
        out[lay.page + page_slot[p]] = jnp.int32(p)
    chip, core = lax.div(group_rank, CORES), lax.rem(group_rank, CORES)
    hops = hop_order(chips)
    for back in range(chips):
        for other in range(CORES):
            at_chip = lax.rem(chip + chips - back, chips)
            at_core = jnp.where(other == 0, core, 1 - core)
            for n, hop in enumerate(hops):
                for flip in range(CORES):
                    from_chip = lax.rem(at_chip + chips - hop, chips)
                    from_core = jnp.where(flip == 0, at_core, 1 - at_core)
                    k = span_of[from_chip * CORES + from_core]
                    place = n * CORES + flip
                    out[lay.origin + (back * CORES + other) * spans + place] = k
                    if back == 0 and other == 0:
                        out[lay.span_at + place] = k
                        out[lay.earlier_at + place] = k - start_of[k]
                        out[lay.target_at + place] = target[k]


def make_tables(lay, spans, pages, ranks, prompt_spans, source, target, page_slot):
    smem = pl.BlockSpec(memory_space=pltpu.SMEM)
    return pl.pallas_call(
        functools.partial(tables_kernel, lay, spans, pages),
        out_shape=jax.ShapeDtypeStruct((lay.length,), jnp.int32),
        in_specs=[smem] * 5,
        out_specs=smem,
        scratch_shapes=[pltpu.SMEM((spans,), jnp.int32)] * 2,
        name="tables",
    )(ranks, prompt_spans, source, target, page_slot)


def head_norm_rope(u, gain, cosine, sine):
    mean_sq = jnp.mean(u * u, axis=-1, keepdims=True)
    u = u * lax.rsqrt(mean_sq + epsilon) * gain
    half = u.shape[-1] // 2
    return u * cosine + pltpu.roll(u, half, 1) * sine


def half_index(lay, sides, side):
    if sides == 1:
        return lambda t: 0
    if side == 0:
        return lambda t: t[lay.tensor_rank]
    return lambda t: 1 - t[lay.tensor_rank]


def summed_dot(lefts, rights):
    total = None
    for left, right in zip(lefts, rights):
        term = jnp.dot(left[...], right[...], preferred_element_type=jnp.float32)
        total = term if total is None else total + term
    return total


def kv_kernel(sides, blocks, table, *refs):
    refs = list(refs)
    take = lambda n: [refs.pop(0) for _ in range(n)]
    xs = [take(blocks) for _ in range(sides)]
    gains, wks, wvs = take(sides), take(sides), take(sides)
    kgain, cosine, sine = take(3)
    normed, (kv,) = take(sides), take(1)
    head = kgain.shape[1]
    width = sum(x[0].shape[1] for x in xs)

    @pl.when(pl.program_id(0) == 0)
    def _():
        at = 0
        for b in range(blocks):
            wide = [x[b][...].astype(jnp.float32) for x in xs]
            total = sum(jnp.sum(w * w, axis=-1, keepdims=True) for w in wide)
            factor = lax.rsqrt(total / width + epsilon)
            rows = xs[0][b].shape[0]
            for w, gain, to in zip(wide, gains, normed):
                to[at : at + rows] = (w * factor * gain[...].astype(jnp.float32)).astype(
                    jnp.bfloat16
                )
            at += rows

    keys = summed_dot(normed, wks).astype(jnp.bfloat16)
    gains = kgain[...].astype(jnp.float32)
    for h in range(keys.shape[1] // head):
        u = keys[:, h * head : (h + 1) * head].astype(jnp.float32)
        kv[0, :, h * head : (h + 1) * head] = head_norm_rope(
            u, gains, cosine[...], sine[...]
        ).astype(jnp.bfloat16)
    kv[1] = summed_dot(normed, wvs).astype(jnp.bfloat16)


def make_kv(lay, table, xs, gains, wk, wv, kgain, cosine, sine, part):
    sides, blocks = len(xs), len(xs[0])
    rows = sum(x.shape[0] for x in xs[0])
    widths = [x[0].shape[1] for x in xs]
    width, cols = wk.shape
    tile = 256 if cols % 256 == 0 else cols
    head = kgain.shape[1]
    fixed = lambda n, t: (0, 0)
    here = lambda n, t: (part, 0)
    weights = []
    for side in range(sides):
        index = half_index(lay, sides, side)
        weights.append(
            pl.BlockSpec((widths[side], tile), lambda n, t, index=index: (index(t), n))
        )
    return pl.pallas_call(
        functools.partial(kv_kernel, sides, blocks),
        grid_spec=pltpu.PrefetchScalarGridSpec(
            num_scalar_prefetch=1,
            grid=(cols // tile,),
            in_specs=[pl.BlockSpec(x.shape, fixed) for side in xs for x in side]
            + [pl.BlockSpec((1, w), fixed) for w in widths]
            + weights
            + weights
            + [
                pl.BlockSpec((1, head), fixed),
                pl.BlockSpec((rows, head), here),
                pl.BlockSpec((rows, head), here),
            ],
            out_specs=[pl.BlockSpec((rows, w), fixed) for w in widths]
            + [pl.BlockSpec((2, rows, tile), lambda n, t: (0, 0, n))],
        ),
        out_shape=[jax.ShapeDtypeStruct((rows, w), jnp.bfloat16) for w in widths]
        + [jax.ShapeDtypeStruct((2, rows, cols), jnp.bfloat16)],
        compiler_params=params(),
        cost_estimate=cost(4 * rows * width * cols, 4 * width * cols + 4 * rows * width),
        name="keys_values",
    )(
        table, *[x for side in xs for x in side], *gains, *[wk] * sides, *[wv] * sides,
        kgain, cosine, sine,
    )


def q_kernel(sides, table, *refs):
    normed, wqs = refs[:sides], refs[sides : 2 * sides]
    qgain, cosine, sine, out = refs[2 * sides :]
    head = qgain.shape[1]
    lin = summed_dot(normed, wqs)
    gains = qgain[...].astype(jnp.float32)
    for h in range(lin.shape[1] // head):
        out[:, h * head : (h + 1) * head] = head_norm_rope(
            lin[:, h * head : (h + 1) * head], gains, cosine[...], sine[...]
        ).astype(jnp.bfloat16)


def make_q(lay, table, normed, wq, qgain, cosine, sine, part):
    sides = len(normed)
    rows = normed[0].shape[0]
    width, cols = wq.shape
    tile = 512 if cols % 512 == 0 else cols
    head = qgain.shape[1]
    fixed = lambda n, t: (0, 0)
    here = lambda n, t: (part, 0)
    weights = []
    for side in range(sides):
        index = half_index(lay, sides, side)
        weights.append(
            pl.BlockSpec(
                (normed[side].shape[1], tile), lambda n, t, index=index: (index(t), n)
            )
        )
    return pl.pallas_call(
        functools.partial(q_kernel, sides),
        grid_spec=pltpu.PrefetchScalarGridSpec(
            num_scalar_prefetch=1,
            grid=(cols // tile,),
            in_specs=[pl.BlockSpec(x.shape, fixed) for x in normed]
            + weights
            + [
                pl.BlockSpec((1, head), fixed),
                pl.BlockSpec((rows, head), here),
                pl.BlockSpec((rows, head), here),
            ],
            out_specs=pl.BlockSpec((rows, tile), lambda n, t: (0, n)),
        ),
        out_shape=jax.ShapeDtypeStruct((rows, cols), jnp.bfloat16),
        compiler_params=params(),
        cost_estimate=cost(2 * rows * width * cols, 2 * width * cols + 2 * rows * (width + cols)),
        name="queries",
    )(table, *normed, *[wq] * sides, qgain, cosine, sine)


def attention_kernel(lay, spans, most, per_kv, head, owners, pages_each, table, *refs):
    q_refs = refs[:PARTS]
    kv_refs = refs[PARTS : PARTS + owners * PARTS]
    out, pages, keys, values = refs[PARTS + owners * PARTS :]
    chips = lay.chips
    here, rows = kv_refs[0].shape[1], kv_refs[0].shape[2]
    group_rank = table[lay.group_rank]
    chip, core = lax.div(group_rank, CORES), lax.rem(group_rank, CORES)
    for o in range(owners):
        back, other = o // CORES, o % CORES
        owner = lax.rem(chip + chips - back, chips) * CORES + (core if other == 0 else 1 - core)
        at = pl.ds(pl.multiple_of(owner * rows, rows), rows)
        for p in range(PARTS):
            for i in range(here):
                k = table[lay.origin + o * spans + p * here + i]
                keys[k, at] = kv_refs[o * PARTS + p][0, i]
                values[k, at] = kv_refs[o * PARTS + p][1, i]

    for i in range(pages_each):
        page = table[lay.page + group_rank * pages_each + i]
        k = lax.div(page, pages_each)
        at = pl.ds(pl.multiple_of(lax.rem(page, pages_each) * PAGE_ROWS, PAGE_ROWS), PAGE_ROWS)
        pages[i, 0] = keys[k, at]
        pages[i, 1] = values[k, at]

    scale = (1.0 / math.sqrt(head)) * math.log2(math.e)
    q_rows, k_rows = per_kv * rows, owners * rows
    row = lax.broadcasted_iota(jnp.int32, (q_rows, k_rows), 0)
    col = lax.broadcasted_iota(jnp.int32, (q_rows, k_rows), 1)
    allowed = col <= group_rank * rows + row % rows

    def one_place(p, i, carry):
        k = table[lay.span_at + p * here + i]
        earlier = table[lay.earlier_at + p * here + i]
        queries = jnp.concatenate(
            [q_refs[p][i, :, g * head : (g + 1) * head] for g in range(per_kv)], axis=0
        )

        def with_earlier(count):
            scores = []
            for back in range(count + 1):
                s = lax.dot_general(
                    queries, keys[k - back], (((1,), (1,)), ((), ())),
                    preferred_element_type=jnp.float32,
                )
                if back == 0:
                    s = jnp.where(allowed, s, very_negative)
                scores.append(s)
            best = scores[0]
            for s in scores[1:]:
                best = jnp.maximum(best, s)
            best = jnp.max(best, axis=-1, keepdims=True)
            total = None
            summed = None
            for back, s in enumerate(scores):
                w = jnp.exp2((s - best) * scale)
                part = jnp.sum(w, axis=-1, keepdims=True)
                term = jnp.dot(
                    w.astype(jnp.bfloat16), values[k - back], preferred_element_type=jnp.float32
                )
                total = part if total is None else total + part
                summed = term if summed is None else summed + term
            result = (summed / total).astype(jnp.bfloat16)
            for g in range(per_kv):
                out[p * here + i, :, g * head : (g + 1) * head] = result[
                    g * rows : (g + 1) * rows
                ]

        for count in range(most):
            pl.when(earlier == count)(functools.partial(with_earlier, count))
        return carry

    for p in range(PARTS):
        lax.fori_loop(0, here, functools.partial(one_place, p), 0)


def make_attention(lay, most, table, queries, gathered, per_kv, head, pages_each):
    here, rows, cols = queries[0].shape
    spans = here * PARTS
    owners = len(gathered)
    own_kv = cols // (per_kv * head)
    q_spec = pl.BlockSpec((here, rows, per_kv * head), lambda h, t: (0, 0, h))
    kv_spec = pl.BlockSpec((2, here, rows, head), lambda h, t: (0, 0, 0, h))
    flat = [x for origin in gathered for x in origin]
    all_rows = spans * rows
    pairs = 2.2 * all_rows * owners * rows * per_kv * own_kv
    return pl.pallas_call(
        functools.partial(
            attention_kernel, lay, spans, most, per_kv, head, owners, pages_each
        ),
        grid_spec=pltpu.PrefetchScalarGridSpec(
            num_scalar_prefetch=1,
            grid=(own_kv,),
            in_specs=[q_spec] * PARTS + [kv_spec] * len(flat),
            out_specs=[
                pl.BlockSpec((spans, rows, per_kv * head), lambda h, t: (0, 0, h)),
                pl.BlockSpec((pages_each, 2, PAGE_ROWS, head), lambda h, t: (0, 0, 0, h)),
            ],
            scratch_shapes=[pltpu.VMEM((spans, owners * rows, head), jnp.bfloat16)] * 2,
        ),
        out_shape=[
            jax.ShapeDtypeStruct((spans, rows, cols), jnp.bfloat16),
            jax.ShapeDtypeStruct((pages_each, 2, PAGE_ROWS, own_kv * head), jnp.bfloat16),
        ],
        compiler_params=params(),
        cost_estimate=cost(
            4 * pairs * head, 4 * all_rows * cols + 2 * len(flat) * flat[0].size, pairs
        ),
        name="attention",
    )(table, *queries, *flat)


def project_kernel(table, attended, wo, *refs):
    refs[-1][...] = jnp.dot(
        attended[...], wo[...], preferred_element_type=jnp.float32
    ).astype(jnp.bfloat16)


def make_projection(lay, table, attended, wo, first, count, tile, name, after=()):
    rows, depth = attended.shape
    return pl.pallas_call(
        project_kernel,
        grid_spec=pltpu.PrefetchScalarGridSpec(
            num_scalar_prefetch=1,
            grid=(count,),
            in_specs=[
                pl.BlockSpec((rows, depth), lambda n, t: (0, 0)),
                pl.BlockSpec((depth, tile), lambda n, t: (0, first(t[lay.tensor_rank]) + n)),
            ]
            + [pl.BlockSpec(memory_space=pl.ANY)] * len(after),
            out_specs=pl.BlockSpec((rows, tile), lambda n, t: (0, n)),
        ),
        out_shape=jax.ShapeDtypeStruct((rows, count * tile), jnp.bfloat16),
        compiler_params=params(),
        cost_estimate=cost(
            2 * rows * depth * count * tile, 2 * (rows * depth + (rows + depth) * count * tile)
        ),
        name=name,
    )(table, attended, wo, *after)


def add_kernel(lay, table, *refs):
    x_refs, own, received, out = refs[:-3], refs[-3], refs[-2], refs[-1]
    for place, x in enumerate(x_refs):
        summed = own[place].astype(jnp.float32) + received[place].astype(jnp.float32)
        out[table[lay.target_at + place]] = (x[...].astype(jnp.float32) + summed).astype(
            jnp.bfloat16
        )


def make_sum(lay, table, arrived, own, received, first):
    spans, rows, cols = received.shape
    unit = math.gcd(first, cols) if first else cols
    steps, start = cols // unit, first // unit
    return pl.pallas_call(
        functools.partial(add_kernel, lay),
        grid_spec=pltpu.PrefetchScalarGridSpec(
            num_scalar_prefetch=1,
            grid=(steps,),
            in_specs=[pl.BlockSpec((rows, unit), lambda n, t: (0, start + n))] * spans
            + [
                pl.BlockSpec((spans, rows, unit), lambda n, t: (0, 0, start + n)),
                pl.BlockSpec((spans, rows, unit), lambda n, t: (0, 0, n)),
            ],
            out_specs=pl.BlockSpec((spans, rows, unit), lambda n, t: (0, 0, n)),
        ),
        out_shape=jax.ShapeDtypeStruct((spans, rows, cols), jnp.bfloat16),
        compiler_params=params(),
        cost_estimate=cost(3 * spans * rows * cols, 8 * spans * rows * cols),
        name="residual",
    )(table, *arrived, own, received)


def rope_tables(earlier, span_len, first_row, rows, head):
    half = head // 2
    freqs = jnp.power(
        jnp.float32(rope_base), -jnp.arange(half, dtype=jnp.float32) * 2.0 / head
    )
    at = earlier[:, None] * span_len + first_row + jnp.arange(rows, dtype=jnp.int32)[None, :]
    angles = at.reshape(-1).astype(jnp.float32)[:, None] * freqs[None, :]
    cosine, sine = jnp.cos(angles), jnp.sin(angles)
    return (
        jnp.concatenate([cosine, cosine], axis=1),
        jnp.concatenate([-sine, sine], axis=1),
    )


def widths_of(tiles):
    return [1, 2, 1, 1] if tiles == 5 else [1, tiles - 1]


def shift(x, owners, hop, flip):
    chips = owners // CORES
    pairs = [
        (z * CORES + c, (z + hop) % chips * CORES + (c ^ flip))
        for z in range(chips)
        for c in range(CORES)
    ]
    return lax.ppermute(x, "group", pairs)


def local(
    hidden_in, ln_gain, wq, wk, wv, q_gain, key_norm_gain, wo,
    prompt_spans, span_source, span_target, page_slot,
):
    _, span_len, cols = hidden_in.shape
    tensor_size = lax.axis_size("tensor")
    owners = lax.axis_size("group")
    tensor_rank = lax.axis_index("tensor")
    group_rank = lax.axis_index("group")
    chips = owners // CORES
    head = q_gain.shape[0]
    rows = span_len // owners
    pages_each = span_len // PAGE_ROWS
    spans = span_source.shape[0]
    here = spans // PARTS
    most = min(spans - (prompt_spans.shape[0] - 1), spans // 2)
    kv_cols = wk.shape[1]
    paired = tensor_size == 2
    swap = [(0, 1), (1, 0)]
    lay = Layout(spans, spans * pages_each, owners)

    if kv_cols < head:
        share = head // kv_cols
        sets = [list(range(i, i + share)) for i in range(0, tensor_size, share)]
        wk, wv = [
            lax.all_gather(w, "tensor", axis=1, tiled=True, axis_index_groups=sets)
            for w in (wk, wv)
        ]
    per_kv = wq.shape[1] // max(head, wk.shape[1])

    chip, core = group_rank // CORES, group_rank % CORES
    split = hidden_in.reshape(owners, rows, cols)
    arrived = []
    for hop in hop_order(chips):
        for flip in range(CORES):
            to = (chip + hop) % chips * CORES + (core + flip) % CORES
            block = lax.dynamic_index_in_dim(split, to, 0, keepdims=False)
            if hop or flip:
                block = shift(block, owners, hop, flip)
            arrived.append(block)

    ranks = jnp.stack([group_rank, tensor_rank]).astype(jnp.int32)
    table = make_tables(
        lay, spans, spans * pages_each, ranks, prompt_spans, span_source, span_target, page_slot
    )
    earlier = table[lay.earlier_at : lay.earlier_at + spans]
    cosine, sine = rope_tables(earlier, span_len, group_rank * rows, rows, head)

    if paired:
        gain = ln_gain[None]
        gains = [gain, lax.ppermute(gain, "tensor", swap)]
        crossed = [lax.ppermute(block, "tensor", swap) for block in arrived]
    else:
        gains = [lax.all_gather(ln_gain, "tensor", axis=0, tiled=True)[None]]

    queries, normed, gathered = [], [], [[] for _ in range(owners)]
    for p in range(PARTS):
        at = slice(p * here, (p + 1) * here)
        if paired:
            xs = [arrived[at], crossed[at]]
        else:
            xs = [[lax.all_gather(jnp.concatenate(arrived[at]), "tensor", axis=1, tiled=True)]]
        *rows_normed, kv = make_kv(
            lay, table, xs, gains, wk, wv, key_norm_gain[None], cosine, sine, p
        )
        normed.append(rows_normed)
        kv = kv.reshape(2, here, rows, kv.shape[2])
        for back in range(chips):
            if back:
                kv = shift(kv, owners, 1, 0)
            gathered[back * CORES].append(kv)
            gathered[back * CORES + 1].append(shift(kv, owners, 0, 1))
    for p in range(PARTS):
        made = make_q(lay, table, normed[p], wq, q_gain[None], cosine, sine, p)
        queries.append(made.reshape(here, rows, made.shape[1]))

    attended, pages = make_attention(
        lay, most, table, queries, gathered, per_kv, head, pages_each
    )
    attended = attended.reshape(spans * rows, -1)

    if paired:
        tile = 512
        half_tiles = cols // tile
        widths = widths_of(half_tiles)
        received, first, last = [], 0, ()
        for width in widths:
            partial = make_projection(
                lay, table, attended, wo,
                lambda r, first=first: (1 - r) * half_tiles + first, width, tile, "send_part",
                last,
            )
            last = (partial,)
            received.append(lax.ppermute(partial, "tensor", swap).reshape(spans, rows, -1))
            first += width
        own = make_projection(
            lay, table, attended, wo, lambda r: r * half_tiles, half_tiles, tile, "own_part", last
        ).reshape(spans, rows, cols)
        pages, received[-2] = lax.optimization_barrier((pages, received[-2]))
        other = lax.ppermute(pages, "tensor", swap)
        cache = jnp.concatenate(
            [jnp.where(tensor_rank == 0, pages, other), jnp.where(tensor_rank == 0, other, pages)],
            axis=3,
        )
        pieces, first = [], 0
        for got in received:
            moved = make_sum(lay, table, arrived, own, got, first)
            pieces.append(
                lax.all_to_all(moved, "group", split_axis=0, concat_axis=0, tiled=True)
            )
            first += got.shape[2]
        mixed = jnp.concatenate(pieces, axis=2).reshape(1, span_len, cols)
    else:
        if kv_cols < head:
            pages = lax.dynamic_slice_in_dim(
                pages, lax.rem(tensor_rank, head // kv_cols) * kv_cols, kv_cols, 3
            )
        cache = lax.all_gather(pages, "tensor", axis=3, tiled=True)
        partial = jnp.dot(attended, wo, preferred_element_type=jnp.float32)
        summed = lax.psum_scatter(
            partial.astype(jnp.bfloat16), "tensor", scatter_dimension=1, tiled=True
        )
        summed = summed.reshape(spans, rows, cols).astype(jnp.float32)
        moved = (jnp.stack(arrived).astype(jnp.float32) + summed).astype(jnp.bfloat16)
        targets = table[lay.target_at : lay.target_at + spans]
        moved = jnp.zeros_like(moved).at[targets].set(moved, unique_indices=True)
        moved = lax.all_to_all(moved, "group", split_axis=0, concat_axis=0, tiled=True)
        mixed = moved.reshape(1, span_len, cols)
    return (mixed, cache)


def solution(mesh):
    in_specs = (
        P(("replica", "group"), None, "tensor"),
        P("tensor"),
        P(None, "tensor"),
        P(None, "tensor"),
        P(None, "tensor"),
        P(),
        P(),
        P("tensor", None),
        P("replica"),
        P("replica"),
        P("replica"),
        P("replica"),
    )
    out_specs = (P(("replica", "group"), None, "tensor"), P(("replica", "group"), None, None, None))
    return jax.shard_map(local, mesh=mesh, in_specs=in_specs, out_specs=out_specs, check_vma=False)
```

time: 433 us -> 370 us (0.85); the launches traced: 427 us -> 369 us
  blocking collectives: 78.2 us -> 0 us
  starting transfers between devices: 24.6 us -> 62.7 us
  waiting for transfers between devices: 150 us -> 185 us
  Pallas kernels: 136 us -> 102 us
  between operations: 14.1 us -> 0.91 us
  local copies, waits for them, and re-layouts: 18.8 us -> 11.1 us
    ppermute x4 -> x35, waiting for transfers between devices: 50.5 us -> 185 us  [the longest x21 88.4 us: shift(): return lax.ppermute(x, 'group', pairs)]
    all_gather x5 -> x0, waiting for transfers between devices: 80.1 us -> none  [the longest x2 56.6 us: local(): gathered.append(lax.all_gather(kv, 'group', axis=0, tiled=False))]
    all_to_all x2 -> x0, blocking collectives: 73.8 us -> none  [local(): lax.all_to_all(split[:, c], 'group', split_axis=0, concat_axis=0, tiled=T...]
    ppermute x4 -> x35, starting transfers between devices: 5.29 us -> 43.8 us  [the longest x21 29.8 us: shift(): return lax.ppermute(x, 'group', pairs)]
    pallas_call x9 -> x8, Pallas kernels: 82.9 us -> 50 us  [the longest x2 22.7 us: make_q(): pl.pallas_call(functools.partial(q_kernel, sides), grid_spec=pltpu.Prefet...]
    all_to_all x4, waiting for transfers between devices: 19.7 us -> 0.01 us  [local(): lax.all_to_all(moved, 'group', split_axis=0, concat_axis=0, tiled=True)]
    unnamed x50 -> x32, local copies, waits for them, and re-layouts: 16.8 us -> 7.56 us
    all_gather x1 -> x0, blocking collectives: 4.39 us -> none  [local(): gain = lax.all_gather(ln_gain, 'tensor', axis=0, tiled=True)[None]]
  transfers between devices with their start and end apart: 13 -> 39, of which waited for: 8 -> 18; matrix products, arithmetic and copies ran while one was open for 1% -> 2% of each run, Pallas kernels for 24% -> 19%
where the time goes in v2:
time: 370 us; the launch traced here: 369 us
  waiting for transfers between devices  185 us (50%)
  Pallas kernels  102 us (28%)
  starting transfers between devices  62.7 us (17%)
  local copies, waits for them, and re-layouts  11.1 us (3%)
  other arithmetic  8.13 us (2%)
    ppermute x21, waiting for transfers between devices, shift(): return lax.ppermute(x, 'group', pairs)  88.4 us
    ppermute x4, waiting for transfers between devices, local(): lax.ppermute(partial, 'tensor', swap).reshape(spans, rows, -1)  40.3 us
    ppermute x8, waiting for transfers between devices, local(): crossed = [lax.ppermute(block, 'tensor', swap) for block in arrived]  31.1 us
    ppermute x21, starting transfers between devices, shift(): return lax.ppermute(x, 'group', pairs)  29.8 us
    pallas_call x1, Pallas kernels, make_attention(): pl.pallas_call(functools.partial(attention_kernel, lay, spans, most, per_...  26.1 us
    ppermute x1, waiting for transfers between devices, local(): other = lax.ppermute(pages, 'tensor', swap)  24.7 us
    pallas_call x5, Pallas kernels, make_projection(): pl.pallas_call(project_kernel, grid_spec=pltpu.PrefetchScalarGridSpec(num...  24 us
    pallas_call x2, Pallas kernels, make_q(): pl.pallas_call(functools.partial(q_kernel, sides), grid_spec=pltpu.Prefet...  22.7 us
  transfers between devices with their start and end apart: 39, of which 18 were waited for; matrix products, arithmetic and copies ran while one was open for 2% of the time, Pallas kernels for 19%

profile of v2, /device:TPU:0, one launch (start us, length us, event | category | flops | bytes accessed | tf_op | source)
XLA Modules:
  0.0 369.0 jit_solution(17160674805366269097)
XLA Ops:
  1.3 2.9 collective-permute-start.11
  4.3 2.7 dynamic-slice_bitcast_fusion
  7.0 1.7 collective-permute-start.6
  9.6 3.3 collective-permute-start.4
  15.7 16.0 %collective-permute-done.6.refs_3_.refs_7_ = bf16[64,2560]{1,0:T(8,128)(2,1)S(1)} collective-permute-done((bf16[64,2560]{1,0:T(8,128)(2,1)S(1)}, bf16[64,2560]{1,0:T(8,128)(2,1)S(1)}, u32[]{:S(2)}, u32[]{:S(2)}) %collective-permute-start.6) | collective-permute-done | bytes 327712 | tf_op jit(solution)/shard_map/ppermute | solution.py:440
  32.2 21.1 %collective-permute-done.5.refs_2_.refs_6_ = bf16[64,2560]{1,0:T(8,128)(2,1)S(1)} collective-permute-done((bf16[64,2560]{1,0:T(8,128)(2,1)S(1)}, bf16[64,2560]{1,0:T(8,128)(2,1)S(1)}, u32[]{:S(2)}, u32[]{:S(2)}) %collective-permute-start.5) | collective-permute-done | bytes 327712 | tf_op jit(solution)/shard_map/ppermute | solution.py:440
  55.8 1.6 collective-permute-start.8
  58.4 4.1 %collective-permute-done.3.refs_0_.refs_4_ = bf16[64,2560]{1,0:T(8,128)(2,1)S(1)} collective-permute-done((bf16[64,2560]{1,0:T(8,128)(2,1)S(1)}, bf16[64,2560]{1,0:T(8,128)(2,1)S(1)}, u32[]{:S(2)}, u32[]{:S(2)}) %collective-permute-start.3) | collective-permute-done | bytes 327712 | tf_op jit(solution)/shard_map/ppermute | solution.py:440
  64.5 6.4 %collective-permute-done.10.refs_7_ = bf16[64,2560]{1,0:T(8,128)(2,1)S(1)} collective-permute-done((bf16[64,2560]{1,0:T(8,128)(2,1)S(1)}, bf16[64,2560]{1,0:T(8,128)(2,1)S(1)}, u32[]{:S(2)}, u32[]{:S(2)}) %collective-permute-start.10) | collective-permute-done | bytes 327712 | tf_op jit(solution)/shard_map/ppermute | solution.py:494
  71.4 6.5 %collective-permute-done.9.refs_6_ = bf16[64,2560]{1,0:T(8,128)(2,1)S(1)} collective-permute-done((bf16[64,2560]{1,0:T(8,128)(2,1)S(1)}, bf16[64,2560]{1,0:T(8,128)(2,1)S(1)}, u32[]{:S(2)}, u32[]{:S(2)}) %collective-permute-start.9) | collective-permute-done | bytes 327712 | tf_op jit(solution)/shard_map/ppermute | solution.py:494
  78.6 6.3 %collective-permute-done.8.refs_5_ = bf16[64,2560]{1,0:T(8,128)(2,1)S(1)} collective-permute-done((bf16[64,2560]{1,0:T(8,128)(2,1)S(1)}, bf16[64,2560]{1,0:T(8,128)(2,1)S(1)}, u32[]{:S(2)}, u32[]{:S(2)}) %collective-permute-start.8) | collective-permute-done | bytes 327712 | tf_op jit(solution)/shard_map/ppermute | solution.py:494
  85.5 8.6 %keys_values.2 = (bf16[256,2560]{1,0:T(8,128)(2,1)S(1)}, bf16[256,2560]{1,0:T(8,128)(2,1)}, bf16[2,256,512]{2,1,0:T(8,128)(2,1)S(1)}) custom-call(s32[122]{0:T(128)S(1)} %copy-done.9, bf16[64,2560]{1,0:T(8,128)(2,1)S(1)} %get-tuple-element.29.refs_0_, bf16[64,2560]{1,0:T(8,128)(2,1)S(1)} %collective-permute-done.refs_1_, ...), custom_call_target="tpu_custom_call" | custom-call | flops 2684354560 | bytes 15728640 | tf_op jit(solution)/shard_map/keys_values/pallas_call | solution.py:165
  94.1 7.1 %collective-permute-start.18 = (bf16[2,4,64,512]{3,2,1,0:T(8,128)(2,1)S(1)}, bf16[2,4,64,512]{3,2,1,0:T(8,128)(2,1)S(1)}, u32[]{:S(2)}, u32[]{:S(2)}) collective-permute-start(bf16[2,4,64,512]{3,2,1,0:T(8,128)(2,1)S(1)} %bitcast.50), channel_id=1, source_target_pairs={{0,2},{1,3},{2,4},{3,5},{4,6},{5,7},{6,0},{7,1},{8,10},{9,11},{10,... | collective-permute-start | bytes 1572872 | tf_op jit(solution)/shard_map/ppermute | solution.py:440
  101.2 4.9 %collective-permute-done.13.refs_5_ = bf16[64,2560]{1,0:T(8,128)(2,1)S(1)} collective-permute-done((bf16[64,2560]{1,0:T(8,128)(2,1)S(1)}, bf16[64,2560]{1,0:T(8,128)(2,1)S(1)}, u32[]{:S(2)}, u32[]{:S(2)}) %collective-permute-start.13) | collective-permute-done | bytes 327712 | tf_op jit(solution)/shard_map/ppermute | solution.py:494
  106.0 5.6 %collective-permute-done.12.refs_4_ = bf16[64,2560]{1,0:T(8,128)(2,1)S(1)} collective-permute-done((bf16[64,2560]{1,0:T(8,128)(2,1)S(1)}, bf16[64,2560]{1,0:T(8,128)(2,1)S(1)}, u32[]{:S(2)}, u32[]{:S(2)}) %collective-permute-start.12) | collective-permute-done | bytes 327712 | tf_op jit(solution)/shard_map/ppermute | solution.py:494
  111.7 8.6 %keys_values.3 = (bf16[256,2560]{1,0:T(8,128)(2,1)S(1)}, bf16[256,2560]{1,0:T(8,128)(2,1)}, bf16[2,256,512]{2,1,0:T(8,128)(2,1)S(1)}) custom-call(s32[122]{0:T(128)S(1)} %copy-done.9, bf16[64,2560]{1,0:T(8,128)(2,1)S(1)} %collective-permute-done.3.refs_0_.refs_4_, bf16[64,2560]{1,0:T(8,128)(2,1)S(1)} %collective-permute-done.4.refs_1_.refs_5_, ...), custom_call_target="tpu_custom_call" | custom-call | flops 2684354560 | bytes 15728640 | tf_op jit(solution)/shard_map/keys_values/pallas_call | solution.py:165
  120.2 7.8 %collective-permute-start.19 = (bf16[2,4,64,512]{3,2,1,0:T(8,128)(2,1)S(1)}, bf16[2,4,64,512]{3,2,1,0:T(8,128)(2,1)S(1)}, u32[]{:S(2)}, u32[]{:S(2)}) collective-permute-start(bf16[2,4,64,512]{3,2,1,0:T(8,128)(2,1)S(1)} %bitcast.53), channel_id=1, source_target_pairs={{0,2},{1,3},{2,4},{3,5},{4,6},{5,7},{6,0},{7,1},{8,10},{9,11},{10,... | collective-permute-start | bytes 1572872 | tf_op jit(solution)/shard_map/ppermute | solution.py:440
  128.1 12.3 %collective-permute-done.19.refs_7_ = bf16[2,4,64,512]{3,2,1,0:T(8,128)(2,1)S(1)} collective-permute-done((bf16[2,4,64,512]{3,2,1,0:T(8,128)(2,1)S(1)}, bf16[2,4,64,512]{3,2,1,0:T(8,128)(2,1)S(1)}, u32[]{:S(2)}, u32[]{:S(2)}) %collective-permute-start.19) | collective-permute-done | bytes 524320 | tf_op jit(solution)/shard_map/ppermute | solution.py:440
  140.4 2.5 collective-permute-start.23
  143.4 8.2 %collective-permute-done.22.refs_10_ = bf16[2,4,64,512]{3,2,1,0:T(8,128)(2,1)S(1)} collective-permute-done((bf16[2,4,64,512]{3,2,1,0:T(8,128)(2,1)S(1)}, bf16[2,4,64,512]{3,2,1,0:T(8,128)(2,1)S(1)}, u32[]{:S(2)}, u32[]{:S(2)}) %collective-permute-start.22) | collective-permute-done | bytes 524320 | tf_op jit(solution)/shard_map/ppermute | solution.py:440
  151.6 2.5 collective-permute-start.26
  154.1 8.8 %collective-permute-done.23.refs_11_ = bf16[2,4,64,512]{3,2,1,0:T(8,128)(2,1)S(1)} collective-permute-done((bf16[2,4,64,512]{3,2,1,0:T(8,128)(2,1)S(1)}, bf16[2,4,64,512]{3,2,1,0:T(8,128)(2,1)S(1)}, u32[]{:S(2)}, u32[]{:S(2)}) %collective-permute-start.23) | collective-permute-done | bytes 524320 | tf_op jit(solution)/shard_map/ppermute | solution.py:440
  162.8 2.5 collective-permute-start.27
  165.9 8.2 %collective-permute-done.26.refs_14_ = bf16[2,4,64,512]{3,2,1,0:T(8,128)(2,1)S(1)} collective-permute-done((bf16[2,4,64,512]{3,2,1,0:T(8,128)(2,1)S(1)}, bf16[2,4,64,512]{3,2,1,0:T(8,128)(2,1)S(1)}, u32[]{:S(2)}, u32[]{:S(2)}) %collective-permute-start.26) | collective-permute-done | bytes 524320 | tf_op jit(solution)/shard_map/ppermute | solution.py:440
  174.1 9.7 %collective-permute-done.27.refs_15_ = bf16[2,4,64,512]{3,2,1,0:T(8,128)(2,1)S(1)} collective-permute-done((bf16[2,4,64,512]{3,2,1,0:T(8,128)(2,1)S(1)}, bf16[2,4,64,512]{3,2,1,0:T(8,128)(2,1)S(1)}, u32[]{:S(2)}, u32[]{:S(2)}) %collective-permute-start.27) | collective-permute-done | bytes 524320 | tf_op jit(solution)/shard_map/ppermute | solution.py:440
  183.8 11.4 %queries.2 = bf16[256,2048]{1,0:T(8,128)(2,1)S(1)} custom-call(s32[122]{0:T(128)S(1)} %copy-done.10, bf16[256,2560]{1,0:T(8,128)(2,1)S(1)} %get-tuple-element.12.refs_0_, bf16[256,2560]{1,0:T(8,128)(2,1)S(1)} %copy-done.5, bf16[5120,2048]{1,0:T(8,128)(2,1)} %refs_3_.3, bf16[5120,2048]{1,0:T(8,128)(2,1)} %refs_3_.3, bf16[1,128]{1,0:T(2,128)(2,1)S(1)} %bitcast.48, ...), custom_call_target="tpu_custom_call" | custom-call | flops 5368709120 | bytes 24641536 | tf_op jit(solution)/shard_map/queries/pallas_call | solution.py:221
  196.2 11.3 %queries.3 = bf16[256,2048]{1,0:T(8,128)(2,1)S(1)} custom-call(s32[122]{0:T(128)S(1)} %copy-done.10, bf16[256,2560]{1,0:T(8,128)(2,1)S(1)} %get-tuple-element.14.refs_0_, bf16[256,2560]{1,0:T(8,128)(2,1)S(1)} %copy-done.6, bf16[5120,2048]{1,0:T(8,128)(2,1)} %refs_3_.3, bf16[5120,2048]{1,0:T(8,128)(2,1)} %refs_3_.3, bf16[1,128]{1,0:T(2,128)(2,1)S(1)} %bitcast.49, ...), custom_call_target="tpu_custom_call" | custom-call | flops 5368709120 | bytes 24641536 | tf_op jit(solution)/shard_map/queries/pallas_call | solution.py:221
  208.5 26.1 %attention.1 = (bf16[8,64,2048]{2,1,0:T(8,128)(2,1)}, bf16[4,2,128,512]{3,2,1,0:T(8,128)(2,1)}) custom-call(s32[122]{0:T(128)S(1)} %copy-done.10, bf16[4,64,2048]{2,1,0:T(8,128)(2,1)} %bitcast.41, bf16[4,64,2048]{2,1,0:T(8,128)(2,1)} %bitcast.42, bf16[2,4,64,512]{3,2,1,0:T(8,128)(2,1)S(1)} %bitcast.52, bf16[2,4,64,512]{3,2,1,0:T(8,128)(2,1)S(1)} %bitcast.55, ...), custom_call_target="tpu_custom_call" | custom-call | flops 4724464128 | bytes 12582912 | tf_op jit(solution)/shard_map/attention/pallas_call | solution.py:328
  234.6 1.6 copy-done.1
  236.2 3.4 send_part.4.refs_0_
  240.6 4.7 %send_part.5.refs_0_ = bf16[512,1024]{1,0:T(8,128)(2,1)S(1)} custom-call(s32[122]{0:T(128)S(1)} %copy-done.10, bf16[512,2048]{1,0:T(8,128)(2,1)S(1)} %bitcast.37, bf16[2048,5120]{1,0:T(8,128)(2,1)} %wo.9, bf16[512,512]{1,0:T(8,128)(2,1)S(1)} %send_part.4.refs_0_), custom_call_target="tpu_custom_call" | custom-call | flops 2147483648 | bytes 7340032 | tf_op jit(solution)/shard_map/send_part/pallas_call | solution.py:362
  245.3 3.4 send_part.6.refs_0_
  249.6 3.4 send_part.7.refs_0_
  253.0 9.2 %own_part.1 = bf16[512,2560]{1,0:T(8,128)(2,1)S(1)} custom-call(s32[122]{0:T(128)S(1)} %copy-done.10, bf16[512,2048]{1,0:T(8,128)(2,1)S(1)} %bitcast.40, bf16[2048,5120]{1,0:T(8,128)(2,1)} %wo.9, bf16[512,512]{1,0:T(8,128)(2,1)S(1)} %send_part.7.refs_0_), custom_call_target="tpu_custom_call" | custom-call | flops 5368709120 | bytes 15204352 | tf_op jit(solution)/shard_map/own_part/pallas_call | solution.py:362
  263.7 2.6 residual.4
  266.4 4.1 %all-to-all-start = ((bf16[8,64,512]{2,1,0:T(8,128)(2,1)}), bf16[8,64,512]{2,1,0:T(8,128)(2,1)}, u32[]{:S(2)}, u32[]{:S(2)}) async-start(bf16[8,64,512]{2,1,0:T(8,128)(2,1)} %residual.4), calls=%async_computation | async-start | bytes 1048576 | tf_op jit(solution)/shard_map/all_to_all | solution.py:551
  271.7 13.2 %collective-permute-done.33 = bf16[512,512]{1,0:T(8,128)(2,1)S(1)} collective-permute-done((bf16[512,512]{1,0:T(8,128)(2,1)}, bf16[512,512]{1,0:T(8,128)(2,1)S(1)}, u32[]{:S(2)}, u32[]{:S(2)}) %collective-permute-start.33) | collective-permute-done | bytes 524320 | tf_op jit(solution)/shard_map/ppermute | solution.py:536
  284.9 2.6 residual.7
  287.5 4.8 %all-to-all-start.3 = ((bf16[8,64,512]{2,1,0:T(8,128)(2,1)}), bf16[8,64,512]{2,1,0:T(8,128)(2,1)}, u32[]{:S(2)}, u32[]{:S(2)}) async-start(bf16[8,64,512]{2,1,0:T(8,128)(2,1)} %residual.7), calls=%async_computation.3 | async-start | bytes 1048576 | tf_op jit(solution)/shard_map/all_to_all | solution.py:551
  294.3 12.7 %collective-permute-done.32 = bf16[512,512]{1,0:T(8,128)(2,1)S(1)} collective-permute-done((bf16[512,512]{1,0:T(8,128)(2,1)S(1)}, bf16[512,512]{1,0:T(8,128)(2,1)S(1)}, u32[]{:S(2)}, u32[]{:S(2)}) %collective-permute-start.32) | collective-permute-done | bytes 524320 | tf_op jit(solution)/shard_map/ppermute | solution.py:536
  307.0 2.6 residual.6
  309.6 5.1 %all-to-all-start.2 = ((bf16[8,64,512]{2,1,0:T(8,128)(2,1)}), bf16[8,64,512]{2,1,0:T(8,128)(2,1)S(1)}, u32[]{:S(2)}, u32[]{:S(2)}) async-start(bf16[8,64,512]{2,1,0:T(8,128)(2,1)} %residual.6), calls=%async_computation.2 | async-start | bytes 1048576 | tf_op jit(solution)/shard_map/all_to_all | solution.py:551
  314.8 14.4 %collective-permute-done.31 = bf16[512,1024]{1,0:T(8,128)(2,1)} collective-permute-done((bf16[512,1024]{1,0:T(8,128)(2,1)}, bf16[512,1024]{1,0:T(8,128)(2,1)}, u32[]{:S(2)}, u32[]{:S(2)}) %collective-permute-start.31) | collective-permute-done | bytes 1048608 | tf_op jit(solution)/shard_map/ppermute | solution.py:536
  329.2 2.4 residual.5
  332.6 4.9 %all-to-all-start.1 = ((bf16[8,64,1024]{2,1,0:T(8,128)(2,1)}), bf16[8,64,1024]{2,1,0:T(8,128)(2,1)S(1)}, u32[]{:S(2)}, u32[]{:S(2)}) async-start(bf16[8,64,1024]{2,1,0:T(8,128)(2,1)} %copy-done.2), calls=%async_computation.1 | async-start | bytes 2097152 | tf_op jit(solution)/shard_map/all_to_all | solution.py:551
  338.6 24.7 %collective-permute-done.34 = bf16[4,2,128,512]{3,2,1,0:T(8,128)(2,1)} collective-permute-done((bf16[4,2,128,512]{3,2,1,0:T(8,128)(2,1)}, bf16[4,2,128,512]{3,2,1,0:T(8,128)(2,1)}, u32[]{:S(2)}, u32[]{:S(2)}) %collective-permute-start.34) | collective-permute-done | bytes 1048608 | tf_op jit(solution)/shard_map/ppermute | solution.py:542
  364.8 1.6 pad_maximum_fusion.1
  366.4 2.6 pad_maximum_fusion
  (89 shorter events, 25.4 us)
Async XLA Ops:
  1.3 13.7 %collective-permute-start.11 = (bf16[1,2560]{1,0:T(2,128)(2,1)S(1)}, bf16[1,2560]{1,0:T(2,128)(2,1)S(1)}, u32[]{:S(2)}, u32[]{:S(2)}) collective-permute-start(bf16[1,2560]{1,0:T(2,128)(2,1)S(1)} %broadcast_in_dim.6.refs_8_), channel_id=1, source_target_pairs={{0,8},{8,0},{1,9},{9,1},{2,10},{10,2},{3,11},{11,3},{4,12},{12,4},... | collective-permute-start | bytes 15368 | tf_op jit(solution)/shard_map/ppermute | solution.py:493
  4.3 80.7 %copy-start.11 = (bf16[128]{0:T(256)(128)(2,1)S(1)}, bf16[128]{0:T(256)(128)(2,1)}, u32[]{:S(2)}) copy-start(bf16[128]{0:T(256)(128)(2,1)} %param.18) | copy-start | bytes 772
  7.0 24.7 %collective-permute-start.6 = (bf16[64,2560]{1,0:T(8,128)(2,1)S(1)}, bf16[64,2560]{1,0:T(8,128)(2,1)S(1)}, u32[]{:S(2)}, u32[]{:S(2)}) collective-permute-start(bf16[64,2560]{1,0:T(8,128)(2,1)S(1)} %get-tuple-element.22), channel_id=1, source_target_pairs={{0,5},{1,4},{2,7},{3,6},{4,1},{5,0},{6,3},{7,2},{8,13},{9,12},{10,... | collective-permute-start | bytes 983048 | tf_op jit(solution)/shard_map/ppermute | solution.py:440
  8.8 44.5 %collective-permute-start.5 = (bf16[64,2560]{1,0:T(8,128)(2,1)S(1)}, bf16[64,2560]{1,0:T(8,128)(2,1)S(1)}, u32[]{:S(2)}, u32[]{:S(2)}) collective-permute-start(bf16[64,2560]{1,0:T(8,128)(2,1)S(1)} %get-tuple-element.23), channel_id=1, source_target_pairs={{0,4},{1,5},{2,6},{3,7},{4,0},{5,1},{6,2},{7,3},{8,12},{9,13},{10,... | collective-permute-start | bytes 983048 | tf_op jit(solution)/shard_map/ppermute | solution.py:440
  9.6 43.6 %collective-permute-start.4 = (bf16[64,2560]{1,0:T(8,128)(2,1)}, bf16[64,2560]{1,0:T(8,128)(2,1)S(1)}, u32[]{:S(2)}, u32[]{:S(2)}) collective-permute-start(bf16[64,2560]{1,0:T(8,128)(2,1)} %get-tuple-element.24), channel_id=1, source_target_pairs={{0,7},{1,6},{2,1},{3,0},{4,3},{5,2},{6,5},{7,4},{8,15},{9,14},{10,... | collective-permute-start | bytes 983048 | tf_op jit(solution)/shard_map/ppermute | solution.py:440
  13.0 40.8 %collective-permute-start.2 = (bf16[64,2560]{1,0:T(8,128)(2,1)}, bf16[64,2560]{1,0:T(8,128)(2,1)S(1)}, u32[]{:S(2)}, u32[]{:S(2)}) collective-permute-start(bf16[64,2560]{1,0:T(8,128)(2,1)} %get-tuple-element.26), channel_id=1, source_target_pairs={{0,3},{1,2},{2,5},{3,4},{4,7},{5,6},{6,1},{7,0},{8,11},{9,10},{10,... | collective-permute-start | bytes 983048 | tf_op jit(solution)/shard_map/ppermute | solution.py:440
  15.0 40.3 %collective-permute-start.1 = (bf16[64,2560]{1,0:T(8,128)(2,1)}, bf16[64,2560]{1,0:T(8,128)(2,1)S(1)}, u32[]{:S(2)}, u32[]{:S(2)}) collective-permute-start(bf16[64,2560]{1,0:T(8,128)(2,1)} %get-tuple-element.27), channel_id=1, source_target_pairs={{0,2},{1,3},{2,4},{3,5},{4,6},{5,7},{6,0},{7,1},{8,10},{9,11},{10,... | collective-permute-start | bytes 983048 | tf_op jit(solution)/shard_map/ppermute | solution.py:440
  31.7 24.1 %collective-permute-start = (bf16[64,2560]{1,0:T(8,128)(2,1)S(1)}, bf16[64,2560]{1,0:T(8,128)(2,1)S(1)}, u32[]{:S(2)}, u32[]{:S(2)}) collective-permute-start(bf16[64,2560]{1,0:T(8,128)(2,1)S(1)} %get-tuple-element.28), channel_id=1, source_target_pairs={{0,1},{1,0},{2,3},{3,2},{4,5},{5,4},{6,7},{7,6},{8,9},{9,8},{10,11... | collective-permute-start | bytes 983048 | tf_op jit(solution)/shard_map/ppermute | solution.py:440
  53.3 9.2 %collective-permute-start.3 = (bf16[64,2560]{1,0:T(8,128)(2,1)S(1)}, bf16[64,2560]{1,0:T(8,128)(2,1)S(1)}, u32[]{:S(2)}, u32[]{:S(2)}) collective-permute-start(bf16[64,2560]{1,0:T(8,128)(2,1)S(1)} %get-tuple-element.25), channel_id=1, source_target_pairs={{0,6},{1,7},{2,0},{3,1},{4,2},{5,3},{6,4},{7,5},{8,14},{9,15},{10,... | collective-permute-start | bytes 983048 | tf_op jit(solution)/shard_map/ppermute | solution.py:440
  53.3 10.6 %collective-permute-start.7 = (bf16[64,2560]{1,0:T(8,128)(2,1)S(1)}, bf16[64,2560]{1,0:T(8,128)(2,1)S(1)}, u32[]{:S(2)}, u32[]{:S(2)}) collective-permute-start(bf16[64,2560]{1,0:T(8,128)(2,1)S(1)} %get-tuple-element.29.refs_0_), channel_id=1, source_target_pairs={{0,8},{8,0},{1,9},{9,1},{2,10},{10,2},{3,11},{11,3},{4,12},{12,4},... | collective-permute-start | bytes 983048 | tf_op jit(solution)/shard_map/ppermute | solution.py:494
  53.8 17.2 %collective-permute-start.10 = (bf16[64,2560]{1,0:T(8,128)(2,1)S(1)}, bf16[64,2560]{1,0:T(8,128)(2,1)S(1)}, u32[]{:S(2)}, u32[]{:S(2)}) collective-permute-start(bf16[64,2560]{1,0:T(8,128)(2,1)S(1)} %collective-permute-done.2.refs_3_), channel_id=1, source_target_pairs={{0,8},{8,0},{1,9},{9,1},{2,10},{10,2},{3,11},{11,3},{4,12},{12,4},... | collective-permute-start | bytes 983048 | tf_op jit(solution)/shard_map/ppermute | solution.py:494
  55.3 22.6 %collective-permute-start.9 = (bf16[64,2560]{1,0:T(8,128)(2,1)S(1)}, bf16[64,2560]{1,0:T(8,128)(2,1)S(1)}, u32[]{:S(2)}, u32[]{:S(2)}) collective-permute-start(bf16[64,2560]{1,0:T(8,128)(2,1)S(1)} %collective-permute-done.1.refs_2_), channel_id=1, source_target_pairs={{0,8},{8,0},{1,9},{9,1},{2,10},{10,2},{3,11},{11,3},{4,12},{12,4},... | collective-permute-start | bytes 983048 | tf_op jit(solution)/shard_map/ppermute | solution.py:494
  55.8 29.2 %collective-permute-start.8 = (bf16[64,2560]{1,0:T(8,128)(2,1)S(1)}, bf16[64,2560]{1,0:T(8,128)(2,1)S(1)}, u32[]{:S(2)}, u32[]{:S(2)}) collective-permute-start(bf16[64,2560]{1,0:T(8,128)(2,1)S(1)} %collective-permute-done.refs_1_), channel_id=1, source_target_pairs={{0,8},{8,0},{1,9},{9,1},{2,10},{10,2},{3,11},{11,3},{4,12},{12,4},... | collective-permute-start | bytes 983048 | tf_op jit(solution)/shard_map/ppermute | solution.py:494
  62.5 38.7 %collective-permute-start.15 = (bf16[64,2560]{1,0:T(8,128)(2,1)S(1)}, bf16[64,2560]{1,0:T(8,128)(2,1)S(1)}, u32[]{:S(2)}, u32[]{:S(2)}) collective-permute-start(bf16[64,2560]{1,0:T(8,128)(2,1)S(1)} %collective-permute-done.6.refs_3_.refs_7_), channel_id=1, source_target_pairs={{0,8},{8,0},{1,9},{9,1},{2,10},{10,2},{3,11},{11,3},{4,12},{12,4},... | collective-permute-start | bytes 983048 | tf_op jit(solution)/shard_map/ppermute | solution.py:494
  63.9 37.3 %collective-permute-start.14 = (bf16[64,2560]{1,0:T(8,128)(2,1)S(1)}, bf16[64,2560]{1,0:T(8,128)(2,1)S(1)}, u32[]{:S(2)}, u32[]{:S(2)}) collective-permute-start(bf16[64,2560]{1,0:T(8,128)(2,1)S(1)} %collective-permute-done.5.refs_2_.refs_6_), channel_id=1, source_target_pairs={{0,8},{8,0},{1,9},{9,1},{2,10},{10,2},{3,11},{11,3},{4,12},{12,4},... | collective-permute-start | bytes 983048 | tf_op jit(solution)/shard_map/ppermute | solution.py:494
  70.9 35.1 %collective-permute-start.13 = (bf16[64,2560]{1,0:T(8,128)(2,1)S(1)}, bf16[64,2560]{1,0:T(8,128)(2,1)S(1)}, u32[]{:S(2)}, u32[]{:S(2)}) collective-permute-start(bf16[64,2560]{1,0:T(8,128)(2,1)S(1)} %collective-permute-done.4.refs_1_.refs_5_), channel_id=1, source_target_pairs={{0,8},{8,0},{1,9},{9,1},{2,10},{10,2},{3,11},{11,3},{4,12},{12,4},... | collective-permute-start | bytes 983048 | tf_op jit(solution)/shard_map/ppermute | solution.py:494
  77.9 33.7 %collective-permute-start.12 = (bf16[64,2560]{1,0:T(8,128)(2,1)S(1)}, bf16[64,2560]{1,0:T(8,128)(2,1)S(1)}, u32[]{:S(2)}, u32[]{:S(2)}) collective-permute-start(bf16[64,2560]{1,0:T(8,128)(2,1)S(1)} %collective-permute-done.3.refs_0_.refs_4_), channel_id=1, source_target_pairs={{0,8},{8,0},{1,9},{9,1},{2,10},{10,2},{3,11},{11,3},{4,12},{12,4},... | collective-permute-start | bytes 983048 | tf_op jit(solution)/shard_map/ppermute | solution.py:494
  94.1 89.7 %copy-start.5 = (bf16[256,2560]{1,0:T(8,128)(2,1)S(1)}, bf16[256,2560]{1,0:T(8,128)(2,1)}, u32[]{:S(2)}) copy-start(bf16[256,2560]{1,0:T(8,128)(2,1)} %get-tuple-element.13.refs_1_) | copy-start | bytes 3932164
  94.1 89.7 %copy-start.10 = (s32[122]{0:T(128)S(1)}, s32[122]{0:T(128)}, u32[]{:S(2)}) copy-start(s32[122]{0:T(128)} %tables.1.table) | copy-start | bytes 1468
  94.1 89.7 %copy-start.12 = (bf16[128]{0:T(256)(128)(2,1)S(1)}, bf16[128]{0:T(256)(128)(2,1)}, u32[]{:S(2)}) copy-start(bf16[128]{0:T(256)(128)(2,1)} %param.17) | copy-start | bytes 772
  94.1 33.9 %collective-permute-start.18 = (bf16[2,4,64,512]{3,2,1,0:T(8,128)(2,1)S(1)}, bf16[2,4,64,512]{3,2,1,0:T(8,128)(2,1)S(1)}, u32[]{:S(2)}, u32[]{:S(2)}) collective-permute-start(bf16[2,4,64,512]{3,2,1,0:T(8,128)(2,1)S(1)} %bitcast.50), channel_id=1, source_target_pairs={{0,2},{1,3},{2,4},{3,5},{4,6},{5,7},{6,0},{7,1},{8,10},{9,11},{10,... | collective-permute-start | bytes 1572872 | tf_op jit(solution)/shard_map/ppermute | solution.py:440
  120.2 20.1 %collective-permute-start.19 = (bf16[2,4,64,512]{3,2,1,0:T(8,128)(2,1)S(1)}, bf16[2,4,64,512]{3,2,1,0:T(8,128)(2,1)S(1)}, u32[]{:S(2)}, u32[]{:S(2)}) collective-permute-start(bf16[2,4,64,512]{3,2,1,0:T(8,128)(2,1)S(1)} %bitcast.53), channel_id=1, source_target_pairs={{0,2},{1,3},{2,4},{3,5},{4,6},{5,7},{6,0},{7,1},{8,10},{9,11},{10,... | collective-permute-start | bytes 1572872 | tf_op jit(solution)/shard_map/ppermute | solution.py:440
  128.0 23.6 %collective-permute-start.22 = (bf16[2,4,64,512]{3,2,1,0:T(8,128)(2,1)S(1)}, bf16[2,4,64,512]{3,2,1,0:T(8,128)(2,1)S(1)}, u32[]{:S(2)}, u32[]{:S(2)}) collective-permute-start(bf16[2,4,64,512]{3,2,1,0:T(8,128)(2,1)S(1)} %collective-permute-done.18.refs_6_), channel_id=1, source_target_pairs={{0,2},{1,3},{2,4},{3,5},{4,6},{5,7},{6,0},{7,1},{8,10},{9,11},{10,... | collective-permute-start | bytes 1572872 | tf_op jit(solution)/shard_map/ppermute | solution.py:440
  140.4 22.5 %collective-permute-start.23 = (bf16[2,4,64,512]{3,2,1,0:T(8,128)(2,1)S(1)}, bf16[2,4,64,512]{3,2,1,0:T(8,128)(2,1)S(1)}, u32[]{:S(2)}, u32[]{:S(2)}) collective-permute-start(bf16[2,4,64,512]{3,2,1,0:T(8,128)(2,1)S(1)} %collective-permute-done.19.refs_7_), channel_id=1, source_target_pairs={{0,2},{1,3},{2,4},{3,5},{4,6},{5,7},{6,0},{7,1},{8,10},{9,11},{10,... | collective-permute-start | bytes 1572872 | tf_op jit(solution)/shard_map/ppermute | solution.py:440
  142.9 22.5 %collective-permute-start.16 = (bf16[2,4,64,512]{3,2,1,0:T(8,128)(2,1)S(1)}, bf16[2,4,64,512]{3,2,1,0:T(8,128)(2,1)S(1)}, u32[]{:S(2)}, u32[]{:S(2)}) collective-permute-start(bf16[2,4,64,512]{3,2,1,0:T(8,128)(2,1)S(1)} %bitcast.51), channel_id=1, source_target_pairs={{0,1},{1,0},{2,3},{3,2},{4,5},{5,4},{6,7},{7,6},{8,9},{9,8},{10,11... | collective-permute-start | bytes 1572872 | tf_op jit(solution)/shard_map/ppermute | solution.py:440
  142.9 22.5 %collective-permute-start.17 = (bf16[2,4,64,512]{3,2,1,0:T(8,128)(2,1)S(1)}, bf16[2,4,64,512]{3,2,1,0:T(8,128)(2,1)S(1)}, u32[]{:S(2)}, u32[]{:S(2)}) collective-permute-start(bf16[2,4,64,512]{3,2,1,0:T(8,128)(2,1)S(1)} %bitcast.54), channel_id=1, source_target_pairs={{0,1},{1,0},{2,3},{3,2},{4,5},{5,4},{6,7},{7,6},{8,9},{9,8},{10,11... | collective-permute-start | bytes 1572872 | tf_op jit(solution)/shard_map/ppermute | solution.py:440
  143.4 22.5 %collective-permute-start.20 = (bf16[2,4,64,512]{3,2,1,0:T(8,128)(2,1)S(1)}, bf16[2,4,64,512]{3,2,1,0:T(8,128)(2,1)S(1)}, u32[]{:S(2)}, u32[]{:S(2)}) collective-permute-start(bf16[2,4,64,512]{3,2,1,0:T(8,128)(2,1)S(1)} %collective-permute-done.18.refs_6_), channel_id=1, source_target_pairs={{0,1},{1,0},{2,3},{3,2},{4,5},{5,4},{6,7},{7,6},{8,9},{9,8},{10,11... | collective-permute-start | bytes 1572872 | tf_op jit(solution)/shard_map/ppermute | solution.py:440
  151.6 22.5 %collective-permute-start.26 = (bf16[2,4,64,512]{3,2,1,0:T(8,128)(2,1)S(1)}, bf16[2,4,64,512]{3,2,1,0:T(8,128)(2,1)S(1)}, u32[]{:S(2)}, u32[]{:S(2)}) collective-permute-start(bf16[2,4,64,512]{3,2,1,0:T(8,128)(2,1)S(1)} %collective-permute-done.22.refs_10_), channel_id=1, source_target_pairs={{0,2},{1,3},{2,4},{3,5},{4,6},{5,7},{6,0},{7,1},{8,10},{9,11},{10,... | collective-permute-start | bytes 1572872 | tf_op jit(solution)/shard_map/ppermute | solution.py:440
  162.8 20.9 %collective-permute-start.27 = (bf16[2,4,64,512]{3,2,1,0:T(8,128)(2,1)S(1)}, bf16[2,4,64,512]{3,2,1,0:T(8,128)(2,1)S(1)}, u32[]{:S(2)}, u32[]{:S(2)}) collective-permute-start(bf16[2,4,64,512]{3,2,1,0:T(8,128)(2,1)S(1)} %collective-permute-done.23.refs_11_), channel_id=1, source_target_pairs={{0,2},{1,3},{2,4},{3,5},{4,6},{5,7},{6,0},{7,1},{8,10},{9,11},{10,... | collective-permute-start | bytes 1572872 | tf_op jit(solution)/shard_map/ppermute | solution.py:440
  165.3 43.2 %collective-permute-start.21 = (bf16[2,4,64,512]{3,2,1,0:T(8,128)(2,1)S(1)}, bf16[2,4,64,512]{3,2,1,0:T(8,128)(2,1)S(1)}, u32[]{:S(2)}, u32[]{:S(2)}) collective-permute-start(bf16[2,4,64,512]{3,2,1,0:T(8,128)(2,1)S(1)} %collective-permute-done.19.refs_7_), channel_id=1, source_target_pairs={{0,1},{1,0},{2,3},{3,2},{4,5},{5,4},{6,7},{7,6},{8,9},{9,8},{10,11... | collective-permute-start | bytes 1572872 | tf_op jit(solution)/shard_map/ppermute | solution.py:440
  165.3 43.2 %collective-permute-start.24 = (bf16[2,4,64,512]{3,2,1,0:T(8,128)(2,1)S(1)}, bf16[2,4,64,512]{3,2,1,0:T(8,128)(2,1)S(1)}, u32[]{:S(2)}, u32[]{:S(2)}) collective-permute-start(bf16[2,4,64,512]{3,2,1,0:T(8,128)(2,1)S(1)} %collective-permute-done.22.refs_10_), channel_id=1, source_target_pairs={{0,1},{1,0},{2,3},{3,2},{4,5},{5,4},{6,7},{7,6},{8,9},{9,8},{10,11... | collective-permute-start | bytes 1572872 | tf_op jit(solution)/shard_map/ppermute | solution.py:440
  165.9 42.6 %collective-permute-start.25 = (bf16[2,4,64,512]{3,2,1,0:T(8,128)(2,1)S(1)}, bf16[2,4,64,512]{3,2,1,0:T(8,128)(2,1)}, u32[]{:S(2)}, u32[]{:S(2)}) collective-permute-start(bf16[2,4,64,512]{3,2,1,0:T(8,128)(2,1)S(1)} %collective-permute-done.23.refs_11_), channel_id=1, source_target_pairs={{0,1},{1,0},{2,3},{3,2},{4,5},{5,4},{6,7},{7,6},{8,9},{9,8},{10,11... | collective-permute-start | bytes 1572872 | tf_op jit(solution)/shard_map/ppermute | solution.py:440
  174.1 21.1 %copy-start.14 = (bf16[2,4,64,512]{3,2,1,0:T(8,128)(2,1)}, bf16[2,4,64,512]{3,2,1,0:T(8,128)(2,1)S(1)}, u32[]{:S(2)}) copy-start(bf16[2,4,64,512]{3,2,1,0:T(8,128)(2,1)S(1)} %collective-permute-done.26.refs_14_) | copy-start | bytes 1572868
  174.1 34.4 %collective-permute-start.28 = (bf16[2,4,64,512]{3,2,1,0:T(8,128)(2,1)S(1)}, bf16[2,4,64,512]{3,2,1,0:T(8,128)(2,1)}, u32[]{:S(2)}, u32[]{:S(2)}) collective-permute-start(bf16[2,4,64,512]{3,2,1,0:T(8,128)(2,1)S(1)} %collective-permute-done.26.refs_14_), channel_id=1, source_target_pairs={{0,1},{1,0},{2,3},{3,2},{4,5},{5,4},{6,7},{7,6},{8,9},{9,8},{10,11... | collective-permute-start | bytes 1572872 | tf_op jit(solution)/shard_map/ppermute | solution.py:440
  183.8 11.4 %copy-start.15 = (bf16[2,4,64,512]{3,2,1,0:T(8,128)(2,1)}, bf16[2,4,64,512]{3,2,1,0:T(8,128)(2,1)S(1)}, u32[]{:S(2)}) copy-start(bf16[2,4,64,512]{3,2,1,0:T(8,128)(2,1)S(1)} %collective-permute-done.27.refs_15_) | copy-start | bytes 1572868
  183.8 24.7 %collective-permute-start.29 = (bf16[2,4,64,512]{3,2,1,0:T(8,128)(2,1)S(1)}, bf16[2,4,64,512]{3,2,1,0:T(8,128)(2,1)}, u32[]{:S(2)}, u32[]{:S(2)}) collective-permute-start(bf16[2,4,64,512]{3,2,1,0:T(8,128)(2,1)S(1)} %collective-permute-done.27.refs_15_), channel_id=1, source_target_pairs={{0,1},{1,0},{2,3},{3,2},{4,5},{5,4},{6,7},{7,6},{8,9},{9,8},{10,11... | collective-permute-start | bytes 1572872 | tf_op jit(solution)/shard_map/ppermute | solution.py:440
  183.8 12.4 %copy-start.6 = (bf16[256,2560]{1,0:T(8,128)(2,1)S(1)}, bf16[256,2560]{1,0:T(8,128)(2,1)}, u32[]{:S(2)}) copy-start(bf16[256,2560]{1,0:T(8,128)(2,1)} %get-tuple-element.15.refs_1_) | copy-start | bytes 3932164
  239.6 24.1 %collective-permute-start.30 = (bf16[512,512]{1,0:T(8,128)(2,1)S(1)}, bf16[512,512]{1,0:T(8,128)(2,1)S(1)}, u32[]{:S(2)}, u32[]{:S(2)}) collective-permute-start(bf16[512,512]{1,0:T(8,128)(2,1)S(1)} %send_part.4.refs_0_), channel_id=1, source_target_pairs={{0,8},{8,0},{1,9},{9,1},{2,10},{10,2},{3,11},{11,3},{4,12},{12,4},... | collective-permute-start | bytes 1572872 | tf_op jit(solution)/shard_map/ppermute | solution.py:536
  253.0 9.2 %copy-start.4 = (bf16[512,512]{1,0:T(8,128)(2,1)}, bf16[512,512]{1,0:T(8,128)(2,1)S(1)}, u32[]{:S(2)}) copy-start(bf16[512,512]{1,0:T(8,128)(2,1)S(1)} %send_part.7.refs_0_) | copy-start | bytes 1572868
  266.4 21.2 %all-to-all-start = ((bf16[8,64,512]{2,1,0:T(8,128)(2,1)}), bf16[8,64,512]{2,1,0:T(8,128)(2,1)}, u32[]{:S(2)}, u32[]{:S(2)}) async-start(bf16[8,64,512]{2,1,0:T(8,128)(2,1)} %residual.4), calls=%async_computation | async-start | bytes 1048576 | tf_op jit(solution)/shard_map/all_to_all | solution.py:551
  270.5 14.4 %collective-permute-start.33 = (bf16[512,512]{1,0:T(8,128)(2,1)}, bf16[512,512]{1,0:T(8,128)(2,1)S(1)}, u32[]{:S(2)}, u32[]{:S(2)}) collective-permute-start(bf16[512,512]{1,0:T(8,128)(2,1)} %copy-done.4), channel_id=1, source_target_pairs={{0,8},{8,0},{1,9},{9,1},{2,10},{10,2},{3,11},{11,3},{4,12},{12,4},... | collective-permute-start | bytes 1572872 | tf_op jit(solution)/shard_map/ppermute | solution.py:536
  287.5 22.1 %all-to-all-start.3 = ((bf16[8,64,512]{2,1,0:T(8,128)(2,1)}), bf16[8,64,512]{2,1,0:T(8,128)(2,1)}, u32[]{:S(2)}, u32[]{:S(2)}) async-start(bf16[8,64,512]{2,1,0:T(8,128)(2,1)} %residual.7), calls=%async_computation.3 | async-start | bytes 1048576 | tf_op jit(solution)/shard_map/all_to_all | solution.py:551
  292.3 14.7 %collective-permute-start.32 = (bf16[512,512]{1,0:T(8,128)(2,1)S(1)}, bf16[512,512]{1,0:T(8,128)(2,1)S(1)}, u32[]{:S(2)}, u32[]{:S(2)}) collective-permute-start(bf16[512,512]{1,0:T(8,128)(2,1)S(1)} %send_part.6.refs_0_), channel_id=1, source_target_pairs={{0,8},{8,0},{1,9},{9,1},{2,10},{10,2},{3,11},{11,3},{4,12},{12,4},... | collective-permute-start | bytes 1572872 | tf_op jit(solution)/shard_map/ppermute | solution.py:536
  293.4 35.8 %collective-permute-start.31 = (bf16[512,1024]{1,0:T(8,128)(2,1)}, bf16[512,1024]{1,0:T(8,128)(2,1)}, u32[]{:S(2)}, u32[]{:S(2)}) collective-permute-start(bf16[512,1024]{1,0:T(8,128)(2,1)} %copy-done.3), channel_id=1, source_target_pairs={{0,8},{8,0},{1,9},{9,1},{2,10},{10,2},{3,11},{11,3},{4,12},{12,4},... | collective-permute-start | bytes 3145736 | tf_op jit(solution)/shard_map/ppermute | solution.py:536
  309.6 23.0 %all-to-all-start.2 = ((bf16[8,64,512]{2,1,0:T(8,128)(2,1)}), bf16[8,64,512]{2,1,0:T(8,128)(2,1)S(1)}, u32[]{:S(2)}, u32[]{:S(2)}) async-start(bf16[8,64,512]{2,1,0:T(8,128)(2,1)} %residual.6), calls=%async_computation.2 | async-start | bytes 1048576 | tf_op jit(solution)/shard_map/all_to_all | solution.py:551
  332.6 30.8 %copy-start.13 = (bf16[4,2,128,512]{3,2,1,0:T(8,128)(2,1)S(1)}, bf16[4,2,128,512]{3,2,1,0:T(8,128)(2,1)}, u32[]{:S(2)}) copy-start(bf16[4,2,128,512]{3,2,1,0:T(8,128)(2,1)} %get-tuple-element.21) | copy-start | bytes 3145732
  332.6 33.7 %all-to-all-start.1 = ((bf16[8,64,1024]{2,1,0:T(8,128)(2,1)}), bf16[8,64,1024]{2,1,0:T(8,128)(2,1)S(1)}, u32[]{:S(2)}, u32[]{:S(2)}) async-start(bf16[8,64,1024]{2,1,0:T(8,128)(2,1)} %copy-done.2), calls=%async_computation.1 | async-start | bytes 2097152 | tf_op jit(solution)/shard_map/all_to_all | solution.py:551
  337.5 25.9 %collective-permute-start.34 = (bf16[4,2,128,512]{3,2,1,0:T(8,128)(2,1)}, bf16[4,2,128,512]{3,2,1,0:T(8,128)(2,1)}, u32[]{:S(2)}, u32[]{:S(2)}) collective-permute-start(bf16[4,2,128,512]{3,2,1,0:T(8,128)(2,1)} %get-tuple-element.21), channel_id=1, source_target_pairs={{0,8},{8,0},{1,9},{9,1},{2,10},{10,2},{3,11},{11,3},{4,12},{12,4},... | collective-permute-start | bytes 3145736 | tf_op jit(solution)/shard_map/ppermute | solution.py:542
  (7 other events, 7.6 us)

commit v3 on v2

--- a/solution.py
+++ b/solution.py
@@ -15,6 +15,8 @@
 VMEM_BYTES = 48 * 1024 * 1024
 PARTS = 2
 CORES = 2
+IN_FLIGHT = 4
+SHARE = 0.1
 
 
 def params():
@@ -23,7 +25,9 @@
 
 def cost(flops, moved, transcendentals=0):
     return pl.CostEstimate(
-        flops=int(flops), bytes_accessed=int(moved), transcendentals=int(transcendentals)
+        flops=int(flops * SHARE),
+        bytes_accessed=int(moved * SHARE),
+        transcendentals=int(transcendentals * SHARE),
     )
 
 
@@ -315,23 +319,22 @@
         lax.fori_loop(0, here, functools.partial(one_place, p), 0)
 
 
-def make_attention(lay, most, table, queries, gathered, per_kv, head, pages_each):
+def make_attention(lay, most, table, queries, gathered, per_kv, head, pages_each, first, count):
     here, rows, cols = queries[0].shape
     spans = here * PARTS
     owners = len(gathered)
-    own_kv = cols // (per_kv * head)
-    q_spec = pl.BlockSpec((here, rows, per_kv * head), lambda h, t: (0, 0, h))
-    kv_spec = pl.BlockSpec((2, here, rows, head), lambda h, t: (0, 0, 0, h))
+    q_spec = pl.BlockSpec((here, rows, per_kv * head), lambda h, t: (0, 0, first + h))
+    kv_spec = pl.BlockSpec((2, here, rows, head), lambda h, t: (0, 0, 0, first + h))
     flat = [x for origin in gathered for x in origin]
     all_rows = spans * rows
-    pairs = 2.2 * all_rows * owners * rows * per_kv * own_kv
+    pairs = 2.2 * all_rows * owners * rows * per_kv * count
     return pl.pallas_call(
         functools.partial(
             attention_kernel, lay, spans, most, per_kv, head, owners, pages_each
         ),
         grid_spec=pltpu.PrefetchScalarGridSpec(
             num_scalar_prefetch=1,
-            grid=(own_kv,),
+            grid=(count,),
             in_specs=[q_spec] * PARTS + [kv_spec] * len(flat),
             out_specs=[
                 pl.BlockSpec((spans, rows, per_kv * head), lambda h, t: (0, 0, h)),
@@ -340,8 +343,8 @@
             scratch_shapes=[pltpu.VMEM((spans, owners * rows, head), jnp.bfloat16)] * 2,
         ),
         out_shape=[
-            jax.ShapeDtypeStruct((spans, rows, cols), jnp.bfloat16),
-            jax.ShapeDtypeStruct((pages_each, 2, PAGE_ROWS, own_kv * head), jnp.bfloat16),
+            jax.ShapeDtypeStruct((spans, rows, count * per_kv * head), jnp.bfloat16),
+            jax.ShapeDtypeStruct((pages_each, 2, PAGE_ROWS, count * head), jnp.bfloat16),
         ],
         compiler_params=params(),
         cost_estimate=cost(
@@ -351,24 +354,28 @@
     )(table, *queries, *flat)
 
 
-def project_kernel(table, attended, wo, *refs):
-    refs[-1][...] = jnp.dot(
-        attended[...], wo[...], preferred_element_type=jnp.float32
-    ).astype(jnp.bfloat16)
-
-
-def make_projection(lay, table, attended, wo, first, count, tile, name, after=()):
-    rows, depth = attended.shape
+def project_kernel(pieces, table, *refs):
+    attended, wo, out = refs[:pieces], refs[pieces], refs[-1]
+    total, at = None, 0
+    for piece in attended:
+        depth = piece.shape[1]
+        term = jnp.dot(piece[...], wo[at : at + depth], preferred_element_type=jnp.float32)
+        total = term if total is None else total + term
+        at += depth
+    out[...] = total.astype(jnp.bfloat16)
+
+
+def make_projection(lay, table, attended, wo, first, count, tile, name, follows=()):
+    rows = attended[0].shape[0]
+    depth = wo.shape[0]
     return pl.pallas_call(
-        project_kernel,
+        functools.partial(project_kernel, len(attended)),
         grid_spec=pltpu.PrefetchScalarGridSpec(
             num_scalar_prefetch=1,
             grid=(count,),
-            in_specs=[
-                pl.BlockSpec((rows, depth), lambda n, t: (0, 0)),
-                pl.BlockSpec((depth, tile), lambda n, t: (0, first(t[lay.tensor_rank]) + n)),
-            ]
-            + [pl.BlockSpec(memory_space=pl.ANY)] * len(after),
+            in_specs=[pl.BlockSpec(x.shape, lambda n, t: (0, 0)) for x in attended]
+            + [pl.BlockSpec((depth, tile), lambda n, t: (0, first(t[lay.tensor_rank]) + n))]
+            + [pl.BlockSpec(memory_space=pl.ANY)] * len(follows),
             out_specs=pl.BlockSpec((rows, tile), lambda n, t: (0, n)),
         ),
         out_shape=jax.ShapeDtypeStruct((rows, count * tile), jnp.bfloat16),
@@ -377,7 +384,7 @@
             2 * rows * depth * count * tile, 2 * (rows * depth + (rows + depth) * count * tile)
         ),
         name=name,
-    )(table, attended, wo, *after)
+    )(table, *attended, wo, *follows)
 
 
 def add_kernel(lay, table, *refs):
@@ -400,7 +407,7 @@
             grid=(steps,),
             in_specs=[pl.BlockSpec((rows, unit), lambda n, t: (0, start + n))] * spans
             + [
-                pl.BlockSpec((spans, rows, unit), lambda n, t: (0, 0, start + n)),
+                pl.BlockSpec((spans, rows, unit), lambda n, t: (0, 0, n)),
                 pl.BlockSpec((spans, rows, unit), lambda n, t: (0, 0, n)),
             ],
             out_specs=pl.BlockSpec((spans, rows, unit), lambda n, t: (0, 0, n)),
@@ -428,6 +435,10 @@
 
 def widths_of(tiles):
     return [1, 2, 1, 1] if tiles == 5 else [1, tiles - 1]
+
+
+def after(x, done):
+    return lax.optimization_barrier((x, done))[0]
 
 
 def shift(x, owners, hop, flip):
@@ -472,14 +483,18 @@
 
     chip, core = group_rank // CORES, group_rank % CORES
     split = hidden_in.reshape(owners, rows, cols)
-    arrived = []
+    arrived, crossed = [], []
     for hop in hop_order(chips):
         for flip in range(CORES):
-            to = (chip + hop) % chips * CORES + (core + flip) % CORES
+            to = lax.rem(chip + hop, chips) * CORES + lax.rem(core + flip, CORES)
             block = lax.dynamic_index_in_dim(split, to, 0, keepdims=False)
             if hop or flip:
+                if paired and len(arrived) > IN_FLIGHT:
+                    block = after(block, crossed[len(arrived) - IN_FLIGHT - 1])
                 block = shift(block, owners, hop, flip)
             arrived.append(block)
+            if paired:
+                crossed.append(lax.ppermute(block, "tensor", swap))
 
     ranks = jnp.stack([group_rank, tensor_rank]).astype(jnp.int32)
     table = make_tables(
@@ -491,68 +506,85 @@
     if paired:
         gain = ln_gain[None]
         gains = [gain, lax.ppermute(gain, "tensor", swap)]
-        crossed = [lax.ppermute(block, "tensor", swap) for block in arrived]
     else:
         gains = [lax.all_gather(ln_gain, "tensor", axis=0, tiled=True)[None]]
 
-    queries, normed, gathered = [], [], [[] for _ in range(owners)]
+    queries, gathered = [], [[] for _ in range(owners)]
     for p in range(PARTS):
         at = slice(p * here, (p + 1) * here)
         if paired:
             xs = [arrived[at], crossed[at]]
         else:
             xs = [[lax.all_gather(jnp.concatenate(arrived[at]), "tensor", axis=1, tiled=True)]]
-        *rows_normed, kv = make_kv(
-            lay, table, xs, gains, wk, wv, key_norm_gain[None], cosine, sine, p
-        )
-        normed.append(rows_normed)
+        kgain = key_norm_gain[None]
+        if queries:
+            kgain = after(kgain, queries[-1])
+        *normed, kv = make_kv(lay, table, xs, gains, wk, wv, kgain, cosine, sine, p)
         kv = kv.reshape(2, here, rows, kv.shape[2])
         for back in range(chips):
             if back:
+                if p and back == chips // 2:
+                    kv = after(kv, queries[-1])
                 kv = shift(kv, owners, 1, 0)
             gathered[back * CORES].append(kv)
             gathered[back * CORES + 1].append(shift(kv, owners, 0, 1))
-    for p in range(PARTS):
-        made = make_q(lay, table, normed[p], wq, q_gain[None], cosine, sine, p)
-        queries.append(made.reshape(here, rows, made.shape[1]))
-
-    attended, pages = make_attention(
-        lay, most, table, queries, gathered, per_kv, head, pages_each
-    )
-    attended = attended.reshape(spans * rows, -1)
+            if back == 1 or chips == 1:
+                qgain = q_gain[None]
+                if p:
+                    qgain = after(qgain, gathered[(chips // 2) * CORES][0])
+                made = make_q(lay, table, normed, wq, qgain, cosine, sine, p)
+                queries.append(made.reshape(here, rows, made.shape[1]))
+
+    own_kv = wk.shape[1] // head
+    sets = [own_kv // 2, own_kv - own_kv // 2] if own_kv > 1 else [own_kv]
+    attended, pages, first = [], [], 0
+    for count in sets:
+        made, cut = make_attention(
+            lay, most, table, queries, gathered, per_kv, head, pages_each, first, count
+        )
+        attended.append(made.reshape(spans * rows, -1))
+        pages.append(cut)
+        first += count
 
     if paired:
         tile = 512
         half_tiles = cols // tile
         widths = widths_of(half_tiles)
-        received, first, last = [], 0, ()
-        for width in widths:
-            partial = make_projection(
-                lay, table, attended, wo,
-                lambda r, first=first: (1 - r) * half_tiles + first, width, tile, "send_part",
-                last,
-            )
-            last = (partial,)
-            received.append(lax.ppermute(partial, "tensor", swap).reshape(spans, rows, -1))
-            first += width
-        own = make_projection(
-            lay, table, attended, wo, lambda r: r * half_tiles, half_tiles, tile, "own_part", last
-        ).reshape(spans, rows, cols)
-        pages, received[-2] = lax.optimization_barrier((pages, received[-2]))
-        other = lax.ppermute(pages, "tensor", swap)
-        cache = jnp.concatenate(
-            [jnp.where(tensor_rank == 0, pages, other), jnp.where(tensor_rank == 0, other, pages)],
-            axis=3,
-        )
-        pieces, first = [], 0
-        for got in received:
-            moved = make_sum(lay, table, arrived, own, got, first)
-            pieces.append(
-                lax.all_to_all(moved, "group", split_axis=0, concat_axis=0, tiled=True)
-            )
-            first += got.shape[2]
+        others = [lax.ppermute(pages[0], "tensor", swap)]
+        own, received, moved, starts = [], [], [], []
+        for n in range(len(widths) + 1):
+            if n < len(widths):
+                first = sum(widths[:n])
+                starts.append(first * tile)
+                follows = (others[0],) if n == 0 else own[-1:] if n == 1 else moved[-1:]
+                sent = make_projection(
+                    lay, table, attended, wo,
+                    lambda r, first=first: (1 - r) * half_tiles + first,
+                    widths[n], tile, "send_part", follows,
+                )
+                received.append(lax.ppermute(sent, "tensor", swap).reshape(spans, rows, -1))
+                own.append(make_projection(
+                    lay, table, attended, wo,
+                    lambda r, first=first: r * half_tiles + first,
+                    widths[n], tile, "own_part", (sent,),
+                ).reshape(spans, rows, -1))
+            if n:
+                moved.append(
+                    make_sum(lay, table, arrived, own[n - 1], received[n - 1], starts[n - 1])
+                )
+        for cut in pages[1:]:
+            others.append(lax.ppermute(after(cut, received[-2]), "tensor", swap))
+        low = [jnp.where(tensor_rank == 0, a, b) for a, b in zip(pages, others)]
+        high = [jnp.where(tensor_rank == 0, b, a) for a, b in zip(pages, others)]
+        cache = jnp.concatenate(low + high, axis=3)
+        pieces = [
+            lax.all_to_all(rows_of, "group", split_axis=0, concat_axis=0, tiled=True)
+            for rows_of in moved
+        ]
         mixed = jnp.concatenate(pieces, axis=2).reshape(1, span_len, cols)
     else:
+        pages = jnp.concatenate(pages, axis=3)
+        attended = jnp.concatenate(attended, axis=1)
         if kv_cols < head:
             pages = lax.dynamic_slice_in_dim(
                 pages, lax.rem(tensor_rank, head // kv_cols) * kv_cols, kv_cols, 3

time: 370 us -> 349 us (0.943)
  waiting for transfers between devices: 185 us -> 161 us
  starting transfers between devices: 62.7 us -> 39.5 us
  blocking collectives: 0 us -> 19.9 us
    all_to_all x0 -> x1, blocking collectives: none -> 19.9 us  [local(): lax.all_to_all(rows_of, 'group', split_axis=0, concat_axis=0, tiled=True)]
    ppermute x21, starting transfers between devices: 29.8 us -> 11.6 us  [shift(): return lax.ppermute(x, 'group', pairs)]
    ppermute x13 -> x14, waiting for transfers between devices: 96.2 us -> 78.6 us  [the longest x4 47.5 us: local(): received.append(lax.ppermute(sent, 'tensor', swap).reshape(spans, rows, -1))]
    ppermute x21, waiting for transfers between devices: 88.4 us -> 71.6 us  [shift(): return lax.ppermute(x, 'group', pairs)]
    all_to_all x4 -> x3, waiting for transfers between devices: 0.01 us -> 10.7 us  [local(): lax.all_to_all(rows_of, 'group', split_axis=0, concat_axis=0, tiled=True)]
    pallas_call x5 -> x8, Pallas kernels: 24 us -> 30.4 us  [make_projection(): pl.pallas_call(functools.partial(project_kernel, len(attended)), grid_spe...]
    all_to_all x4 -> x3, starting transfers between devices: 18.9 us -> 13.2 us  [local(): lax.all_to_all(rows_of, 'group', split_axis=0, concat_axis=0, tiled=True)]
    pallas_call x4, Pallas kernels: 10.3 us -> 5.09 us  [make_sum(): pl.pallas_call(functools.partial(add_kernel, lay), grid_spec=pltpu.Prefet...]
  transfers between devices with their start and end apart: 39 -> 39, of which waited for: 18 -> 15; matrix products, arithmetic and copies ran while one was open for 2% -> 2% of each run, Pallas kernels for 19% -> 25%
where the time goes in v3:
time: 349 us; the launch traced here: 348 us
  waiting for transfers between devices  161 us (46%)
  Pallas kernels  105 us (30%)
  starting transfers between devices  39.5 us (11%)
  blocking collectives  19.9 us (6%)
  local copies, waits for them, and re-layouts  14.6 us (4%)
  other arithmetic  7.18 us (2%)
    ppermute x21, waiting for transfers between devices, shift(): return lax.ppermute(x, 'group', pairs)  71.6 us
    ppermute x4, waiting for transfers between devices, local(): received.append(lax.ppermute(sent, 'tensor', swap).reshape(spans, rows, -1))  47.5 us
    pallas_call x8, Pallas kernels, make_projection(): pl.pallas_call(functools.partial(project_kernel, len(attended)), grid_spe...  30.4 us
    pallas_call x2, Pallas kernels, make_attention(): pl.pallas_call(functools.partial(attention_kernel, lay, spans, most, per_...  28.3 us
    pallas_call x2, Pallas kernels, make_q(): pl.pallas_call(functools.partial(q_kernel, sides), grid_spec=pltpu.Prefet...  22.6 us
    all_to_all x1, blocking collectives, local(): lax.all_to_all(rows_of, 'group', split_axis=0, concat_axis=0, tiled=True)  19.9 us
    ppermute x8, waiting for transfers between devices, local(): crossed.append(lax.ppermute(block, 'tensor', swap))  18 us
    pallas_call x2, Pallas kernels, make_kv(): pl.pallas_call(functools.partial(kv_kernel, sides, blocks), grid_spec=plt...  17.1 us
  transfers between devices with their start and end apart: 39, of which 15 were waited for; matrix products, arithmetic and copies ran while one was open for 2% of the time, Pallas kernels for 25%

profile of v3, /device:TPU:0, one launch (start us, length us, event | category | flops | bytes accessed | tf_op | source)
XLA Modules:
  0.0 348.4 jit_solution(14586085740034928919)
XLA Ops:
  1.3 2.9 collective-permute-start.11
  4.3 2.7 dynamic-slice_bitcast_fusion
  7.7 1.6 collective-permute-start.1
  11.1 1.4 tables.1.table
  13.4 12.4 %collective-permute-done.1.refs_2_ = bf16[64,2560]{1,0:T(8,128)(2,1)S(1)} collective-permute-done((bf16[64,2560]{1,0:T(8,128)(2,1)}, bf16[64,2560]{1,0:T(8,128)(2,1)S(1)}, u32[]{:S(2)}, u32[]{:S(2)}) %collective-permute-start.1) | collective-permute-done | bytes 327712 | tf_op jit(solution)/shard_map/ppermute | solution.py:451
  25.9 1.9 collective-permute-start.6
  29.0 1.7 collective-permute-start.3
  30.8 5.6 %collective-permute-done.8.refs_6_ = bf16[64,2560]{1,0:T(8,128)(2,1)S(1)} collective-permute-done((bf16[64,2560]{1,0:T(8,128)(2,1)S(1)}, bf16[64,2560]{1,0:T(8,128)(2,1)S(1)}, u32[]{:S(2)}, u32[]{:S(2)}) %collective-permute-start.8) | collective-permute-done | bytes 327712 | tf_op jit(solution)/shard_map/ppermute | solution.py:497
  36.4 7.0 %collective-permute-done.6.refs_5_ = bf16[64,2560]{1,0:T(8,128)(2,1)S(1)} collective-permute-done((bf16[64,2560]{1,0:T(8,128)(2,1)S(1)}, bf16[64,2560]{1,0:T(8,128)(2,1)S(1)}, u32[]{:S(2)}, u32[]{:S(2)}) %collective-permute-start.6) | collective-permute-done | bytes 327712 | tf_op jit(solution)/shard_map/ppermute | solution.py:497
  44.0 5.3 %collective-permute-done.10.refs_7_ = bf16[64,2560]{1,0:T(8,128)(2,1)S(1)} collective-permute-done((bf16[64,2560]{1,0:T(8,128)(2,1)S(1)}, bf16[64,2560]{1,0:T(8,128)(2,1)S(1)}, u32[]{:S(2)}, u32[]{:S(2)}) %collective-permute-start.10) | collective-permute-done | bytes 327712 | tf_op jit(solution)/shard_map/ppermute | solution.py:497
  50.0 8.6 %keys_values.2 = (bf16[256,2560]{1,0:T(8,128)(2,1)S(1)}, bf16[256,2560]{1,0:T(8,128)(2,1)}, bf16[2,256,512]{2,1,0:T(8,128)(2,1)S(1)}) custom-call(s32[122]{0:T(128)S(1)} %copy-done.30, bf16[64,2560]{1,0:T(8,128)(2,1)S(1)} %get-tuple-element.43.refs_0_, bf16[64,2560]{1,0:T(8,128)(2,1)S(1)} %collective-permute-done.refs_1_, ...), custom_call_target="tpu_custom_call" | custom-call | flops 268435456 | bytes 1572864 | tf_op jit(solution)/shard_map/keys_values/pallas_call | solution.py:169
  58.9 1.7 collective-permute-start.13
  60.6 17.9 %collective-permute-done.9.refs_3_.refs_7_ = bf16[64,2560]{1,0:T(8,128)(2,1)S(1)} collective-permute-done((bf16[64,2560]{1,0:T(8,128)(2,1)S(1)}, bf16[64,2560]{1,0:T(8,128)(2,1)S(1)}, u32[]{:S(2)}, u32[]{:S(2)}) %collective-permute-start.9) | collective-permute-done | bytes 327712 | tf_op jit(solution)/shard_map/ppermute | solution.py:451
  79.0 4.7 %collective-permute-done.7.refs_2_.refs_6_ = bf16[64,2560]{1,0:T(8,128)(2,1)S(1)} collective-permute-done((bf16[64,2560]{1,0:T(8,128)(2,1)S(1)}, bf16[64,2560]{1,0:T(8,128)(2,1)S(1)}, u32[]{:S(2)}, u32[]{:S(2)}) %collective-permute-start.7) | collective-permute-done | bytes 327712 | tf_op jit(solution)/shard_map/ppermute | solution.py:451
  85.2 1.3 copy-done.24
  86.5 11.3 %queries.2 = bf16[256,2048]{1,0:T(8,128)(2,1)S(1)} custom-call(s32[122]{0:T(128)S(1)} %copy-done.31, bf16[256,2560]{1,0:T(8,128)(2,1)S(1)} %get-tuple-element.22.refs_0_, bf16[256,2560]{1,0:T(8,128)(2,1)S(1)} %copy-done.24, bf16[5120,2048]{1,0:T(8,128)(2,1)} %refs_3_.3, bf16[5120,2048]{1,0:T(8,128)(2,1)} %refs_3_.3, bf16[1,128]{1,0:T(2,128)(2,1)S(1)} %bitcast.74, ...), custom_call_target="tpu_custom_call" | custom-call | flops 536870912 | bytes 2464153 | tf_op jit(solution)/shard_map/queries/pallas_call | solution.py:225
  98.9 8.6 %keys_values.3 = (bf16[256,2560]{1,0:T(8,128)(2,1)S(1)}, bf16[256,2560]{1,0:T(8,128)(2,1)}, bf16[2,256,512]{2,1,0:T(8,128)(2,1)S(1)}) custom-call(s32[122]{0:T(128)S(1)} %copy-done.31, bf16[64,2560]{1,0:T(8,128)(2,1)S(1)} %collective-permute-done.3.refs_0_.refs_4_, bf16[64,2560]{1,0:T(8,128)(2,1)S(1)} %collective-permute-done.5.refs_1_.refs_5_, ...), custom_call_target="tpu_custom_call" | custom-call | flops 268435456 | bytes 1572864 | tf_op jit(solution)/shard_map/keys_values/pallas_call | solution.py:169
  107.4 2.5 collective-permute-start.20
  109.9 1.3 copy-done.25
  111.2 11.3 %queries.3 = bf16[256,2048]{1,0:T(8,128)(2,1)S(1)} custom-call(s32[122]{0:T(128)S(1)} %copy-done.31, bf16[256,2560]{1,0:T(8,128)(2,1)S(1)} %get-tuple-element.25.refs_0_, bf16[256,2560]{1,0:T(8,128)(2,1)S(1)} %copy-done.25, bf16[5120,2048]{1,0:T(8,128)(2,1)} %refs_3_.3, bf16[5120,2048]{1,0:T(8,128)(2,1)} %refs_3_.3, bf16[1,128]{1,0:T(2,128)(2,1)S(1)} %bitcast.75, ...), custom_call_target="tpu_custom_call" | custom-call | flops 536870912 | bytes 2464153 | tf_op jit(solution)/shard_map/queries/pallas_call | solution.py:225
  125.4 14.7 %collective-permute-done.23.refs_11_ = bf16[2,4,64,512]{3,2,1,0:T(8,128)(2,1)S(1)} collective-permute-done((bf16[2,4,64,512]{3,2,1,0:T(8,128)(2,1)S(1)}, bf16[2,4,64,512]{3,2,1,0:T(8,128)(2,1)S(1)}, u32[]{:S(2)}, u32[]{:S(2)}) %collective-permute-start.23) | collective-permute-done | bytes 524320 | tf_op jit(solution)/shard_map/ppermute | solution.py:451
  140.7 10.7 %collective-permute-done.26.refs_14_ = bf16[2,4,64,512]{3,2,1,0:T(8,128)(2,1)S(1)} collective-permute-done((bf16[2,4,64,512]{3,2,1,0:T(8,128)(2,1)S(1)}, bf16[2,4,64,512]{3,2,1,0:T(8,128)(2,1)S(1)}, u32[]{:S(2)}, u32[]{:S(2)}) %collective-permute-start.26) | collective-permute-done | bytes 524320 | tf_op jit(solution)/shard_map/ppermute | solution.py:451
  151.9 9.4 %collective-permute-done.27.refs_15_ = bf16[2,4,64,512]{3,2,1,0:T(8,128)(2,1)S(1)} collective-permute-done((bf16[2,4,64,512]{3,2,1,0:T(8,128)(2,1)S(1)}, bf16[2,4,64,512]{3,2,1,0:T(8,128)(2,1)S(1)}, u32[]{:S(2)}, u32[]{:S(2)}) %collective-permute-start.27) | collective-permute-done | bytes 524320 | tf_op jit(solution)/shard_map/ppermute | solution.py:451
  161.4 1.8 collective-permute-done.29.refs_17_
  164.0 14.2 %attention.2 = (bf16[8,64,1024]{2,1,0:T(8,128)(2,1)}, bf16[4,2,128,256]{3,2,1,0:T(8,128)(2,1)S(1)}) custom-call(s32[122]{0:T(128)S(1)} %copy-done.31, bf16[4,64,2048]{2,1,0:T(8,128)(2,1)} %bitcast.52, bf16[4,64,2048]{2,1,0:T(8,128)(2,1)} %bitcast.54, bf16[2,4,64,512]{3,2,1,0:T(8,128)(2,1)S(1)} %bitcast.61, bf16[2,4,64,512]{3,2,1,0:T(8,128)(2,1)S(1)} %bitcast.65, ...), custom_call_target="tpu_custom_call" | custom-call | flops 236223200 | bytes 1258291 | tf_op jit(solution)/shard_map/attention/pallas_call | solution.py:331
  178.2 1.3 collective-permute-start.30
  179.4 14.2 %attention.3 = (bf16[8,64,1024]{2,1,0:T(8,128)(2,1)}, bf16[4,2,128,256]{3,2,1,0:T(8,128)(2,1)S(1)}) custom-call(s32[122]{0:T(128)S(1)} %copy-done.31, bf16[4,64,2048]{2,1,0:T(8,128)(2,1)} %bitcast.53, bf16[4,64,2048]{2,1,0:T(8,128)(2,1)} %bitcast.55, bf16[2,4,64,512]{3,2,1,0:T(8,128)(2,1)S(1)} %bitcast.62, bf16[2,4,64,512]{3,2,1,0:T(8,128)(2,1)S(1)} %bitcast.66, ...), custom_call_target="tpu_custom_call" | custom-call | flops 236223200 | bytes 1258291 | tf_op jit(solution)/shard_map/attention/pallas_call | solution.py:331
  193.7 1.6 copy-done.1
  195.2 3.4 send_part.4.refs_3_
  199.6 3.4 own_part.4
  203.0 9.4 %collective-permute-done.31 = bf16[512,512]{1,0:T(8,128)(2,1)S(1)} collective-permute-done((bf16[512,512]{1,0:T(8,128)(2,1)S(1)}, bf16[512,512]{1,0:T(8,128)(2,1)S(1)}, u32[]{:S(2)}, u32[]{:S(2)}) %collective-permute-start.31) | collective-permute-done | bytes 524320 | tf_op jit(solution)/shard_map/ppermute | solution.py:565
  214.7 4.2 %all-to-all-start = ((bf16[8,64,512]{2,1,0:T(8,128)(2,1)}), bf16[8,64,512]{2,1,0:T(8,128)(2,1)}, u32[]{:S(2)}, u32[]{:S(2)}) async-start(bf16[8,64,512]{2,1,0:T(8,128)(2,1)} %copy-done.19), calls=%async_computation | async-start | bytes 1048576 | tf_op jit(solution)/shard_map/all_to_all | solution.py:581
  220.0 5.5 %send_part.5.refs_3_ = bf16[512,1024]{1,0:T(8,128)(2,1)} custom-call(s32[122]{0:T(128)S(1)} %copy-done.31, bf16[512,1024]{1,0:T(8,128)(2,1)S(1)} %bitcast.38, bf16[512,1024]{1,0:T(8,128)(2,1)S(1)} %bitcast.46, bf16[2048,5120]{1,0:T(8,128)(2,1)} %refs_2_.19, bf16[8,64,512]{2,1,0:T(8,128)(2,1)S(1)} %bitcast.57), custom_call_target="tpu_custom_call" | custom-call | flops 214748368 | bytes 734003 | tf_op jit(solution)/shard_map/send_part/pallas_call | solution.py:371
  226.3 3.4 send_part.6.refs_3_
  230.9 3.4 own_part.6
  234.3 28.0 %collective-permute-done.33 = bf16[512,512]{1,0:T(8,128)(2,1)S(1)} collective-permute-done((bf16[512,512]{1,0:T(8,128)(2,1)S(1)}, bf16[512,512]{1,0:T(8,128)(2,1)S(1)}, u32[]{:S(2)}, u32[]{:S(2)}) %collective-permute-start.33) | collective-permute-done | bytes 524320 | tf_op jit(solution)/shard_map/ppermute | solution.py:565
  263.8 4.8 %all-to-all-start.2 = ((bf16[8,64,512]{2,1,0:T(8,128)(2,1)}), bf16[8,64,512]{2,1,0:T(8,128)(2,1)}, u32[]{:S(2)}, u32[]{:S(2)}) async-start(bf16[8,64,512]{2,1,0:T(8,128)(2,1)} %copy-done.21), calls=%async_computation.2 | async-start | bytes 1048576 | tf_op jit(solution)/shard_map/all_to_all | solution.py:581
  268.7 4.7 %own_part.5 = bf16[512,1024]{1,0:T(8,128)(2,1)S(1)} custom-call(s32[122]{0:T(128)S(1)} %copy-done.31, bf16[512,1024]{1,0:T(8,128)(2,1)S(1)} %bitcast.41, bf16[512,1024]{1,0:T(8,128)(2,1)S(1)} %bitcast.49, bf16[2048,5120]{1,0:T(8,128)(2,1)} %refs_2_.19, bf16[512,1024]{1,0:T(8,128)(2,1)} %send_part.5.refs_3_), custom_call_target="tpu_custom_call" | custom-call | flops 214748368 | bytes 734003 | tf_op jit(solution)/shard_map/own_part/pallas_call | solution.py:371
  273.4 2.9 residual.5.refs_3_
  276.3 3.4 send_part.7.refs_3_
  280.6 3.4 own_part.7
  284.0 10.1 %collective-permute-done.34 = bf16[512,512]{1,0:T(8,128)(2,1)S(1)} collective-permute-done((bf16[512,512]{1,0:T(8,128)(2,1)S(1)}, bf16[512,512]{1,0:T(8,128)(2,1)S(1)}, u32[]{:S(2)}, u32[]{:S(2)}) %collective-permute-start.34) | collective-permute-done | bytes 524320 | tf_op jit(solution)/shard_map/ppermute | solution.py:565
  294.8 19.9 %all_to_all.20 = bf16[8,64,512]{2,1,0:T(8,128)(2,1)S(1)} all-to-all(bf16[8,64,512]{2,1,0:T(8,128)(2,1)S(1)} %residual.7), channel_id=1, replica_groups=mesh['replica'=2,'tensor'=2,'group'=8] {'group'}, dimensions={0} | all-to-all | bytes 1048576 | tf_op jit(solution)/shard_map/all_to_all | solution.py:581
  314.7 4.2 %all-to-all-start.1 = ((bf16[8,64,1024]{2,1,0:T(8,128)(2,1)}), bf16[8,64,1024]{2,1,0:T(8,128)(2,1)}, u32[]{:S(2)}, u32[]{:S(2)}) async-start(bf16[8,64,1024]{2,1,0:T(8,128)(2,1)} %residual.5.refs_3_), calls=%async_computation.1 | async-start | bytes 2097152 | tf_op jit(solution)/shard_map/all_to_all | solution.py:581
  320.0 13.2 %collective-permute-done.35 = bf16[4,2,128,256]{3,2,1,0:T(8,128)(2,1)S(1)} collective-permute-done((bf16[4,2,128,256]{3,2,1,0:T(8,128)(2,1)S(1)}, bf16[4,2,128,256]{3,2,1,0:T(8,128)(2,1)S(1)}, u32[]{:S(2)}, u32[]{:S(2)}) %collective-permute-start.35) | collective-permute-done | bytes 524320 | tf_op jit(solution)/shard_map/ppermute | solution.py:576
  333.3 1.6 pad_maximum_fusion.1
  334.9 10.7 %all-to-all-done.1 = bf16[8,64,1024]{2,1,0:T(8,128)(2,1)} async-done(((bf16[8,64,1024]{2,1,0:T(8,128)(2,1)}), bf16[8,64,1024]{2,1,0:T(8,128)(2,1)}, u32[]{:S(2)}, u32[]{:S(2)}) %all-to-all-start.1) | async-done | bytes 1048608 | tf_op jit(solution)/shard_map/all_to_all | solution.py:581
  345.6 2.8 pad_maximum_fusion
  (143 shorter events, 25.5 us)
Async XLA Ops:
  0.6 48.7 %copy-start.32 = (bf16[128]{0:T(256)(128)(2,1)S(1)}, bf16[128]{0:T(256)(128)(2,1)}, u32[]{:S(2)}) copy-start(bf16[128]{0:T(256)(128)(2,1)} %param.18) | copy-start | bytes 772
  1.3 42.1 %collective-permute-start.11 = (bf16[1,2560]{1,0:T(2,128)(2,1)S(1)}, bf16[1,2560]{1,0:T(2,128)(2,1)S(1)}, u32[]{:S(2)}, u32[]{:S(2)}) collective-permute-start(bf16[1,2560]{1,0:T(2,128)(2,1)S(1)} %broadcast_in_dim.6.refs_8_), channel_id=1, source_target_pairs={{0,8},{8,0},{1,9},{9,1},{2,10},{10,2},{3,11},{11,3},{4,12},{12,4},... | collective-permute-start | bytes 15368 | tf_op jit(solution)/shard_map/ppermute | solution.py:508
  7.0 20.9 %collective-permute-start.2 = (bf16[64,2560]{1,0:T(8,128)(2,1)S(1)}, bf16[64,2560]{1,0:T(8,128)(2,1)S(1)}, u32[]{:S(2)}, u32[]{:S(2)}) collective-permute-start(bf16[64,2560]{1,0:T(8,128)(2,1)S(1)} %get-tuple-element.40), channel_id=1, source_target_pairs={{0,3},{1,2},{2,5},{3,4},{4,7},{5,6},{6,1},{7,0},{8,11},{9,10},{10,... | collective-permute-start | bytes 983048 | tf_op jit(solution)/shard_map/ppermute | solution.py:451
  7.7 18.1 %collective-permute-start.1 = (bf16[64,2560]{1,0:T(8,128)(2,1)}, bf16[64,2560]{1,0:T(8,128)(2,1)S(1)}, u32[]{:S(2)}, u32[]{:S(2)}) collective-permute-start(bf16[64,2560]{1,0:T(8,128)(2,1)} %get-tuple-element.41), channel_id=1, source_target_pairs={{0,2},{1,3},{2,4},{3,5},{4,6},{5,7},{6,0},{7,1},{8,10},{9,11},{10,... | collective-permute-start | bytes 983048 | tf_op jit(solution)/shard_map/ppermute | solution.py:451
  9.3 16.6 %collective-permute-start = (bf16[64,2560]{1,0:T(8,128)(2,1)}, bf16[64,2560]{1,0:T(8,128)(2,1)S(1)}, u32[]{:S(2)}, u32[]{:S(2)}) collective-permute-start(bf16[64,2560]{1,0:T(8,128)(2,1)} %get-tuple-element.42), channel_id=1, source_target_pairs={{0,1},{1,0},{2,3},{3,2},{4,5},{5,4},{6,7},{7,6},{8,9},{9,8},{10,11... | collective-permute-start | bytes 983048 | tf_op jit(solution)/shard_map/ppermute | solution.py:451
  9.9 19.1 %collective-permute-start.4 = (bf16[64,2560]{1,0:T(8,128)(2,1)S(1)}, bf16[64,2560]{1,0:T(8,128)(2,1)S(1)}, u32[]{:S(2)}, u32[]{:S(2)}) collective-permute-start(bf16[64,2560]{1,0:T(8,128)(2,1)S(1)} %get-tuple-element.43.refs_0_), channel_id=1, source_target_pairs={{0,8},{8,0},{1,9},{9,1},{2,10},{10,2},{3,11},{11,3},{4,12},{12,4},... | collective-permute-start | bytes 983048 | tf_op jit(solution)/shard_map/ppermute | solution.py:497
  25.8 10.6 %collective-permute-start.8 = (bf16[64,2560]{1,0:T(8,128)(2,1)S(1)}, bf16[64,2560]{1,0:T(8,128)(2,1)S(1)}, u32[]{:S(2)}, u32[]{:S(2)}) collective-permute-start(bf16[64,2560]{1,0:T(8,128)(2,1)S(1)} %collective-permute-done.1.refs_2_), channel_id=1, source_target_pairs={{0,8},{8,0},{1,9},{9,1},{2,10},{10,2},{3,11},{11,3},{4,12},{12,4},... | collective-permute-start | bytes 983048 | tf_op jit(solution)/shard_map/ppermute | solution.py:497
  25.9 17.5 %collective-permute-start.6 = (bf16[64,2560]{1,0:T(8,128)(2,1)S(1)}, bf16[64,2560]{1,0:T(8,128)(2,1)S(1)}, u32[]{:S(2)}, u32[]{:S(2)}) collective-permute-start(bf16[64,2560]{1,0:T(8,128)(2,1)S(1)} %collective-permute-done.refs_1_), channel_id=1, source_target_pairs={{0,8},{8,0},{1,9},{9,1},{2,10},{10,2},{3,11},{11,3},{4,12},{12,4},... | collective-permute-start | bytes 983048 | tf_op jit(solution)/shard_map/ppermute | solution.py:497
  27.8 21.5 %collective-permute-start.10 = (bf16[64,2560]{1,0:T(8,128)(2,1)S(1)}, bf16[64,2560]{1,0:T(8,128)(2,1)S(1)}, u32[]{:S(2)}, u32[]{:S(2)}) collective-permute-start(bf16[64,2560]{1,0:T(8,128)(2,1)S(1)} %collective-permute-done.2.refs_3_), channel_id=1, source_target_pairs={{0,8},{8,0},{1,9},{9,1},{2,10},{10,2},{3,11},{11,3},{4,12},{12,4},... | collective-permute-start | bytes 983048 | tf_op jit(solution)/shard_map/ppermute | solution.py:497
  29.0 29.5 %collective-permute-start.3 = (bf16[64,2560]{1,0:T(8,128)(2,1)S(1)}, bf16[64,2560]{1,0:T(8,128)(2,1)S(1)}, u32[]{:S(2)}, u32[]{:S(2)}) collective-permute-start(bf16[64,2560]{1,0:T(8,128)(2,1)S(1)} %get-tuple-element.39), channel_id=1, source_target_pairs={{0,6},{1,7},{2,0},{3,1},{4,2},{5,3},{6,4},{7,5},{8,14},{9,15},{10,... | collective-permute-start | bytes 983048 | tf_op jit(solution)/shard_map/ppermute | solution.py:451
  36.4 22.5 %collective-permute-start.5 = (bf16[64,2560]{1,0:T(8,128)(2,1)S(1)}, bf16[64,2560]{1,0:T(8,128)(2,1)S(1)}, u32[]{:S(2)}, u32[]{:S(2)}) collective-permute-start(bf16[64,2560]{1,0:T(8,128)(2,1)S(1)} %get-tuple-element.19), channel_id=1, source_target_pairs={{0,7},{1,6},{2,1},{3,0},{4,3},{5,2},{6,5},{7,4},{8,15},{9,14},{10,... | collective-permute-start | bytes 983048 | tf_op jit(solution)/shard_map/ppermute | solution.py:451
  43.4 35.1 %collective-permute-start.9 = (bf16[64,2560]{1,0:T(8,128)(2,1)S(1)}, bf16[64,2560]{1,0:T(8,128)(2,1)S(1)}, u32[]{:S(2)}, u32[]{:S(2)}) collective-permute-start(bf16[64,2560]{1,0:T(8,128)(2,1)S(1)} %get-tuple-element.21), channel_id=1, source_target_pairs={{0,5},{1,4},{2,7},{3,6},{4,1},{5,0},{6,3},{7,2},{8,13},{9,12},{10,... | collective-permute-start | bytes 983048 | tf_op jit(solution)/shard_map/ppermute | solution.py:451
  43.4 40.3 %collective-permute-start.7 = (bf16[64,2560]{1,0:T(8,128)(2,1)S(1)}, bf16[64,2560]{1,0:T(8,128)(2,1)S(1)}, u32[]{:S(2)}, u32[]{:S(2)}) collective-permute-start(bf16[64,2560]{1,0:T(8,128)(2,1)S(1)} %get-tuple-element.20), channel_id=1, source_target_pairs={{0,4},{1,5},{2,6},{3,7},{4,0},{5,1},{6,2},{7,3},{8,12},{9,13},{10,... | collective-permute-start | bytes 983048 | tf_op jit(solution)/shard_map/ppermute | solution.py:451
  50.0 35.3 %copy-start.31 = (s32[122]{0:T(128)S(1)}, s32[122]{0:T(128)}, u32[]{:S(2)}) copy-start(s32[122]{0:T(128)} %tables.1.table) | copy-start | bytes 1468
  50.0 35.3 %copy-start.33 = (bf16[128]{0:T(256)(128)(2,1)S(1)}, bf16[128]{0:T(256)(128)(2,1)}, u32[]{:S(2)}) copy-start(bf16[128]{0:T(256)(128)(2,1)} %param.17) | copy-start | bytes 772
  58.5 25.6 %collective-permute-start.16 = (bf16[2,4,64,512]{3,2,1,0:T(8,128)(2,1)S(1)}, bf16[2,4,64,512]{3,2,1,0:T(8,128)(2,1)S(1)}, u32[]{:S(2)}, u32[]{:S(2)}) collective-permute-start(bf16[2,4,64,512]{3,2,1,0:T(8,128)(2,1)S(1)} %bitcast.59), channel_id=1, source_target_pairs={{0,2},{1,3},{2,4},{3,5},{4,6},{5,7},{6,0},{7,1},{8,10},{9,11},{10,... | collective-permute-start | bytes 1572872 | tf_op jit(solution)/shard_map/ppermute | solution.py:451
  58.5 153.9 %copy-start.5 = (bf16[64,2560]{1,0:T(8,128)(2,1)}, bf16[64,2560]{1,0:T(8,128)(2,1)S(1)}, u32[]{:S(2)}) copy-start(bf16[64,2560]{1,0:T(8,128)(2,1)S(1)} %collective-permute-done.3.refs_0_.refs_4_) | copy-start | bytes 983044
  58.5 40.3 %collective-permute-start.12 = (bf16[64,2560]{1,0:T(8,128)(2,1)S(1)}, bf16[64,2560]{1,0:T(8,128)(2,1)S(1)}, u32[]{:S(2)}, u32[]{:S(2)}) collective-permute-start(bf16[64,2560]{1,0:T(8,128)(2,1)S(1)} %collective-permute-done.3.refs_0_.refs_4_), channel_id=1, source_target_pairs={{0,8},{8,0},{1,9},{9,1},{2,10},{10,2},{3,11},{11,3},{4,12},{12,4},... | collective-permute-start | bytes 983048 | tf_op jit(solution)/shard_map/ppermute | solution.py:497
  58.9 153.5 %copy-start.8 = (bf16[64,2560]{1,0:T(8,128)(2,1)}, bf16[64,2560]{1,0:T(8,128)(2,1)S(1)}, u32[]{:S(2)}) copy-start(bf16[64,2560]{1,0:T(8,128)(2,1)S(1)} %collective-permute-done.5.refs_1_.refs_5_) | copy-start | bytes 983044
  58.9 40.0 %collective-permute-start.13 = (bf16[64,2560]{1,0:T(8,128)(2,1)S(1)}, bf16[64,2560]{1,0:T(8,128)(2,1)S(1)}, u32[]{:S(2)}, u32[]{:S(2)}) collective-permute-start(bf16[64,2560]{1,0:T(8,128)(2,1)S(1)} %collective-permute-done.5.refs_1_.refs_5_), channel_id=1, source_target_pairs={{0,8},{8,0},{1,9},{9,1},{2,10},{10,2},{3,11},{11,3},{4,12},{12,4},... | collective-permute-start | bytes 983048 | tf_op jit(solution)/shard_map/ppermute | solution.py:497
  78.5 133.9 %copy-start.11 = (bf16[64,2560]{1,0:T(8,128)(2,1)}, bf16[64,2560]{1,0:T(8,128)(2,1)S(1)}, u32[]{:S(2)}) copy-start(bf16[64,2560]{1,0:T(8,128)(2,1)S(1)} %collective-permute-done.9.refs_3_.refs_7_) | copy-start | bytes 983044
  78.5 20.3 %collective-permute-start.15 = (bf16[64,2560]{1,0:T(8,128)(2,1)S(1)}, bf16[64,2560]{1,0:T(8,128)(2,1)S(1)}, u32[]{:S(2)}, u32[]{:S(2)}) collective-permute-start(bf16[64,2560]{1,0:T(8,128)(2,1)S(1)} %collective-permute-done.9.refs_3_.refs_7_), channel_id=1, source_target_pairs={{0,8},{8,0},{1,9},{9,1},{2,10},{10,2},{3,11},{11,3},{4,12},{12,4},... | collective-permute-start | bytes 983048 | tf_op jit(solution)/shard_map/ppermute | solution.py:497
  83.7 128.7 %copy-start.14 = (bf16[64,2560]{1,0:T(8,128)(2,1)}, bf16[64,2560]{1,0:T(8,128)(2,1)S(1)}, u32[]{:S(2)}) copy-start(bf16[64,2560]{1,0:T(8,128)(2,1)S(1)} %collective-permute-done.7.refs_2_.refs_6_) | copy-start | bytes 983044
  83.7 15.1 %collective-permute-start.14 = (bf16[64,2560]{1,0:T(8,128)(2,1)S(1)}, bf16[64,2560]{1,0:T(8,128)(2,1)S(1)}, u32[]{:S(2)}, u32[]{:S(2)}) collective-permute-start(bf16[64,2560]{1,0:T(8,128)(2,1)S(1)} %collective-permute-done.7.refs_2_.refs_6_), channel_id=1, source_target_pairs={{0,8},{8,0},{1,9},{9,1},{2,10},{10,2},{3,11},{11,3},{4,12},{12,4},... | collective-permute-start | bytes 983048 | tf_op jit(solution)/shard_map/ppermute | solution.py:497
  84.1 25.8 %collective-permute-start.17 = (bf16[2,4,64,512]{3,2,1,0:T(8,128)(2,1)S(1)}, bf16[2,4,64,512]{3,2,1,0:T(8,128)(2,1)S(1)}, u32[]{:S(2)}, u32[]{:S(2)}) collective-permute-start(bf16[2,4,64,512]{3,2,1,0:T(8,128)(2,1)S(1)} %collective-permute-done.16.refs_6_), channel_id=1, source_target_pairs={{0,2},{1,3},{2,4},{3,5},{4,6},{5,7},{6,0},{7,1},{8,10},{9,11},{10,... | collective-permute-start | bytes 1572872 | tf_op jit(solution)/shard_map/ppermute | solution.py:451
  107.4 16.1 %collective-permute-start.20 = (bf16[2,4,64,512]{3,2,1,0:T(8,128)(2,1)S(1)}, bf16[2,4,64,512]{3,2,1,0:T(8,128)(2,1)S(1)}, u32[]{:S(2)}, u32[]{:S(2)}) collective-permute-start(bf16[2,4,64,512]{3,2,1,0:T(8,128)(2,1)S(1)} %bitcast.63), channel_id=1, source_target_pairs={{0,2},{1,3},{2,4},{3,5},{4,6},{5,7},{6,0},{7,1},{8,10},{9,11},{10,... | collective-permute-start | bytes 1572872 | tf_op jit(solution)/shard_map/ppermute | solution.py:451
  123.5 16.6 %collective-permute-start.23 = (bf16[2,4,64,512]{3,2,1,0:T(8,128)(2,1)S(1)}, bf16[2,4,64,512]{3,2,1,0:T(8,128)(2,1)S(1)}, u32[]{:S(2)}, u32[]{:S(2)}) collective-permute-start(bf16[2,4,64,512]{3,2,1,0:T(8,128)(2,1)S(1)} %collective-permute-done.20.refs_7_), channel_id=1, source_target_pairs={{0,2},{1,3},{2,4},{3,5},{4,6},{5,7},{6,0},{7,1},{8,10},{9,11},{10,... | collective-permute-start | bytes 1572872 | tf_op jit(solution)/shard_map/ppermute | solution.py:451
  124.0 16.1 %collective-permute-start.18 = (bf16[2,4,64,512]{3,2,1,0:T(8,128)(2,1)S(1)}, bf16[2,4,64,512]{3,2,1,0:T(8,128)(2,1)S(1)}, u32[]{:S(2)}, u32[]{:S(2)}) collective-permute-start(bf16[2,4,64,512]{3,2,1,0:T(8,128)(2,1)S(1)} %bitcast.60), channel_id=1, source_target_pairs={{0,1},{1,0},{2,3},{3,2},{4,5},{5,4},{6,7},{7,6},{8,9},{9,8},{10,11... | collective-permute-start | bytes 1572872 | tf_op jit(solution)/shard_map/ppermute | solution.py:451
  124.0 16.1 %collective-permute-start.21 = (bf16[2,4,64,512]{3,2,1,0:T(8,128)(2,1)S(1)}, bf16[2,4,64,512]{3,2,1,0:T(8,128)(2,1)S(1)}, u32[]{:S(2)}, u32[]{:S(2)}) collective-permute-start(bf16[2,4,64,512]{3,2,1,0:T(8,128)(2,1)S(1)} %collective-permute-done.16.refs_6_), channel_id=1, source_target_pairs={{0,1},{1,0},{2,3},{3,2},{4,5},{5,4},{6,7},{7,6},{8,9},{9,8},{10,11... | collective-permute-start | bytes 1572872 | tf_op jit(solution)/shard_map/ppermute | solution.py:451
  124.6 26.9 %collective-permute-start.26 = (bf16[2,4,64,512]{3,2,1,0:T(8,128)(2,1)S(1)}, bf16[2,4,64,512]{3,2,1,0:T(8,128)(2,1)S(1)}, u32[]{:S(2)}, u32[]{:S(2)}) collective-permute-start(bf16[2,4,64,512]{3,2,1,0:T(8,128)(2,1)S(1)} %collective-permute-done.17.refs_10_), channel_id=1, source_target_pairs={{0,2},{1,3},{2,4},{3,5},{4,6},{5,7},{6,0},{7,1},{8,10},{9,11},{10,... | collective-permute-start | bytes 1572872 | tf_op jit(solution)/shard_map/ppermute | solution.py:451
  125.4 26.0 %collective-permute-start.19 = (bf16[2,4,64,512]{3,2,1,0:T(8,128)(2,1)S(1)}, bf16[2,4,64,512]{3,2,1,0:T(8,128)(2,1)S(1)}, u32[]{:S(2)}, u32[]{:S(2)}) collective-permute-start(bf16[2,4,64,512]{3,2,1,0:T(8,128)(2,1)S(1)} %bitcast.64), channel_id=1, source_target_pairs={{0,1},{1,0},{2,3},{3,2},{4,5},{5,4},{6,7},{7,6},{8,9},{9,8},{10,11... | collective-permute-start | bytes 1572872 | tf_op jit(solution)/shard_map/ppermute | solution.py:451
  140.2 21.1 %collective-permute-start.27 = (bf16[2,4,64,512]{3,2,1,0:T(8,128)(2,1)S(1)}, bf16[2,4,64,512]{3,2,1,0:T(8,128)(2,1)S(1)}, u32[]{:S(2)}, u32[]{:S(2)}) collective-permute-start(bf16[2,4,64,512]{3,2,1,0:T(8,128)(2,1)S(1)} %collective-permute-done.23.refs_11_), channel_id=1, source_target_pairs={{0,2},{1,3},{2,4},{3,5},{4,6},{5,7},{6,0},{7,1},{8,10},{9,11},{10,... | collective-permute-start | bytes 1572872 | tf_op jit(solution)/shard_map/ppermute | solution.py:451
  140.2 21.1 %collective-permute-start.24 = (bf16[2,4,64,512]{3,2,1,0:T(8,128)(2,1)S(1)}, bf16[2,4,64,512]{3,2,1,0:T(8,128)(2,1)S(1)}, u32[]{:S(2)}, u32[]{:S(2)}) collective-permute-start(bf16[2,4,64,512]{3,2,1,0:T(8,128)(2,1)S(1)} %collective-permute-done.17.refs_10_), channel_id=1, source_target_pairs={{0,1},{1,0},{2,3},{3,2},{4,5},{5,4},{6,7},{7,6},{8,9},{9,8},{10,11... | collective-permute-start | bytes 1572872 | tf_op jit(solution)/shard_map/ppermute | solution.py:451
  140.2 21.1 %collective-permute-start.22 = (bf16[2,4,64,512]{3,2,1,0:T(8,128)(2,1)S(1)}, bf16[2,4,64,512]{3,2,1,0:T(8,128)(2,1)S(1)}, u32[]{:S(2)}, u32[]{:S(2)}) collective-permute-start(bf16[2,4,64,512]{3,2,1,0:T(8,128)(2,1)S(1)} %collective-permute-done.20.refs_7_), channel_id=1, source_target_pairs={{0,1},{1,0},{2,3},{3,2},{4,5},{5,4},{6,7},{7,6},{8,9},{9,8},{10,11... | collective-permute-start | bytes 1572872 | tf_op jit(solution)/shard_map/ppermute | solution.py:451
  151.4 9.9 %collective-permute-start.28 = (bf16[2,4,64,512]{3,2,1,0:T(8,128)(2,1)S(1)}, bf16[2,4,64,512]{3,2,1,0:T(8,128)(2,1)S(1)}, u32[]{:S(2)}, u32[]{:S(2)}) collective-permute-start(bf16[2,4,64,512]{3,2,1,0:T(8,128)(2,1)S(1)} %collective-permute-done.26.refs_14_), channel_id=1, source_target_pairs={{0,1},{1,0},{2,3},{3,2},{4,5},{5,4},{6,7},{7,6},{8,9},{9,8},{10,11... | collective-permute-start | bytes 1572872 | tf_op jit(solution)/shard_map/ppermute | solution.py:451
  151.4 9.9 %collective-permute-start.25 = (bf16[2,4,64,512]{3,2,1,0:T(8,128)(2,1)S(1)}, bf16[2,4,64,512]{3,2,1,0:T(8,128)(2,1)S(1)}, u32[]{:S(2)}, u32[]{:S(2)}) collective-permute-start(bf16[2,4,64,512]{3,2,1,0:T(8,128)(2,1)S(1)} %collective-permute-done.23.refs_11_), channel_id=1, source_target_pairs={{0,1},{1,0},{2,3},{3,2},{4,5},{5,4},{6,7},{7,6},{8,9},{9,8},{10,11... | collective-permute-start | bytes 1572872 | tf_op jit(solution)/shard_map/ppermute | solution.py:451
  161.3 1.9 collective-permute-start.29
  178.2 15.4 %collective-permute-start.30 = (bf16[4,2,128,256]{3,2,1,0:T(8,128)(2,1)S(1)}, bf16[4,2,128,256]{3,2,1,0:T(8,128)(2,1)S(1)}, u32[]{:S(2)}, u32[]{:S(2)}) collective-permute-start(bf16[4,2,128,256]{3,2,1,0:T(8,128)(2,1)S(1)} %get-tuple-element.33), channel_id=1, source_target_pairs={{0,8},{8,0},{1,9},{9,1},{2,10},{10,2},{3,11},{11,3},{4,12},{12,4},... | collective-permute-start | bytes 1572872 | tf_op jit(solution)/shard_map/ppermute | solution.py:553
  198.6 13.7 %collective-permute-start.31 = (bf16[512,512]{1,0:T(8,128)(2,1)S(1)}, bf16[512,512]{1,0:T(8,128)(2,1)S(1)}, u32[]{:S(2)}, u32[]{:S(2)}) collective-permute-start(bf16[512,512]{1,0:T(8,128)(2,1)S(1)} %send_part.4.refs_3_), channel_id=1, source_target_pairs={{0,8},{8,0},{1,9},{9,1},{2,10},{10,2},{3,11},{11,3},{4,12},{12,4},... | collective-permute-start | bytes 1572872 | tf_op jit(solution)/shard_map/ppermute | solution.py:565
  214.7 49.1 %all-to-all-start = ((bf16[8,64,512]{2,1,0:T(8,128)(2,1)}), bf16[8,64,512]{2,1,0:T(8,128)(2,1)}, u32[]{:S(2)}, u32[]{:S(2)}) async-start(bf16[8,64,512]{2,1,0:T(8,128)(2,1)} %copy-done.19), calls=%async_computation | async-start | bytes 1048576 | tf_op jit(solution)/shard_map/all_to_all | solution.py:581
  225.4 48.0 %collective-permute-start.32 = (bf16[512,1024]{1,0:T(8,128)(2,1)}, bf16[512,1024]{1,0:T(8,128)(2,1)}, u32[]{:S(2)}, u32[]{:S(2)}) collective-permute-start(bf16[512,1024]{1,0:T(8,128)(2,1)} %send_part.5.refs_3_), channel_id=1, source_target_pairs={{0,8},{8,0},{1,9},{9,1},{2,10},{10,2},{3,11},{11,3},{4,12},{12,4},... | collective-permute-start | bytes 3145736 | tf_op jit(solution)/shard_map/ppermute | solution.py:565
  229.7 32.6 %collective-permute-start.33 = (bf16[512,512]{1,0:T(8,128)(2,1)S(1)}, bf16[512,512]{1,0:T(8,128)(2,1)S(1)}, u32[]{:S(2)}, u32[]{:S(2)}) collective-permute-start(bf16[512,512]{1,0:T(8,128)(2,1)S(1)} %send_part.6.refs_3_), channel_id=1, source_target_pairs={{0,8},{8,0},{1,9},{9,1},{2,10},{10,2},{3,11},{11,3},{4,12},{12,4},... | collective-permute-start | bytes 1572872 | tf_op jit(solution)/shard_map/ppermute | solution.py:565
  263.8 31.0 %all-to-all-start.2 = ((bf16[8,64,512]{2,1,0:T(8,128)(2,1)}), bf16[8,64,512]{2,1,0:T(8,128)(2,1)}, u32[]{:S(2)}, u32[]{:S(2)}) async-start(bf16[8,64,512]{2,1,0:T(8,128)(2,1)} %copy-done.21), calls=%async_computation.2 | async-start | bytes 1048576 | tf_op jit(solution)/shard_map/all_to_all | solution.py:581
  279.7 14.4 %collective-permute-start.34 = (bf16[512,512]{1,0:T(8,128)(2,1)S(1)}, bf16[512,512]{1,0:T(8,128)(2,1)S(1)}, u32[]{:S(2)}, u32[]{:S(2)}) collective-permute-start(bf16[512,512]{1,0:T(8,128)(2,1)S(1)} %send_part.7.refs_3_), channel_id=1, source_target_pairs={{0,8},{8,0},{1,9},{9,1},{2,10},{10,2},{3,11},{11,3},{4,12},{12,4},... | collective-permute-start | bytes 1572872 | tf_op jit(solution)/shard_map/ppermute | solution.py:565
  284.0 35.9 %copy-start.23 = (bf16[4,2,128,256]{3,2,1,0:T(8,128)(2,1)S(1)}, bf16[4,2,128,256]{3,2,1,0:T(8,128)(2,1)}, u32[]{:S(2)}) copy-start(bf16[4,2,128,256]{3,2,1,0:T(8,128)(2,1)} %copy-done.22) | copy-start | bytes 1572868
  284.0 35.9 %copy-start.29 = (bf16[4,2,128,256]{3,2,1,0:T(8,128)(2,1)S(1)}, bf16[4,2,128,256]{3,2,1,0:T(8,128)(2,1)}, u32[]{:S(2)}) copy-start(bf16[4,2,128,256]{3,2,1,0:T(8,128)(2,1)} %copy-done.28) | copy-start | bytes 1572868
  314.7 30.8 %all-to-all-start.1 = ((bf16[8,64,1024]{2,1,0:T(8,128)(2,1)}), bf16[8,64,1024]{2,1,0:T(8,128)(2,1)}, u32[]{:S(2)}, u32[]{:S(2)}) async-start(bf16[8,64,1024]{2,1,0:T(8,128)(2,1)} %residual.5.refs_3_), calls=%async_computation.1 | async-start | bytes 2097152 | tf_op jit(solution)/shard_map/all_to_all | solution.py:581
  319.0 14.2 %collective-permute-start.35 = (bf16[4,2,128,256]{3,2,1,0:T(8,128)(2,1)S(1)}, bf16[4,2,128,256]{3,2,1,0:T(8,128)(2,1)S(1)}, u32[]{:S(2)}, u32[]{:S(2)}) collective-permute-start(bf16[4,2,128,256]{3,2,1,0:T(8,128)(2,1)S(1)} %copy-done.27), channel_id=1, source_target_pairs={{0,8},{8,0},{1,9},{9,1},{2,10},{10,2},{3,11},{11,3},{4,12},{12,4},... | collective-permute-start | bytes 1572872 | tf_op jit(solution)/shard_map/ppermute | solution.py:576
  (31 other events, 278.2 us)

commit v4 on v3

--- a/solution.py
+++ b/solution.py
@@ -15,7 +15,6 @@
 VMEM_BYTES = 48 * 1024 * 1024
 PARTS = 2
 CORES = 2
-IN_FLIGHT = 4
 SHARE = 0.1
 
 
@@ -41,7 +40,8 @@
         self.span_at = 0
         self.earlier_at = self.span_at + spans
         self.target_at = self.earlier_at + spans
-        self.page = self.target_at + spans
+        self.sent_as = self.target_at + spans
+        self.page = self.sent_as + spans
         self.origin = self.page + pages
         self.group_rank = self.origin + owners * spans
         self.tensor_rank = self.group_rank + 1
@@ -79,7 +79,14 @@
                     if back == 0 and other == 0:
                         out[lay.span_at + place] = k
                         out[lay.earlier_at + place] = k - start_of[k]
-                        out[lay.target_at + place] = target[k]
+                        owner = target[k]
+                        ahead = lax.rem(lax.div(owner, CORES) + chips - chip, chips)
+                        turn = jnp.int32(0)
+                        for m, other_hop in enumerate(hops):
+                            turn = jnp.where(ahead == other_hop, jnp.int32(m), turn)
+                        crossing = jnp.where(lax.rem(owner, CORES) == core, 0, 1)
+                        out[lay.target_at + place] = owner
+                        out[lay.sent_as + place] = turn * CORES + crossing
 
 
 def make_tables(lay, spans, pages, ranks, prompt_spans, source, target, page_slot):
@@ -354,31 +361,41 @@
     )(table, *queries, *flat)
 
 
-def project_kernel(pieces, table, *refs):
-    attended, wo, out = refs[:pieces], refs[pieces], refs[-1]
+def project_kernel(pieces, follows, tile, table, *refs):
+    attended, wo, outs = refs[:pieces], refs[pieces], refs[pieces + 1 + follows :]
     total, at = None, 0
     for piece in attended:
         depth = piece.shape[1]
         term = jnp.dot(piece[...], wo[at : at + depth], preferred_element_type=jnp.float32)
         total = term if total is None else total + term
         at += depth
-    out[...] = total.astype(jnp.bfloat16)
-
-
-def make_projection(lay, table, attended, wo, first, count, tile, name, follows=()):
+    total = total.astype(jnp.bfloat16)
+    step = 0
+    for out in outs:
+        for at in range(0, out.shape[1], tile):
+
+            @pl.when(pl.program_id(0) == step)
+            def _(out=out, at=at):
+                out[:, at : at + tile] = total
+
+            step += 1
+
+
+def make_projection(lay, table, attended, wo, tile, first, widths, name, follows=()):
     rows = attended[0].shape[0]
     depth = wo.shape[0]
+    count = sum(widths)
     return pl.pallas_call(
-        functools.partial(project_kernel, len(attended)),
+        functools.partial(project_kernel, len(attended), len(follows), tile),
         grid_spec=pltpu.PrefetchScalarGridSpec(
             num_scalar_prefetch=1,
             grid=(count,),
             in_specs=[pl.BlockSpec(x.shape, lambda n, t: (0, 0)) for x in attended]
             + [pl.BlockSpec((depth, tile), lambda n, t: (0, first(t[lay.tensor_rank]) + n))]
             + [pl.BlockSpec(memory_space=pl.ANY)] * len(follows),
-            out_specs=pl.BlockSpec((rows, tile), lambda n, t: (0, n)),
-        ),
-        out_shape=jax.ShapeDtypeStruct((rows, count * tile), jnp.bfloat16),
+            out_specs=[pl.BlockSpec((rows, w * tile), lambda n, t: (0, 0)) for w in widths],
+        ),
+        out_shape=[jax.ShapeDtypeStruct((rows, w * tile), jnp.bfloat16) for w in widths],
         compiler_params=params(),
         cost_estimate=cost(
             2 * rows * depth * count * tile, 2 * (rows * depth + (rows + depth) * count * tile)
@@ -387,36 +404,75 @@
     )(table, *attended, wo, *follows)
 
 
-def add_kernel(lay, table, *refs):
-    x_refs, own, received, out = refs[:-3], refs[-3], refs[-2], refs[-1]
-    for place, x in enumerate(x_refs):
-        summed = own[place].astype(jnp.float32) + received[place].astype(jnp.float32)
-        out[table[lay.target_at + place]] = (x[...].astype(jnp.float32) + summed).astype(
-            jnp.bfloat16
-        )
+def add_kernel(lay, blocks, table, *refs):
+    x_refs, own, received = refs[:blocks], refs[blocks], refs[blocks + 1]
+    outs, moved = refs[blocks + 2 : -1], refs[-1]
+    rows = moved.shape[1]
+    place = 0
+    for x in x_refs:
+        for at in range(0, x.shape[0], rows):
+            summed = own[place].astype(jnp.float32) + received[place].astype(jnp.float32)
+            moved[table[lay.sent_as + place]] = (
+                x[at : at + rows].astype(jnp.float32) + summed
+            ).astype(jnp.bfloat16)
+            place += 1
+    for n, out in enumerate(outs):
+        for flip in range(CORES):
+            out[flip] = moved[n * CORES + flip]
 
 
 def make_sum(lay, table, arrived, own, received, first):
     spans, rows, cols = received.shape
-    unit = math.gcd(first, cols) if first else cols
-    steps, start = cols // unit, first // unit
+    chunk = first // cols
+    whole = lambda n, t: (0, 0, 0)
     return pl.pallas_call(
-        functools.partial(add_kernel, lay),
+        functools.partial(add_kernel, lay, len(arrived)),
         grid_spec=pltpu.PrefetchScalarGridSpec(
             num_scalar_prefetch=1,
-            grid=(steps,),
-            in_specs=[pl.BlockSpec((rows, unit), lambda n, t: (0, start + n))] * spans
-            + [
-                pl.BlockSpec((spans, rows, unit), lambda n, t: (0, 0, n)),
-                pl.BlockSpec((spans, rows, unit), lambda n, t: (0, 0, n)),
-            ],
-            out_specs=pl.BlockSpec((spans, rows, unit), lambda n, t: (0, 0, n)),
-        ),
-        out_shape=jax.ShapeDtypeStruct((spans, rows, cols), jnp.bfloat16),
+            grid=(1,),
+            in_specs=[pl.BlockSpec((x.shape[0], cols), lambda n, t: (0, chunk)) for x in arrived]
+            + [pl.BlockSpec((spans, rows, cols), whole)] * 2,
+            out_specs=[pl.BlockSpec((CORES, rows, cols), whole)] * lay.chips,
+            scratch_shapes=[pltpu.VMEM((spans, rows, cols), jnp.bfloat16)],
+        ),
+        out_shape=[jax.ShapeDtypeStruct((CORES, rows, cols), jnp.bfloat16)] * lay.chips,
         compiler_params=params(),
         cost_estimate=cost(3 * spans * rows * cols, 8 * spans * rows * cols),
         name="residual",
     )(table, *arrived, own, received)
+
+
+def place_kernel(lay, table, *refs):
+    same, swapped, out = refs[: lay.chips], refs[lay.chips], refs[-1]
+    rows = swapped.shape[1]
+    group_rank = table[lay.group_rank]
+    chip, core = lax.div(group_rank, CORES), lax.rem(group_rank, CORES)
+    for n, hop in enumerate(hop_order(lay.chips)):
+        owner = lax.rem(chip + lay.chips - hop, lay.chips) * CORES
+        for block, at_core in ((same[n][0], core), (swapped[n], 1 - core)):
+            at = pl.multiple_of((owner + at_core) * rows, rows)
+            out[pl.ds(at, rows)] = block
+
+
+def make_placed(lay, table, same, swapped, first, cols, whole):
+    chips, rows, tile = swapped.shape
+    chunk = first // tile
+    return pl.pallas_call(
+        functools.partial(place_kernel, lay),
+        grid_spec=pltpu.PrefetchScalarGridSpec(
+            num_scalar_prefetch=1,
+            grid=(1,),
+            in_specs=[pl.BlockSpec((CORES, rows, tile), lambda n, t: (0, 0, 0))] * chips
+            + [pl.BlockSpec((chips, rows, tile), lambda n, t: (0, 0, 0))]
+            + [pl.BlockSpec(memory_space=pl.ANY)] * len(whole),
+            out_specs=pl.BlockSpec((chips * CORES * rows, tile), lambda n, t: (0, chunk)),
+        ),
+        out_shape=jax.ShapeDtypeStruct((chips * CORES * rows, cols), jnp.bfloat16),
+        input_output_aliases={chips + 2: 0} if whole else {},
+        compiler_params=params(),
+        cost_estimate=cost(0, 4 * chips * CORES * rows * tile),
+        name="placed",
+    )(table, *same, swapped, *whole)
 
 
 def rope_tables(earlier, span_len, first_row, rows, head):
@@ -431,10 +487,6 @@
         jnp.concatenate([cosine, cosine], axis=1),
         jnp.concatenate([-sine, sine], axis=1),
     )
-
-
-def widths_of(tiles):
-    return [1, 2, 1, 1] if tiles == 5 else [1, tiles - 1]
 
 
 def after(x, done):
@@ -482,19 +534,20 @@
     per_kv = wq.shape[1] // max(head, wk.shape[1])
 
     chip, core = group_rank // CORES, group_rank % CORES
-    split = hidden_in.reshape(owners, rows, cols)
-    arrived, crossed = [], []
+    split = hidden_in.reshape(chips, CORES, rows, cols)
+    mine, theirs = [
+        lax.dynamic_index_in_dim(split, at, 1, keepdims=False) for at in (core, 1 - core)
+    ]
+    theirs = shift(theirs, owners, 0, 1)
+    pairs = []
     for hop in hop_order(chips):
-        for flip in range(CORES):
-            to = lax.rem(chip + hop, chips) * CORES + lax.rem(core + flip, CORES)
-            block = lax.dynamic_index_in_dim(split, to, 0, keepdims=False)
-            if hop or flip:
-                if paired and len(arrived) > IN_FLIGHT:
-                    block = after(block, crossed[len(arrived) - IN_FLIGHT - 1])
-                block = shift(block, owners, hop, flip)
-            arrived.append(block)
-            if paired:
-                crossed.append(lax.ppermute(block, "tensor", swap))
+        at = lax.rem(chip + hop, chips)
+        pairs.append([lax.dynamic_index_in_dim(x, at, 0, keepdims=False) for x in (mine, theirs)])
+    arrived = [jnp.concatenate(pairs[0])]
+    moves = [(hop, [jnp.concatenate(pair)]) for hop, pair in zip(hop_order(chips), pairs)][1:]
+    if len(moves) > 1:
+        moves[-1] = (moves[-1][0], pairs[-1])
+    moves = [(hop, block) for hop, blocks in moves for block in blocks]
 
     ranks = jnp.stack([group_rank, tensor_rank]).astype(jnp.int32)
     table = make_tables(
@@ -503,22 +556,22 @@
     earlier = table[lay.earlier_at : lay.earlier_at + spans]
     cosine, sine = rope_tables(earlier, span_len, group_rank * rows, rows, head)
 
+    cross = lambda x: lax.ppermute(x, "tensor", swap)
+    crossed = [cross(arrived[0])] if paired else []
     if paired:
         gain = ln_gain[None]
-        gains = [gain, lax.ppermute(gain, "tensor", swap)]
+        gains = [gain, cross(after(gain, crossed[0]))]
     else:
         gains = [lax.all_gather(ln_gain, "tensor", axis=0, tiled=True)[None]]
 
     queries, gathered = [], [[] for _ in range(owners)]
-    for p in range(PARTS):
-        at = slice(p * here, (p + 1) * here)
+
+    def make_part(p, own_rows, crossed_rows):
         if paired:
-            xs = [arrived[at], crossed[at]]
+            xs = [own_rows, crossed_rows]
         else:
-            xs = [[lax.all_gather(jnp.concatenate(arrived[at]), "tensor", axis=1, tiled=True)]]
+            xs = [[lax.all_gather(jnp.concatenate(own_rows), "tensor", axis=1, tiled=True)]]
         kgain = key_norm_gain[None]
-        if queries:
-            kgain = after(kgain, queries[-1])
         *normed, kv = make_kv(lay, table, xs, gains, wk, wv, kgain, cosine, sine, p)
         kv = kv.reshape(2, here, rows, kv.shape[2])
         for back in range(chips):
@@ -535,6 +588,22 @@
                 made = make_q(lay, table, normed, wq, qgain, cosine, sine, p)
                 queries.append(made.reshape(here, rows, made.shape[1]))
 
+    begun = 0
+    for m in range(len(moves) + 1):
+        if m:
+            hop, block = moves[m - 1]
+            if paired and m > 1:
+                block = after(block, crossed[m - 2])
+            arrived.append(shift(block, owners, hop, 0))
+            if paired:
+                block = arrived[-1]
+                if m == len(moves) and queries:
+                    block = after(block, queries[0])
+                crossed.append(cross(block))
+        if sum(x.shape[0] for x in arrived[begun:]) == here * rows:
+            make_part(len(queries), arrived[begun:], crossed[begun:])
+            begun = len(arrived)
+
     own_kv = wk.shape[1] // head
     sets = [own_kv // 2, own_kv - own_kv // 2] if own_kv > 1 else [own_kv]
     attended, pages, first = [], [], 0
@@ -547,41 +616,40 @@
         first += count
 
     if paired:
-        tile = 512
-        half_tiles = cols // tile
-        widths = widths_of(half_tiles)
-        others = [lax.ppermute(pages[0], "tensor", swap)]
-        own, received, moved, starts = [], [], [], []
-        for n in range(len(widths) + 1):
-            if n < len(widths):
-                first = sum(widths[:n])
-                starts.append(first * tile)
-                follows = (others[0],) if n == 0 else own[-1:] if n == 1 else moved[-1:]
-                sent = make_projection(
-                    lay, table, attended, wo,
-                    lambda r, first=first: (1 - r) * half_tiles + first,
-                    widths[n], tile, "send_part", follows,
-                )
-                received.append(lax.ppermute(sent, "tensor", swap).reshape(spans, rows, -1))
-                own.append(make_projection(
-                    lay, table, attended, wo,
-                    lambda r, first=first: r * half_tiles + first,
-                    widths[n], tile, "own_part", (sent,),
-                ).reshape(spans, rows, -1))
+        tile = 512 if cols % 512 == 0 else cols
+        tiles = cols // tile
+        widths = [2, 2, 1] if tiles == 5 else [tiles]
+        others = [cross(pages[0])]
+        project = functools.partial(make_projection, lay, table, attended, wo, tile)
+        send = project(lambda r: (1 - r) * tiles, widths[:1], "send_part", (others[0],))
+        if widths[1:]:
+            send += project(
+                lambda r: (1 - r) * tiles + widths[0], widths[1:], "send_part", (send[0],)
+            )
+        own = project(lambda r: r * tiles, widths, "own_part", (send[-1],))
+        whole, received, landed, first = (), [], [], 0
+        for n, sent in enumerate(send):
             if n:
-                moved.append(
-                    make_sum(lay, table, arrived, own[n - 1], received[n - 1], starts[n - 1])
-                )
+                sent = after(sent, (received[-1], own, landed[-2:-1]))
+            received.append(cross(sent))
+            moved = make_sum(
+                lay, table, arrived, own[n].reshape(spans, rows, -1),
+                received[-1].reshape(spans, rows, -1), first,
+            )
+            same = [
+                shift(x, owners, hop, 0) if hop else x
+                for hop, x in zip(hop_order(chips), moved)
+            ]
+            landed.append(same)
+            swapped = shift(jnp.concatenate([x[1:] for x in same]), owners, 0, 1)
+            whole = (make_placed(lay, table, same, swapped, first, cols, whole),)
+            first += sent.shape[1]
+        mixed = whole[0].reshape(1, span_len, cols)
         for cut in pages[1:]:
-            others.append(lax.ppermute(after(cut, received[-2]), "tensor", swap))
+            others.append(cross(after(cut, received[-1])))
         low = [jnp.where(tensor_rank == 0, a, b) for a, b in zip(pages, others)]
         high = [jnp.where(tensor_rank == 0, b, a) for a, b in zip(pages, others)]
         cache = jnp.concatenate(low + high, axis=3)
-        pieces = [
-            lax.all_to_all(rows_of, "group", split_axis=0, concat_axis=0, tiled=True)
-            for rows_of in moved
-        ]
-        mixed = jnp.concatenate(pieces, axis=2).reshape(1, span_len, cols)
     else:
         pages = jnp.concatenate(pages, axis=3)
         attended = jnp.concatenate(attended, axis=1)
@@ -595,7 +663,8 @@
             partial.astype(jnp.bfloat16), "tensor", scatter_dimension=1, tiled=True
         )
         summed = summed.reshape(spans, rows, cols).astype(jnp.float32)
-        moved = (jnp.stack(arrived).astype(jnp.float32) + summed).astype(jnp.bfloat16)
+        x = jnp.concatenate(arrived).reshape(spans, rows, cols).astype(jnp.float32)
+        moved = (x + summed).astype(jnp.bfloat16)
         targets = table[lay.target_at : lay.target_at + spans]
         moved = jnp.zeros_like(moved).at[targets].set(moved, unique_indices=True)
         moved = lax.all_to_all(moved, "group", split_axis=0, concat_axis=0, tiled=True)

time: 349 us -> 300 us (0.86)
  waiting for transfers between devices: 161 us -> 138 us
  blocking collectives: 19.9 us -> 0 us
  Pallas kernels: 105 us -> 101 us
    ppermute x15 -> x11, waiting for transfers between devices: 78.6 us -> 48.7 us  [local(): cross = lambda x: lax.ppermute(x, 'tensor', swap)]
    all_to_all x1 -> x0, blocking collectives: 19.9 us -> none  [local(): lax.all_to_all(rows_of, 'group', split_axis=0, concat_axis=0, tiled=True)]
    ppermute x21 -> x31, waiting for transfers between devices: 71.6 us -> 89.6 us  [shift(): return lax.ppermute(x, 'group', pairs)]
    all_to_all x3 -> x0, starting transfers between devices: 13.2 us -> none  [local(): lax.all_to_all(rows_of, 'group', split_axis=0, concat_axis=0, tiled=True)]
    all_to_all x3 -> x0, waiting for transfers between devices: 10.7 us -> none  [local(): lax.all_to_all(rows_of, 'group', split_axis=0, concat_axis=0, tiled=True)]
    ppermute x21 -> x31, starting transfers between devices: 11.6 us -> 21.7 us  [shift(): return lax.ppermute(x, 'group', pairs)]
    pallas_call x12 -> x9, Pallas kernels: 35.5 us -> 30 us  [the longest x3 20.7 us: make_projection(): pl.pallas_call(functools.partial(project_kernel, len(attended), len(follo...]
    unnamed x80 -> x66, local copies, waits for them, and re-layouts: 11.1 us -> 7.16 us
  transfers between devices with their start and end apart: 39 -> 42, of which waited for: 15 -> 21; matrix products, arithmetic and copies ran while one was open for 2% -> 3% of each run, Pallas kernels for 25% -> 27%
where the time goes in v4:
time: 300 us
  waiting for transfers between devices  138 us (46%)
  Pallas kernels  101 us (34%)
  starting transfers between devices  36.4 us (12%)
  local copies, waits for them, and re-layouts  13.7 us (5%)
  other arithmetic  9.19 us (3%)
    ppermute x31, waiting for transfers between devices, shift(): return lax.ppermute(x, 'group', pairs)  89.6 us
    ppermute x11, waiting for transfers between devices, local(): cross = lambda x: lax.ppermute(x, 'tensor', swap)  48.7 us
    pallas_call x2, Pallas kernels, make_attention(): pl.pallas_call(functools.partial(attention_kernel, lay, spans, most, per_...  28.5 us
    pallas_call x2, Pallas kernels, make_q(): pl.pallas_call(functools.partial(q_kernel, sides), grid_spec=pltpu.Prefet...  22.6 us
    ppermute x31, starting transfers between devices, shift(): return lax.ppermute(x, 'group', pairs)  21.7 us
    pallas_call x3, Pallas kernels, make_projection(): pl.pallas_call(functools.partial(project_kernel, len(attended), len(follo...  20.7 us
    pallas_call x2, Pallas kernels, make_kv(): pl.pallas_call(functools.partial(kv_kernel, sides, blocks), grid_spec=plt...  18.1 us
    ppermute x11, starting transfers between devices, local(): cross = lambda x: lax.ppermute(x, 'tensor', swap)  14.6 us
  transfers between devices with their start and end apart: 42, of which 21 were waited for; matrix products, arithmetic and copies ran while one was open for 3% of the time, Pallas kernels for 27%

profile of v4, /device:TPU:0, one launch (start us, length us, event | category | flops | bytes accessed | tf_op | source)
XLA Modules:
  0.0 299.5 jit_solution(13840005268591939538)
XLA Ops:
  0.7 2.6 dynamic-slice_bitcast_fusion
  4.6 2.2 collective-permute-done
  6.7 2.1 dynamic-slice_bitcast_fusion.1
  8.9 2.9 collective-permute-start.2
  12.7 1.6 collective-permute-start.1
  15.2 11.7 %collective-permute-done.2.refs_2_ = bf16[128,2560]{1,0:T(8,128)(2,1)S(1)} collective-permute-done((bf16[128,2560]{1,0:T(8,128)(2,1)S(1)}, bf16[128,2560]{1,0:T(8,128)(2,1)S(1)}, u32[]{:S(2)}, u32[]{:S(2)}) %collective-permute-start.2) | collective-permute-done | bytes 655392 | tf_op jit(solution)/shard_map/ppermute | solution.py:559
  26.9 3.9 %collective-permute-start.3 = (bf16[128,2560]{1,0:T(8,128)(2,1)}, bf16[128,2560]{1,0:T(8,128)(2,1)S(1)}, u32[]{:S(2)}, u32[]{:S(2)}) collective-permute-start(bf16[128,2560]{1,0:T(8,128)(2,1)} %pad_maximum_fusion.3), channel_id=1, source_target_pairs={{0,6},{1,7},{2,0},{3,1},{4,2},{5,3},{6,4},{7,5},{8,14},{9,15},{10,... | collective-permute-start | bytes 1966088 | tf_op jit(solution)/shard_map/ppermute | solution.py:503
  31.4 1.5 tables.1.table
  32.9 1.6 collective-permute-start.4
  34.5 10.9 %collective-permute-done.3.refs_0_.refs_2_ = bf16[128,2560]{1,0:T(8,128)(2,1)S(1)} collective-permute-done((bf16[128,2560]{1,0:T(8,128)(2,1)}, bf16[128,2560]{1,0:T(8,128)(2,1)S(1)}, u32[]{:S(2)}, u32[]{:S(2)}) %collective-permute-start.3) | collective-permute-done | bytes 655392 | tf_op jit(solution)/shard_map/ppermute | solution.py:503
  49.9 12.9 %collective-permute-done.6.refs_3_ = bf16[128,2560]{1,0:T(8,128)(2,1)S(1)} collective-permute-done((bf16[128,2560]{1,0:T(8,128)(2,1)S(1)}, bf16[128,2560]{1,0:T(8,128)(2,1)S(1)}, u32[]{:S(2)}, u32[]{:S(2)}) %collective-permute-start.6) | collective-permute-done | bytes 655392 | tf_op jit(solution)/shard_map/ppermute | solution.py:559
  63.0 9.5 %keys_values.2 = (bf16[256,2560]{1,0:T(8,128)(2,1)S(1)}, bf16[256,2560]{1,0:T(8,128)(2,1)}, bf16[2,256,512]{2,1,0:T(8,128)(2,1)S(1)}) custom-call(s32[130]{0:T(256)S(1)} %copy-done.22, bf16[128,2560]{1,0:T(8,128)(2,1)S(1)} %pad_maximum_fusion.1.refs_0_, bf16[128,2560]{1,0:T(8,128)(2,1)S(1)} %collective-permute-done.1.refs_1_, ...), custom_call_target="tpu_custom_call" | custom-call | flops 268435456 | bytes 1572864 | tf_op jit(solution)/shard_map/keys_values/pallas_call | solution.py:176
  72.5 1.6 collective-permute-start.11
  75.4 11.3 %queries.2 = bf16[256,2048]{1,0:T(8,128)(2,1)S(1)} custom-call(s32[130]{0:T(256)S(1)} %copy-done.22, bf16[256,2560]{1,0:T(8,128)(2,1)S(1)} %get-tuple-element.43.refs_0_, bf16[256,2560]{1,0:T(8,128)(2,1)S(1)} %copy-done.5, bf16[5120,2048]{1,0:T(8,128)(2,1)} %refs_3_.3, bf16[5120,2048]{1,0:T(8,128)(2,1)} %refs_3_.3, bf16[1,128]{1,0:T(2,128)(2,1)S(1)} %bitcast.62, ...), custom_call_target="tpu_custom_call" | custom-call | flops 536870912 | bytes 2464153 | tf_op jit(solution)/shard_map/queries/pallas_call | solution.py:232
  87.7 1.5 collective-permute-start.9
  89.2 2.1 collective-permute-done.7.refs_2_.refs_4_
  92.3 4.1 %collective-permute-done.9.refs_4_ = bf16[64,2560]{1,0:T(8,128)(2,1)S(1)} collective-permute-done((bf16[64,2560]{1,0:T(8,128)(2,1)S(1)}, bf16[64,2560]{1,0:T(8,128)(2,1)S(1)}, u32[]{:S(2)}, u32[]{:S(2)}) %collective-permute-start.9) | collective-permute-done | bytes 327712 | tf_op jit(solution)/shard_map/ppermute | solution.py:559
  96.5 5.8 %collective-permute-done.10.refs_5_ = bf16[64,2560]{1,0:T(8,128)(2,1)S(1)} collective-permute-done((bf16[64,2560]{1,0:T(8,128)(2,1)S(1)}, bf16[64,2560]{1,0:T(8,128)(2,1)S(1)}, u32[]{:S(2)}, u32[]{:S(2)}) %collective-permute-start.10) | collective-permute-done | bytes 327712 | tf_op jit(solution)/shard_map/ppermute | solution.py:559
  102.3 8.6 %keys_values.3 = (bf16[256,2560]{1,0:T(8,128)(2,1)S(1)}, bf16[256,2560]{1,0:T(8,128)(2,1)}, bf16[2,256,512]{2,1,0:T(8,128)(2,1)S(1)}) custom-call(s32[130]{0:T(256)S(1)} %copy-done.22, bf16[128,2560]{1,0:T(8,128)(2,1)S(1)} %collective-permute-done.3.refs_0_.refs_2_, bf16[64,2560]{1,0:T(8,128)(2,1)S(1)} %collective-permute-done.5.refs_1_.refs_3_, ...), custom_call_target="tpu_custom_call" | custom-call | flops 268435456 | bytes 1572864 | tf_op jit(solution)/shard_map/keys_values/pallas_call | solution.py:176
  110.8 2.9 collective-permute-start.15
  115.1 11.3 %queries.3 = bf16[256,2048]{1,0:T(8,128)(2,1)S(1)} custom-call(s32[130]{0:T(256)S(1)} %copy-done.22, bf16[256,2560]{1,0:T(8,128)(2,1)S(1)} %get-tuple-element.46.refs_0_, bf16[256,2560]{1,0:T(8,128)(2,1)S(1)} %copy-done.4, bf16[5120,2048]{1,0:T(8,128)(2,1)} %refs_3_.3, bf16[5120,2048]{1,0:T(8,128)(2,1)} %refs_3_.3, bf16[1,128]{1,0:T(2,128)(2,1)S(1)} %bitcast.63, ...), custom_call_target="tpu_custom_call" | custom-call | flops 536870912 | bytes 2464153 | tf_op jit(solution)/shard_map/queries/pallas_call | solution.py:232
  127.7 1.5 collective-permute-start.21
  129.6 14.4 %collective-permute-done.18.refs_11_ = bf16[2,4,64,512]{3,2,1,0:T(8,128)(2,1)S(1)} collective-permute-done((bf16[2,4,64,512]{3,2,1,0:T(8,128)(2,1)S(1)}, bf16[2,4,64,512]{3,2,1,0:T(8,128)(2,1)S(1)}, u32[]{:S(2)}, u32[]{:S(2)}) %collective-permute-start.18) | collective-permute-done | bytes 524320 | tf_op jit(solution)/shard_map/ppermute | solution.py:503
  144.0 11.2 %collective-permute-done.21.refs_14_ = bf16[2,4,64,512]{3,2,1,0:T(8,128)(2,1)S(1)} collective-permute-done((bf16[2,4,64,512]{3,2,1,0:T(8,128)(2,1)S(1)}, bf16[2,4,64,512]{3,2,1,0:T(8,128)(2,1)S(1)}, u32[]{:S(2)}, u32[]{:S(2)}) %collective-permute-start.21) | collective-permute-done | bytes 524320 | tf_op jit(solution)/shard_map/ppermute | solution.py:503
  155.9 7.3 %collective-permute-done.22.refs_15_ = bf16[2,4,64,512]{3,2,1,0:T(8,128)(2,1)S(1)} collective-permute-done((bf16[2,4,64,512]{3,2,1,0:T(8,128)(2,1)S(1)}, bf16[2,4,64,512]{3,2,1,0:T(8,128)(2,1)S(1)}, u32[]{:S(2)}, u32[]{:S(2)}) %collective-permute-start.22) | collective-permute-done | bytes 524320 | tf_op jit(solution)/shard_map/ppermute | solution.py:503
  163.3 1.9 collective-permute-done.24.refs_17_
  165.9 14.3 %attention.2 = (bf16[8,64,1024]{2,1,0:T(8,128)(2,1)}, bf16[4,2,128,256]{3,2,1,0:T(8,128)(2,1)S(1)}) custom-call(s32[130]{0:T(256)S(1)} %copy-done.22, bf16[4,64,2048]{2,1,0:T(8,128)(2,1)} %bitcast.42, bf16[4,64,2048]{2,1,0:T(8,128)(2,1)} %bitcast.44, bf16[2,4,64,512]{3,2,1,0:T(8,128)(2,1)S(1)} %bitcast.48, bf16[2,4,64,512]{3,2,1,0:T(8,128)(2,1)S(1)} %bitcast.52, ...), custom_call_target="tpu_custom_call" | custom-call | flops 236223200 | bytes 1258291 | tf_op jit(solution)/shard_map/attention/pallas_call | solution.py:338
  180.3 14.2 %attention.3 = (bf16[8,64,1024]{2,1,0:T(8,128)(2,1)}, bf16[4,2,128,256]{3,2,1,0:T(8,128)(2,1)}) custom-call(s32[130]{0:T(256)S(1)} %copy-done.22, bf16[4,64,2048]{2,1,0:T(8,128)(2,1)} %bitcast.43, bf16[4,64,2048]{2,1,0:T(8,128)(2,1)} %bitcast.45, bf16[2,4,64,512]{3,2,1,0:T(8,128)(2,1)S(1)} %bitcast.49, bf16[2,4,64,512]{3,2,1,0:T(8,128)(2,1)S(1)} %bitcast.53, ...), custom_call_target="tpu_custom_call" | custom-call | flops 236223200 | bytes 1258291 | tf_op jit(solution)/shard_map/attention/pallas_call | solution.py:338
  195.8 5.0 %send_part.2.refs_3_ = bf16[512,1024]{1,0:T(8,128)(2,1)S(1)} custom-call(s32[130]{0:T(256)S(1)} %copy-done.22, bf16[512,1024]{1,0:T(8,128)(2,1)S(1)} %bitcast.36, bf16[512,1024]{1,0:T(8,128)(2,1)S(1)} %bitcast.39, bf16[2048,5120]{1,0:T(8,128)(2,1)} %refs_2_.9, bf16[4,2,128,256]{3,2,1,0:T(8,128)(2,1)S(1)} %collective-permute-done.25.refs_3_), custom_call_target="tpu_custom_call" | custom-call | flops 214748368 | bytes 734003 | tf_op jit(solution)/shard_map/send_part/pallas_call | solution.py:388
  200.8 2.1 collective-permute-start.26
  202.8 6.4 %send_part.3 = (bf16[512,1024]{1,0:T(8,128)(2,1)S(1)}, bf16[512,512]{1,0:T(8,128)(2,1)S(1)}) custom-call(s32[130]{0:T(256)S(1)} %copy-done.22, bf16[512,1024]{1,0:T(8,128)(2,1)S(1)} %bitcast.37, bf16[512,1024]{1,0:T(8,128)(2,1)S(1)} %bitcast.40, bf16[2048,5120]{1,0:T(8,128)(2,1)} %refs_2_.9, bf16[512,1024]{1,0:T(8,128)(2,1)S(1)} %send_part.2.refs_3_), custom_call_target="tpu_custom_call" | custom-call | flops 322122560 | bytes 996147 | tf_op jit(solution)/shard_map/send_part/pallas_call | solution.py:388
  209.2 9.3 %own_part.1 = (bf16[512,1024]{1,0:T(8,128)(2,1)S(1)}, bf16[512,1024]{1,0:T(8,128)(2,1)S(1)}, bf16[512,512]{1,0:T(8,128)(2,1)S(1)}) custom-call(s32[130]{0:T(256)S(1)} %copy-done.22, bf16[512,1024]{1,0:T(8,128)(2,1)S(1)} %bitcast.38, bf16[512,1024]{1,0:T(8,128)(2,1)S(1)} %bitcast.41, bf16[2048,5120]{1,0:T(8,128)(2,1)} %refs_2_.9, ...), custom_call_target="tpu_custom_call" | custom-call | flops 536870912 | bytes 1520435 | tf_op jit(solution)/shard_map/own_part/pallas_call | solution.py:388
  218.5 7.5 %collective-permute-done.26 = bf16[512,1024]{1,0:T(8,128)(2,1)S(1)} collective-permute-done((bf16[512,1024]{1,0:T(8,128)(2,1)S(1)}, bf16[512,1024]{1,0:T(8,128)(2,1)S(1)}, u32[]{:S(2)}, u32[]{:S(2)}) %collective-permute-start.26) | collective-permute-done | bytes 1048608 | tf_op jit(solution)/shard_map/ppermute | solution.py:559
  226.0 1.7 collective-permute-start.27
  228.9 3.8 %collective-permute-start.29 = (bf16[2,64,1024]{2,1,0:T(8,128)(2,1)S(1)}, bf16[2,64,1024]{2,1,0:T(8,128)(2,1)S(1)}, u32[]{:S(2)}, u32[]{:S(2)}) collective-permute-start(bf16[2,64,1024]{2,1,0:T(8,128)(2,1)S(1)} %get-tuple-element.63), channel_id=1, source_target_pairs={{0,6},{1,7},{2,0},{3,1},{4,2},{5,3},{6,4},{7,5},{8,14},{9,15},{10,... | collective-permute-start | bytes 786440 | tf_op jit(solution)/shard_map/ppermute | solution.py:503
  232.8 7.2 %collective-permute-done.28.refs_1_ = bf16[2,64,1024]{2,1,0:T(8,128)(2,1)S(1)} collective-permute-done((bf16[2,64,1024]{2,1,0:T(8,128)(2,1)S(1)}, bf16[2,64,1024]{2,1,0:T(8,128)(2,1)S(1)}, u32[]{:S(2)}, u32[]{:S(2)}) %collective-permute-start.28) | collective-permute-done | bytes 262176 | tf_op jit(solution)/shard_map/ppermute | solution.py:503
  240.0 3.5 %collective-permute-done.29.refs_2_ = bf16[2,64,1024]{2,1,0:T(8,128)(2,1)S(1)} collective-permute-done((bf16[2,64,1024]{2,1,0:T(8,128)(2,1)S(1)}, bf16[2,64,1024]{2,1,0:T(8,128)(2,1)S(1)}, u32[]{:S(2)}, u32[]{:S(2)}) %collective-permute-start.29) | collective-permute-done | bytes 262176 | tf_op jit(solution)/shard_map/ppermute | solution.py:503
  243.5 8.6 %collective-permute-done.30.refs_3_ = bf16[2,64,1024]{2,1,0:T(8,128)(2,1)S(1)} collective-permute-done((bf16[2,64,1024]{2,1,0:T(8,128)(2,1)S(1)}, bf16[2,64,1024]{2,1,0:T(8,128)(2,1)S(1)}, u32[]{:S(2)}, u32[]{:S(2)}) %collective-permute-start.30) | collective-permute-done | bytes 262176 | tf_op jit(solution)/shard_map/ppermute | solution.py:503
  253.9 3.8 %collective-permute-start.37 = (bf16[2,64,1024]{2,1,0:T(8,128)(2,1)S(1)}, bf16[2,64,1024]{2,1,0:T(8,128)(2,1)S(1)}, u32[]{:S(2)}, u32[]{:S(2)}) collective-permute-start(bf16[2,64,1024]{2,1,0:T(8,128)(2,1)S(1)} %get-tuple-element.72), channel_id=1, source_target_pairs={{0,6},{1,7},{2,0},{3,1},{4,2},{5,3},{6,4},{7,5},{8,14},{9,15},{10,... | collective-permute-start | bytes 786440 | tf_op jit(solution)/shard_map/ppermute | solution.py:503
  257.8 5.6 %collective-permute-done.31 = bf16[512,512]{1,0:T(8,128)(2,1)S(1)} collective-permute-done((bf16[512,512]{1,0:T(8,128)(2,1)S(1)}, bf16[512,512]{1,0:T(8,128)(2,1)S(1)}, u32[]{:S(2)}, u32[]{:S(2)}) %collective-permute-start.31) | collective-permute-done | bytes 524320 | tf_op jit(solution)/shard_map/ppermute | solution.py:559
  263.4 1.5 residual.4
  266.2 14.2 %collective-permute-done.38.refs_3_ = bf16[2,64,1024]{2,1,0:T(8,128)(2,1)S(1)} collective-permute-done((bf16[2,64,1024]{2,1,0:T(8,128)(2,1)S(1)}, bf16[2,64,1024]{2,1,0:T(8,128)(2,1)S(1)}, u32[]{:S(2)}, u32[]{:S(2)}) %collective-permute-start.38) | collective-permute-done | bytes 262176 | tf_op jit(solution)/shard_map/ppermute | solution.py:503
  283.1 3.9 %collective-permute-done.33.refs_2_ = bf16[2,64,512]{2,1,0:T(8,128)(2,1)S(1)} collective-permute-done((bf16[2,64,512]{2,1,0:T(8,128)(2,1)}, bf16[2,64,512]{2,1,0:T(8,128)(2,1)S(1)}, u32[]{:S(2)}, u32[]{:S(2)}) %collective-permute-start.33) | collective-permute-done | bytes 131104 | tf_op jit(solution)/shard_map/ppermute | solution.py:503
  287.0 1.8 collective-permute-done.34.refs_3_
  290.0 1.6 placed.3.refs_5_
  291.7 1.6 placed.4.refs_5_
  293.3 2.3 placed.5
  297.9 1.6 pad_maximum_fusion
  (153 shorter events, 28.0 us)
Async XLA Ops:
  3.3 3.5 %collective-permute-start = (bf16[4,64,2560]{2,1,0:T(8,128)(2,1)}, bf16[4,64,2560]{2,1,0:T(8,128)(2,1)}, u32[]{:S(2)}, u32[]{:S(2)}) collective-permute-start(bf16[4,64,2560]{2,1,0:T(8,128)(2,1)} %dynamic-slice_bitcast_fusion), channel_id=1, source_target_pairs={{0,1},{1,0},{2,3},{3,2},{4,5},{5,4},{6,7},{7,6},{8,9},{9,8},{10,11... | collective-permute-start | bytes 3932168 | tf_op jit(solution)/shard_map/ppermute | solution.py:503
  8.9 38.0 %copy-start.32 = (bf16[2560]{0:T(1024)(128)(2,1)S(1)}, bf16[2560]{0:T(1024)(128)(2,1)}, u32[]{:S(2)}) copy-start(bf16[2560]{0:T(1024)(128)(2,1)} %param.13) | copy-start | bytes 15364
  8.9 18.0 %collective-permute-start.2 = (bf16[128,2560]{1,0:T(8,128)(2,1)S(1)}, bf16[128,2560]{1,0:T(8,128)(2,1)S(1)}, u32[]{:S(2)}, u32[]{:S(2)}) collective-permute-start(bf16[128,2560]{1,0:T(8,128)(2,1)S(1)} %pad_maximum_fusion.1.refs_0_), channel_id=1, source_target_pairs={{0,8},{8,0},{1,9},{9,1},{2,10},{10,2},{3,11},{11,3},{4,12},{12,4},... | collective-permute-start | bytes 1966088 | tf_op jit(solution)/shard_map/ppermute | solution.py:559
  11.8 51.2 %copy-start.23 = (bf16[128]{0:T(256)(128)(2,1)S(1)}, bf16[128]{0:T(256)(128)(2,1)}, u32[]{:S(2)}) copy-start(bf16[128]{0:T(256)(128)(2,1)} %param.18) | copy-start | bytes 772
  12.7 20.2 %collective-permute-start.1 = (bf16[128,2560]{1,0:T(8,128)(2,1)}, bf16[128,2560]{1,0:T(8,128)(2,1)S(1)}, u32[]{:S(2)}, u32[]{:S(2)}) collective-permute-start(bf16[128,2560]{1,0:T(8,128)(2,1)} %pad_maximum_fusion.2), channel_id=1, source_target_pairs={{0,2},{1,3},{2,4},{3,5},{4,6},{5,7},{6,0},{7,1},{8,10},{9,11},{10,... | collective-permute-start | bytes 1966088 | tf_op jit(solution)/shard_map/ppermute | solution.py:503
  26.9 18.5 %collective-permute-start.3 = (bf16[128,2560]{1,0:T(8,128)(2,1)}, bf16[128,2560]{1,0:T(8,128)(2,1)S(1)}, u32[]{:S(2)}, u32[]{:S(2)}) collective-permute-start(bf16[128,2560]{1,0:T(8,128)(2,1)} %pad_maximum_fusion.3), channel_id=1, source_target_pairs={{0,6},{1,7},{2,0},{3,1},{4,2},{5,3},{6,4},{7,5},{8,14},{9,15},{10,... | collective-permute-start | bytes 1966088 | tf_op jit(solution)/shard_map/ppermute | solution.py:503
  32.9 30.1 %copy-start.22 = (s32[130]{0:T(256)S(1)}, s32[130]{0:T(256)}, u32[]{:S(2)}) copy-start(s32[130]{0:T(256)} %tables.1.table) | copy-start | bytes 1564
  32.9 16.5 %collective-permute-start.4 = (bf16[128,2560]{1,0:T(8,128)(2,1)S(1)}, bf16[128,2560]{1,0:T(8,128)(2,1)}, u32[]{:S(2)}, u32[]{:S(2)}) collective-permute-start(bf16[128,2560]{1,0:T(8,128)(2,1)S(1)} %collective-permute-done.1.refs_1_), channel_id=1, source_target_pairs={{0,8},{8,0},{1,9},{9,1},{2,10},{10,2},{3,11},{11,3},{4,12},{12,4},... | collective-permute-start | bytes 1966088 | tf_op jit(solution)/shard_map/ppermute | solution.py:559
  45.3 17.5 %collective-permute-start.6 = (bf16[128,2560]{1,0:T(8,128)(2,1)S(1)}, bf16[128,2560]{1,0:T(8,128)(2,1)S(1)}, u32[]{:S(2)}, u32[]{:S(2)}) collective-permute-start(bf16[128,2560]{1,0:T(8,128)(2,1)S(1)} %collective-permute-done.3.refs_0_.refs_2_), channel_id=1, source_target_pairs={{0,8},{8,0},{1,9},{9,1},{2,10},{10,2},{3,11},{11,3},{4,12},{12,4},... | collective-permute-start | bytes 1966088 | tf_op jit(solution)/shard_map/ppermute | solution.py:559
  47.9 15.1 %collective-permute-start.8 = (bf16[1,2560]{1,0:T(2,128)(2,1)S(1)}, bf16[1,2560]{1,0:T(2,128)(2,1)S(1)}, u32[]{:S(2)}, u32[]{:S(2)}) collective-permute-start(bf16[1,2560]{1,0:T(2,128)(2,1)S(1)} %broadcast_in_dim.6.refs_4_.refs_6_), channel_id=1, source_target_pairs={{0,8},{8,0},{1,9},{9,1},{2,10},{10,2},{3,11},{11,3},{4,12},{12,4},... | collective-permute-start | bytes 15368 | tf_op jit(solution)/shard_map/ppermute | solution.py:559
  49.4 38.4 %collective-permute-start.5 = (bf16[64,2560]{1,0:T(8,128)(2,1)}, bf16[64,2560]{1,0:T(8,128)(2,1)S(1)}, u32[]{:S(2)}, u32[]{:S(2)}) collective-permute-start(bf16[64,2560]{1,0:T(8,128)(2,1)} %get-tuple-element.40), channel_id=1, source_target_pairs={{0,4},{1,5},{2,6},{3,7},{4,0},{5,1},{6,2},{7,3},{8,12},{9,13},{10,... | collective-permute-start | bytes 983048 | tf_op jit(solution)/shard_map/ppermute | solution.py:503
  62.8 28.6 %collective-permute-start.7 = (bf16[64,2560]{1,0:T(8,128)(2,1)}, bf16[64,2560]{1,0:T(8,128)(2,1)S(1)}, u32[]{:S(2)}, u32[]{:S(2)}) collective-permute-start(bf16[64,2560]{1,0:T(8,128)(2,1)} %get-tuple-element.41), channel_id=1, source_target_pairs={{0,4},{1,5},{2,6},{3,7},{4,0},{5,1},{6,2},{7,3},{8,12},{9,13},{10,... | collective-permute-start | bytes 983048 | tf_op jit(solution)/shard_map/ppermute | solution.py:503
  72.5 19.8 %collective-permute-start.11 = (bf16[2,4,64,512]{3,2,1,0:T(8,128)(2,1)S(1)}, bf16[2,4,64,512]{3,2,1,0:T(8,128)(2,1)S(1)}, u32[]{:S(2)}, u32[]{:S(2)}) collective-permute-start(bf16[2,4,64,512]{3,2,1,0:T(8,128)(2,1)S(1)} %bitcast.46), channel_id=1, source_target_pairs={{0,2},{1,3},{2,4},{3,5},{4,6},{5,7},{6,0},{7,1},{8,10},{9,11},{10,... | collective-permute-start | bytes 1572872 | tf_op jit(solution)/shard_map/ppermute | solution.py:503
  87.7 8.7 %collective-permute-start.9 = (bf16[64,2560]{1,0:T(8,128)(2,1)S(1)}, bf16[64,2560]{1,0:T(8,128)(2,1)S(1)}, u32[]{:S(2)}, u32[]{:S(2)}) collective-permute-start(bf16[64,2560]{1,0:T(8,128)(2,1)S(1)} %collective-permute-done.5.refs_1_.refs_3_), channel_id=1, source_target_pairs={{0,8},{8,0},{1,9},{9,1},{2,10},{10,2},{3,11},{11,3},{4,12},{12,4},... | collective-permute-start | bytes 983048 | tf_op jit(solution)/shard_map/ppermute | solution.py:559
  91.3 10.9 %collective-permute-start.10 = (bf16[64,2560]{1,0:T(8,128)(2,1)S(1)}, bf16[64,2560]{1,0:T(8,128)(2,1)S(1)}, u32[]{:S(2)}, u32[]{:S(2)}) collective-permute-start(bf16[64,2560]{1,0:T(8,128)(2,1)S(1)} %collective-permute-done.7.refs_2_.refs_4_), channel_id=1, source_target_pairs={{0,8},{8,0},{1,9},{9,1},{2,10},{10,2},{3,11},{11,3},{4,12},{12,4},... | collective-permute-start | bytes 983048 | tf_op jit(solution)/shard_map/ppermute | solution.py:559
  92.3 21.4 %collective-permute-start.12 = (bf16[2,4,64,512]{3,2,1,0:T(8,128)(2,1)S(1)}, bf16[2,4,64,512]{3,2,1,0:T(8,128)(2,1)S(1)}, u32[]{:S(2)}, u32[]{:S(2)}) collective-permute-start(bf16[2,4,64,512]{3,2,1,0:T(8,128)(2,1)S(1)} %collective-permute-done.11.refs_6_), channel_id=1, source_target_pairs={{0,2},{1,3},{2,4},{3,5},{4,6},{5,7},{6,0},{7,1},{8,10},{9,11},{10,... | collective-permute-start | bytes 1572872 | tf_op jit(solution)/shard_map/ppermute | solution.py:503
  110.8 16.5 %collective-permute-start.15 = (bf16[2,4,64,512]{3,2,1,0:T(8,128)(2,1)S(1)}, bf16[2,4,64,512]{3,2,1,0:T(8,128)(2,1)S(1)}, u32[]{:S(2)}, u32[]{:S(2)}) collective-permute-start(bf16[2,4,64,512]{3,2,1,0:T(8,128)(2,1)S(1)} %bitcast.50), channel_id=1, source_target_pairs={{0,2},{1,3},{2,4},{3,5},{4,6},{5,7},{6,0},{7,1},{8,10},{9,11},{10,... | collective-permute-start | bytes 1572872 | tf_op jit(solution)/shard_map/ppermute | solution.py:503
  127.4 16.7 %collective-permute-start.18 = (bf16[2,4,64,512]{3,2,1,0:T(8,128)(2,1)S(1)}, bf16[2,4,64,512]{3,2,1,0:T(8,128)(2,1)S(1)}, u32[]{:S(2)}, u32[]{:S(2)}) collective-permute-start(bf16[2,4,64,512]{3,2,1,0:T(8,128)(2,1)S(1)} %collective-permute-done.15.refs_7_), channel_id=1, source_target_pairs={{0,2},{1,3},{2,4},{3,5},{4,6},{5,7},{6,0},{7,1},{8,10},{9,11},{10,... | collective-permute-start | bytes 1572872 | tf_op jit(solution)/shard_map/ppermute | solution.py:503
  127.7 16.4 %collective-permute-start.13 = (bf16[2,4,64,512]{3,2,1,0:T(8,128)(2,1)S(1)}, bf16[2,4,64,512]{3,2,1,0:T(8,128)(2,1)S(1)}, u32[]{:S(2)}, u32[]{:S(2)}) collective-permute-start(bf16[2,4,64,512]{3,2,1,0:T(8,128)(2,1)S(1)} %bitcast.47), channel_id=1, source_target_pairs={{0,1},{1,0},{2,3},{3,2},{4,5},{5,4},{6,7},{7,6},{8,9},{9,8},{10,11... | collective-permute-start | bytes 1572872 | tf_op jit(solution)/shard_map/ppermute | solution.py:503
  127.7 27.6 %collective-permute-start.21 = (bf16[2,4,64,512]{3,2,1,0:T(8,128)(2,1)S(1)}, bf16[2,4,64,512]{3,2,1,0:T(8,128)(2,1)S(1)}, u32[]{:S(2)}, u32[]{:S(2)}) collective-permute-start(bf16[2,4,64,512]{3,2,1,0:T(8,128)(2,1)S(1)} %collective-permute-done.12.refs_10_), channel_id=1, source_target_pairs={{0,2},{1,3},{2,4},{3,5},{4,6},{5,7},{6,0},{7,1},{8,10},{9,11},{10,... | collective-permute-start | bytes 1572872 | tf_op jit(solution)/shard_map/ppermute | solution.py:503
  129.1 26.2 %collective-permute-start.16 = (bf16[2,4,64,512]{3,2,1,0:T(8,128)(2,1)S(1)}, bf16[2,4,64,512]{3,2,1,0:T(8,128)(2,1)S(1)}, u32[]{:S(2)}, u32[]{:S(2)}) collective-permute-start(bf16[2,4,64,512]{3,2,1,0:T(8,128)(2,1)S(1)} %collective-permute-done.11.refs_6_), channel_id=1, source_target_pairs={{0,1},{1,0},{2,3},{3,2},{4,5},{5,4},{6,7},{7,6},{8,9},{9,8},{10,11... | collective-permute-start | bytes 1572872 | tf_op jit(solution)/shard_map/ppermute | solution.py:503
  129.4 26.4 %collective-permute-start.19 = (bf16[2,4,64,512]{3,2,1,0:T(8,128)(2,1)S(1)}, bf16[2,4,64,512]{3,2,1,0:T(8,128)(2,1)S(1)}, u32[]{:S(2)}, u32[]{:S(2)}) collective-permute-start(bf16[2,4,64,512]{3,2,1,0:T(8,128)(2,1)S(1)} %collective-permute-done.12.refs_10_), channel_id=1, source_target_pairs={{0,1},{1,0},{2,3},{3,2},{4,5},{5,4},{6,7},{7,6},{8,9},{9,8},{10,11... | collective-permute-start | bytes 1572872 | tf_op jit(solution)/shard_map/ppermute | solution.py:503
  144.0 19.2 %collective-permute-start.22 = (bf16[2,4,64,512]{3,2,1,0:T(8,128)(2,1)S(1)}, bf16[2,4,64,512]{3,2,1,0:T(8,128)(2,1)S(1)}, u32[]{:S(2)}, u32[]{:S(2)}) collective-permute-start(bf16[2,4,64,512]{3,2,1,0:T(8,128)(2,1)S(1)} %collective-permute-done.18.refs_11_), channel_id=1, source_target_pairs={{0,2},{1,3},{2,4},{3,5},{4,6},{5,7},{6,0},{7,1},{8,10},{9,11},{10,... | collective-permute-start | bytes 1572872 | tf_op jit(solution)/shard_map/ppermute | solution.py:503
  144.0 19.2 %collective-permute-start.14 = (bf16[2,4,64,512]{3,2,1,0:T(8,128)(2,1)S(1)}, bf16[2,4,64,512]{3,2,1,0:T(8,128)(2,1)S(1)}, u32[]{:S(2)}, u32[]{:S(2)}) collective-permute-start(bf16[2,4,64,512]{3,2,1,0:T(8,128)(2,1)S(1)} %bitcast.51), channel_id=1, source_target_pairs={{0,1},{1,0},{2,3},{3,2},{4,5},{5,4},{6,7},{7,6},{8,9},{9,8},{10,11... | collective-permute-start | bytes 1572872 | tf_op jit(solution)/shard_map/ppermute | solution.py:503
  155.3 7.9 %collective-permute-start.23 = (bf16[2,4,64,512]{3,2,1,0:T(8,128)(2,1)S(1)}, bf16[2,4,64,512]{3,2,1,0:T(8,128)(2,1)S(1)}, u32[]{:S(2)}, u32[]{:S(2)}) collective-permute-start(bf16[2,4,64,512]{3,2,1,0:T(8,128)(2,1)S(1)} %collective-permute-done.21.refs_14_), channel_id=1, source_target_pairs={{0,1},{1,0},{2,3},{3,2},{4,5},{5,4},{6,7},{7,6},{8,9},{9,8},{10,11... | collective-permute-start | bytes 1572872 | tf_op jit(solution)/shard_map/ppermute | solution.py:503
  155.3 7.9 %collective-permute-start.17 = (bf16[2,4,64,512]{3,2,1,0:T(8,128)(2,1)S(1)}, bf16[2,4,64,512]{3,2,1,0:T(8,128)(2,1)S(1)}, u32[]{:S(2)}, u32[]{:S(2)}) collective-permute-start(bf16[2,4,64,512]{3,2,1,0:T(8,128)(2,1)S(1)} %collective-permute-done.15.refs_7_), channel_id=1, source_target_pairs={{0,1},{1,0},{2,3},{3,2},{4,5},{5,4},{6,7},{7,6},{8,9},{9,8},{10,11... | collective-permute-start | bytes 1572872 | tf_op jit(solution)/shard_map/ppermute | solution.py:503
  155.8 7.4 %collective-permute-start.20 = (bf16[2,4,64,512]{3,2,1,0:T(8,128)(2,1)S(1)}, bf16[2,4,64,512]{3,2,1,0:T(8,128)(2,1)S(1)}, u32[]{:S(2)}, u32[]{:S(2)}) collective-permute-start(bf16[2,4,64,512]{3,2,1,0:T(8,128)(2,1)S(1)} %collective-permute-done.18.refs_11_), channel_id=1, source_target_pairs={{0,1},{1,0},{2,3},{3,2},{4,5},{5,4},{6,7},{7,6},{8,9},{9,8},{10,11... | collective-permute-start | bytes 1572872 | tf_op jit(solution)/shard_map/ppermute | solution.py:503
  163.2 1.9 collective-permute-start.24
  180.2 14.3 %collective-permute-start.25 = (bf16[4,2,128,256]{3,2,1,0:T(8,128)(2,1)S(1)}, bf16[4,2,128,256]{3,2,1,0:T(8,128)(2,1)S(1)}, u32[]{:S(2)}, u32[]{:S(2)}) collective-permute-start(bf16[4,2,128,256]{3,2,1,0:T(8,128)(2,1)S(1)} %get-tuple-element.54), channel_id=1, source_target_pairs={{0,8},{8,0},{1,9},{9,1},{2,10},{10,2},{3,11},{11,3},{4,12},{12,4},... | collective-permute-start | bytes 1572872 | tf_op jit(solution)/shard_map/ppermute | solution.py:559
  200.8 25.2 %collective-permute-start.26 = (bf16[512,1024]{1,0:T(8,128)(2,1)S(1)}, bf16[512,1024]{1,0:T(8,128)(2,1)S(1)}, u32[]{:S(2)}, u32[]{:S(2)}) collective-permute-start(bf16[512,1024]{1,0:T(8,128)(2,1)S(1)} %send_part.2.refs_3_), channel_id=1, source_target_pairs={{0,8},{8,0},{1,9},{9,1},{2,10},{10,2},{3,11},{11,3},{4,12},{12,4},... | collective-permute-start | bytes 3145736 | tf_op jit(solution)/shard_map/ppermute | solution.py:559
  226.0 26.1 %collective-permute-start.27 = (bf16[512,1024]{1,0:T(8,128)(2,1)S(1)}, bf16[512,1024]{1,0:T(8,128)(2,1)S(1)}, u32[]{:S(2)}, u32[]{:S(2)}) collective-permute-start(bf16[512,1024]{1,0:T(8,128)(2,1)S(1)} %get-tuple-element.60), channel_id=1, source_target_pairs={{0,8},{8,0},{1,9},{9,1},{2,10},{10,2},{3,11},{11,3},{4,12},{12,4},... | collective-permute-start | bytes 3145736 | tf_op jit(solution)/shard_map/ppermute | solution.py:559
  228.9 11.1 %collective-permute-start.28 = (bf16[2,64,1024]{2,1,0:T(8,128)(2,1)S(1)}, bf16[2,64,1024]{2,1,0:T(8,128)(2,1)S(1)}, u32[]{:S(2)}, u32[]{:S(2)}) collective-permute-start(bf16[2,64,1024]{2,1,0:T(8,128)(2,1)S(1)} %get-tuple-element.62), channel_id=1, source_target_pairs={{0,2},{1,3},{2,4},{3,5},{4,6},{5,7},{6,0},{7,1},{8,10},{9,11},{10,... | collective-permute-start | bytes 786440 | tf_op jit(solution)/shard_map/ppermute | solution.py:503
  228.9 14.6 %collective-permute-start.29 = (bf16[2,64,1024]{2,1,0:T(8,128)(2,1)S(1)}, bf16[2,64,1024]{2,1,0:T(8,128)(2,1)S(1)}, u32[]{:S(2)}, u32[]{:S(2)}) collective-permute-start(bf16[2,64,1024]{2,1,0:T(8,128)(2,1)S(1)} %get-tuple-element.63), channel_id=1, source_target_pairs={{0,6},{1,7},{2,0},{3,1},{4,2},{5,3},{6,4},{7,5},{8,14},{9,15},{10,... | collective-permute-start | bytes 786440 | tf_op jit(solution)/shard_map/ppermute | solution.py:503
  232.8 19.3 %collective-permute-start.30 = (bf16[2,64,1024]{2,1,0:T(8,128)(2,1)S(1)}, bf16[2,64,1024]{2,1,0:T(8,128)(2,1)S(1)}, u32[]{:S(2)}, u32[]{:S(2)}) collective-permute-start(bf16[2,64,1024]{2,1,0:T(8,128)(2,1)S(1)} %get-tuple-element.64), channel_id=1, source_target_pairs={{0,4},{1,5},{2,6},{3,7},{4,0},{5,1},{6,2},{7,3},{8,12},{9,13},{10,... | collective-permute-start | bytes 786440 | tf_op jit(solution)/shard_map/ppermute | solution.py:503
  240.0 17.8 %copy-start.6 = (bf16[2,64,1024]{2,1,0:T(8,128)(2,1)}, bf16[2,64,1024]{2,1,0:T(8,128)(2,1)S(1)}, u32[]{:S(2)}) copy-start(bf16[2,64,1024]{2,1,0:T(8,128)(2,1)S(1)} %collective-permute-done.28.refs_1_) | copy-start | bytes 786436
  252.1 11.4 %collective-permute-start.31 = (bf16[512,512]{1,0:T(8,128)(2,1)S(1)}, bf16[512,512]{1,0:T(8,128)(2,1)S(1)}, u32[]{:S(2)}, u32[]{:S(2)}) collective-permute-start(bf16[512,512]{1,0:T(8,128)(2,1)S(1)} %get-tuple-element.65.refs_3_), channel_id=1, source_target_pairs={{0,8},{8,0},{1,9},{9,1},{2,10},{10,2},{3,11},{11,3},{4,12},{12,4},... | collective-permute-start | bytes 1572872 | tf_op jit(solution)/shard_map/ppermute | solution.py:559
  253.9 12.0 %collective-permute-start.36 = (bf16[2,64,1024]{2,1,0:T(8,128)(2,1)S(1)}, bf16[2,64,1024]{2,1,0:T(8,128)(2,1)S(1)}, u32[]{:S(2)}, u32[]{:S(2)}) collective-permute-start(bf16[2,64,1024]{2,1,0:T(8,128)(2,1)S(1)} %get-tuple-element.71), channel_id=1, source_target_pairs={{0,2},{1,3},{2,4},{3,5},{4,6},{5,7},{6,0},{7,1},{8,10},{9,11},{10,... | collective-permute-start | bytes 786440 | tf_op jit(solution)/shard_map/ppermute | solution.py:503
  253.9 12.3 %collective-permute-start.37 = (bf16[2,64,1024]{2,1,0:T(8,128)(2,1)S(1)}, bf16[2,64,1024]{2,1,0:T(8,128)(2,1)S(1)}, u32[]{:S(2)}, u32[]{:S(2)}) collective-permute-start(bf16[2,64,1024]{2,1,0:T(8,128)(2,1)S(1)} %get-tuple-element.72), channel_id=1, source_target_pairs={{0,6},{1,7},{2,0},{3,1},{4,2},{5,3},{6,4},{7,5},{8,14},{9,15},{10,... | collective-permute-start | bytes 786440 | tf_op jit(solution)/shard_map/ppermute | solution.py:503
  257.7 22.7 %collective-permute-start.38 = (bf16[2,64,1024]{2,1,0:T(8,128)(2,1)S(1)}, bf16[2,64,1024]{2,1,0:T(8,128)(2,1)S(1)}, u32[]{:S(2)}, u32[]{:S(2)}) collective-permute-start(bf16[2,64,1024]{2,1,0:T(8,128)(2,1)S(1)} %get-tuple-element.73), channel_id=1, source_target_pairs={{0,4},{1,5},{2,6},{3,7},{4,0},{5,1},{6,2},{7,3},{8,12},{9,13},{10,... | collective-permute-start | bytes 786440 | tf_op jit(solution)/shard_map/ppermute | solution.py:503
  264.9 24.9 %copy-start.21 = (bf16[4,2,128,256]{3,2,1,0:T(8,128)(2,1)S(1)}, bf16[4,2,128,256]{3,2,1,0:T(8,128)(2,1)}, u32[]{:S(2)}) copy-start(bf16[4,2,128,256]{3,2,1,0:T(8,128)(2,1)} %copy-done.20) | copy-start | bytes 1572868
  264.9 17.0 %collective-permute-start.32 = (bf16[2,64,512]{2,1,0:T(8,128)(2,1)S(1)}, bf16[2,64,512]{2,1,0:T(8,128)(2,1)S(1)}, u32[]{:S(2)}, u32[]{:S(2)}) collective-permute-start(bf16[2,64,512]{2,1,0:T(8,128)(2,1)S(1)} %get-tuple-element.67), channel_id=1, source_target_pairs={{0,2},{1,3},{2,4},{3,5},{4,6},{5,7},{6,0},{7,1},{8,10},{9,11},{10,... | collective-permute-start | bytes 393224 | tf_op jit(solution)/shard_map/ppermute | solution.py:503
  265.8 24.2 %collective-permute-start.40 = (bf16[4,64,1024]{2,1,0:T(8,128)(2,1)}, bf16[4,64,1024]{2,1,0:T(8,128)(2,1)S(1)}, u32[]{:S(2)}, u32[]{:S(2)}) collective-permute-start(bf16[4,64,1024]{2,1,0:T(8,128)(2,1)} %pad_maximum_fusion.5), channel_id=1, source_target_pairs={{0,1},{1,0},{2,3},{3,2},{4,5},{5,4},{6,7},{7,6},{8,9},{9,8},{10,11... | collective-permute-start | bytes 1572872 | tf_op jit(solution)/shard_map/ppermute | solution.py:503
  265.9 14.6 %copy-start.14 = (bf16[2,64,1024]{2,1,0:T(8,128)(2,1)}, bf16[2,64,1024]{2,1,0:T(8,128)(2,1)S(1)}, u32[]{:S(2)}) copy-start(bf16[2,64,1024]{2,1,0:T(8,128)(2,1)S(1)} %collective-permute-done.36.refs_1_) | copy-start | bytes 786436
  280.4 6.6 %collective-permute-start.33 = (bf16[2,64,512]{2,1,0:T(8,128)(2,1)}, bf16[2,64,512]{2,1,0:T(8,128)(2,1)S(1)}, u32[]{:S(2)}, u32[]{:S(2)}) collective-permute-start(bf16[2,64,512]{2,1,0:T(8,128)(2,1)} %get-tuple-element.68), channel_id=1, source_target_pairs={{0,6},{1,7},{2,0},{3,1},{4,2},{5,3},{6,4},{7,5},{8,14},{9,15},{10,... | collective-permute-start | bytes 393224 | tf_op jit(solution)/shard_map/ppermute | solution.py:503
  280.5 8.4 %collective-permute-start.34 = (bf16[2,64,512]{2,1,0:T(8,128)(2,1)}, bf16[2,64,512]{2,1,0:T(8,128)(2,1)}, u32[]{:S(2)}, u32[]{:S(2)}) collective-permute-start(bf16[2,64,512]{2,1,0:T(8,128)(2,1)} %get-tuple-element.69), channel_id=1, source_target_pairs={{0,4},{1,5},{2,6},{3,7},{4,0},{5,1},{6,2},{7,3},{8,12},{9,13},{10,... | collective-permute-start | bytes 393224 | tf_op jit(solution)/shard_map/ppermute | solution.py:503
  282.0 9.7 %collective-permute-start.39 = (bf16[4,64,1024]{2,1,0:T(8,128)(2,1)}, bf16[4,64,1024]{2,1,0:T(8,128)(2,1)S(1)}, u32[]{:S(2)}, u32[]{:S(2)}) collective-permute-start(bf16[4,64,1024]{2,1,0:T(8,128)(2,1)} %pad_maximum_fusion.4), channel_id=1, source_target_pairs={{0,1},{1,0},{2,3},{3,2},{4,5},{5,4},{6,7},{7,6},{8,9},{9,8},{10,11... | collective-permute-start | bytes 1572872 | tf_op jit(solution)/shard_map/ppermute | solution.py:503
  282.0 14.7 %collective-permute-start.41 = (bf16[4,2,128,256]{3,2,1,0:T(8,128)(2,1)}, bf16[4,2,128,256]{3,2,1,0:T(8,128)(2,1)}, u32[]{:S(2)}, u32[]{:S(2)}) collective-permute-start(bf16[4,2,128,256]{3,2,1,0:T(8,128)(2,1)} %get-tuple-element.75), channel_id=1, source_target_pairs={{0,8},{8,0},{1,9},{9,1},{2,10},{10,2},{3,11},{11,3},{4,12},{12,4},... | collective-permute-start | bytes 1572872 | tf_op jit(solution)/shard_map/ppermute | solution.py:559
  289.8 3.5 %collective-permute-start.35 = (bf16[4,64,512]{2,1,0:T(8,128)(2,1)S(1)}, bf16[4,64,512]{2,1,0:T(8,128)(2,1)S(1)}, u32[]{:S(2)}, u32[]{:S(2)}) collective-permute-start(bf16[4,64,512]{2,1,0:T(8,128)(2,1)S(1)} %pad_maximum_fusion.8), channel_id=1, source_target_pairs={{0,1},{1,0},{2,3},{3,2},{4,5},{5,4},{6,7},{7,6},{8,9},{9,8},{10,11... | collective-permute-start | bytes 786440 | tf_op jit(solution)/shard_map/ppermute | solution.py:503
  (30 other events, 177.9 us)

commit v5 on v4

--- a/solution.py
+++ b/solution.py
@@ -534,20 +534,26 @@
     per_kv = wq.shape[1] // max(head, wk.shape[1])
 
     chip, core = group_rank // CORES, group_rank % CORES
-    split = hidden_in.reshape(chips, CORES, rows, cols)
-    mine, theirs = [
-        lax.dynamic_index_in_dim(split, at, 1, keepdims=False) for at in (core, 1 - core)
-    ]
-    theirs = shift(theirs, owners, 0, 1)
-    pairs = []
-    for hop in hop_order(chips):
-        at = lax.rem(chip + hop, chips)
-        pairs.append([lax.dynamic_index_in_dim(x, at, 0, keepdims=False) for x in (mine, theirs)])
-    arrived = [jnp.concatenate(pairs[0])]
-    moves = [(hop, [jnp.concatenate(pair)]) for hop, pair in zip(hop_order(chips), pairs)][1:]
-    if len(moves) > 1:
-        moves[-1] = (moves[-1][0], pairs[-1])
-    moves = [(hop, block) for hop, blocks in moves for block in blocks]
+    split = hidden_in.reshape(owners, rows, cols)
+
+    def rows_for(hop, flip):
+        to = lax.rem(chip + hop, chips) * CORES + lax.rem(core + flip, CORES)
+        return lax.dynamic_index_in_dim(split, to, 0, keepdims=False)
+
+    hops = hop_order(chips)
+    paired_hops = hops[2:]
+    near = [shift(rows_for(hop, flip), owners, hop, flip) for hop in hops[1:2] for flip in range(CORES)]
+    swapped = shift(
+        jnp.stack([rows_for(hop, 1) for hop in hops[:1] + paired_hops]), owners, 0, 1
+    )
+    arrived = [rows_for(0, 0), swapped[0]] + near
+    moves = []
+    for n, hop in enumerate(paired_hops):
+        pair = [rows_for(hop, 0), swapped[1 + n]]
+        if n < len(paired_hops) - 1:
+            moves.append((hop, jnp.concatenate(pair)))
+        else:
+            moves += [(hop, block) for block in pair]
 
     ranks = jnp.stack([group_rank, tensor_rank]).astype(jnp.int32)
     table = make_tables(
@@ -557,52 +563,52 @@
     cosine, sine = rope_tables(earlier, span_len, group_rank * rows, rows, head)
 
     cross = lambda x: lax.ppermute(x, "tensor", swap)
-    crossed = [cross(arrived[0])] if paired else []
+    crossed = [cross(x) for x in arrived] if paired else []
     if paired:
         gain = ln_gain[None]
-        gains = [gain, cross(after(gain, crossed[0]))]
+        gains = [gain, cross(after(gain, crossed[1]))]
     else:
         gains = [lax.all_gather(ln_gain, "tensor", axis=0, tiled=True)[None]]
+    for n, (hop, block) in enumerate(moves):
+        if paired:
+            landed = arrived[-1:] if n else near
+            block = after(block, (landed, crossed[2 * n : 2 * n + 2] if n < 2 else crossed[n + 2]))
+        arrived.append(shift(block, owners, hop, 0))
+        if paired:
+            crossed.append(cross(arrived[-1]))
+
+    kgain = after(key_norm_gain[None], arrived[-1])
+    kvs, norms, begun = [], [], 0
+    for n in range(1, len(arrived) + 1):
+        if sum(x.shape[0] for x in arrived[begun:n]) == here * rows:
+            if paired:
+                xs = [arrived[begun:n], crossed[begun:n]]
+            else:
+                whole = jnp.concatenate(arrived[begun:n])
+                xs = [[lax.all_gather(whole, "tensor", axis=1, tiled=True)]]
+            *normed, kv = make_kv(
+                lay, table, xs, gains, wk, wv, kgain, cosine, sine, len(kvs)
+            )
+            kvs.append(kv.reshape(2, here, rows, kv.shape[2]))
+            norms.append(normed)
+            begun = n
 
     queries, gathered = [], [[] for _ in range(owners)]
-
-    def make_part(p, own_rows, crossed_rows):
-        if paired:
-            xs = [own_rows, crossed_rows]
-        else:
-            xs = [[lax.all_gather(jnp.concatenate(own_rows), "tensor", axis=1, tiled=True)]]
-        kgain = key_norm_gain[None]
-        *normed, kv = make_kv(lay, table, xs, gains, wk, wv, kgain, cosine, sine, p)
-        kv = kv.reshape(2, here, rows, kv.shape[2])
-        for back in range(chips):
+    ready = kvs[-1]
+    for back in range(chips):
+        for p in range(PARTS):
             if back:
-                if p and back == chips // 2:
-                    kv = after(kv, queries[-1])
-                kv = shift(kv, owners, 1, 0)
-            gathered[back * CORES].append(kv)
-            gathered[back * CORES + 1].append(shift(kv, owners, 0, 1))
-            if back == 1 or chips == 1:
-                qgain = q_gain[None]
-                if p:
-                    qgain = after(qgain, gathered[(chips // 2) * CORES][0])
-                made = make_q(lay, table, normed, wq, qgain, cosine, sine, p)
+                if back == min(2, chips - 1):
+                    kvs[p] = after(kvs[p], queries[p])
+                kvs[p] = shift(kvs[p], owners, 1, 0)
+            gathered[back * CORES].append(kvs[p])
+            gathered[back * CORES + 1].append(shift(kvs[p], owners, 0, 1))
+            if back == min(1, chips - 1):
+                made = make_q(
+                    lay, table, norms[p], wq, after(q_gain[None], ready), cosine, sine, p
+                )
                 queries.append(made.reshape(here, rows, made.shape[1]))
-
-    begun = 0
-    for m in range(len(moves) + 1):
-        if m:
-            hop, block = moves[m - 1]
-            if paired and m > 1:
-                block = after(block, crossed[m - 2])
-            arrived.append(shift(block, owners, hop, 0))
-            if paired:
-                block = arrived[-1]
-                if m == len(moves) and queries:
-                    block = after(block, queries[0])
-                crossed.append(cross(block))
-        if sum(x.shape[0] for x in arrived[begun:]) == here * rows:
-            make_part(len(queries), arrived[begun:], crossed[begun:])
-            begun = len(arrived)
+                ready = kvs[p]
 
     own_kv = wk.shape[1] // head
     sets = [own_kv // 2, own_kv - own_kv // 2] if own_kv > 1 else [own_kv]

time: 300 us -> 310 us (1.033)
  waiting for transfers between devices: 138 us -> 148 us
  local copies, waits for them, and re-layouts: 13.7 us -> 18.2 us
    ppermute x31 -> x32, waiting for transfers between devices: 89.6 us -> 126 us  [shift(): return lax.ppermute(x, 'group', pairs)]
    ppermute x11 -> x13, waiting for transfers between devices: 48.7 us -> 21.9 us  [local(): cross = lambda x: lax.ppermute(x, 'tensor', swap)]
    unnamed x66 -> x86, local copies, waits for them, and re-layouts: 7.16 us -> 13.7 us
    ppermute x11 -> x13, starting transfers between devices: 14.6 us -> 13.9 us  [local(): cross = lambda x: lax.ppermute(x, 'tensor', swap)]
    ppermute x31 -> x32, starting transfers between devices: 21.7 us -> 21.6 us  [shift(): return lax.ppermute(x, 'group', pairs)]
  transfers between devices with their start and end apart: 42 -> 45, of which waited for: 21 -> 19; matrix products, arithmetic and copies ran while one was open for 3% -> 2% of each run, Pallas kernels for 27% -> 26%
where the time goes in v5:
time: 310 us; the launch traced here: 309 us
  waiting for transfers between devices  148 us (48%)
  Pallas kernels  98.8 us (32%)
  starting transfers between devices  35.5 us (11%)
  local copies, waits for them, and re-layouts  18.2 us (6%)
  other arithmetic  7.56 us (2%)
    ppermute x32, waiting for transfers between devices, shift(): return lax.ppermute(x, 'group', pairs)  126 us
    pallas_call x2, Pallas kernels, make_attention(): pl.pallas_call(functools.partial(attention_kernel, lay, spans, most, per_...  28.5 us
    pallas_call x2, Pallas kernels, make_q(): pl.pallas_call(functools.partial(q_kernel, sides), grid_spec=pltpu.Prefet...  22.6 us
    ppermute x13, waiting for transfers between devices, local(): cross = lambda x: lax.ppermute(x, 'tensor', swap)  21.9 us
    ppermute x32, starting transfers between devices, shift(): return lax.ppermute(x, 'group', pairs)  21.6 us
    pallas_call x3, Pallas kernels, make_projection(): pl.pallas_call(functools.partial(project_kernel, len(attended), len(follo...  20.7 us
    pallas_call x2, Pallas kernels, make_kv(): pl.pallas_call(functools.partial(kv_kernel, sides, blocks), grid_spec=plt...  17.2 us
    ppermute x13, starting transfers between devices, local(): cross = lambda x: lax.ppermute(x, 'tensor', swap)  13.9 us
  transfers between devices with their start and end apart: 45, of which 19 were waited for; matrix products, arithmetic and copies ran while one was open for 2% of the time, Pallas kernels for 26%

profile of v5, /device:TPU:0, one launch (start us, length us, event | category | flops | bytes accessed | tf_op | source)
XLA Modules:
  0.0 309.4 jit_solution(6490748630124224440)
XLA Ops:
  0.7 2.7 dynamic-slice_bitcast_fusion
  4.0 2.7 collective-permute-start.2
  6.7 1.6 collective-permute-start.1
  8.3 1.5 collective-permute-start.3
  11.2 5.6 %collective-permute-done.2.refs_3_ = bf16[64,2560]{1,0:T(8,128)(2,1)S(1)} collective-permute-done((bf16[64,2560]{1,0:T(8,128)(2,1)S(1)}, bf16[64,2560]{1,0:T(8,128)(2,1)S(1)}, u32[]{:S(2)}, u32[]{:S(2)}) %collective-permute-start.2) | collective-permute-done | bytes 327712 | tf_op jit(solution)/shard_map/ppermute | solution.py:503
  16.8 7.3 %collective-permute-done.1.refs_2_ = bf16[64,2560]{1,0:T(8,128)(2,1)S(1)} collective-permute-done((bf16[64,2560]{1,0:T(8,128)(2,1)S(1)}, bf16[64,2560]{1,0:T(8,128)(2,1)S(1)}, u32[]{:S(2)}, u32[]{:S(2)}) %collective-permute-start.1) | collective-permute-done | bytes 327712 | tf_op jit(solution)/shard_map/ppermute | solution.py:503
  25.5 2.2 collective-permute-start.5
  27.7 1.5 collective-permute-start.7
  29.8 12.3 %collective-permute-done.5.refs_0_.refs_4_ = bf16[128,2560]{1,0:T(8,128)(2,1)S(1)} collective-permute-done((bf16[128,2560]{1,0:T(8,128)(2,1)S(1)}, bf16[128,2560]{1,0:T(8,128)(2,1)S(1)}, u32[]{:S(2)}, u32[]{:S(2)}) %collective-permute-start.5) | collective-permute-done | bytes 655392 | tf_op jit(solution)/shard_map/ppermute | solution.py:503
  42.0 1.3 collective-permute-start.9
  46.2 1.5 tables.1.table
  48.4 12.6 %collective-permute-done.8.refs_1_.refs_5_ = bf16[64,2560]{1,0:T(8,128)(2,1)S(1)} collective-permute-done((bf16[64,2560]{1,0:T(8,128)(2,1)}, bf16[64,2560]{1,0:T(8,128)(2,1)S(1)}, u32[]{:S(2)}, u32[]{:S(2)}) %collective-permute-start.8) | collective-permute-done | bytes 327712 | tf_op jit(solution)/shard_map/ppermute | solution.py:503
  61.9 15.4 %collective-permute-done.10.refs_2_.refs_6_ = bf16[64,2560]{1,0:T(8,128)(2,1)S(1)} collective-permute-done((bf16[64,2560]{1,0:T(8,128)(2,1)}, bf16[64,2560]{1,0:T(8,128)(2,1)S(1)}, u32[]{:S(2)}, u32[]{:S(2)}) %collective-permute-start.10) | collective-permute-done | bytes 327712 | tf_op jit(solution)/shard_map/ppermute | solution.py:503
  80.7 6.6 %collective-permute-done.11.refs_9_.refs_7_ = bf16[1,2560]{1,0:T(2,128)(2,1)S(1)} collective-permute-done((bf16[1,2560]{1,0:T(2,128)(2,1)S(1)}, bf16[1,2560]{1,0:T(2,128)(2,1)S(1)}, u32[]{:S(2)}, u32[]{:S(2)}) %collective-permute-start.11) | collective-permute-done | bytes 5152 | tf_op jit(solution)/shard_map/ppermute | solution.py:565
  91.8 8.6 %keys_values.2 = (bf16[256,2560]{1,0:T(8,128)(2,1)S(1)}, bf16[256,2560]{1,0:T(8,128)(2,1)}, bf16[2,256,512]{2,1,0:T(8,128)(2,1)S(1)}) custom-call(s32[130]{0:T(256)S(1)} %copy-done.32, bf16[64,2560]{1,0:T(8,128)(2,1)S(1)} %get-tuple-element.87.refs_0_, bf16[64,2560]{1,0:T(8,128)(2,1)S(1)} %get-tuple-element.94.refs_1_, ...), custom_call_target="tpu_custom_call" | custom-call | flops 268435456 | bytes 1572864 | tf_op jit(solution)/shard_map/keys_values/pallas_call | solution.py:176
  100.4 8.6 %keys_values.3 = (bf16[256,2560]{1,0:T(8,128)(2,1)S(1)}, bf16[256,2560]{1,0:T(8,128)(2,1)}, bf16[2,256,512]{2,1,0:T(8,128)(2,1)S(1)}) custom-call(s32[130]{0:T(256)S(1)} %copy-done.32, bf16[128,2560]{1,0:T(8,128)(2,1)S(1)} %collective-permute-done.5.refs_0_.refs_4_, bf16[64,2560]{1,0:T(8,128)(2,1)S(1)} %collective-permute-done.8.refs_1_.refs_5_, ...), custom_call_target="tpu_custom_call" | custom-call | flops 268435456 | bytes 1572864 | tf_op jit(solution)/shard_map/keys_values/pallas_call | solution.py:176
  109.2 11.3 %queries.2 = bf16[256,2048]{1,0:T(8,128)(2,1)S(1)} custom-call(s32[130]{0:T(256)S(1)} %copy-done.32, bf16[256,2560]{1,0:T(8,128)(2,1)S(1)} %get-tuple-element.46.refs_0_, bf16[256,2560]{1,0:T(8,128)(2,1)S(1)} %copy-done.4, bf16[5120,2048]{1,0:T(8,128)(2,1)} %refs_3_.3, bf16[5120,2048]{1,0:T(8,128)(2,1)} %refs_3_.3, bf16[1,128]{1,0:T(2,128)(2,1)S(1)} %bitcast.60, ...), custom_call_target="tpu_custom_call" | custom-call | flops 536870912 | bytes 2464153 | tf_op jit(solution)/shard_map/queries/pallas_call | solution.py:232
  121.5 3.5 %collective-permute-start.20 = (bf16[2,4,64,512]{3,2,1,0:T(8,128)(2,1)S(1)}, bf16[2,4,64,512]{3,2,1,0:T(8,128)(2,1)S(1)}, u32[]{:S(2)}, u32[]{:S(2)}) collective-permute-start(bf16[2,4,64,512]{3,2,1,0:T(8,128)(2,1)S(1)} %collective-permute-done.14.refs_6_), channel_id=1, source_target_pairs={{0,2},{1,3},{2,4},{3,5},{4,6},{5,7},{6,0},{7,1},{8,10},{9,11},{10,... | collective-permute-start | bytes 1572872 | tf_op jit(solution)/shard_map/ppermute | solution.py:503
  125.0 11.3 %queries.3 = bf16[256,2048]{1,0:T(8,128)(2,1)S(1)} custom-call(s32[130]{0:T(256)S(1)} %copy-done.32, bf16[256,2560]{1,0:T(8,128)(2,1)S(1)} %get-tuple-element.50.refs_0_, bf16[256,2560]{1,0:T(8,128)(2,1)S(1)} %copy-done.5, bf16[5120,2048]{1,0:T(8,128)(2,1)} %refs_3_.3, bf16[5120,2048]{1,0:T(8,128)(2,1)} %refs_3_.3, bf16[1,128]{1,0:T(2,128)(2,1)S(1)} %bitcast.61, ...), custom_call_target="tpu_custom_call" | custom-call | flops 536870912 | bytes 2464153 | tf_op jit(solution)/shard_map/queries/pallas_call | solution.py:232
  139.1 14.8 %collective-permute-done.21.refs_11_ = bf16[2,4,64,512]{3,2,1,0:T(8,128)(2,1)S(1)} collective-permute-done((bf16[2,4,64,512]{3,2,1,0:T(8,128)(2,1)S(1)}, bf16[2,4,64,512]{3,2,1,0:T(8,128)(2,1)S(1)}, u32[]{:S(2)}, u32[]{:S(2)}) %collective-permute-start.21) | collective-permute-done | bytes 524320 | tf_op jit(solution)/shard_map/ppermute | solution.py:503
  154.5 10.6 %collective-permute-done.24.refs_14_ = bf16[2,4,64,512]{3,2,1,0:T(8,128)(2,1)S(1)} collective-permute-done((bf16[2,4,64,512]{3,2,1,0:T(8,128)(2,1)S(1)}, bf16[2,4,64,512]{3,2,1,0:T(8,128)(2,1)S(1)}, u32[]{:S(2)}, u32[]{:S(2)}) %collective-permute-start.24) | collective-permute-done | bytes 524320 | tf_op jit(solution)/shard_map/ppermute | solution.py:503
  165.2 8.5 %collective-permute-done.25.refs_15_ = bf16[2,4,64,512]{3,2,1,0:T(8,128)(2,1)S(1)} collective-permute-done((bf16[2,4,64,512]{3,2,1,0:T(8,128)(2,1)S(1)}, bf16[2,4,64,512]{3,2,1,0:T(8,128)(2,1)S(1)}, u32[]{:S(2)}, u32[]{:S(2)}) %collective-permute-start.25) | collective-permute-done | bytes 524320 | tf_op jit(solution)/shard_map/ppermute | solution.py:503
  173.8 1.8 collective-permute-done.27.refs_17_
  176.4 14.3 %attention.2 = (bf16[8,64,1024]{2,1,0:T(8,128)(2,1)}, bf16[4,2,128,256]{3,2,1,0:T(8,128)(2,1)S(1)}) custom-call(s32[130]{0:T(256)S(1)} %copy-done.32, bf16[4,64,2048]{2,1,0:T(8,128)(2,1)} %bitcast.40, bf16[4,64,2048]{2,1,0:T(8,128)(2,1)} %bitcast.42, bf16[2,4,64,512]{3,2,1,0:T(8,128)(2,1)S(1)} %bitcast.46, bf16[2,4,64,512]{3,2,1,0:T(8,128)(2,1)S(1)} %bitcast.50, ...), custom_call_target="tpu_custom_call" | custom-call | flops 236223200 | bytes 1258291 | tf_op jit(solution)/shard_map/attention/pallas_call | solution.py:338
  191.5 14.2 %attention.3 = (bf16[8,64,1024]{2,1,0:T(8,128)(2,1)}, bf16[4,2,128,256]{3,2,1,0:T(8,128)(2,1)}) custom-call(s32[130]{0:T(256)S(1)} %copy-done.32, bf16[4,64,2048]{2,1,0:T(8,128)(2,1)} %bitcast.41, bf16[4,64,2048]{2,1,0:T(8,128)(2,1)} %bitcast.43, bf16[2,4,64,512]{3,2,1,0:T(8,128)(2,1)S(1)} %bitcast.47, bf16[2,4,64,512]{3,2,1,0:T(8,128)(2,1)S(1)} %bitcast.51, ...), custom_call_target="tpu_custom_call" | custom-call | flops 236223200 | bytes 1258291 | tf_op jit(solution)/shard_map/attention/pallas_call | solution.py:338
  206.9 5.0 %send_part.2.refs_3_ = bf16[512,1024]{1,0:T(8,128)(2,1)S(1)} custom-call(s32[130]{0:T(256)S(1)} %copy-done.32, bf16[512,1024]{1,0:T(8,128)(2,1)S(1)} %bitcast.34, bf16[512,1024]{1,0:T(8,128)(2,1)S(1)} %bitcast.37, bf16[2048,5120]{1,0:T(8,128)(2,1)} %refs_2_.9, bf16[4,2,128,256]{3,2,1,0:T(8,128)(2,1)S(1)} %collective-permute-done.28.refs_3_), custom_call_target="tpu_custom_call" | custom-call | flops 214748368 | bytes 734003 | tf_op jit(solution)/shard_map/send_part/pallas_call | solution.py:388
  211.9 1.4 collective-permute-start.29
  213.3 6.4 %send_part.3 = (bf16[512,1024]{1,0:T(8,128)(2,1)S(1)}, bf16[512,512]{1,0:T(8,128)(2,1)S(1)}) custom-call(s32[130]{0:T(256)S(1)} %copy-done.32, bf16[512,1024]{1,0:T(8,128)(2,1)S(1)} %bitcast.35, bf16[512,1024]{1,0:T(8,128)(2,1)S(1)} %bitcast.38, bf16[2048,5120]{1,0:T(8,128)(2,1)} %refs_2_.9, bf16[512,1024]{1,0:T(8,128)(2,1)S(1)} %send_part.2.refs_3_), custom_call_target="tpu_custom_call" | custom-call | flops 322122560 | bytes 996147 | tf_op jit(solution)/shard_map/send_part/pallas_call | solution.py:388
  219.7 9.3 %own_part.1 = (bf16[512,1024]{1,0:T(8,128)(2,1)S(1)}, bf16[512,1024]{1,0:T(8,128)(2,1)S(1)}, bf16[512,512]{1,0:T(8,128)(2,1)S(1)}) custom-call(s32[130]{0:T(256)S(1)} %copy-done.32, bf16[512,1024]{1,0:T(8,128)(2,1)S(1)} %bitcast.36, bf16[512,1024]{1,0:T(8,128)(2,1)S(1)} %bitcast.39, bf16[2048,5120]{1,0:T(8,128)(2,1)} %refs_2_.9, ...), custom_call_target="tpu_custom_call" | custom-call | flops 536870912 | bytes 1520435 | tf_op jit(solution)/shard_map/own_part/pallas_call | solution.py:388
  229.0 7.8 %collective-permute-done.29 = bf16[512,1024]{1,0:T(8,128)(2,1)S(1)} collective-permute-done((bf16[512,1024]{1,0:T(8,128)(2,1)S(1)}, bf16[512,1024]{1,0:T(8,128)(2,1)S(1)}, u32[]{:S(2)}, u32[]{:S(2)}) %collective-permute-start.29) | collective-permute-done | bytes 1048608 | tf_op jit(solution)/shard_map/ppermute | solution.py:565
  236.9 1.3 collective-permute-start.30
  239.4 3.8 %collective-permute-start.32 = (bf16[2,64,1024]{2,1,0:T(8,128)(2,1)S(1)}, bf16[2,64,1024]{2,1,0:T(8,128)(2,1)S(1)}, u32[]{:S(2)}, u32[]{:S(2)}) collective-permute-start(bf16[2,64,1024]{2,1,0:T(8,128)(2,1)S(1)} %get-tuple-element.67), channel_id=1, source_target_pairs={{0,6},{1,7},{2,0},{3,1},{4,2},{5,3},{6,4},{7,5},{8,14},{9,15},{10,... | collective-permute-start | bytes 786440 | tf_op jit(solution)/shard_map/ppermute | solution.py:503
  243.2 7.2 %collective-permute-done.31.refs_1_ = bf16[2,64,1024]{2,1,0:T(8,128)(2,1)S(1)} collective-permute-done((bf16[2,64,1024]{2,1,0:T(8,128)(2,1)S(1)}, bf16[2,64,1024]{2,1,0:T(8,128)(2,1)S(1)}, u32[]{:S(2)}, u32[]{:S(2)}) %collective-permute-start.31) | collective-permute-done | bytes 262176 | tf_op jit(solution)/shard_map/ppermute | solution.py:503
  250.5 3.8 %collective-permute-done.32.refs_2_ = bf16[2,64,1024]{2,1,0:T(8,128)(2,1)S(1)} collective-permute-done((bf16[2,64,1024]{2,1,0:T(8,128)(2,1)S(1)}, bf16[2,64,1024]{2,1,0:T(8,128)(2,1)S(1)}, u32[]{:S(2)}, u32[]{:S(2)}) %collective-permute-start.32) | collective-permute-done | bytes 262176 | tf_op jit(solution)/shard_map/ppermute | solution.py:503
  254.3 7.9 %collective-permute-done.33.refs_3_ = bf16[2,64,1024]{2,1,0:T(8,128)(2,1)S(1)} collective-permute-done((bf16[2,64,1024]{2,1,0:T(8,128)(2,1)S(1)}, bf16[2,64,1024]{2,1,0:T(8,128)(2,1)S(1)}, u32[]{:S(2)}, u32[]{:S(2)}) %collective-permute-start.33) | collective-permute-done | bytes 262176 | tf_op jit(solution)/shard_map/ppermute | solution.py:503
  264.3 3.8 %collective-permute-start.40 = (bf16[2,64,1024]{2,1,0:T(8,128)(2,1)S(1)}, bf16[2,64,1024]{2,1,0:T(8,128)(2,1)S(1)}, u32[]{:S(2)}, u32[]{:S(2)}) collective-permute-start(bf16[2,64,1024]{2,1,0:T(8,128)(2,1)S(1)} %get-tuple-element.76), channel_id=1, source_target_pairs={{0,6},{1,7},{2,0},{3,1},{4,2},{5,3},{6,4},{7,5},{8,14},{9,15},{10,... | collective-permute-start | bytes 786440 | tf_op jit(solution)/shard_map/ppermute | solution.py:503
  268.2 5.3 %collective-permute-done.34 = bf16[512,512]{1,0:T(8,128)(2,1)S(1)} collective-permute-done((bf16[512,512]{1,0:T(8,128)(2,1)S(1)}, bf16[512,512]{1,0:T(8,128)(2,1)S(1)}, u32[]{:S(2)}, u32[]{:S(2)}) %collective-permute-start.34) | collective-permute-done | bytes 524320 | tf_op jit(solution)/shard_map/ppermute | solution.py:565
  273.5 1.5 residual.4
  277.4 12.8 %collective-permute-done.41.refs_3_ = bf16[2,64,1024]{2,1,0:T(8,128)(2,1)S(1)} collective-permute-done((bf16[2,64,1024]{2,1,0:T(8,128)(2,1)S(1)}, bf16[2,64,1024]{2,1,0:T(8,128)(2,1)S(1)}, u32[]{:S(2)}, u32[]{:S(2)}) %collective-permute-start.41) | collective-permute-done | bytes 262176 | tf_op jit(solution)/shard_map/ppermute | solution.py:503
  291.8 1.3 collective-permute-start.44
  294.0 3.6 %collective-permute-done.36.refs_2_ = bf16[2,64,512]{2,1,0:T(8,128)(2,1)S(1)} collective-permute-done((bf16[2,64,512]{2,1,0:T(8,128)(2,1)}, bf16[2,64,512]{2,1,0:T(8,128)(2,1)S(1)}, u32[]{:S(2)}, u32[]{:S(2)}) %collective-permute-start.36) | collective-permute-done | bytes 131104 | tf_op jit(solution)/shard_map/ppermute | solution.py:503
  297.6 1.7 collective-permute-done.37.refs_3_
  299.6 1.6 placed.3.refs_5_
  301.3 1.6 placed.4.refs_5_
  302.9 1.4 placed.5
  304.3 2.2 collective-permute-done.44
  306.5 1.3 broadcast_select_fusion.2
  307.8 1.6 pad_maximum_fusion
  (177 shorter events, 32.1 us)
Async XLA Ops:
  3.4 57.8 %copy-start.42 = (bf16[2560]{0:T(1024)(128)(2,1)S(1)}, bf16[2560]{0:T(1024)(128)(2,1)}, u32[]{:S(2)}) copy-start(bf16[2560]{0:T(1024)(128)(2,1)} %param.13) | copy-start | bytes 15364
  3.5 6.3 %collective-permute-start = (bf16[3,64,2560]{2,1,0:T(8,128)(2,1)S(1)}, bf16[3,64,2560]{2,1,0:T(8,128)(2,1)S(1)}, u32[]{:S(2)}, u32[]{:S(2)}) collective-permute-start(bf16[3,64,2560]{2,1,0:T(8,128)(2,1)S(1)} %pad_maximum_fusion.1), channel_id=1, source_target_pairs={{0,1},{1,0},{2,3},{3,2},{4,5},{5,4},{6,7},{7,6},{8,9},{9,8},{10,11... | collective-permute-start | bytes 2949128 | tf_op jit(solution)/shard_map/ppermute | solution.py:503
  4.0 12.7 %collective-permute-start.2 = (bf16[64,2560]{1,0:T(8,128)(2,1)S(1)}, bf16[64,2560]{1,0:T(8,128)(2,1)S(1)}, u32[]{:S(2)}, u32[]{:S(2)}) collective-permute-start(bf16[64,2560]{1,0:T(8,128)(2,1)S(1)} %get-tuple-element.82), channel_id=1, source_target_pairs={{0,3},{1,2},{2,5},{3,4},{4,7},{5,6},{6,1},{7,0},{8,11},{9,10},{10,... | collective-permute-start | bytes 983048 | tf_op jit(solution)/shard_map/ppermute | solution.py:503
  6.7 17.3 %collective-permute-start.1 = (bf16[64,2560]{1,0:T(8,128)(2,1)S(1)}, bf16[64,2560]{1,0:T(8,128)(2,1)S(1)}, u32[]{:S(2)}, u32[]{:S(2)}) collective-permute-start(bf16[64,2560]{1,0:T(8,128)(2,1)S(1)} %get-tuple-element.83), channel_id=1, source_target_pairs={{0,2},{1,3},{2,4},{3,5},{4,6},{5,7},{6,0},{7,1},{8,10},{9,11},{10,... | collective-permute-start | bytes 983048 | tf_op jit(solution)/shard_map/ppermute | solution.py:503
  8.3 78.9 %copy-start.34 = (bf16[128]{0:T(256)(128)(2,1)S(1)}, bf16[128]{0:T(256)(128)(2,1)}, u32[]{:S(2)}) copy-start(bf16[128]{0:T(256)(128)(2,1)} %param.18) | copy-start | bytes 772
  8.3 15.7 %collective-permute-start.3 = (bf16[64,2560]{1,0:T(8,128)(2,1)S(1)}, bf16[64,2560]{1,0:T(8,128)(2,1)S(1)}, u32[]{:S(2)}, u32[]{:S(2)}) collective-permute-start(bf16[64,2560]{1,0:T(8,128)(2,1)S(1)} %get-tuple-element.87.refs_0_), channel_id=1, source_target_pairs={{0,8},{8,0},{1,9},{9,1},{2,10},{10,2},{3,11},{11,3},{4,12},{12,4},... | collective-permute-start | bytes 983048 | tf_op jit(solution)/shard_map/ppermute | solution.py:565
  10.6 14.2 %collective-permute-start.4 = (bf16[64,2560]{1,0:T(8,128)(2,1)S(1)}, bf16[64,2560]{1,0:T(8,128)(2,1)S(1)}, u32[]{:S(2)}, u32[]{:S(2)}) collective-permute-start(bf16[64,2560]{1,0:T(8,128)(2,1)S(1)} %get-tuple-element.94.refs_1_), channel_id=1, source_target_pairs={{0,8},{8,0},{1,9},{9,1},{2,10},{10,2},{3,11},{11,3},{4,12},{12,4},... | collective-permute-start | bytes 983048 | tf_op jit(solution)/shard_map/ppermute | solution.py:565
  25.5 16.5 %collective-permute-start.5 = (bf16[128,2560]{1,0:T(8,128)(2,1)S(1)}, bf16[128,2560]{1,0:T(8,128)(2,1)S(1)}, u32[]{:S(2)}, u32[]{:S(2)}) collective-permute-start(bf16[128,2560]{1,0:T(8,128)(2,1)S(1)} %pad_maximum_fusion.2), channel_id=1, source_target_pairs={{0,6},{1,7},{2,0},{3,1},{4,2},{5,3},{6,4},{7,5},{8,14},{9,15},{10,... | collective-permute-start | bytes 1966088 | tf_op jit(solution)/shard_map/ppermute | solution.py:503
  27.7 15.6 %collective-permute-start.7 = (bf16[64,2560]{1,0:T(8,128)(2,1)S(1)}, bf16[64,2560]{1,0:T(8,128)(2,1)S(1)}, u32[]{:S(2)}, u32[]{:S(2)}) collective-permute-start(bf16[64,2560]{1,0:T(8,128)(2,1)S(1)} %collective-permute-done.2.refs_3_), channel_id=1, source_target_pairs={{0,8},{8,0},{1,9},{9,1},{2,10},{10,2},{3,11},{11,3},{4,12},{12,4},... | collective-permute-start | bytes 983048 | tf_op jit(solution)/shard_map/ppermute | solution.py:565
  29.2 14.9 %collective-permute-start.6 = (bf16[64,2560]{1,0:T(8,128)(2,1)S(1)}, bf16[64,2560]{1,0:T(8,128)(2,1)S(1)}, u32[]{:S(2)}, u32[]{:S(2)}) collective-permute-start(bf16[64,2560]{1,0:T(8,128)(2,1)S(1)} %collective-permute-done.1.refs_2_), channel_id=1, source_target_pairs={{0,8},{8,0},{1,9},{9,1},{2,10},{10,2},{3,11},{11,3},{4,12},{12,4},... | collective-permute-start | bytes 983048 | tf_op jit(solution)/shard_map/ppermute | solution.py:565
  42.0 19.0 %collective-permute-start.9 = (bf16[128,2560]{1,0:T(8,128)(2,1)S(1)}, bf16[128,2560]{1,0:T(8,128)(2,1)S(1)}, u32[]{:S(2)}, u32[]{:S(2)}) collective-permute-start(bf16[128,2560]{1,0:T(8,128)(2,1)S(1)} %collective-permute-done.5.refs_0_.refs_4_), channel_id=1, source_target_pairs={{0,8},{8,0},{1,9},{9,1},{2,10},{10,2},{3,11},{11,3},{4,12},{12,4},... | collective-permute-start | bytes 1966088 | tf_op jit(solution)/shard_map/ppermute | solution.py:565
  44.8 16.2 %collective-permute-start.8 = (bf16[64,2560]{1,0:T(8,128)(2,1)}, bf16[64,2560]{1,0:T(8,128)(2,1)S(1)}, u32[]{:S(2)}, u32[]{:S(2)}) collective-permute-start(bf16[64,2560]{1,0:T(8,128)(2,1)} %get-tuple-element.42), channel_id=1, source_target_pairs={{0,4},{1,5},{2,6},{3,7},{4,0},{5,1},{6,2},{7,3},{8,12},{9,13},{10,... | collective-permute-start | bytes 983048 | tf_op jit(solution)/shard_map/ppermute | solution.py:503
  61.1 16.3 %collective-permute-start.10 = (bf16[64,2560]{1,0:T(8,128)(2,1)}, bf16[64,2560]{1,0:T(8,128)(2,1)S(1)}, u32[]{:S(2)}, u32[]{:S(2)}) collective-permute-start(bf16[64,2560]{1,0:T(8,128)(2,1)} %get-tuple-element.43), channel_id=1, source_target_pairs={{0,4},{1,5},{2,6},{3,7},{4,0},{5,1},{6,2},{7,3},{8,12},{9,13},{10,... | collective-permute-start | bytes 983048 | tf_op jit(solution)/shard_map/ppermute | solution.py:503
  61.2 39.1 %collective-permute-start.12 = (bf16[64,2560]{1,0:T(8,128)(2,1)S(1)}, bf16[64,2560]{1,0:T(8,128)(2,1)S(1)}, u32[]{:S(2)}, u32[]{:S(2)}) collective-permute-start(bf16[64,2560]{1,0:T(8,128)(2,1)S(1)} %collective-permute-done.8.refs_1_.refs_5_), channel_id=1, source_target_pairs={{0,8},{8,0},{1,9},{9,1},{2,10},{10,2},{3,11},{11,3},{4,12},{12,4},... | collective-permute-start | bytes 983048 | tf_op jit(solution)/shard_map/ppermute | solution.py:565
  77.4 23.0 %collective-permute-start.13 = (bf16[64,2560]{1,0:T(8,128)(2,1)S(1)}, bf16[64,2560]{1,0:T(8,128)(2,1)S(1)}, u32[]{:S(2)}, u32[]{:S(2)}) collective-permute-start(bf16[64,2560]{1,0:T(8,128)(2,1)S(1)} %collective-permute-done.10.refs_2_.refs_6_), channel_id=1, source_target_pairs={{0,8},{8,0},{1,9},{9,1},{2,10},{10,2},{3,11},{11,3},{4,12},{12,4},... | collective-permute-start | bytes 983048 | tf_op jit(solution)/shard_map/ppermute | solution.py:565
  79.3 7.9 %collective-permute-start.11 = (bf16[1,2560]{1,0:T(2,128)(2,1)S(1)}, bf16[1,2560]{1,0:T(2,128)(2,1)S(1)}, u32[]{:S(2)}, u32[]{:S(2)}) collective-permute-start(bf16[1,2560]{1,0:T(2,128)(2,1)S(1)} %broadcast_in_dim.6.refs_8_.refs_6_), channel_id=1, source_target_pairs={{0,8},{8,0},{1,9},{9,1},{2,10},{10,2},{3,11},{11,3},{4,12},{12,4},... | collective-permute-start | bytes 15368 | tf_op jit(solution)/shard_map/ppermute | solution.py:565
  100.4 21.1 %collective-permute-start.14 = (bf16[2,4,64,512]{3,2,1,0:T(8,128)(2,1)S(1)}, bf16[2,4,64,512]{3,2,1,0:T(8,128)(2,1)S(1)}, u32[]{:S(2)}, u32[]{:S(2)}) collective-permute-start(bf16[2,4,64,512]{3,2,1,0:T(8,128)(2,1)S(1)} %bitcast.44), channel_id=1, source_target_pairs={{0,2},{1,3},{2,4},{3,5},{4,6},{5,7},{6,0},{7,1},{8,10},{9,11},{10,... | collective-permute-start | bytes 1572872 | tf_op jit(solution)/shard_map/ppermute | solution.py:503
  109.0 28.3 %collective-permute-start.17 = (bf16[2,4,64,512]{3,2,1,0:T(8,128)(2,1)S(1)}, bf16[2,4,64,512]{3,2,1,0:T(8,128)(2,1)S(1)}, u32[]{:S(2)}, u32[]{:S(2)}) collective-permute-start(bf16[2,4,64,512]{3,2,1,0:T(8,128)(2,1)S(1)} %bitcast.48), channel_id=1, source_target_pairs={{0,2},{1,3},{2,4},{3,5},{4,6},{5,7},{6,0},{7,1},{8,10},{9,11},{10,... | collective-permute-start | bytes 1572872 | tf_op jit(solution)/shard_map/ppermute | solution.py:503
  121.5 17.6 %collective-permute-start.20 = (bf16[2,4,64,512]{3,2,1,0:T(8,128)(2,1)S(1)}, bf16[2,4,64,512]{3,2,1,0:T(8,128)(2,1)S(1)}, u32[]{:S(2)}, u32[]{:S(2)}) collective-permute-start(bf16[2,4,64,512]{3,2,1,0:T(8,128)(2,1)S(1)} %collective-permute-done.14.refs_6_), channel_id=1, source_target_pairs={{0,2},{1,3},{2,4},{3,5},{4,6},{5,7},{6,0},{7,1},{8,10},{9,11},{10,... | collective-permute-start | bytes 1572872 | tf_op jit(solution)/shard_map/ppermute | solution.py:503
  137.3 16.7 %collective-permute-start.21 = (bf16[2,4,64,512]{3,2,1,0:T(8,128)(2,1)S(1)}, bf16[2,4,64,512]{3,2,1,0:T(8,128)(2,1)S(1)}, u32[]{:S(2)}, u32[]{:S(2)}) collective-permute-start(bf16[2,4,64,512]{3,2,1,0:T(8,128)(2,1)S(1)} %collective-permute-done.17.refs_7_), channel_id=1, source_target_pairs={{0,2},{1,3},{2,4},{3,5},{4,6},{5,7},{6,0},{7,1},{8,10},{9,11},{10,... | collective-permute-start | bytes 1572872 | tf_op jit(solution)/shard_map/ppermute | solution.py:503
  138.5 15.4 %collective-permute-start.15 = (bf16[2,4,64,512]{3,2,1,0:T(8,128)(2,1)S(1)}, bf16[2,4,64,512]{3,2,1,0:T(8,128)(2,1)S(1)}, u32[]{:S(2)}, u32[]{:S(2)}) collective-permute-start(bf16[2,4,64,512]{3,2,1,0:T(8,128)(2,1)S(1)} %bitcast.45), channel_id=1, source_target_pairs={{0,1},{1,0},{2,3},{3,2},{4,5},{5,4},{6,7},{7,6},{8,9},{9,8},{10,11... | collective-permute-start | bytes 1572872 | tf_op jit(solution)/shard_map/ppermute | solution.py:503
  138.5 15.4 %collective-permute-start.16 = (bf16[2,4,64,512]{3,2,1,0:T(8,128)(2,1)S(1)}, bf16[2,4,64,512]{3,2,1,0:T(8,128)(2,1)S(1)}, u32[]{:S(2)}, u32[]{:S(2)}) collective-permute-start(bf16[2,4,64,512]{3,2,1,0:T(8,128)(2,1)S(1)} %bitcast.49), channel_id=1, source_target_pairs={{0,1},{1,0},{2,3},{3,2},{4,5},{5,4},{6,7},{7,6},{8,9},{9,8},{10,11... | collective-permute-start | bytes 1572872 | tf_op jit(solution)/shard_map/ppermute | solution.py:503
  139.0 15.4 %collective-permute-start.18 = (bf16[2,4,64,512]{3,2,1,0:T(8,128)(2,1)S(1)}, bf16[2,4,64,512]{3,2,1,0:T(8,128)(2,1)S(1)}, u32[]{:S(2)}, u32[]{:S(2)}) collective-permute-start(bf16[2,4,64,512]{3,2,1,0:T(8,128)(2,1)S(1)} %collective-permute-done.14.refs_6_), channel_id=1, source_target_pairs={{0,1},{1,0},{2,3},{3,2},{4,5},{5,4},{6,7},{7,6},{8,9},{9,8},{10,11... | collective-permute-start | bytes 1572872 | tf_op jit(solution)/shard_map/ppermute | solution.py:503
  139.0 26.1 %collective-permute-start.24 = (bf16[2,4,64,512]{3,2,1,0:T(8,128)(2,1)S(1)}, bf16[2,4,64,512]{3,2,1,0:T(8,128)(2,1)S(1)}, u32[]{:S(2)}, u32[]{:S(2)}) collective-permute-start(bf16[2,4,64,512]{3,2,1,0:T(8,128)(2,1)S(1)} %collective-permute-done.20.refs_10_), channel_id=1, source_target_pairs={{0,2},{1,3},{2,4},{3,5},{4,6},{5,7},{6,0},{7,1},{8,10},{9,11},{10,... | collective-permute-start | bytes 1572872 | tf_op jit(solution)/shard_map/ppermute | solution.py:503
  153.9 19.8 %collective-permute-start.25 = (bf16[2,4,64,512]{3,2,1,0:T(8,128)(2,1)S(1)}, bf16[2,4,64,512]{3,2,1,0:T(8,128)(2,1)S(1)}, u32[]{:S(2)}, u32[]{:S(2)}) collective-permute-start(bf16[2,4,64,512]{3,2,1,0:T(8,128)(2,1)S(1)} %collective-permute-done.21.refs_11_), channel_id=1, source_target_pairs={{0,2},{1,3},{2,4},{3,5},{4,6},{5,7},{6,0},{7,1},{8,10},{9,11},{10,... | collective-permute-start | bytes 1572872 | tf_op jit(solution)/shard_map/ppermute | solution.py:503
  153.9 19.8 %collective-permute-start.19 = (bf16[2,4,64,512]{3,2,1,0:T(8,128)(2,1)S(1)}, bf16[2,4,64,512]{3,2,1,0:T(8,128)(2,1)S(1)}, u32[]{:S(2)}, u32[]{:S(2)}) collective-permute-start(bf16[2,4,64,512]{3,2,1,0:T(8,128)(2,1)S(1)} %collective-permute-done.17.refs_7_), channel_id=1, source_target_pairs={{0,1},{1,0},{2,3},{3,2},{4,5},{5,4},{6,7},{7,6},{8,9},{9,8},{10,11... | collective-permute-start | bytes 1572872 | tf_op jit(solution)/shard_map/ppermute | solution.py:503
  153.9 19.8 %collective-permute-start.22 = (bf16[2,4,64,512]{3,2,1,0:T(8,128)(2,1)S(1)}, bf16[2,4,64,512]{3,2,1,0:T(8,128)(2,1)S(1)}, u32[]{:S(2)}, u32[]{:S(2)}) collective-permute-start(bf16[2,4,64,512]{3,2,1,0:T(8,128)(2,1)S(1)} %collective-permute-done.20.refs_10_), channel_id=1, source_target_pairs={{0,1},{1,0},{2,3},{3,2},{4,5},{5,4},{6,7},{7,6},{8,9},{9,8},{10,11... | collective-permute-start | bytes 1572872 | tf_op jit(solution)/shard_map/ppermute | solution.py:503
  154.4 19.3 %collective-permute-start.23 = (bf16[2,4,64,512]{3,2,1,0:T(8,128)(2,1)S(1)}, bf16[2,4,64,512]{3,2,1,0:T(8,128)(2,1)S(1)}, u32[]{:S(2)}, u32[]{:S(2)}) collective-permute-start(bf16[2,4,64,512]{3,2,1,0:T(8,128)(2,1)S(1)} %collective-permute-done.21.refs_11_), channel_id=1, source_target_pairs={{0,1},{1,0},{2,3},{3,2},{4,5},{5,4},{6,7},{7,6},{8,9},{9,8},{10,11... | collective-permute-start | bytes 1572872 | tf_op jit(solution)/shard_map/ppermute | solution.py:503
  165.2 8.6 %collective-permute-start.26 = (bf16[2,4,64,512]{3,2,1,0:T(8,128)(2,1)S(1)}, bf16[2,4,64,512]{3,2,1,0:T(8,128)(2,1)S(1)}, u32[]{:S(2)}, u32[]{:S(2)}) collective-permute-start(bf16[2,4,64,512]{3,2,1,0:T(8,128)(2,1)S(1)} %collective-permute-done.24.refs_14_), channel_id=1, source_target_pairs={{0,1},{1,0},{2,3},{3,2},{4,5},{5,4},{6,7},{7,6},{8,9},{9,8},{10,11... | collective-permute-start | bytes 1572872 | tf_op jit(solution)/shard_map/ppermute | solution.py:503
  173.7 1.9 collective-permute-start.27
  190.7 15.0 %collective-permute-start.28 = (bf16[4,2,128,256]{3,2,1,0:T(8,128)(2,1)S(1)}, bf16[4,2,128,256]{3,2,1,0:T(8,128)(2,1)S(1)}, u32[]{:S(2)}, u32[]{:S(2)}) collective-permute-start(bf16[4,2,128,256]{3,2,1,0:T(8,128)(2,1)S(1)} %get-tuple-element.58), channel_id=1, source_target_pairs={{0,8},{8,0},{1,9},{9,1},{2,10},{10,2},{3,11},{11,3},{4,12},{12,4},... | collective-permute-start | bytes 1572872 | tf_op jit(solution)/shard_map/ppermute | solution.py:565
  211.9 25.0 %collective-permute-start.29 = (bf16[512,1024]{1,0:T(8,128)(2,1)S(1)}, bf16[512,1024]{1,0:T(8,128)(2,1)S(1)}, u32[]{:S(2)}, u32[]{:S(2)}) collective-permute-start(bf16[512,1024]{1,0:T(8,128)(2,1)S(1)} %send_part.2.refs_3_), channel_id=1, source_target_pairs={{0,8},{8,0},{1,9},{9,1},{2,10},{10,2},{3,11},{11,3},{4,12},{12,4},... | collective-permute-start | bytes 3145736 | tf_op jit(solution)/shard_map/ppermute | solution.py:565
  236.9 25.3 %collective-permute-start.30 = (bf16[512,1024]{1,0:T(8,128)(2,1)S(1)}, bf16[512,1024]{1,0:T(8,128)(2,1)S(1)}, u32[]{:S(2)}, u32[]{:S(2)}) collective-permute-start(bf16[512,1024]{1,0:T(8,128)(2,1)S(1)} %get-tuple-element.64), channel_id=1, source_target_pairs={{0,8},{8,0},{1,9},{9,1},{2,10},{10,2},{3,11},{11,3},{4,12},{12,4},... | collective-permute-start | bytes 3145736 | tf_op jit(solution)/shard_map/ppermute | solution.py:565
  239.4 11.1 %collective-permute-start.31 = (bf16[2,64,1024]{2,1,0:T(8,128)(2,1)S(1)}, bf16[2,64,1024]{2,1,0:T(8,128)(2,1)S(1)}, u32[]{:S(2)}, u32[]{:S(2)}) collective-permute-start(bf16[2,64,1024]{2,1,0:T(8,128)(2,1)S(1)} %get-tuple-element.66), channel_id=1, source_target_pairs={{0,2},{1,3},{2,4},{3,5},{4,6},{5,7},{6,0},{7,1},{8,10},{9,11},{10,... | collective-permute-start | bytes 786440 | tf_op jit(solution)/shard_map/ppermute | solution.py:503
  239.4 14.8 %collective-permute-start.32 = (bf16[2,64,1024]{2,1,0:T(8,128)(2,1)S(1)}, bf16[2,64,1024]{2,1,0:T(8,128)(2,1)S(1)}, u32[]{:S(2)}, u32[]{:S(2)}) collective-permute-start(bf16[2,64,1024]{2,1,0:T(8,128)(2,1)S(1)} %get-tuple-element.67), channel_id=1, source_target_pairs={{0,6},{1,7},{2,0},{3,1},{4,2},{5,3},{6,4},{7,5},{8,14},{9,15},{10,... | collective-permute-start | bytes 786440 | tf_op jit(solution)/shard_map/ppermute | solution.py:503
  243.2 18.9 %collective-permute-start.33 = (bf16[2,64,1024]{2,1,0:T(8,128)(2,1)S(1)}, bf16[2,64,1024]{2,1,0:T(8,128)(2,1)S(1)}, u32[]{:S(2)}, u32[]{:S(2)}) collective-permute-start(bf16[2,64,1024]{2,1,0:T(8,128)(2,1)S(1)} %get-tuple-element.68), channel_id=1, source_target_pairs={{0,4},{1,5},{2,6},{3,7},{4,0},{5,1},{6,2},{7,3},{8,12},{9,13},{10,... | collective-permute-start | bytes 786440 | tf_op jit(solution)/shard_map/ppermute | solution.py:503
  262.2 11.4 %collective-permute-start.34 = (bf16[512,512]{1,0:T(8,128)(2,1)S(1)}, bf16[512,512]{1,0:T(8,128)(2,1)S(1)}, u32[]{:S(2)}, u32[]{:S(2)}) collective-permute-start(bf16[512,512]{1,0:T(8,128)(2,1)S(1)} %get-tuple-element.69.refs_3_), channel_id=1, source_target_pairs={{0,8},{8,0},{1,9},{9,1},{2,10},{10,2},{3,11},{11,3},{4,12},{12,4},... | collective-permute-start | bytes 1572872 | tf_op jit(solution)/shard_map/ppermute | solution.py:565
  264.3 11.7 %collective-permute-start.39 = (bf16[2,64,1024]{2,1,0:T(8,128)(2,1)S(1)}, bf16[2,64,1024]{2,1,0:T(8,128)(2,1)S(1)}, u32[]{:S(2)}, u32[]{:S(2)}) collective-permute-start(bf16[2,64,1024]{2,1,0:T(8,128)(2,1)S(1)} %get-tuple-element.75), channel_id=1, source_target_pairs={{0,2},{1,3},{2,4},{3,5},{4,6},{5,7},{6,0},{7,1},{8,10},{9,11},{10,... | collective-permute-start | bytes 786440 | tf_op jit(solution)/shard_map/ppermute | solution.py:503
  264.3 12.3 %collective-permute-start.40 = (bf16[2,64,1024]{2,1,0:T(8,128)(2,1)S(1)}, bf16[2,64,1024]{2,1,0:T(8,128)(2,1)S(1)}, u32[]{:S(2)}, u32[]{:S(2)}) collective-permute-start(bf16[2,64,1024]{2,1,0:T(8,128)(2,1)S(1)} %get-tuple-element.76), channel_id=1, source_target_pairs={{0,6},{1,7},{2,0},{3,1},{4,2},{5,3},{6,4},{7,5},{8,14},{9,15},{10,... | collective-permute-start | bytes 786440 | tf_op jit(solution)/shard_map/ppermute | solution.py:503
  268.1 22.1 %collective-permute-start.41 = (bf16[2,64,1024]{2,1,0:T(8,128)(2,1)S(1)}, bf16[2,64,1024]{2,1,0:T(8,128)(2,1)S(1)}, u32[]{:S(2)}, u32[]{:S(2)}) collective-permute-start(bf16[2,64,1024]{2,1,0:T(8,128)(2,1)S(1)} %get-tuple-element.77), channel_id=1, source_target_pairs={{0,4},{1,5},{2,6},{3,7},{4,0},{5,1},{6,2},{7,3},{8,12},{9,13},{10,... | collective-permute-start | bytes 786440 | tf_op jit(solution)/shard_map/ppermute | solution.py:503
  275.0 24.5 %copy-start.21 = (bf16[4,2,128,256]{3,2,1,0:T(8,128)(2,1)S(1)}, bf16[4,2,128,256]{3,2,1,0:T(8,128)(2,1)}, u32[]{:S(2)}) copy-start(bf16[4,2,128,256]{3,2,1,0:T(8,128)(2,1)} %copy-done.20) | copy-start | bytes 1572868
  275.0 16.8 %collective-permute-start.35 = (bf16[2,64,512]{2,1,0:T(8,128)(2,1)S(1)}, bf16[2,64,512]{2,1,0:T(8,128)(2,1)S(1)}, u32[]{:S(2)}, u32[]{:S(2)}) collective-permute-start(bf16[2,64,512]{2,1,0:T(8,128)(2,1)S(1)} %get-tuple-element.71), channel_id=1, source_target_pairs={{0,2},{1,3},{2,4},{3,5},{4,6},{5,7},{6,0},{7,1},{8,10},{9,11},{10,... | collective-permute-start | bytes 393224 | tf_op jit(solution)/shard_map/ppermute | solution.py:503
  275.9 23.7 %collective-permute-start.43 = (bf16[4,64,1024]{2,1,0:T(8,128)(2,1)}, bf16[4,64,1024]{2,1,0:T(8,128)(2,1)S(1)}, u32[]{:S(2)}, u32[]{:S(2)}) collective-permute-start(bf16[4,64,1024]{2,1,0:T(8,128)(2,1)} %pad_maximum_fusion.4), channel_id=1, source_target_pairs={{0,1},{1,0},{2,3},{3,2},{4,5},{5,4},{6,7},{7,6},{8,9},{9,8},{10,11... | collective-permute-start | bytes 1572872 | tf_op jit(solution)/shard_map/ppermute | solution.py:503
  290.9 6.6 %collective-permute-start.36 = (bf16[2,64,512]{2,1,0:T(8,128)(2,1)}, bf16[2,64,512]{2,1,0:T(8,128)(2,1)S(1)}, u32[]{:S(2)}, u32[]{:S(2)}) collective-permute-start(bf16[2,64,512]{2,1,0:T(8,128)(2,1)} %get-tuple-element.72), channel_id=1, source_target_pairs={{0,6},{1,7},{2,0},{3,1},{4,2},{5,3},{6,4},{7,5},{8,14},{9,15},{10,... | collective-permute-start | bytes 393224 | tf_op jit(solution)/shard_map/ppermute | solution.py:503
  291.0 8.4 %collective-permute-start.37 = (bf16[2,64,512]{2,1,0:T(8,128)(2,1)}, bf16[2,64,512]{2,1,0:T(8,128)(2,1)S(1)}, u32[]{:S(2)}, u32[]{:S(2)}) collective-permute-start(bf16[2,64,512]{2,1,0:T(8,128)(2,1)} %get-tuple-element.73), channel_id=1, source_target_pairs={{0,4},{1,5},{2,6},{3,7},{4,0},{5,1},{6,2},{7,3},{8,12},{9,13},{10,... | collective-permute-start | bytes 393224 | tf_op jit(solution)/shard_map/ppermute | solution.py:503
  291.8 9.4 %collective-permute-start.42 = (bf16[4,64,1024]{2,1,0:T(8,128)(2,1)}, bf16[4,64,1024]{2,1,0:T(8,128)(2,1)S(1)}, u32[]{:S(2)}, u32[]{:S(2)}) collective-permute-start(bf16[4,64,1024]{2,1,0:T(8,128)(2,1)} %pad_maximum_fusion.3), channel_id=1, source_target_pairs={{0,1},{1,0},{2,3},{3,2},{4,5},{5,4},{6,7},{7,6},{8,9},{9,8},{10,11... | collective-permute-start | bytes 1572872 | tf_op jit(solution)/shard_map/ppermute | solution.py:503
  291.8 14.7 %collective-permute-start.44 = (bf16[4,2,128,256]{3,2,1,0:T(8,128)(2,1)}, bf16[4,2,128,256]{3,2,1,0:T(8,128)(2,1)}, u32[]{:S(2)}, u32[]{:S(2)}) collective-permute-start(bf16[4,2,128,256]{3,2,1,0:T(8,128)(2,1)} %get-tuple-element.79), channel_id=1, source_target_pairs={{0,8},{8,0},{1,9},{9,1},{2,10},{10,2},{3,11},{11,3},{4,12},{12,4},... | collective-permute-start | bytes 1572872 | tf_op jit(solution)/shard_map/ppermute | solution.py:565
  299.4 3.5 %collective-permute-start.38 = (bf16[4,64,512]{2,1,0:T(8,128)(2,1)S(1)}, bf16[4,64,512]{2,1,0:T(8,128)(2,1)S(1)}, u32[]{:S(2)}, u32[]{:S(2)}) collective-permute-start(bf16[4,64,512]{2,1,0:T(8,128)(2,1)S(1)} %pad_maximum_fusion.7), channel_id=1, source_target_pairs={{0,1},{1,0},{2,3},{3,2},{4,5},{5,4},{6,7},{7,6},{8,9},{9,8},{10,11... | collective-permute-start | bytes 786440 | tf_op jit(solution)/shard_map/ppermute | solution.py:503
  (43 other events, 283.9 us)

commit v6 on v5

--- a/solution.py
+++ b/solution.py
@@ -12,14 +12,13 @@
 epsilon = 1e-06
 rope_base = 1000000.0
 very_negative = -1e30
-VMEM_BYTES = 48 * 1024 * 1024
 PARTS = 2
 CORES = 2
 SHARE = 0.1
 
 
-def params():
-    return pltpu.CompilerParams(vmem_limit_bytes=VMEM_BYTES)
+def params(mebibytes):
+    return pltpu.CompilerParams(vmem_limit_bytes=mebibytes * 1024 * 1024)
 
 
 def cost(flops, moved, transcendentals=0):
@@ -192,7 +191,7 @@
         ),
         out_shape=[jax.ShapeDtypeStruct((rows, w), jnp.bfloat16) for w in widths]
         + [jax.ShapeDtypeStruct((2, rows, cols), jnp.bfloat16)],
-        compiler_params=params(),
+        compiler_params=params(32),
         cost_estimate=cost(4 * rows * width * cols, 4 * width * cols + 4 * rows * width),
         name="keys_values",
     )(
@@ -244,7 +243,7 @@
             out_specs=pl.BlockSpec((rows, tile), lambda n, t: (0, n)),
         ),
         out_shape=jax.ShapeDtypeStruct((rows, cols), jnp.bfloat16),
-        compiler_params=params(),
+        compiler_params=params(24),
         cost_estimate=cost(2 * rows * width * cols, 2 * width * cols + 2 * rows * (width + cols)),
         name="queries",
     )(table, *normed, *[wq] * sides, qgain, cosine, sine)
@@ -353,7 +352,7 @@
             jax.ShapeDtypeStruct((spans, rows, count * per_kv * head), jnp.bfloat16),
             jax.ShapeDtypeStruct((pages_each, 2, PAGE_ROWS, count * head), jnp.bfloat16),
         ],
-        compiler_params=params(),
+        compiler_params=params(20),
         cost_estimate=cost(
             4 * pairs * head, 4 * all_rows * cols + 2 * len(flat) * flat[0].size, pairs
         ),
@@ -396,7 +395,7 @@
             out_specs=[pl.BlockSpec((rows, w * tile), lambda n, t: (0, 0)) for w in widths],
         ),
         out_shape=[jax.ShapeDtypeStruct((rows, w * tile), jnp.bfloat16) for w in widths],
-        compiler_params=params(),
+        compiler_params=params(20),
         cost_estimate=cost(
             2 * rows * depth * count * tile, 2 * (rows * depth + (rows + depth) * count * tile)
         ),
@@ -436,7 +435,7 @@
             scratch_shapes=[pltpu.VMEM((spans, rows, cols), jnp.bfloat16)],
         ),
         out_shape=[jax.ShapeDtypeStruct((CORES, rows, cols), jnp.bfloat16)] * lay.chips,
-        compiler_params=params(),
+        compiler_params=params(12),
         cost_estimate=cost(3 * spans * rows * cols, 8 * spans * rows * cols),
         name="residual",
     )(table, *arrived, own, received)
@@ -469,7 +468,7 @@
         ),
         out_shape=jax.ShapeDtypeStruct((chips * CORES * rows, cols), jnp.bfloat16),
         input_output_aliases={chips + 2: 0} if whole else {},
-        compiler_params=params(),
+        compiler_params=params(12),
         cost_estimate=cost(0, 4 * chips * CORES * rows * tile),
         name="placed",
     )(table, *same, swapped, *whole)
@@ -540,9 +539,13 @@
         to = lax.rem(chip + hop, chips) * CORES + lax.rem(core + flip, CORES)
         return lax.dynamic_index_in_dim(split, to, 0, keepdims=False)
 
+    cross = lambda x: lax.ppermute(x, "tensor", swap)
+
     hops = hop_order(chips)
     paired_hops = hops[2:]
-    near = [shift(rows_for(hop, flip), owners, hop, flip) for hop in hops[1:2] for flip in range(CORES)]
+    near = [rows_for(hop, flip) for hop in hops[1:2] for flip in range(CORES)]
+    split = after(split, near)
+    near = [shift(x, owners, hops[1], flip) for flip, x in enumerate(near)]
     swapped = shift(
         jnp.stack([rows_for(hop, 1) for hop in hops[:1] + paired_hops]), owners, 0, 1
     )
@@ -562,53 +565,62 @@
     earlier = table[lay.earlier_at : lay.earlier_at + spans]
     cosine, sine = rope_tables(earlier, span_len, group_rank * rows, rows, head)
 
-    cross = lambda x: lax.ppermute(x, "tensor", swap)
     crossed = [cross(x) for x in arrived] if paired else []
     if paired:
         gain = ln_gain[None]
-        gains = [gain, cross(after(gain, crossed[1]))]
+        gains = [gain, cross(after(gain, swapped))]
     else:
         gains = [lax.all_gather(ln_gain, "tensor", axis=0, tiled=True)[None]]
-    for n, (hop, block) in enumerate(moves):
+
+    kvs, norms = [], []
+
+    def make_part(own_rows, crossed_rows, done):
         if paired:
-            landed = arrived[-1:] if n else near
-            block = after(block, (landed, crossed[2 * n : 2 * n + 2] if n < 2 else crossed[n + 2]))
-        arrived.append(shift(block, owners, hop, 0))
-        if paired:
-            crossed.append(cross(arrived[-1]))
-
-    kgain = after(key_norm_gain[None], arrived[-1])
-    kvs, norms, begun = [], [], 0
-    for n in range(1, len(arrived) + 1):
-        if sum(x.shape[0] for x in arrived[begun:n]) == here * rows:
+            xs = [own_rows, crossed_rows]
+        else:
+            xs = [[lax.all_gather(jnp.concatenate(own_rows), "tensor", axis=1, tiled=True)]]
+        kgain = after(key_norm_gain[None], done)
+        *normed, kv = make_kv(lay, table, xs, gains, wk, wv, kgain, cosine, sine, len(kvs))
+        kvs.append([kv.reshape(2, here, rows, kv.shape[2])])
+        norms.append(normed)
+
+    def one_back(p, done=()):
+        kvs[p].append(shift(after(kvs[p][-1], done) if done else kvs[p][-1], owners, 1, 0))
+
+    begun = 0
+    for n in range(len(moves) + 1):
+        if n:
+            hop, block = moves[n - 1]
             if paired:
-                xs = [arrived[begun:n], crossed[begun:n]]
-            else:
-                whole = jnp.concatenate(arrived[begun:n])
-                xs = [[lax.all_gather(whole, "tensor", axis=1, tiled=True)]]
-            *normed, kv = make_kv(
-                lay, table, xs, gains, wk, wv, kgain, cosine, sine, len(kvs)
-            )
-            kvs.append(kv.reshape(2, here, rows, kv.shape[2]))
-            norms.append(normed)
-            begun = n
-
-    queries, gathered = [], [[] for _ in range(owners)]
-    ready = kvs[-1]
+                landed = arrived[-1:] if n > 1 else near
+                matching = crossed[2 * n - 2 : 2 * n] if n < 3 else crossed[n + 1]
+                block = after(block, (landed, matching, gains))
+            arrived.append(shift(block, owners, hop, 0))
+            if paired:
+                block = arrived[-1]
+                if n == len(moves) and kvs:
+                    block = after(block, kvs[0][0])
+                crossed.append(cross(block))
+        if sum(x.shape[0] for x in arrived[begun:]) == here * rows:
+            make_part(arrived[begun:], crossed[begun:], kvs[0][1:2] if kvs else arrived[0])
+            begun = len(arrived)
+            for _ in range(min(2, chips - 1) if len(kvs) == 1 else min(1, chips - 1)):
+                one_back(len(kvs) - 1)
+
+    queries, done = [], (kvs[1][0], kvs[0][-1])
+    for p in range(PARTS):
+        made = make_q(
+            lay, table, norms[p], wq, after(q_gain[None], done), cosine, sine, p
+        )
+        queries.append(made.reshape(here, rows, made.shape[1]))
+        done = queries[-1]
+    for p in range(PARTS):
+        while len(kvs[p]) < chips:
+            one_back(p, (queries, kvs[0][-1]) if p else ())
+    gathered = []
     for back in range(chips):
-        for p in range(PARTS):
-            if back:
-                if back == min(2, chips - 1):
-                    kvs[p] = after(kvs[p], queries[p])
-                kvs[p] = shift(kvs[p], owners, 1, 0)
-            gathered[back * CORES].append(kvs[p])
-            gathered[back * CORES + 1].append(shift(kvs[p], owners, 0, 1))
-            if back == min(1, chips - 1):
-                made = make_q(
-                    lay, table, norms[p], wq, after(q_gain[None], ready), cosine, sine, p
-                )
-                queries.append(made.reshape(here, rows, made.shape[1]))
-                ready = kvs[p]
+        gathered.append([kv[back] for kv in kvs])
+        gathered.append([shift(kv[back], owners, 0, 1) for kv in kvs])
 
     own_kv = wk.shape[1] // head
     sets = [own_kv // 2, own_kv - own_kv // 2] if own_kv > 1 else [own_kv]

time: 310 us -> 341 us (1.10)
  local copies, waits for them, and re-layouts: 18.2 us -> 47.2 us
  waiting for transfers between devices: 148 us -> 166 us
  Pallas kernels: 98.8 us -> 85.3 us
  starting transfers between devices: 35.5 us -> 31.6 us
    unnamed x86 -> x88, local copies, waits for them, and re-layouts: 13.7 us -> 41.1 us
    ppermute x13, waiting for transfers between devices: 21.9 us -> 31.4 us  [local(): cross = lambda x: lax.ppermute(x, 'tensor', swap)]
    ppermute x32, waiting for transfers between devices: 126 us -> 134 us  [shift(): return lax.ppermute(x, 'group', pairs)]
    pallas_call x2, Pallas kernels: 17.2 us -> 12.4 us  [make_kv(): pl.pallas_call(functools.partial(kv_kernel, sides, blocks), grid_spec=plt...]
    ppermute x32, starting transfers between devices: 21.6 us -> 17.5 us  [shift(): return lax.ppermute(x, 'group', pairs)]
    pallas_call x3, Pallas kernels: 20.7 us -> 16.6 us  [make_projection(): pl.pallas_call(functools.partial(project_kernel, len(attended), len(follo...]
    pallas_call x2, Pallas kernels: 22.6 us -> 19.1 us  [make_q(): pl.pallas_call(functools.partial(q_kernel, sides), grid_spec=pltpu.Prefet...]
  transfers between devices with their start and end apart: 45 -> 45, of which waited for: 19 -> 22; matrix products, arithmetic and copies ran while one was open for 2% -> 2% of each run, Pallas kernels for 26% -> 20%
where the time goes in v6:
time: 341 us; the launch traced here: 340 us
  waiting for transfers between devices  166 us (49%)
  Pallas kernels  85.3 us (25%)
  local copies, waits for them, and re-layouts  47.2 us (14%)
  starting transfers between devices  31.6 us (9%)
  other arithmetic  9.36 us (3%)
    ppermute x32, waiting for transfers between devices, shift(): return lax.ppermute(x, 'group', pairs)  134 us
    unnamed x88, local copies, waits for them, and re-layouts  41.1 us
    ppermute x13, waiting for transfers between devices, local(): cross = lambda x: lax.ppermute(x, 'tensor', swap)  31.4 us
    pallas_call x2, Pallas kernels, make_attention(): pl.pallas_call(functools.partial(attention_kernel, lay, spans, most, per_...  26.4 us
    pallas_call x2, Pallas kernels, make_q(): pl.pallas_call(functools.partial(q_kernel, sides), grid_spec=pltpu.Prefet...  19.1 us
    ppermute x32, starting transfers between devices, shift(): return lax.ppermute(x, 'group', pairs)  17.5 us
    pallas_call x3, Pallas kernels, make_projection(): pl.pallas_call(functools.partial(project_kernel, len(attended), len(follo...  16.6 us
    ppermute x13, starting transfers between devices, local(): cross = lambda x: lax.ppermute(x, 'tensor', swap)  14.1 us
  transfers between devices with their start and end apart: 45, of which 22 were waited for; matrix products, arithmetic and copies ran while one was open for 2% of the time, Pallas kernels for 20%

profile of v6, /device:TPU:0, one launch (start us, length us, event | category | flops | bytes accessed | tf_op | source)
XLA Modules:
  0.0 340.3 jit_solution(11518309647793342888)
XLA Ops:
  0.7 1.9 dynamic-slice_bitcast_fusion.3
  2.7 2.3 dynamic-slice_bitcast_fusion
  6.5 2.7 collective-permute-start.2
  9.2 1.6 collective-permute-start.1
  10.8 1.5 collective-permute-start.3
  16.1 3.4 %collective-permute-done.2.refs_3_ = bf16[64,2560]{1,0:T(8,128)(2,1)S(1)} collective-permute-done((bf16[64,2560]{1,0:T(8,128)(2,1)}, bf16[64,2560]{1,0:T(8,128)(2,1)S(1)}, u32[]{:S(2)}, u32[]{:S(2)}) %collective-permute-start.2) | collective-permute-done | bytes 327712 | tf_op jit(solution)/shard_map/ppermute | solution.py:502
  19.5 7.2 %collective-permute-done.1.refs_2_ = bf16[64,2560]{1,0:T(8,128)(2,1)S(1)} collective-permute-done((bf16[64,2560]{1,0:T(8,128)(2,1)}, bf16[64,2560]{1,0:T(8,128)(2,1)S(1)}, u32[]{:S(2)}, u32[]{:S(2)}) %collective-permute-start.1) | collective-permute-done | bytes 327712 | tf_op jit(solution)/shard_map/ppermute | solution.py:502
  28.1 2.2 collective-permute-start.6
  31.0 1.5 tables.1.table
  33.4 1.5 collective-permute-start.8
  35.5 8.8 %collective-permute-done.6.refs_0_.refs_4_ = bf16[128,2560]{1,0:T(8,128)(2,1)S(1)} collective-permute-done((bf16[128,2560]{1,0:T(8,128)(2,1)}, bf16[128,2560]{1,0:T(8,128)(2,1)S(1)}, u32[]{:S(2)}, u32[]{:S(2)}) %collective-permute-start.6) | collective-permute-done | bytes 655392 | tf_op jit(solution)/shard_map/ppermute | solution.py:502
  46.7 4.4 %collective-permute-done.7.refs_6_ = bf16[64,2560]{1,0:T(8,128)(2,1)S(1)} collective-permute-done((bf16[64,2560]{1,0:T(8,128)(2,1)S(1)}, bf16[64,2560]{1,0:T(8,128)(2,1)S(1)}, u32[]{:S(2)}, u32[]{:S(2)}) %collective-permute-start.7) | collective-permute-done | bytes 327712 | tf_op jit(solution)/shard_map/ppermute | solution.py:542
  51.1 2.5 copy-done.3
  53.6 2.5 copy-done.4
  57.8 6.2 %keys_values.2 = (bf16[256,2560]{1,0:T(8,128)(2,1)S(1)}, bf16[256,2560]{1,0:T(8,128)(2,1)S(1)}, bf16[2,256,512]{2,1,0:T(8,128)(2,1)S(1)}) custom-call(s32[130]{0:T(256)S(1)} %copy-done.32, bf16[64,2560]{1,0:T(8,128)(2,1)S(1)} %get-tuple-element.91.refs_0_, bf16[64,2560]{1,0:T(8,128)(2,1)S(1)} %get-tuple-element.100.refs_1_, ...), custom_call_target="tpu_custom_call" | custom-call | flops 268435456 | bytes 1572864 | tf_op jit(solution)/shard_map/keys_values/pallas_call | solution.py:175
  67.5 27.1 %collective-permute-done.9.refs_1_.refs_5_ = bf16[64,2560]{1,0:T(8,128)(2,1)S(1)} collective-permute-done((bf16[64,2560]{1,0:T(8,128)(2,1)S(1)}, bf16[64,2560]{1,0:T(8,128)(2,1)S(1)}, u32[]{:S(2)}, u32[]{:S(2)}) %collective-permute-start.9) | collective-permute-done | bytes 327712 | tf_op jit(solution)/shard_map/ppermute | solution.py:502
  96.0 21.3 %collective-permute-done.11.refs_2_.refs_6_ = bf16[64,2560]{1,0:T(8,128)(2,1)S(1)} collective-permute-done((bf16[64,2560]{1,0:T(8,128)(2,1)S(1)}, bf16[64,2560]{1,0:T(8,128)(2,1)S(1)}, u32[]{:S(2)}, u32[]{:S(2)}) %collective-permute-start.11) | collective-permute-done | bytes 327712 | tf_op jit(solution)/shard_map/ppermute | solution.py:502
  118.7 8.1 %collective-permute-done.13.refs_5_ = bf16[64,2560]{1,0:T(8,128)(2,1)S(1)} collective-permute-done((bf16[64,2560]{1,0:T(8,128)(2,1)S(1)}, bf16[64,2560]{1,0:T(8,128)(2,1)S(1)}, u32[]{:S(2)}, u32[]{:S(2)}) %collective-permute-start.13) | collective-permute-done | bytes 327712 | tf_op jit(solution)/shard_map/ppermute | solution.py:542
  126.9 2.5 copy-done.5
  130.1 6.2 %keys_values.3 = (bf16[256,2560]{1,0:T(8,128)(2,1)S(1)}, bf16[256,2560]{1,0:T(8,128)(2,1)S(1)}, bf16[2,256,512]{2,1,0:T(8,128)(2,1)S(1)}) custom-call(s32[130]{0:T(256)S(1)} %copy-done.32, bf16[128,2560]{1,0:T(8,128)(2,1)S(1)} %collective-permute-done.6.refs_0_.refs_4_, bf16[64,2560]{1,0:T(8,128)(2,1)S(1)} %collective-permute-done.9.refs_1_.refs_5_, ...), custom_call_target="tpu_custom_call" | custom-call | flops 268435456 | bytes 1572864 | tf_op jit(solution)/shard_map/keys_values/pallas_call | solution.py:175
  138.5 7.0 %copy-done = bf16[5120,2048]{1,0:T(8,128)(2,1)S(1)} copy-done((bf16[5120,2048]{1,0:T(8,128)(2,1)S(1)}, bf16[5120,2048]{1,0:T(8,128)(2,1)}, u32[]{:S(2)}) %copy-start) | copy-done | bytes 20971544
  148.0 9.6 %queries.2 = bf16[256,2048]{1,0:T(8,128)(2,1)S(1)} custom-call(s32[130]{0:T(256)S(1)} %copy-done.33, bf16[256,2560]{1,0:T(8,128)(2,1)S(1)} %copy-done.7, bf16[256,2560]{1,0:T(8,128)(2,1)S(1)} %copy-done.9, bf16[5120,2048]{1,0:T(8,128)(2,1)S(1)} %copy-done, bf16[5120,2048]{1,0:T(8,128)(2,1)S(1)} %copy-done, bf16[1,128]{1,0:T(2,128)(2,1)S(1)} %bitcast.62, ...), custom_call_target="tpu_custom_call" | custom-call | flops 536870912 | bytes 2464153 | tf_op jit(solution)/shard_map/queries/pallas_call | solution.py:231
  157.6 7.0 %copy-done.1 = bf16[5120,2048]{1,0:T(8,128)(2,1)S(1)} copy-done((bf16[5120,2048]{1,0:T(8,128)(2,1)S(1)}, bf16[5120,2048]{1,0:T(8,128)(2,1)}, u32[]{:S(2)}) %copy-start.1) | copy-done | bytes 20971544
  164.6 9.5 %queries.3 = bf16[256,2048]{1,0:T(8,128)(2,1)S(1)} custom-call(s32[130]{0:T(256)S(1)} %copy-done.33, bf16[256,2560]{1,0:T(8,128)(2,1)S(1)} %copy-done.11, bf16[256,2560]{1,0:T(8,128)(2,1)S(1)} %copy-done.13, bf16[5120,2048]{1,0:T(8,128)(2,1)S(1)} %copy-done.1, bf16[5120,2048]{1,0:T(8,128)(2,1)S(1)} %copy-done.1, bf16[1,128]{1,0:T(2,128)(2,1)S(1)} %bitcast.63, ...), custom_call_target="tpu_custom_call" | custom-call | flops 536870912 | bytes 2464153 | tf_op jit(solution)/shard_map/queries/pallas_call | solution.py:231
  174.9 14.1 %collective-permute-done.22.refs_11_ = bf16[2,4,64,512]{3,2,1,0:T(8,128)(2,1)S(1)} collective-permute-done((bf16[2,4,64,512]{3,2,1,0:T(8,128)(2,1)S(1)}, bf16[2,4,64,512]{3,2,1,0:T(8,128)(2,1)S(1)}, u32[]{:S(2)}, u32[]{:S(2)}) %collective-permute-start.22) | collective-permute-done | bytes 524320 | tf_op jit(solution)/shard_map/ppermute | solution.py:502
  190.1 12.8 %collective-permute-done.25.refs_15_ = bf16[2,4,64,512]{3,2,1,0:T(8,128)(2,1)S(1)} collective-permute-done((bf16[2,4,64,512]{3,2,1,0:T(8,128)(2,1)S(1)}, bf16[2,4,64,512]{3,2,1,0:T(8,128)(2,1)S(1)}, u32[]{:S(2)}, u32[]{:S(2)}) %collective-permute-start.25) | collective-permute-done | bytes 524320 | tf_op jit(solution)/shard_map/ppermute | solution.py:502
  202.9 1.9 collective-permute-done.27.refs_17_
  204.8 12.9 %attention.2 = (bf16[8,64,1024]{2,1,0:T(8,128)(2,1)S(1)}, bf16[4,2,128,256]{3,2,1,0:T(8,128)(2,1)S(1)}) custom-call(s32[130]{0:T(256)S(1)} %copy-done.33, bf16[4,64,2048]{2,1,0:T(8,128)(2,1)S(1)} %bitcast.42, bf16[4,64,2048]{2,1,0:T(8,128)(2,1)S(1)} %bitcast.44, bf16[2,4,64,512]{3,2,1,0:T(8,128)(2,1)S(1)} %bitcast.48, bf16[2,4,64,512]{3,2,1,0:T(8,128)(2,1)S(1)} %bitcast.52, ...), custom_call_target="tpu_custom_call" | custom-call | flops 236223200 | bytes 1258291 | tf_op jit(solution)/shard_map/attention/pallas_call | solution.py:337
  217.7 1.6 collective-permute-start.28
  219.3 13.5 %attention.3 = (bf16[8,64,1024]{2,1,0:T(8,128)(2,1)S(1)}, bf16[4,2,128,256]{3,2,1,0:T(8,128)(2,1)}) custom-call(s32[130]{0:T(256)S(1)} %copy-done.33, bf16[4,64,2048]{2,1,0:T(8,128)(2,1)S(1)} %bitcast.43, bf16[4,64,2048]{2,1,0:T(8,128)(2,1)S(1)} %bitcast.45, bf16[2,4,64,512]{3,2,1,0:T(8,128)(2,1)S(1)} %bitcast.49, bf16[2,4,64,512]{3,2,1,0:T(8,128)(2,1)S(1)} %bitcast.53, ...), custom_call_target="tpu_custom_call" | custom-call | flops 236223200 | bytes 1258291 | tf_op jit(solution)/shard_map/attention/pallas_call | solution.py:337
  232.8 7.0 %copy-done.2 = bf16[2048,5120]{1,0:T(8,128)(2,1)S(1)} copy-done((bf16[2048,5120]{1,0:T(8,128)(2,1)S(1)}, bf16[2048,5120]{1,0:T(8,128)(2,1)}, u32[]{:S(2)}) %copy-start.2) | copy-done | bytes 20971544
  239.8 3.7 %send_part.2.refs_3_ = bf16[512,1024]{1,0:T(8,128)(2,1)S(1)} custom-call(s32[130]{0:T(256)S(1)} %copy-done.33, bf16[512,1024]{1,0:T(8,128)(2,1)S(1)} %bitcast.36, bf16[512,1024]{1,0:T(8,128)(2,1)S(1)} %bitcast.39, bf16[2048,5120]{1,0:T(8,128)(2,1)S(1)} %copy-done.2, bf16[4,2,128,256]{3,2,1,0:T(8,128)(2,1)S(1)} %collective-permute-done.28.refs_3_), custom_call_target="tpu_custom_call" | custom-call | flops 214748368 | bytes 734003 | tf_op jit(solution)/shard_map/send_part/pallas_call | solution.py:387
  244.1 5.0 %send_part.3 = (bf16[512,1024]{1,0:T(8,128)(2,1)S(1)}, bf16[512,512]{1,0:T(8,128)(2,1)S(1)}) custom-call(s32[130]{0:T(256)S(1)} %copy-done.33, bf16[512,1024]{1,0:T(8,128)(2,1)S(1)} %bitcast.37, bf16[512,1024]{1,0:T(8,128)(2,1)S(1)} %bitcast.40, bf16[2048,5120]{1,0:T(8,128)(2,1)S(1)} %copy-done.2, bf16[512,1024]{1,0:T(8,128)(2,1)S(1)} %send_part.2.refs_3_), custom_call_target="tpu_custom_call" | custom-call | flops 322122560 | bytes 996147 | tf_op jit(solution)/shard_map/send_part/pallas_call | solution.py:387
  249.1 7.9 %own_part.1 = (bf16[512,1024]{1,0:T(8,128)(2,1)S(1)}, bf16[512,1024]{1,0:T(8,128)(2,1)S(1)}, bf16[512,512]{1,0:T(8,128)(2,1)S(1)}) custom-call(s32[130]{0:T(256)S(1)} %copy-done.33, bf16[512,1024]{1,0:T(8,128)(2,1)S(1)} %bitcast.38, bf16[512,1024]{1,0:T(8,128)(2,1)S(1)} %bitcast.41, bf16[2048,5120]{1,0:T(8,128)(2,1)S(1)} %copy-done.2, ...), custom_call_target="tpu_custom_call" | custom-call | flops 536870912 | bytes 1520435 | tf_op jit(solution)/shard_map/own_part/pallas_call | solution.py:387
  257.0 11.5 %collective-permute-done.29 = bf16[512,1024]{1,0:T(8,128)(2,1)S(1)} collective-permute-done((bf16[512,1024]{1,0:T(8,128)(2,1)S(1)}, bf16[512,1024]{1,0:T(8,128)(2,1)S(1)}, u32[]{:S(2)}, u32[]{:S(2)}) %collective-permute-start.29) | collective-permute-done | bytes 1048608 | tf_op jit(solution)/shard_map/ppermute | solution.py:542
  270.2 3.8 %collective-permute-start.32 = (bf16[2,64,1024]{2,1,0:T(8,128)(2,1)S(1)}, bf16[2,64,1024]{2,1,0:T(8,128)(2,1)S(1)}, u32[]{:S(2)}, u32[]{:S(2)}) collective-permute-start(bf16[2,64,1024]{2,1,0:T(8,128)(2,1)S(1)} %get-tuple-element.73), channel_id=1, source_target_pairs={{0,6},{1,7},{2,0},{3,1},{4,2},{5,3},{6,4},{7,5},{8,14},{9,15},{10,... | collective-permute-start | bytes 786440 | tf_op jit(solution)/shard_map/ppermute | solution.py:502
  274.0 7.2 %collective-permute-done.31.refs_1_ = bf16[2,64,1024]{2,1,0:T(8,128)(2,1)S(1)} collective-permute-done((bf16[2,64,1024]{2,1,0:T(8,128)(2,1)S(1)}, bf16[2,64,1024]{2,1,0:T(8,128)(2,1)S(1)}, u32[]{:S(2)}, u32[]{:S(2)}) %collective-permute-start.31) | collective-permute-done | bytes 262176 | tf_op jit(solution)/shard_map/ppermute | solution.py:502
  281.2 4.7 %collective-permute-done.32.refs_2_ = bf16[2,64,1024]{2,1,0:T(8,128)(2,1)S(1)} collective-permute-done((bf16[2,64,1024]{2,1,0:T(8,128)(2,1)S(1)}, bf16[2,64,1024]{2,1,0:T(8,128)(2,1)S(1)}, u32[]{:S(2)}, u32[]{:S(2)}) %collective-permute-start.32) | collective-permute-done | bytes 262176 | tf_op jit(solution)/shard_map/ppermute | solution.py:502
  286.0 6.2 %collective-permute-done.33.refs_3_ = bf16[2,64,1024]{2,1,0:T(8,128)(2,1)S(1)} collective-permute-done((bf16[2,64,1024]{2,1,0:T(8,128)(2,1)S(1)}, bf16[2,64,1024]{2,1,0:T(8,128)(2,1)S(1)}, u32[]{:S(2)}, u32[]{:S(2)}) %collective-permute-start.33) | collective-permute-done | bytes 262176 | tf_op jit(solution)/shard_map/ppermute | solution.py:502
  294.9 3.8 %collective-permute-start.40 = (bf16[2,64,1024]{2,1,0:T(8,128)(2,1)S(1)}, bf16[2,64,1024]{2,1,0:T(8,128)(2,1)S(1)}, u32[]{:S(2)}, u32[]{:S(2)}) collective-permute-start(bf16[2,64,1024]{2,1,0:T(8,128)(2,1)S(1)} %get-tuple-element.82), channel_id=1, source_target_pairs={{0,6},{1,7},{2,0},{3,1},{4,2},{5,3},{6,4},{7,5},{8,14},{9,15},{10,... | collective-permute-start | bytes 786440 | tf_op jit(solution)/shard_map/ppermute | solution.py:502
  298.8 5.6 %collective-permute-done.34 = bf16[512,512]{1,0:T(8,128)(2,1)S(1)} collective-permute-done((bf16[512,512]{1,0:T(8,128)(2,1)S(1)}, bf16[512,512]{1,0:T(8,128)(2,1)S(1)}, u32[]{:S(2)}, u32[]{:S(2)}) %collective-permute-start.34) | collective-permute-done | bytes 524320 | tf_op jit(solution)/shard_map/ppermute | solution.py:542
  304.4 1.5 residual.4
  308.7 12.5 %collective-permute-done.41.refs_3_ = bf16[2,64,1024]{2,1,0:T(8,128)(2,1)S(1)} collective-permute-done((bf16[2,64,1024]{2,1,0:T(8,128)(2,1)S(1)}, bf16[2,64,1024]{2,1,0:T(8,128)(2,1)S(1)}, u32[]{:S(2)}, u32[]{:S(2)}) %collective-permute-start.41) | collective-permute-done | bytes 262176 | tf_op jit(solution)/shard_map/ppermute | solution.py:502
  323.4 5.1 %collective-permute-done.36.refs_2_ = bf16[2,64,512]{2,1,0:T(8,128)(2,1)S(1)} collective-permute-done((bf16[2,64,512]{2,1,0:T(8,128)(2,1)}, bf16[2,64,512]{2,1,0:T(8,128)(2,1)S(1)}, u32[]{:S(2)}, u32[]{:S(2)}) %collective-permute-start.36) | collective-permute-done | bytes 131104 | tf_op jit(solution)/shard_map/ppermute | solution.py:502
  331.1 1.6 placed.3.refs_5_
  332.7 1.6 placed.4.refs_5_
  334.3 2.3 placed.5
  338.7 1.6 pad_maximum_fusion
  (181 shorter events, 41.2 us)
Async XLA Ops:
  6.1 6.2 %collective-permute-start = (bf16[3,64,2560]{2,1,0:T(8,128)(2,1)}, bf16[3,64,2560]{2,1,0:T(8,128)(2,1)S(1)}, u32[]{:S(2)}, u32[]{:S(2)}) collective-permute-start(bf16[3,64,2560]{2,1,0:T(8,128)(2,1)} %pad_maximum_fusion.1), channel_id=1, source_target_pairs={{0,1},{1,0},{2,3},{3,2},{4,5},{5,4},{6,7},{7,6},{8,9},{9,8},{10,11... | collective-permute-start | bytes 2949128 | tf_op jit(solution)/shard_map/ppermute | solution.py:502
  6.5 13.0 %collective-permute-start.2 = (bf16[64,2560]{1,0:T(8,128)(2,1)}, bf16[64,2560]{1,0:T(8,128)(2,1)S(1)}, u32[]{:S(2)}, u32[]{:S(2)}) collective-permute-start(bf16[64,2560]{1,0:T(8,128)(2,1)} %get-tuple-element.92), channel_id=1, source_target_pairs={{0,3},{1,2},{2,5},{3,4},{4,7},{5,6},{6,1},{7,0},{8,11},{9,10},{10,... | collective-permute-start | bytes 983048 | tf_op jit(solution)/shard_map/ppermute | solution.py:502
  9.2 17.5 %collective-permute-start.1 = (bf16[64,2560]{1,0:T(8,128)(2,1)}, bf16[64,2560]{1,0:T(8,128)(2,1)S(1)}, u32[]{:S(2)}, u32[]{:S(2)}) collective-permute-start(bf16[64,2560]{1,0:T(8,128)(2,1)} %get-tuple-element.93), channel_id=1, source_target_pairs={{0,2},{1,3},{2,4},{3,5},{4,6},{5,7},{6,0},{7,1},{8,10},{9,11},{10,... | collective-permute-start | bytes 983048 | tf_op jit(solution)/shard_map/ppermute | solution.py:502
  10.8 16.0 %collective-permute-start.3 = (bf16[64,2560]{1,0:T(8,128)(2,1)S(1)}, bf16[64,2560]{1,0:T(8,128)(2,1)S(1)}, u32[]{:S(2)}, u32[]{:S(2)}) collective-permute-start(bf16[64,2560]{1,0:T(8,128)(2,1)S(1)} %get-tuple-element.91.refs_0_), channel_id=1, source_target_pairs={{0,8},{8,0},{1,9},{9,1},{2,10},{10,2},{3,11},{11,3},{4,12},{12,4},... | collective-permute-start | bytes 983048 | tf_op jit(solution)/shard_map/ppermute | solution.py:542
  12.3 14.4 %collective-permute-start.5 = (bf16[1,2560]{1,0:T(2,128)(2,1)S(1)}, bf16[1,2560]{1,0:T(2,128)(2,1)S(1)}, u32[]{:S(2)}, u32[]{:S(2)}) collective-permute-start(bf16[1,2560]{1,0:T(2,128)(2,1)S(1)} %broadcast_in_dim.6.refs_8_.refs_6_), channel_id=1, source_target_pairs={{0,8},{8,0},{1,9},{9,1},{2,10},{10,2},{3,11},{11,3},{4,12},{12,4},... | collective-permute-start | bytes 15368 | tf_op jit(solution)/shard_map/ppermute | solution.py:542
  13.7 13.7 %collective-permute-start.4 = (bf16[64,2560]{1,0:T(8,128)(2,1)S(1)}, bf16[64,2560]{1,0:T(8,128)(2,1)S(1)}, u32[]{:S(2)}, u32[]{:S(2)}) collective-permute-start(bf16[64,2560]{1,0:T(8,128)(2,1)S(1)} %get-tuple-element.100.refs_1_), channel_id=1, source_target_pairs={{0,8},{8,0},{1,9},{9,1},{2,10},{10,2},{3,11},{11,3},{4,12},{12,4},... | collective-permute-start | bytes 983048 | tf_op jit(solution)/shard_map/ppermute | solution.py:542
  28.1 16.2 %collective-permute-start.6 = (bf16[128,2560]{1,0:T(8,128)(2,1)}, bf16[128,2560]{1,0:T(8,128)(2,1)S(1)}, u32[]{:S(2)}, u32[]{:S(2)}) collective-permute-start(bf16[128,2560]{1,0:T(8,128)(2,1)} %pad_maximum_fusion.2), channel_id=1, source_target_pairs={{0,6},{1,7},{2,0},{3,1},{4,2},{5,3},{6,4},{7,5},{8,14},{9,15},{10,... | collective-permute-start | bytes 1966088 | tf_op jit(solution)/shard_map/ppermute | solution.py:502
  33.3 93.5 %slice-start = ((s8[5242880]{0:T(1024)(128)(4,1)}), s8[1048576]{0:T(1024)(128)(4,1)S(1)}, s32[]{:S(2)}) async-start(s8[5242880]{0:T(1024)(128)(4,1)} %bitcast.34), calls=%async_computation | async-start | bytes 2097152
  33.4 13.3 %collective-permute-start.8 = (bf16[64,2560]{1,0:T(8,128)(2,1)S(1)}, bf16[64,2560]{1,0:T(8,128)(2,1)S(1)}, u32[]{:S(2)}, u32[]{:S(2)}) collective-permute-start(bf16[64,2560]{1,0:T(8,128)(2,1)S(1)} %collective-permute-done.2.refs_3_), channel_id=1, source_target_pairs={{0,8},{8,0},{1,9},{9,1},{2,10},{10,2},{3,11},{11,3},{4,12},{12,4},... | collective-permute-start | bytes 983048 | tf_op jit(solution)/shard_map/ppermute | solution.py:542
  34.9 16.2 %collective-permute-start.7 = (bf16[64,2560]{1,0:T(8,128)(2,1)S(1)}, bf16[64,2560]{1,0:T(8,128)(2,1)S(1)}, u32[]{:S(2)}, u32[]{:S(2)}) collective-permute-start(bf16[64,2560]{1,0:T(8,128)(2,1)S(1)} %collective-permute-done.1.refs_2_), channel_id=1, source_target_pairs={{0,8},{8,0},{1,9},{9,1},{2,10},{10,2},{3,11},{11,3},{4,12},{12,4},... | collective-permute-start | bytes 983048 | tf_op jit(solution)/shard_map/ppermute | solution.py:542
  44.2 50.4 %collective-permute-start.10 = (bf16[128,2560]{1,0:T(8,128)(2,1)S(1)}, bf16[128,2560]{1,0:T(8,128)(2,1)S(1)}, u32[]{:S(2)}, u32[]{:S(2)}) collective-permute-start(bf16[128,2560]{1,0:T(8,128)(2,1)S(1)} %collective-permute-done.6.refs_0_.refs_4_), channel_id=1, source_target_pairs={{0,8},{8,0},{1,9},{9,1},{2,10},{10,2},{3,11},{11,3},{4,12},{12,4},... | collective-permute-start | bytes 1966088 | tf_op jit(solution)/shard_map/ppermute | solution.py:542
  57.8 69.1 %slice-start.1 = ((s8[5242880]{0:T(1024)(128)(4,1)}), s8[4194304]{0:T(1024)(128)(4,1)S(1)}, s32[]{:S(2)}) async-start(s8[5242880]{0:T(1024)(128)(4,1)} %bitcast.34), calls=%async_computation.1 | async-start | bytes 8388608
  57.8 69.1 %copy-start.37 = (bf16[128]{0:T(256)(128)(2,1)S(1)}, bf16[128]{0:T(256)(128)(2,1)}, u32[]{:S(2)}) copy-start(bf16[128]{0:T(256)(128)(2,1)} %param.18) | copy-start | bytes 772
  66.7 28.0 %collective-permute-start.14 = (bf16[2,4,64,512]{3,2,1,0:T(8,128)(2,1)S(1)}, bf16[2,4,64,512]{3,2,1,0:T(8,128)(2,1)S(1)}, u32[]{:S(2)}, u32[]{:S(2)}) collective-permute-start(bf16[2,4,64,512]{3,2,1,0:T(8,128)(2,1)S(1)} %bitcast.46), channel_id=1, source_target_pairs={{0,2},{1,3},{2,4},{3,5},{4,6},{5,7},{6,0},{7,1},{8,10},{9,11},{10,... | collective-permute-start | bytes 1572872 | tf_op jit(solution)/shard_map/ppermute | solution.py:502
  66.7 27.9 %collective-permute-start.9 = (bf16[64,2560]{1,0:T(8,128)(2,1)S(1)}, bf16[64,2560]{1,0:T(8,128)(2,1)S(1)}, u32[]{:S(2)}, u32[]{:S(2)}) collective-permute-start(bf16[64,2560]{1,0:T(8,128)(2,1)S(1)} %copy-done.39), channel_id=1, source_target_pairs={{0,4},{1,5},{2,6},{3,7},{4,0},{5,1},{6,2},{7,3},{8,12},{9,13},{10,... | collective-permute-start | bytes 983048 | tf_op jit(solution)/shard_map/ppermute | solution.py:502
  94.6 22.6 %collective-permute-start.11 = (bf16[64,2560]{1,0:T(8,128)(2,1)S(1)}, bf16[64,2560]{1,0:T(8,128)(2,1)S(1)}, u32[]{:S(2)}, u32[]{:S(2)}) collective-permute-start(bf16[64,2560]{1,0:T(8,128)(2,1)S(1)} %copy-done.40), channel_id=1, source_target_pairs={{0,4},{1,5},{2,6},{3,7},{4,0},{5,1},{6,2},{7,3},{8,12},{9,13},{10,... | collective-permute-start | bytes 983048 | tf_op jit(solution)/shard_map/ppermute | solution.py:502
  94.7 24.0 %collective-permute-start.15 = (bf16[2,4,64,512]{3,2,1,0:T(8,128)(2,1)S(1)}, bf16[2,4,64,512]{3,2,1,0:T(8,128)(2,1)S(1)}, u32[]{:S(2)}, u32[]{:S(2)}) collective-permute-start(bf16[2,4,64,512]{3,2,1,0:T(8,128)(2,1)S(1)} %collective-permute-done.14.refs_6_), channel_id=1, source_target_pairs={{0,2},{1,3},{2,4},{3,5},{4,6},{5,7},{6,0},{7,1},{8,10},{9,11},{10,... | collective-permute-start | bytes 1572872 | tf_op jit(solution)/shard_map/ppermute | solution.py:502
  94.8 24.0 %collective-permute-start.12 = (bf16[64,2560]{1,0:T(8,128)(2,1)S(1)}, bf16[64,2560]{1,0:T(8,128)(2,1)S(1)}, u32[]{:S(2)}, u32[]{:S(2)}) collective-permute-start(bf16[64,2560]{1,0:T(8,128)(2,1)S(1)} %collective-permute-done.9.refs_1_.refs_5_), channel_id=1, source_target_pairs={{0,8},{8,0},{1,9},{9,1},{2,10},{10,2},{3,11},{11,3},{4,12},{12,4},... | collective-permute-start | bytes 983048 | tf_op jit(solution)/shard_map/ppermute | solution.py:542
  117.2 9.6 %collective-permute-start.13 = (bf16[64,2560]{1,0:T(8,128)(2,1)S(1)}, bf16[64,2560]{1,0:T(8,128)(2,1)S(1)}, u32[]{:S(2)}, u32[]{:S(2)}) collective-permute-start(bf16[64,2560]{1,0:T(8,128)(2,1)S(1)} %collective-permute-done.11.refs_2_.refs_6_), channel_id=1, source_target_pairs={{0,8},{8,0},{1,9},{9,1},{2,10},{10,2},{3,11},{11,3},{4,12},{12,4},... | collective-permute-start | bytes 983048 | tf_op jit(solution)/shard_map/ppermute | solution.py:542
  118.7 55.4 %collective-permute-start.21 = (bf16[2,4,64,512]{3,2,1,0:T(8,128)(2,1)S(1)}, bf16[2,4,64,512]{3,2,1,0:T(8,128)(2,1)S(1)}, u32[]{:S(2)}, u32[]{:S(2)}) collective-permute-start(bf16[2,4,64,512]{3,2,1,0:T(8,128)(2,1)S(1)} %collective-permute-done.15.refs_10_), channel_id=1, source_target_pairs={{0,2},{1,3},{2,4},{3,5},{4,6},{5,7},{6,0},{7,1},{8,10},{9,11},{10,... | collective-permute-start | bytes 1572872 | tf_op jit(solution)/shard_map/ppermute | solution.py:502
  138.4 35.7 %collective-permute-start.18 = (bf16[2,4,64,512]{3,2,1,0:T(8,128)(2,1)S(1)}, bf16[2,4,64,512]{3,2,1,0:T(8,128)(2,1)S(1)}, u32[]{:S(2)}, u32[]{:S(2)}) collective-permute-start(bf16[2,4,64,512]{3,2,1,0:T(8,128)(2,1)S(1)} %bitcast.50), channel_id=1, source_target_pairs={{0,2},{1,3},{2,4},{3,5},{4,6},{5,7},{6,0},{7,1},{8,10},{9,11},{10,... | collective-permute-start | bytes 1572872 | tf_op jit(solution)/shard_map/ppermute | solution.py:502
  174.2 14.9 %collective-permute-start.22 = (bf16[2,4,64,512]{3,2,1,0:T(8,128)(2,1)S(1)}, bf16[2,4,64,512]{3,2,1,0:T(8,128)(2,1)S(1)}, u32[]{:S(2)}, u32[]{:S(2)}) collective-permute-start(bf16[2,4,64,512]{3,2,1,0:T(8,128)(2,1)S(1)} %collective-permute-done.18.refs_7_), channel_id=1, source_target_pairs={{0,2},{1,3},{2,4},{3,5},{4,6},{5,7},{6,0},{7,1},{8,10},{9,11},{10,... | collective-permute-start | bytes 1572872 | tf_op jit(solution)/shard_map/ppermute | solution.py:502
  174.3 14.7 %collective-permute-start.16 = (bf16[2,4,64,512]{3,2,1,0:T(8,128)(2,1)S(1)}, bf16[2,4,64,512]{3,2,1,0:T(8,128)(2,1)S(1)}, u32[]{:S(2)}, u32[]{:S(2)}) collective-permute-start(bf16[2,4,64,512]{3,2,1,0:T(8,128)(2,1)S(1)} %bitcast.47), channel_id=1, source_target_pairs={{0,1},{1,0},{2,3},{3,2},{4,5},{5,4},{6,7},{7,6},{8,9},{9,8},{10,11... | collective-permute-start | bytes 1572872 | tf_op jit(solution)/shard_map/ppermute | solution.py:502
  174.3 15.2 %collective-permute-start.19 = (bf16[2,4,64,512]{3,2,1,0:T(8,128)(2,1)S(1)}, bf16[2,4,64,512]{3,2,1,0:T(8,128)(2,1)S(1)}, u32[]{:S(2)}, u32[]{:S(2)}) collective-permute-start(bf16[2,4,64,512]{3,2,1,0:T(8,128)(2,1)S(1)} %collective-permute-done.14.refs_6_), channel_id=1, source_target_pairs={{0,1},{1,0},{2,3},{3,2},{4,5},{5,4},{6,7},{7,6},{8,9},{9,8},{10,11... | collective-permute-start | bytes 1572872 | tf_op jit(solution)/shard_map/ppermute | solution.py:502
  174.8 14.8 %collective-permute-start.23 = (bf16[2,4,64,512]{3,2,1,0:T(8,128)(2,1)S(1)}, bf16[2,4,64,512]{3,2,1,0:T(8,128)(2,1)S(1)}, u32[]{:S(2)}, u32[]{:S(2)}) collective-permute-start(bf16[2,4,64,512]{3,2,1,0:T(8,128)(2,1)S(1)} %collective-permute-done.15.refs_10_), channel_id=1, source_target_pairs={{0,1},{1,0},{2,3},{3,2},{4,5},{5,4},{6,7},{7,6},{8,9},{9,8},{10,11... | collective-permute-start | bytes 1572872 | tf_op jit(solution)/shard_map/ppermute | solution.py:502
  189.0 13.9 %collective-permute-start.25 = (bf16[2,4,64,512]{3,2,1,0:T(8,128)(2,1)S(1)}, bf16[2,4,64,512]{3,2,1,0:T(8,128)(2,1)S(1)}, u32[]{:S(2)}, u32[]{:S(2)}) collective-permute-start(bf16[2,4,64,512]{3,2,1,0:T(8,128)(2,1)S(1)} %collective-permute-done.22.refs_11_), channel_id=1, source_target_pairs={{0,2},{1,3},{2,4},{3,5},{4,6},{5,7},{6,0},{7,1},{8,10},{9,11},{10,... | collective-permute-start | bytes 1572872 | tf_op jit(solution)/shard_map/ppermute | solution.py:502
  189.0 13.9 %collective-permute-start.26 = (bf16[2,4,64,512]{3,2,1,0:T(8,128)(2,1)S(1)}, bf16[2,4,64,512]{3,2,1,0:T(8,128)(2,1)S(1)}, u32[]{:S(2)}, u32[]{:S(2)}) collective-permute-start(bf16[2,4,64,512]{3,2,1,0:T(8,128)(2,1)S(1)} %collective-permute-done.21.refs_14_), channel_id=1, source_target_pairs={{0,1},{1,0},{2,3},{3,2},{4,5},{5,4},{6,7},{7,6},{8,9},{9,8},{10,11... | collective-permute-start | bytes 1572872 | tf_op jit(solution)/shard_map/ppermute | solution.py:502
  189.0 13.9 %collective-permute-start.17 = (bf16[2,4,64,512]{3,2,1,0:T(8,128)(2,1)S(1)}, bf16[2,4,64,512]{3,2,1,0:T(8,128)(2,1)S(1)}, u32[]{:S(2)}, u32[]{:S(2)}) collective-permute-start(bf16[2,4,64,512]{3,2,1,0:T(8,128)(2,1)S(1)} %bitcast.51), channel_id=1, source_target_pairs={{0,1},{1,0},{2,3},{3,2},{4,5},{5,4},{6,7},{7,6},{8,9},{9,8},{10,11... | collective-permute-start | bytes 1572872 | tf_op jit(solution)/shard_map/ppermute | solution.py:502
  189.5 13.4 %collective-permute-start.20 = (bf16[2,4,64,512]{3,2,1,0:T(8,128)(2,1)S(1)}, bf16[2,4,64,512]{3,2,1,0:T(8,128)(2,1)S(1)}, u32[]{:S(2)}, u32[]{:S(2)}) collective-permute-start(bf16[2,4,64,512]{3,2,1,0:T(8,128)(2,1)S(1)} %collective-permute-done.18.refs_7_), channel_id=1, source_target_pairs={{0,1},{1,0},{2,3},{3,2},{4,5},{5,4},{6,7},{7,6},{8,9},{9,8},{10,11... | collective-permute-start | bytes 1572872 | tf_op jit(solution)/shard_map/ppermute | solution.py:502
  189.6 13.3 %collective-permute-start.24 = (bf16[2,4,64,512]{3,2,1,0:T(8,128)(2,1)S(1)}, bf16[2,4,64,512]{3,2,1,0:T(8,128)(2,1)S(1)}, u32[]{:S(2)}, u32[]{:S(2)}) collective-permute-start(bf16[2,4,64,512]{3,2,1,0:T(8,128)(2,1)S(1)} %collective-permute-done.22.refs_11_), channel_id=1, source_target_pairs={{0,1},{1,0},{2,3},{3,2},{4,5},{5,4},{6,7},{7,6},{8,9},{9,8},{10,11... | collective-permute-start | bytes 1572872 | tf_op jit(solution)/shard_map/ppermute | solution.py:502
  202.9 1.9 collective-permute-start.27
  217.7 15.1 %collective-permute-start.28 = (bf16[4,2,128,256]{3,2,1,0:T(8,128)(2,1)S(1)}, bf16[4,2,128,256]{3,2,1,0:T(8,128)(2,1)S(1)}, u32[]{:S(2)}, u32[]{:S(2)}) collective-permute-start(bf16[4,2,128,256]{3,2,1,0:T(8,128)(2,1)S(1)} %get-tuple-element.64), channel_id=1, source_target_pairs={{0,8},{8,0},{1,9},{9,1},{2,10},{10,2},{3,11},{11,3},{4,12},{12,4},... | collective-permute-start | bytes 1572872 | tf_op jit(solution)/shard_map/ppermute | solution.py:542
  243.5 25.0 %collective-permute-start.29 = (bf16[512,1024]{1,0:T(8,128)(2,1)S(1)}, bf16[512,1024]{1,0:T(8,128)(2,1)S(1)}, u32[]{:S(2)}, u32[]{:S(2)}) collective-permute-start(bf16[512,1024]{1,0:T(8,128)(2,1)S(1)} %send_part.2.refs_3_), channel_id=1, source_target_pairs={{0,8},{8,0},{1,9},{9,1},{2,10},{10,2},{3,11},{11,3},{4,12},{12,4},... | collective-permute-start | bytes 3145736 | tf_op jit(solution)/shard_map/ppermute | solution.py:542
  268.5 24.0 %collective-permute-start.30 = (bf16[512,1024]{1,0:T(8,128)(2,1)S(1)}, bf16[512,1024]{1,0:T(8,128)(2,1)S(1)}, u32[]{:S(2)}, u32[]{:S(2)}) collective-permute-start(bf16[512,1024]{1,0:T(8,128)(2,1)S(1)} %get-tuple-element.70), channel_id=1, source_target_pairs={{0,8},{8,0},{1,9},{9,1},{2,10},{10,2},{3,11},{11,3},{4,12},{12,4},... | collective-permute-start | bytes 3145736 | tf_op jit(solution)/shard_map/ppermute | solution.py:542
  270.1 11.1 %collective-permute-start.31 = (bf16[2,64,1024]{2,1,0:T(8,128)(2,1)S(1)}, bf16[2,64,1024]{2,1,0:T(8,128)(2,1)S(1)}, u32[]{:S(2)}, u32[]{:S(2)}) collective-permute-start(bf16[2,64,1024]{2,1,0:T(8,128)(2,1)S(1)} %get-tuple-element.72), channel_id=1, source_target_pairs={{0,2},{1,3},{2,4},{3,5},{4,6},{5,7},{6,0},{7,1},{8,10},{9,11},{10,... | collective-permute-start | bytes 786440 | tf_op jit(solution)/shard_map/ppermute | solution.py:502
  270.2 15.8 %collective-permute-start.32 = (bf16[2,64,1024]{2,1,0:T(8,128)(2,1)S(1)}, bf16[2,64,1024]{2,1,0:T(8,128)(2,1)S(1)}, u32[]{:S(2)}, u32[]{:S(2)}) collective-permute-start(bf16[2,64,1024]{2,1,0:T(8,128)(2,1)S(1)} %get-tuple-element.73), channel_id=1, source_target_pairs={{0,6},{1,7},{2,0},{3,1},{4,2},{5,3},{6,4},{7,5},{8,14},{9,15},{10,... | collective-permute-start | bytes 786440 | tf_op jit(solution)/shard_map/ppermute | solution.py:502
  274.0 18.1 %collective-permute-start.33 = (bf16[2,64,1024]{2,1,0:T(8,128)(2,1)S(1)}, bf16[2,64,1024]{2,1,0:T(8,128)(2,1)S(1)}, u32[]{:S(2)}, u32[]{:S(2)}) collective-permute-start(bf16[2,64,1024]{2,1,0:T(8,128)(2,1)S(1)} %get-tuple-element.74), channel_id=1, source_target_pairs={{0,4},{1,5},{2,6},{3,7},{4,0},{5,1},{6,2},{7,3},{8,12},{9,13},{10,... | collective-permute-start | bytes 786440 | tf_op jit(solution)/shard_map/ppermute | solution.py:502
  292.5 11.9 %collective-permute-start.34 = (bf16[512,512]{1,0:T(8,128)(2,1)S(1)}, bf16[512,512]{1,0:T(8,128)(2,1)S(1)}, u32[]{:S(2)}, u32[]{:S(2)}) collective-permute-start(bf16[512,512]{1,0:T(8,128)(2,1)S(1)} %get-tuple-element.75.refs_3_), channel_id=1, source_target_pairs={{0,8},{8,0},{1,9},{9,1},{2,10},{10,2},{3,11},{11,3},{4,12},{12,4},... | collective-permute-start | bytes 1572872 | tf_op jit(solution)/shard_map/ppermute | solution.py:542
  294.8 12.0 %collective-permute-start.39 = (bf16[2,64,1024]{2,1,0:T(8,128)(2,1)S(1)}, bf16[2,64,1024]{2,1,0:T(8,128)(2,1)S(1)}, u32[]{:S(2)}, u32[]{:S(2)}) collective-permute-start(bf16[2,64,1024]{2,1,0:T(8,128)(2,1)S(1)} %get-tuple-element.81), channel_id=1, source_target_pairs={{0,2},{1,3},{2,4},{3,5},{4,6},{5,7},{6,0},{7,1},{8,10},{9,11},{10,... | collective-permute-start | bytes 786440 | tf_op jit(solution)/shard_map/ppermute | solution.py:502
  294.9 13.1 %collective-permute-start.40 = (bf16[2,64,1024]{2,1,0:T(8,128)(2,1)S(1)}, bf16[2,64,1024]{2,1,0:T(8,128)(2,1)S(1)}, u32[]{:S(2)}, u32[]{:S(2)}) collective-permute-start(bf16[2,64,1024]{2,1,0:T(8,128)(2,1)S(1)} %get-tuple-element.82), channel_id=1, source_target_pairs={{0,6},{1,7},{2,0},{3,1},{4,2},{5,3},{6,4},{7,5},{8,14},{9,15},{10,... | collective-permute-start | bytes 786440 | tf_op jit(solution)/shard_map/ppermute | solution.py:502
  298.7 22.5 %collective-permute-start.41 = (bf16[2,64,1024]{2,1,0:T(8,128)(2,1)S(1)}, bf16[2,64,1024]{2,1,0:T(8,128)(2,1)S(1)}, u32[]{:S(2)}, u32[]{:S(2)}) collective-permute-start(bf16[2,64,1024]{2,1,0:T(8,128)(2,1)S(1)} %get-tuple-element.83), channel_id=1, source_target_pairs={{0,4},{1,5},{2,6},{3,7},{4,0},{5,1},{6,2},{7,3},{8,12},{9,13},{10,... | collective-permute-start | bytes 786440 | tf_op jit(solution)/shard_map/ppermute | solution.py:502
  305.9 16.9 %collective-permute-start.35 = (bf16[2,64,512]{2,1,0:T(8,128)(2,1)S(1)}, bf16[2,64,512]{2,1,0:T(8,128)(2,1)S(1)}, u32[]{:S(2)}, u32[]{:S(2)}) collective-permute-start(bf16[2,64,512]{2,1,0:T(8,128)(2,1)S(1)} %get-tuple-element.77), channel_id=1, source_target_pairs={{0,2},{1,3},{2,4},{3,5},{4,6},{5,7},{6,0},{7,1},{8,10},{9,11},{10,... | collective-permute-start | bytes 393224 | tf_op jit(solution)/shard_map/ppermute | solution.py:502
  306.8 24.3 %collective-permute-start.43 = (bf16[4,64,1024]{2,1,0:T(8,128)(2,1)}, bf16[4,64,1024]{2,1,0:T(8,128)(2,1)S(1)}, u32[]{:S(2)}, u32[]{:S(2)}) collective-permute-start(bf16[4,64,1024]{2,1,0:T(8,128)(2,1)} %pad_maximum_fusion.4), channel_id=1, source_target_pairs={{0,1},{1,0},{2,3},{3,2},{4,5},{5,4},{6,7},{7,6},{8,9},{9,8},{10,11... | collective-permute-start | bytes 1572872 | tf_op jit(solution)/shard_map/ppermute | solution.py:502
  321.9 6.6 %collective-permute-start.36 = (bf16[2,64,512]{2,1,0:T(8,128)(2,1)}, bf16[2,64,512]{2,1,0:T(8,128)(2,1)S(1)}, u32[]{:S(2)}, u32[]{:S(2)}) collective-permute-start(bf16[2,64,512]{2,1,0:T(8,128)(2,1)} %get-tuple-element.78), channel_id=1, source_target_pairs={{0,6},{1,7},{2,0},{3,1},{4,2},{5,3},{6,4},{7,5},{8,14},{9,15},{10,... | collective-permute-start | bytes 393224 | tf_op jit(solution)/shard_map/ppermute | solution.py:502
  321.9 8.1 %collective-permute-start.37 = (bf16[2,64,512]{2,1,0:T(8,128)(2,1)}, bf16[2,64,512]{2,1,0:T(8,128)(2,1)}, u32[]{:S(2)}, u32[]{:S(2)}) collective-permute-start(bf16[2,64,512]{2,1,0:T(8,128)(2,1)} %get-tuple-element.79), channel_id=1, source_target_pairs={{0,4},{1,5},{2,6},{3,7},{4,0},{5,1},{6,2},{7,3},{8,12},{9,13},{10,... | collective-permute-start | bytes 393224 | tf_op jit(solution)/shard_map/ppermute | solution.py:502
  322.8 10.0 %collective-permute-start.42 = (bf16[4,64,1024]{2,1,0:T(8,128)(2,1)}, bf16[4,64,1024]{2,1,0:T(8,128)(2,1)S(1)}, u32[]{:S(2)}, u32[]{:S(2)}) collective-permute-start(bf16[4,64,1024]{2,1,0:T(8,128)(2,1)} %pad_maximum_fusion.3), channel_id=1, source_target_pairs={{0,1},{1,0},{2,3},{3,2},{4,5},{5,4},{6,7},{7,6},{8,9},{9,8},{10,11... | collective-permute-start | bytes 1572872 | tf_op jit(solution)/shard_map/ppermute | solution.py:502
  322.8 14.7 %collective-permute-start.44 = (bf16[4,2,128,256]{3,2,1,0:T(8,128)(2,1)}, bf16[4,2,128,256]{3,2,1,0:T(8,128)(2,1)}, u32[]{:S(2)}, u32[]{:S(2)}) collective-permute-start(bf16[4,2,128,256]{3,2,1,0:T(8,128)(2,1)} %get-tuple-element.85), channel_id=1, source_target_pairs={{0,8},{8,0},{1,9},{9,1},{2,10},{10,2},{3,11},{11,3},{4,12},{12,4},... | collective-permute-start | bytes 1572872 | tf_op jit(solution)/shard_map/ppermute | solution.py:542
  330.9 3.5 %collective-permute-start.38 = (bf16[4,64,512]{2,1,0:T(8,128)(2,1)S(1)}, bf16[4,64,512]{2,1,0:T(8,128)(2,1)S(1)}, u32[]{:S(2)}, u32[]{:S(2)}) collective-permute-start(bf16[4,64,512]{2,1,0:T(8,128)(2,1)S(1)} %pad_maximum_fusion.7), channel_id=1, source_target_pairs={{0,1},{1,0},{2,3},{3,2},{4,5},{5,4},{6,7},{7,6},{8,9},{9,8},{10,11... | collective-permute-start | bytes 786440 | tf_op jit(solution)/shard_map/ppermute | solution.py:502
  (44 other events, 432.1 us)

commit v7 on v6

--- a/solution.py
+++ b/solution.py
@@ -14,11 +14,15 @@
 very_negative = -1e30
 PARTS = 2
 CORES = 2
-SHARE = 0.1
+SHARE = 0.02
 
 
 def params(mebibytes):
     return pltpu.CompilerParams(vmem_limit_bytes=mebibytes * 1024 * 1024)
+
+
+def in_hbm(x):
+    return pltpu.with_memory_space_constraint(x, pltpu.HBM)
 
 
 def cost(flops, moved, transcendentals=0):
@@ -195,7 +199,8 @@
         cost_estimate=cost(4 * rows * width * cols, 4 * width * cols + 4 * rows * width),
         name="keys_values",
     )(
-        table, *[x for side in xs for x in side], *gains, *[wk] * sides, *[wv] * sides,
+        table, *[x for side in xs for x in side], *gains,
+        *[in_hbm(wk)] * sides, *[in_hbm(wv)] * sides,
         kgain, cosine, sine,
     )
 
@@ -246,7 +251,7 @@
         compiler_params=params(24),
         cost_estimate=cost(2 * rows * width * cols, 2 * width * cols + 2 * rows * (width + cols)),
         name="queries",
-    )(table, *normed, *[wq] * sides, qgain, cosine, sine)
+    )(table, *normed, *[in_hbm(wq)] * sides, qgain, cosine, sine)
 
 
 def attention_kernel(lay, spans, most, per_kv, head, owners, pages_each, table, *refs):
@@ -400,7 +405,7 @@
             2 * rows * depth * count * tile, 2 * (rows * depth + (rows + depth) * count * tile)
         ),
         name=name,
-    )(table, *attended, wo, *follows)
+    )(table, *attended, in_hbm(wo), *follows)
 
 
 def add_kernel(lay, blocks, table, *refs):
@@ -544,7 +549,6 @@
     hops = hop_order(chips)
     paired_hops = hops[2:]
     near = [rows_for(hop, flip) for hop in hops[1:2] for flip in range(CORES)]
-    split = after(split, near)
     near = [shift(x, owners, hops[1], flip) for flip, x in enumerate(near)]
     swapped = shift(
         jnp.stack([rows_for(hop, 1) for hop in hops[:1] + paired_hops]), owners, 0, 1
@@ -574,18 +578,19 @@
 
     kvs, norms = [], []
 
-    def make_part(own_rows, crossed_rows, done):
+    def make_part(own_rows, crossed_rows):
         if paired:
             xs = [own_rows, crossed_rows]
         else:
             xs = [[lax.all_gather(jnp.concatenate(own_rows), "tensor", axis=1, tiled=True)]]
-        kgain = after(key_norm_gain[None], done)
-        *normed, kv = make_kv(lay, table, xs, gains, wk, wv, kgain, cosine, sine, len(kvs))
+        *normed, kv = make_kv(
+            lay, table, xs, gains, wk, wv, key_norm_gain[None], cosine, sine, len(kvs)
+        )
         kvs.append([kv.reshape(2, here, rows, kv.shape[2])])
         norms.append(normed)
 
     def one_back(p, done=()):
-        kvs[p].append(shift(after(kvs[p][-1], done) if done else kvs[p][-1], owners, 1, 0))
+        kvs[p].append(shift(after(kvs[p][-1], done), owners, 1, 0))
 
     begun = 0
     for n in range(len(moves) + 1):
@@ -602,12 +607,12 @@
                     block = after(block, kvs[0][0])
                 crossed.append(cross(block))
         if sum(x.shape[0] for x in arrived[begun:]) == here * rows:
-            make_part(arrived[begun:], crossed[begun:], kvs[0][1:2] if kvs else arrived[0])
+            make_part(arrived[begun:], crossed[begun:])
             begun = len(arrived)
             for _ in range(min(2, chips - 1) if len(kvs) == 1 else min(1, chips - 1)):
                 one_back(len(kvs) - 1)
 
-    queries, done = [], (kvs[1][0], kvs[0][-1])
+    queries, done = [], kvs[1][0]
     for p in range(PARTS):
         made = make_q(
             lay, table, norms[p], wq, after(q_gain[None], done), cosine, sine, p
@@ -616,7 +621,7 @@
         done = queries[-1]
     for p in range(PARTS):
         while len(kvs[p]) < chips:
-            one_back(p, (queries, kvs[0][-1]) if p else ())
+            one_back(p, queries[p])
     gathered = []
     for back in range(chips):
         gathered.append([kv[back] for kv in kvs])

time: 341 us -> 296 us (0.87)
  local copies, waits for them, and re-layouts: 47.2 us -> 10.7 us
  waiting for transfers between devices: 166 us -> 140 us
  Pallas kernels: 85.3 us -> 97.8 us
  starting transfers between devices: 31.6 us -> 37.4 us
    unnamed x88 -> x54, local copies, waits for them, and re-layouts: 41.1 us -> 6.25 us
    ppermute x32, waiting for transfers between devices: 134 us -> 112 us  [shift(): return lax.ppermute(x, 'group', pairs)]
    ppermute x32, starting transfers between devices: 17.5 us -> 23.6 us  [shift(): return lax.ppermute(x, 'group', pairs)]
    pallas_call x3, Pallas kernels: 16.6 us -> 20.7 us  [make_projection(): pl.pallas_call(functools.partial(project_kernel, len(attended), len(follo...]
    pallas_call x2, Pallas kernels: 12.4 us -> 16.4 us  [make_kv(): pl.pallas_call(functools.partial(kv_kernel, sides, blocks), grid_spec=plt...]
    pallas_call x2, Pallas kernels: 19.1 us -> 22.6 us  [make_q(): pl.pallas_call(functools.partial(q_kernel, sides), grid_spec=pltpu.Prefet...]
  transfers between devices with their start and end apart: 45 -> 45, of which waited for: 22 -> 21; matrix products, arithmetic and copies ran while one was open for 2% -> 2% of each run, Pallas kernels for 20% -> 27%
where the time goes in v7:
time: 296 us; the launch traced here: 295 us
  waiting for transfers between devices  140 us (47%)
  Pallas kernels  97.8 us (33%)
  starting transfers between devices  37.4 us (13%)
  local copies, waits for them, and re-layouts  10.7 us (4%)
  other arithmetic  8.33 us (3%)
    ppermute x32, waiting for transfers between devices, shift(): return lax.ppermute(x, 'group', pairs)  112 us
    ppermute x13, waiting for transfers between devices, local(): cross = lambda x: lax.ppermute(x, 'tensor', swap)  28.2 us
    pallas_call x2, Pallas kernels, make_attention(): pl.pallas_call(functools.partial(attention_kernel, lay, spans, most, per_...  27.2 us
    ppermute x32, starting transfers between devices, shift(): return lax.ppermute(x, 'group', pairs)  23.6 us
    pallas_call x2, Pallas kernels, make_q(): pl.pallas_call(functools.partial(q_kernel, sides), grid_spec=pltpu.Prefet...  22.6 us
    pallas_call x3, Pallas kernels, make_projection(): pl.pallas_call(functools.partial(project_kernel, len(attended), len(follo...  20.7 us
    pallas_call x2, Pallas kernels, make_kv(): pl.pallas_call(functools.partial(kv_kernel, sides, blocks), grid_spec=plt...  16.4 us
    ppermute x13, starting transfers between devices, local(): cross = lambda x: lax.ppermute(x, 'tensor', swap)  13.8 us
  transfers between devices with their start and end apart: 45, of which 21 were waited for; matrix products, arithmetic and copies ran while one was open for 2% of the time, Pallas kernels for 27%

profile of v7, /device:TPU:0, one launch (start us, length us, event | category | flops | bytes accessed | tf_op | source)
XLA Modules:
  0.0 295.5 jit_solution(726556046784219142)
XLA Ops:
  0.7 2.7 dynamic-slice_bitcast_fusion
  4.0 2.7 collective-permute-start.2
  6.7 1.6 collective-permute-start.1
  8.3 1.5 collective-permute-start.3
  11.2 1.5 collective-permute-start.4
  13.6 3.2 %collective-permute-done.2.refs_3_ = bf16[64,2560]{1,0:T(8,128)(2,1)S(1)} collective-permute-done((bf16[64,2560]{1,0:T(8,128)(2,1)S(1)}, bf16[64,2560]{1,0:T(8,128)(2,1)S(1)}, u32[]{:S(2)}, u32[]{:S(2)}) %collective-permute-start.2) | collective-permute-done | bytes 327712 | tf_op jit(solution)/shard_map/ppermute | solution.py:507
  16.8 7.3 %collective-permute-done.1.refs_2_ = bf16[64,2560]{1,0:T(8,128)(2,1)S(1)} collective-permute-done((bf16[64,2560]{1,0:T(8,128)(2,1)S(1)}, bf16[64,2560]{1,0:T(8,128)(2,1)S(1)}, u32[]{:S(2)}, u32[]{:S(2)}) %collective-permute-start.1) | collective-permute-done | bytes 327712 | tf_op jit(solution)/shard_map/ppermute | solution.py:507
  25.7 2.2 collective-permute-start.6
  27.9 1.5 collective-permute-start.8
  29.9 11.5 %collective-permute-done.6.refs_0_.refs_4_ = bf16[128,2560]{1,0:T(8,128)(2,1)S(1)} collective-permute-done((bf16[128,2560]{1,0:T(8,128)(2,1)}, bf16[128,2560]{1,0:T(8,128)(2,1)S(1)}, u32[]{:S(2)}, u32[]{:S(2)}) %collective-permute-start.6) | collective-permute-done | bytes 655392 | tf_op jit(solution)/shard_map/ppermute | solution.py:507
  41.5 1.4 collective-permute-start.10
  43.5 1.5 tables.1.table
  46.5 1.5 collective-permute-start.9
  48.2 13.9 %collective-permute-done.9.refs_1_.refs_5_ = bf16[64,2560]{1,0:T(8,128)(2,1)S(1)} collective-permute-done((bf16[64,2560]{1,0:T(8,128)(2,1)}, bf16[64,2560]{1,0:T(8,128)(2,1)S(1)}, u32[]{:S(2)}, u32[]{:S(2)}) %collective-permute-start.9) | collective-permute-done | bytes 327712 | tf_op jit(solution)/shard_map/ppermute | solution.py:507
  65.9 8.4 %keys_values.2 = (bf16[256,2560]{1,0:T(8,128)(2,1)S(1)}, bf16[256,2560]{1,0:T(8,128)(2,1)S(1)}, bf16[2,256,512]{2,1,0:T(8,128)(2,1)S(1)}) custom-call(s32[130]{0:T(256)S(1)} %copy-done.22, bf16[64,2560]{1,0:T(8,128)(2,1)S(1)} %get-tuple-element.89.refs_0_, bf16[64,2560]{1,0:T(8,128)(2,1)S(1)} %get-tuple-element.96.refs_1_, ...), custom_call_target="tpu_custom_call" | custom-call | flops 53687092 | bytes 314572 | tf_op jit(solution)/shard_map/keys_values/pallas_call | solution.py:179
  75.0 3.4 %collective-permute-done.11.refs_2_.refs_6_ = bf16[64,2560]{1,0:T(8,128)(2,1)S(1)} collective-permute-done((bf16[64,2560]{1,0:T(8,128)(2,1)}, bf16[64,2560]{1,0:T(8,128)(2,1)S(1)}, u32[]{:S(2)}, u32[]{:S(2)}) %collective-permute-start.11) | collective-permute-done | bytes 327712 | tf_op jit(solution)/shard_map/ppermute | solution.py:507
  79.6 5.4 %collective-permute-done.12.refs_4_ = bf16[64,2560]{1,0:T(8,128)(2,1)S(1)} collective-permute-done((bf16[64,2560]{1,0:T(8,128)(2,1)S(1)}, bf16[64,2560]{1,0:T(8,128)(2,1)S(1)}, u32[]{:S(2)}, u32[]{:S(2)}) %collective-permute-start.12) | collective-permute-done | bytes 327712 | tf_op jit(solution)/shard_map/ppermute | solution.py:547
  85.0 4.6 %collective-permute-done.13.refs_5_ = bf16[64,2560]{1,0:T(8,128)(2,1)S(1)} collective-permute-done((bf16[64,2560]{1,0:T(8,128)(2,1)S(1)}, bf16[64,2560]{1,0:T(8,128)(2,1)S(1)}, u32[]{:S(2)}, u32[]{:S(2)}) %collective-permute-start.13) | collective-permute-done | bytes 327712 | tf_op jit(solution)/shard_map/ppermute | solution.py:547
  89.7 8.0 %keys_values.3 = (bf16[256,2560]{1,0:T(8,128)(2,1)S(1)}, bf16[256,2560]{1,0:T(8,128)(2,1)S(1)}, bf16[2,256,512]{2,1,0:T(8,128)(2,1)S(1)}) custom-call(s32[130]{0:T(256)S(1)} %copy-done.22, bf16[128,2560]{1,0:T(8,128)(2,1)S(1)} %collective-permute-done.6.refs_0_.refs_4_, bf16[64,2560]{1,0:T(8,128)(2,1)S(1)} %collective-permute-done.9.refs_1_.refs_5_, ...), custom_call_target="tpu_custom_call" | custom-call | flops 53687092 | bytes 314572 | tf_op jit(solution)/shard_map/keys_values/pallas_call | solution.py:179
  97.6 4.3 %collective-permute-start.17 = (bf16[2,4,64,512]{3,2,1,0:T(8,128)(2,1)S(1)}, bf16[2,4,64,512]{3,2,1,0:T(8,128)(2,1)S(1)}, u32[]{:S(2)}, u32[]{:S(2)}) collective-permute-start(bf16[2,4,64,512]{3,2,1,0:T(8,128)(2,1)S(1)} %bitcast.48), channel_id=1, source_target_pairs={{0,2},{1,3},{2,4},{3,5},{4,6},{5,7},{6,0},{7,1},{8,10},{9,11},{10,... | collective-permute-start | bytes 1572872 | tf_op jit(solution)/shard_map/ppermute | solution.py:507
  102.0 11.3 %queries.2 = bf16[256,2048]{1,0:T(8,128)(2,1)S(1)} custom-call(s32[130]{0:T(256)S(1)} %copy-done.22, bf16[256,2560]{1,0:T(8,128)(2,1)S(1)} %get-tuple-element.46.refs_0_, bf16[256,2560]{1,0:T(8,128)(2,1)S(1)} %get-tuple-element.47.refs_1_, bf16[5120,2048]{1,0:T(8,128)(2,1)} %refs_3_.3, bf16[5120,2048]{1,0:T(8,128)(2,1)} %refs_3_.3, ...), custom_call_target="tpu_custom_call" | custom-call | flops 107374184 | bytes 492830 | tf_op jit(solution)/shard_map/queries/pallas_call | solution.py:236
  113.3 11.3 %queries.3 = bf16[256,2048]{1,0:T(8,128)(2,1)S(1)} custom-call(s32[130]{0:T(256)S(1)} %copy-done.22, bf16[256,2560]{1,0:T(8,128)(2,1)S(1)} %get-tuple-element.52.refs_0_, bf16[256,2560]{1,0:T(8,128)(2,1)S(1)} %get-tuple-element.53.refs_1_, bf16[5120,2048]{1,0:T(8,128)(2,1)} %refs_3_.3, bf16[5120,2048]{1,0:T(8,128)(2,1)} %refs_3_.3, ...), custom_call_target="tpu_custom_call" | custom-call | flops 107374184 | bytes 492830 | tf_op jit(solution)/shard_map/queries/pallas_call | solution.py:236
  126.2 15.2 %collective-permute-done.21.refs_11_ = bf16[2,4,64,512]{3,2,1,0:T(8,128)(2,1)S(1)} collective-permute-done((bf16[2,4,64,512]{3,2,1,0:T(8,128)(2,1)S(1)}, bf16[2,4,64,512]{3,2,1,0:T(8,128)(2,1)S(1)}, u32[]{:S(2)}, u32[]{:S(2)}) %collective-permute-start.21) | collective-permute-done | bytes 524320 | tf_op jit(solution)/shard_map/ppermute | solution.py:507
  141.9 10.7 %collective-permute-done.24.refs_14_ = bf16[2,4,64,512]{3,2,1,0:T(8,128)(2,1)S(1)} collective-permute-done((bf16[2,4,64,512]{3,2,1,0:T(8,128)(2,1)S(1)}, bf16[2,4,64,512]{3,2,1,0:T(8,128)(2,1)S(1)}, u32[]{:S(2)}, u32[]{:S(2)}) %collective-permute-start.24) | collective-permute-done | bytes 524320 | tf_op jit(solution)/shard_map/ppermute | solution.py:507
  153.1 8.2 %collective-permute-done.25.refs_15_ = bf16[2,4,64,512]{3,2,1,0:T(8,128)(2,1)S(1)} collective-permute-done((bf16[2,4,64,512]{3,2,1,0:T(8,128)(2,1)S(1)}, bf16[2,4,64,512]{3,2,1,0:T(8,128)(2,1)S(1)}, u32[]{:S(2)}, u32[]{:S(2)}) %collective-permute-start.25) | collective-permute-done | bytes 524320 | tf_op jit(solution)/shard_map/ppermute | solution.py:507
  161.4 1.9 collective-permute-done.27.refs_17_
  163.3 13.3 %attention.2 = (bf16[8,64,1024]{2,1,0:T(8,128)(2,1)S(1)}, bf16[4,2,128,256]{3,2,1,0:T(8,128)(2,1)S(1)}) custom-call(s32[130]{0:T(256)S(1)} %copy-done.23, bf16[4,64,2048]{2,1,0:T(8,128)(2,1)S(1)} %bitcast.40, bf16[4,64,2048]{2,1,0:T(8,128)(2,1)S(1)} %bitcast.42, bf16[2,4,64,512]{3,2,1,0:T(8,128)(2,1)S(1)} %bitcast.46, bf16[2,4,64,512]{3,2,1,0:T(8,128)(2,1)S(1)} %bitcast.50, ...), custom_call_target="tpu_custom_call" | custom-call | flops 47244640 | bytes 251658 | tf_op jit(solution)/shard_map/attention/pallas_call | solution.py:342
  177.6 13.9 %attention.3 = (bf16[8,64,1024]{2,1,0:T(8,128)(2,1)S(1)}, bf16[4,2,128,256]{3,2,1,0:T(8,128)(2,1)}) custom-call(s32[130]{0:T(256)S(1)} %copy-done.23, bf16[4,64,2048]{2,1,0:T(8,128)(2,1)S(1)} %bitcast.41, bf16[4,64,2048]{2,1,0:T(8,128)(2,1)S(1)} %bitcast.43, bf16[2,4,64,512]{3,2,1,0:T(8,128)(2,1)S(1)} %bitcast.47, bf16[2,4,64,512]{3,2,1,0:T(8,128)(2,1)S(1)} %bitcast.51, ...), custom_call_target="tpu_custom_call" | custom-call | flops 47244640 | bytes 251658 | tf_op jit(solution)/shard_map/attention/pallas_call | solution.py:342
  191.5 5.0 %send_part.2.refs_3_ = bf16[512,1024]{1,0:T(8,128)(2,1)S(1)} custom-call(s32[130]{0:T(256)S(1)} %copy-done.23, bf16[512,1024]{1,0:T(8,128)(2,1)S(1)} %bitcast.34, bf16[512,1024]{1,0:T(8,128)(2,1)S(1)} %bitcast.37, bf16[2048,5120]{1,0:T(8,128)(2,1)} %refs_2_.9, bf16[4,2,128,256]{3,2,1,0:T(8,128)(2,1)S(1)} %collective-permute-done.28.refs_3_), custom_call_target="tpu_custom_call" | custom-call | flops 42949672 | bytes 146800 | tf_op jit(solution)/shard_map/send_part/pallas_call | solution.py:392
  197.6 6.4 %send_part.3 = (bf16[512,1024]{1,0:T(8,128)(2,1)S(1)}, bf16[512,512]{1,0:T(8,128)(2,1)S(1)}) custom-call(s32[130]{0:T(256)S(1)} %copy-done.23, bf16[512,1024]{1,0:T(8,128)(2,1)S(1)} %bitcast.35, bf16[512,1024]{1,0:T(8,128)(2,1)S(1)} %bitcast.38, bf16[2048,5120]{1,0:T(8,128)(2,1)} %refs_2_.9, bf16[512,1024]{1,0:T(8,128)(2,1)S(1)} %send_part.2.refs_3_), custom_call_target="tpu_custom_call" | custom-call | flops 64424508 | bytes 199229 | tf_op jit(solution)/shard_map/send_part/pallas_call | solution.py:392
  204.0 9.3 %own_part.1 = (bf16[512,1024]{1,0:T(8,128)(2,1)S(1)}, bf16[512,1024]{1,0:T(8,128)(2,1)S(1)}, bf16[512,512]{1,0:T(8,128)(2,1)S(1)}) custom-call(s32[130]{0:T(256)S(1)} %copy-done.23, bf16[512,1024]{1,0:T(8,128)(2,1)S(1)} %bitcast.36, bf16[512,1024]{1,0:T(8,128)(2,1)S(1)} %bitcast.39, bf16[2048,5120]{1,0:T(8,128)(2,1)} %refs_2_.9, ...), custom_call_target="tpu_custom_call" | custom-call | flops 107374184 | bytes 304087 | tf_op jit(solution)/shard_map/own_part/pallas_call | solution.py:392
  213.3 8.1 %collective-permute-done.29 = bf16[512,1024]{1,0:T(8,128)(2,1)S(1)} collective-permute-done((bf16[512,1024]{1,0:T(8,128)(2,1)S(1)}, bf16[512,1024]{1,0:T(8,128)(2,1)S(1)}, u32[]{:S(2)}, u32[]{:S(2)}) %collective-permute-start.29) | collective-permute-done | bytes 1048608 | tf_op jit(solution)/shard_map/ppermute | solution.py:547
  222.5 1.1 residual.3
  223.7 3.8 %collective-permute-start.32 = (bf16[2,64,1024]{2,1,0:T(8,128)(2,1)S(1)}, bf16[2,64,1024]{2,1,0:T(8,128)(2,1)S(1)}, u32[]{:S(2)}, u32[]{:S(2)}) collective-permute-start(bf16[2,64,1024]{2,1,0:T(8,128)(2,1)S(1)} %get-tuple-element.69), channel_id=1, source_target_pairs={{0,6},{1,7},{2,0},{3,1},{4,2},{5,3},{6,4},{7,5},{8,14},{9,15},{10,... | collective-permute-start | bytes 786440 | tf_op jit(solution)/shard_map/ppermute | solution.py:507
  227.5 7.2 %collective-permute-done.31.refs_1_ = bf16[2,64,1024]{2,1,0:T(8,128)(2,1)S(1)} collective-permute-done((bf16[2,64,1024]{2,1,0:T(8,128)(2,1)S(1)}, bf16[2,64,1024]{2,1,0:T(8,128)(2,1)S(1)}, u32[]{:S(2)}, u32[]{:S(2)}) %collective-permute-start.31) | collective-permute-done | bytes 262176 | tf_op jit(solution)/shard_map/ppermute | solution.py:507
  234.8 2.4 collective-permute-done.32.refs_2_
  237.2 10.5 %collective-permute-done.33.refs_3_ = bf16[2,64,1024]{2,1,0:T(8,128)(2,1)S(1)} collective-permute-done((bf16[2,64,1024]{2,1,0:T(8,128)(2,1)S(1)}, bf16[2,64,1024]{2,1,0:T(8,128)(2,1)S(1)}, u32[]{:S(2)}, u32[]{:S(2)}) %collective-permute-start.33) | collective-permute-done | bytes 262176 | tf_op jit(solution)/shard_map/ppermute | solution.py:507
  249.9 3.8 %collective-permute-start.40 = (bf16[2,64,1024]{2,1,0:T(8,128)(2,1)S(1)}, bf16[2,64,1024]{2,1,0:T(8,128)(2,1)S(1)}, u32[]{:S(2)}, u32[]{:S(2)}) collective-permute-start(bf16[2,64,1024]{2,1,0:T(8,128)(2,1)S(1)} %get-tuple-element.78), channel_id=1, source_target_pairs={{0,6},{1,7},{2,0},{3,1},{4,2},{5,3},{6,4},{7,5},{8,14},{9,15},{10,... | collective-permute-start | bytes 786440 | tf_op jit(solution)/shard_map/ppermute | solution.py:507
  253.7 6.1 %collective-permute-done.34 = bf16[512,512]{1,0:T(8,128)(2,1)S(1)} collective-permute-done((bf16[512,512]{1,0:T(8,128)(2,1)S(1)}, bf16[512,512]{1,0:T(8,128)(2,1)S(1)}, u32[]{:S(2)}, u32[]{:S(2)}) %collective-permute-start.34) | collective-permute-done | bytes 524320 | tf_op jit(solution)/shard_map/ppermute | solution.py:547
  259.8 1.5 residual.4
  264.5 11.8 %collective-permute-done.41.refs_3_ = bf16[2,64,1024]{2,1,0:T(8,128)(2,1)S(1)} collective-permute-done((bf16[2,64,1024]{2,1,0:T(8,128)(2,1)S(1)}, bf16[2,64,1024]{2,1,0:T(8,128)(2,1)S(1)}, u32[]{:S(2)}, u32[]{:S(2)}) %collective-permute-start.41) | collective-permute-done | bytes 262176 | tf_op jit(solution)/shard_map/ppermute | solution.py:507
  279.8 3.8 %collective-permute-done.36.refs_2_ = bf16[2,64,512]{2,1,0:T(8,128)(2,1)S(1)} collective-permute-done((bf16[2,64,512]{2,1,0:T(8,128)(2,1)}, bf16[2,64,512]{2,1,0:T(8,128)(2,1)S(1)}, u32[]{:S(2)}, u32[]{:S(2)}) %collective-permute-start.36) | collective-permute-done | bytes 131104 | tf_op jit(solution)/shard_map/ppermute | solution.py:507
  283.9 1.6 placed.3.refs_5_
  285.6 2.6 placed.4.refs_5_
  288.2 1.4 placed.5
  289.6 3.0 %collective-permute-done.44 = bf16[4,2,128,256]{3,2,1,0:T(8,128)(2,1)} collective-permute-done((bf16[4,2,128,256]{3,2,1,0:T(8,128)(2,1)}, bf16[4,2,128,256]{3,2,1,0:T(8,128)(2,1)}, u32[]{:S(2)}, u32[]{:S(2)}) %collective-permute-start.44) | collective-permute-done | bytes 524320 | tf_op jit(solution)/shard_map/ppermute | solution.py:547
  292.6 1.3 broadcast_select_fusion.2
  293.9 1.6 pad_maximum_fusion
  (145 shorter events, 27.9 us)
Async XLA Ops:
  3.5 6.3 %collective-permute-start = (bf16[3,64,2560]{2,1,0:T(8,128)(2,1)S(1)}, bf16[3,64,2560]{2,1,0:T(8,128)(2,1)S(1)}, u32[]{:S(2)}, u32[]{:S(2)}) collective-permute-start(bf16[3,64,2560]{2,1,0:T(8,128)(2,1)S(1)} %pad_maximum_fusion.1), channel_id=1, source_target_pairs={{0,1},{1,0},{2,3},{3,2},{4,5},{5,4},{6,7},{7,6},{8,9},{9,8},{10,11... | collective-permute-start | bytes 2949128 | tf_op jit(solution)/shard_map/ppermute | solution.py:507
  4.0 12.7 %collective-permute-start.2 = (bf16[64,2560]{1,0:T(8,128)(2,1)S(1)}, bf16[64,2560]{1,0:T(8,128)(2,1)S(1)}, u32[]{:S(2)}, u32[]{:S(2)}) collective-permute-start(bf16[64,2560]{1,0:T(8,128)(2,1)S(1)} %get-tuple-element.84), channel_id=1, source_target_pairs={{0,3},{1,2},{2,5},{3,4},{4,7},{5,6},{6,1},{7,0},{8,11},{9,10},{10,... | collective-permute-start | bytes 983048 | tf_op jit(solution)/shard_map/ppermute | solution.py:507
  6.7 17.3 %collective-permute-start.1 = (bf16[64,2560]{1,0:T(8,128)(2,1)S(1)}, bf16[64,2560]{1,0:T(8,128)(2,1)S(1)}, u32[]{:S(2)}, u32[]{:S(2)}) collective-permute-start(bf16[64,2560]{1,0:T(8,128)(2,1)S(1)} %get-tuple-element.85), channel_id=1, source_target_pairs={{0,2},{1,3},{2,4},{3,5},{4,6},{5,7},{6,0},{7,1},{8,10},{9,11},{10,... | collective-permute-start | bytes 983048 | tf_op jit(solution)/shard_map/ppermute | solution.py:507
  8.3 15.7 %collective-permute-start.3 = (bf16[64,2560]{1,0:T(8,128)(2,1)S(1)}, bf16[64,2560]{1,0:T(8,128)(2,1)S(1)}, u32[]{:S(2)}, u32[]{:S(2)}) collective-permute-start(bf16[64,2560]{1,0:T(8,128)(2,1)S(1)} %get-tuple-element.89.refs_0_), channel_id=1, source_target_pairs={{0,8},{8,0},{1,9},{9,1},{2,10},{10,2},{3,11},{11,3},{4,12},{12,4},... | collective-permute-start | bytes 983048 | tf_op jit(solution)/shard_map/ppermute | solution.py:547
  9.8 53.5 %copy-start.24 = (bf16[128]{0:T(256)(128)(2,1)S(1)}, bf16[128]{0:T(256)(128)(2,1)}, u32[]{:S(2)}) copy-start(bf16[128]{0:T(256)(128)(2,1)} %param.18) | copy-start | bytes 772
  9.8 14.2 %collective-permute-start.5 = (bf16[1,2560]{1,0:T(2,128)(2,1)S(1)}, bf16[1,2560]{1,0:T(2,128)(2,1)S(1)}, u32[]{:S(2)}, u32[]{:S(2)}) collective-permute-start(bf16[1,2560]{1,0:T(2,128)(2,1)S(1)} %broadcast_in_dim.6.refs_8_.refs_6_), channel_id=1, source_target_pairs={{0,8},{8,0},{1,9},{9,1},{2,10},{10,2},{3,11},{11,3},{4,12},{12,4},... | collective-permute-start | bytes 15368 | tf_op jit(solution)/shard_map/ppermute | solution.py:547
  11.2 13.7 %collective-permute-start.4 = (bf16[64,2560]{1,0:T(8,128)(2,1)S(1)}, bf16[64,2560]{1,0:T(8,128)(2,1)S(1)}, u32[]{:S(2)}, u32[]{:S(2)}) collective-permute-start(bf16[64,2560]{1,0:T(8,128)(2,1)S(1)} %get-tuple-element.96.refs_1_), channel_id=1, source_target_pairs={{0,8},{8,0},{1,9},{9,1},{2,10},{10,2},{3,11},{11,3},{4,12},{12,4},... | collective-permute-start | bytes 983048 | tf_op jit(solution)/shard_map/ppermute | solution.py:547
  25.7 15.8 %collective-permute-start.6 = (bf16[128,2560]{1,0:T(8,128)(2,1)}, bf16[128,2560]{1,0:T(8,128)(2,1)S(1)}, u32[]{:S(2)}, u32[]{:S(2)}) collective-permute-start(bf16[128,2560]{1,0:T(8,128)(2,1)} %pad_maximum_fusion.2), channel_id=1, source_target_pairs={{0,6},{1,7},{2,0},{3,1},{4,2},{5,3},{6,4},{7,5},{8,14},{9,15},{10,... | collective-permute-start | bytes 1966088 | tf_op jit(solution)/shard_map/ppermute | solution.py:507
  27.9 17.9 %collective-permute-start.8 = (bf16[64,2560]{1,0:T(8,128)(2,1)S(1)}, bf16[64,2560]{1,0:T(8,128)(2,1)S(1)}, u32[]{:S(2)}, u32[]{:S(2)}) collective-permute-start(bf16[64,2560]{1,0:T(8,128)(2,1)S(1)} %collective-permute-done.2.refs_3_), channel_id=1, source_target_pairs={{0,8},{8,0},{1,9},{9,1},{2,10},{10,2},{3,11},{11,3},{4,12},{12,4},... | collective-permute-start | bytes 983048 | tf_op jit(solution)/shard_map/ppermute | solution.py:547
  29.4 17.1 %collective-permute-start.7 = (bf16[64,2560]{1,0:T(8,128)(2,1)S(1)}, bf16[64,2560]{1,0:T(8,128)(2,1)}, u32[]{:S(2)}, u32[]{:S(2)}) collective-permute-start(bf16[64,2560]{1,0:T(8,128)(2,1)S(1)} %collective-permute-done.1.refs_2_), channel_id=1, source_target_pairs={{0,8},{8,0},{1,9},{9,1},{2,10},{10,2},{3,11},{11,3},{4,12},{12,4},... | collective-permute-start | bytes 983048 | tf_op jit(solution)/shard_map/ppermute | solution.py:547
  41.5 20.6 %collective-permute-start.10 = (bf16[128,2560]{1,0:T(8,128)(2,1)S(1)}, bf16[128,2560]{1,0:T(8,128)(2,1)S(1)}, u32[]{:S(2)}, u32[]{:S(2)}) collective-permute-start(bf16[128,2560]{1,0:T(8,128)(2,1)S(1)} %collective-permute-done.6.refs_0_.refs_4_), channel_id=1, source_target_pairs={{0,8},{8,0},{1,9},{9,1},{2,10},{10,2},{3,11},{11,3},{4,12},{12,4},... | collective-permute-start | bytes 1966088 | tf_op jit(solution)/shard_map/ppermute | solution.py:547
  46.5 15.6 %collective-permute-start.9 = (bf16[64,2560]{1,0:T(8,128)(2,1)}, bf16[64,2560]{1,0:T(8,128)(2,1)S(1)}, u32[]{:S(2)}, u32[]{:S(2)}) collective-permute-start(bf16[64,2560]{1,0:T(8,128)(2,1)} %get-tuple-element.44), channel_id=1, source_target_pairs={{0,4},{1,5},{2,6},{3,7},{4,0},{5,1},{6,2},{7,3},{8,12},{9,13},{10,... | collective-permute-start | bytes 983048 | tf_op jit(solution)/shard_map/ppermute | solution.py:507
  62.1 16.4 %collective-permute-start.11 = (bf16[64,2560]{1,0:T(8,128)(2,1)}, bf16[64,2560]{1,0:T(8,128)(2,1)S(1)}, u32[]{:S(2)}, u32[]{:S(2)}) collective-permute-start(bf16[64,2560]{1,0:T(8,128)(2,1)} %get-tuple-element.45), channel_id=1, source_target_pairs={{0,4},{1,5},{2,6},{3,7},{4,0},{5,1},{6,2},{7,3},{8,12},{9,13},{10,... | collective-permute-start | bytes 983048 | tf_op jit(solution)/shard_map/ppermute | solution.py:507
  74.3 10.7 %collective-permute-start.12 = (bf16[64,2560]{1,0:T(8,128)(2,1)S(1)}, bf16[64,2560]{1,0:T(8,128)(2,1)S(1)}, u32[]{:S(2)}, u32[]{:S(2)}) collective-permute-start(bf16[64,2560]{1,0:T(8,128)(2,1)S(1)} %collective-permute-done.9.refs_1_.refs_5_), channel_id=1, source_target_pairs={{0,8},{8,0},{1,9},{9,1},{2,10},{10,2},{3,11},{11,3},{4,12},{12,4},... | collective-permute-start | bytes 983048 | tf_op jit(solution)/shard_map/ppermute | solution.py:547
  78.5 23.5 %copy-start.25 = (bf16[128]{0:T(256)(128)(2,1)S(1)}, bf16[128]{0:T(256)(128)(2,1)}, u32[]{:S(2)}) copy-start(bf16[128]{0:T(256)(128)(2,1)} %param.17) | copy-start | bytes 772
  78.5 11.2 %collective-permute-start.13 = (bf16[64,2560]{1,0:T(8,128)(2,1)S(1)}, bf16[64,2560]{1,0:T(8,128)(2,1)S(1)}, u32[]{:S(2)}, u32[]{:S(2)}) collective-permute-start(bf16[64,2560]{1,0:T(8,128)(2,1)S(1)} %collective-permute-done.11.refs_2_.refs_6_), channel_id=1, source_target_pairs={{0,8},{8,0},{1,9},{9,1},{2,10},{10,2},{3,11},{11,3},{4,12},{12,4},... | collective-permute-start | bytes 983048 | tf_op jit(solution)/shard_map/ppermute | solution.py:547
  79.2 22.7 %collective-permute-start.16 = (bf16[2,4,64,512]{3,2,1,0:T(8,128)(2,1)S(1)}, bf16[2,4,64,512]{3,2,1,0:T(8,128)(2,1)S(1)}, u32[]{:S(2)}, u32[]{:S(2)}) collective-permute-start(bf16[2,4,64,512]{3,2,1,0:T(8,128)(2,1)S(1)} %bitcast.44), channel_id=1, source_target_pairs={{0,2},{1,3},{2,4},{3,5},{4,6},{5,7},{6,0},{7,1},{8,10},{9,11},{10,... | collective-permute-start | bytes 1572872 | tf_op jit(solution)/shard_map/ppermute | solution.py:507
  97.6 27.0 %collective-permute-start.17 = (bf16[2,4,64,512]{3,2,1,0:T(8,128)(2,1)S(1)}, bf16[2,4,64,512]{3,2,1,0:T(8,128)(2,1)S(1)}, u32[]{:S(2)}, u32[]{:S(2)}) collective-permute-start(bf16[2,4,64,512]{3,2,1,0:T(8,128)(2,1)S(1)} %bitcast.48), channel_id=1, source_target_pairs={{0,2},{1,3},{2,4},{3,5},{4,6},{5,7},{6,0},{7,1},{8,10},{9,11},{10,... | collective-permute-start | bytes 1572872 | tf_op jit(solution)/shard_map/ppermute | solution.py:507
  101.9 24.1 %collective-permute-start.20 = (bf16[2,4,64,512]{3,2,1,0:T(8,128)(2,1)S(1)}, bf16[2,4,64,512]{3,2,1,0:T(8,128)(2,1)S(1)}, u32[]{:S(2)}, u32[]{:S(2)}) collective-permute-start(bf16[2,4,64,512]{3,2,1,0:T(8,128)(2,1)S(1)} %collective-permute-done.16.refs_6_), channel_id=1, source_target_pairs={{0,2},{1,3},{2,4},{3,5},{4,6},{5,7},{6,0},{7,1},{8,10},{9,11},{10,... | collective-permute-start | bytes 1572872 | tf_op jit(solution)/shard_map/ppermute | solution.py:507
  113.3 49.9 %copy-start.23 = (s32[130]{0:T(256)S(1)}, s32[130]{0:T(256)}, u32[]{:S(2)}) copy-start(s32[130]{0:T(256)} %tables.1.table) | copy-start | bytes 1564
  124.7 16.7 %collective-permute-start.21 = (bf16[2,4,64,512]{3,2,1,0:T(8,128)(2,1)S(1)}, bf16[2,4,64,512]{3,2,1,0:T(8,128)(2,1)S(1)}, u32[]{:S(2)}, u32[]{:S(2)}) collective-permute-start(bf16[2,4,64,512]{3,2,1,0:T(8,128)(2,1)S(1)} %collective-permute-done.17.refs_7_), channel_id=1, source_target_pairs={{0,2},{1,3},{2,4},{3,5},{4,6},{5,7},{6,0},{7,1},{8,10},{9,11},{10,... | collective-permute-start | bytes 1572872 | tf_op jit(solution)/shard_map/ppermute | solution.py:507
  125.5 15.9 %collective-permute-start.14 = (bf16[2,4,64,512]{3,2,1,0:T(8,128)(2,1)S(1)}, bf16[2,4,64,512]{3,2,1,0:T(8,128)(2,1)S(1)}, u32[]{:S(2)}, u32[]{:S(2)}) collective-permute-start(bf16[2,4,64,512]{3,2,1,0:T(8,128)(2,1)S(1)} %bitcast.45), channel_id=1, source_target_pairs={{0,1},{1,0},{2,3},{3,2},{4,5},{5,4},{6,7},{7,6},{8,9},{9,8},{10,11... | collective-permute-start | bytes 1572872 | tf_op jit(solution)/shard_map/ppermute | solution.py:507
  125.5 15.9 %collective-permute-start.18 = (bf16[2,4,64,512]{3,2,1,0:T(8,128)(2,1)S(1)}, bf16[2,4,64,512]{3,2,1,0:T(8,128)(2,1)S(1)}, u32[]{:S(2)}, u32[]{:S(2)}) collective-permute-start(bf16[2,4,64,512]{3,2,1,0:T(8,128)(2,1)S(1)} %collective-permute-done.16.refs_6_), channel_id=1, source_target_pairs={{0,1},{1,0},{2,3},{3,2},{4,5},{5,4},{6,7},{7,6},{8,9},{9,8},{10,11... | collective-permute-start | bytes 1572872 | tf_op jit(solution)/shard_map/ppermute | solution.py:507
  126.0 26.6 %collective-permute-start.22 = (bf16[2,4,64,512]{3,2,1,0:T(8,128)(2,1)S(1)}, bf16[2,4,64,512]{3,2,1,0:T(8,128)(2,1)S(1)}, u32[]{:S(2)}, u32[]{:S(2)}) collective-permute-start(bf16[2,4,64,512]{3,2,1,0:T(8,128)(2,1)S(1)} %collective-permute-done.20.refs_10_), channel_id=1, source_target_pairs={{0,1},{1,0},{2,3},{3,2},{4,5},{5,4},{6,7},{7,6},{8,9},{9,8},{10,11... | collective-permute-start | bytes 1572872 | tf_op jit(solution)/shard_map/ppermute | solution.py:507
  126.0 26.6 %collective-permute-start.24 = (bf16[2,4,64,512]{3,2,1,0:T(8,128)(2,1)S(1)}, bf16[2,4,64,512]{3,2,1,0:T(8,128)(2,1)S(1)}, u32[]{:S(2)}, u32[]{:S(2)}) collective-permute-start(bf16[2,4,64,512]{3,2,1,0:T(8,128)(2,1)S(1)} %collective-permute-done.20.refs_10_), channel_id=1, source_target_pairs={{0,2},{1,3},{2,4},{3,5},{4,6},{5,7},{6,0},{7,1},{8,10},{9,11},{10,... | collective-permute-start | bytes 1572872 | tf_op jit(solution)/shard_map/ppermute | solution.py:507
  141.4 20.0 %collective-permute-start.25 = (bf16[2,4,64,512]{3,2,1,0:T(8,128)(2,1)S(1)}, bf16[2,4,64,512]{3,2,1,0:T(8,128)(2,1)S(1)}, u32[]{:S(2)}, u32[]{:S(2)}) collective-permute-start(bf16[2,4,64,512]{3,2,1,0:T(8,128)(2,1)S(1)} %collective-permute-done.21.refs_11_), channel_id=1, source_target_pairs={{0,2},{1,3},{2,4},{3,5},{4,6},{5,7},{6,0},{7,1},{8,10},{9,11},{10,... | collective-permute-start | bytes 1572872 | tf_op jit(solution)/shard_map/ppermute | solution.py:507
  141.4 20.0 %collective-permute-start.15 = (bf16[2,4,64,512]{3,2,1,0:T(8,128)(2,1)S(1)}, bf16[2,4,64,512]{3,2,1,0:T(8,128)(2,1)S(1)}, u32[]{:S(2)}, u32[]{:S(2)}) collective-permute-start(bf16[2,4,64,512]{3,2,1,0:T(8,128)(2,1)S(1)} %bitcast.49), channel_id=1, source_target_pairs={{0,1},{1,0},{2,3},{3,2},{4,5},{5,4},{6,7},{7,6},{8,9},{9,8},{10,11... | collective-permute-start | bytes 1572872 | tf_op jit(solution)/shard_map/ppermute | solution.py:507
  141.4 20.0 %collective-permute-start.19 = (bf16[2,4,64,512]{3,2,1,0:T(8,128)(2,1)S(1)}, bf16[2,4,64,512]{3,2,1,0:T(8,128)(2,1)S(1)}, u32[]{:S(2)}, u32[]{:S(2)}) collective-permute-start(bf16[2,4,64,512]{3,2,1,0:T(8,128)(2,1)S(1)} %collective-permute-done.17.refs_7_), channel_id=1, source_target_pairs={{0,1},{1,0},{2,3},{3,2},{4,5},{5,4},{6,7},{7,6},{8,9},{9,8},{10,11... | collective-permute-start | bytes 1572872 | tf_op jit(solution)/shard_map/ppermute | solution.py:507
  152.6 8.7 %collective-permute-start.26 = (bf16[2,4,64,512]{3,2,1,0:T(8,128)(2,1)S(1)}, bf16[2,4,64,512]{3,2,1,0:T(8,128)(2,1)S(1)}, u32[]{:S(2)}, u32[]{:S(2)}) collective-permute-start(bf16[2,4,64,512]{3,2,1,0:T(8,128)(2,1)S(1)} %collective-permute-done.24.refs_14_), channel_id=1, source_target_pairs={{0,1},{1,0},{2,3},{3,2},{4,5},{5,4},{6,7},{7,6},{8,9},{9,8},{10,11... | collective-permute-start | bytes 1572872 | tf_op jit(solution)/shard_map/ppermute | solution.py:507
  152.6 8.8 %collective-permute-start.23 = (bf16[2,4,64,512]{3,2,1,0:T(8,128)(2,1)S(1)}, bf16[2,4,64,512]{3,2,1,0:T(8,128)(2,1)S(1)}, u32[]{:S(2)}, u32[]{:S(2)}) collective-permute-start(bf16[2,4,64,512]{3,2,1,0:T(8,128)(2,1)S(1)} %collective-permute-done.21.refs_11_), channel_id=1, source_target_pairs={{0,1},{1,0},{2,3},{3,2},{4,5},{5,4},{6,7},{7,6},{8,9},{9,8},{10,11... | collective-permute-start | bytes 1572872 | tf_op jit(solution)/shard_map/ppermute | solution.py:507
  161.3 1.9 collective-permute-start.27
  176.5 14.9 %collective-permute-start.28 = (bf16[4,2,128,256]{3,2,1,0:T(8,128)(2,1)S(1)}, bf16[4,2,128,256]{3,2,1,0:T(8,128)(2,1)S(1)}, u32[]{:S(2)}, u32[]{:S(2)}) collective-permute-start(bf16[4,2,128,256]{3,2,1,0:T(8,128)(2,1)S(1)} %get-tuple-element.60), channel_id=1, source_target_pairs={{0,8},{8,0},{1,9},{9,1},{2,10},{10,2},{3,11},{11,3},{4,12},{12,4},... | collective-permute-start | bytes 1572872 | tf_op jit(solution)/shard_map/ppermute | solution.py:547
  196.5 25.0 %collective-permute-start.29 = (bf16[512,1024]{1,0:T(8,128)(2,1)S(1)}, bf16[512,1024]{1,0:T(8,128)(2,1)S(1)}, u32[]{:S(2)}, u32[]{:S(2)}) collective-permute-start(bf16[512,1024]{1,0:T(8,128)(2,1)S(1)} %send_part.2.refs_3_), channel_id=1, source_target_pairs={{0,8},{8,0},{1,9},{9,1},{2,10},{10,2},{3,11},{11,3},{4,12},{12,4},... | collective-permute-start | bytes 3145736 | tf_op jit(solution)/shard_map/ppermute | solution.py:547
  221.4 26.2 %collective-permute-start.30 = (bf16[512,1024]{1,0:T(8,128)(2,1)S(1)}, bf16[512,1024]{1,0:T(8,128)(2,1)S(1)}, u32[]{:S(2)}, u32[]{:S(2)}) collective-permute-start(bf16[512,1024]{1,0:T(8,128)(2,1)S(1)} %get-tuple-element.66), channel_id=1, source_target_pairs={{0,8},{8,0},{1,9},{9,1},{2,10},{10,2},{3,11},{11,3},{4,12},{12,4},... | collective-permute-start | bytes 3145736 | tf_op jit(solution)/shard_map/ppermute | solution.py:547
  223.7 11.1 %collective-permute-start.31 = (bf16[2,64,1024]{2,1,0:T(8,128)(2,1)S(1)}, bf16[2,64,1024]{2,1,0:T(8,128)(2,1)S(1)}, u32[]{:S(2)}, u32[]{:S(2)}) collective-permute-start(bf16[2,64,1024]{2,1,0:T(8,128)(2,1)S(1)} %get-tuple-element.68), channel_id=1, source_target_pairs={{0,2},{1,3},{2,4},{3,5},{4,6},{5,7},{6,0},{7,1},{8,10},{9,11},{10,... | collective-permute-start | bytes 786440 | tf_op jit(solution)/shard_map/ppermute | solution.py:507
  223.7 13.5 %collective-permute-start.32 = (bf16[2,64,1024]{2,1,0:T(8,128)(2,1)S(1)}, bf16[2,64,1024]{2,1,0:T(8,128)(2,1)S(1)}, u32[]{:S(2)}, u32[]{:S(2)}) collective-permute-start(bf16[2,64,1024]{2,1,0:T(8,128)(2,1)S(1)} %get-tuple-element.69), channel_id=1, source_target_pairs={{0,6},{1,7},{2,0},{3,1},{4,2},{5,3},{6,4},{7,5},{8,14},{9,15},{10,... | collective-permute-start | bytes 786440 | tf_op jit(solution)/shard_map/ppermute | solution.py:507
  227.5 20.1 %collective-permute-start.33 = (bf16[2,64,1024]{2,1,0:T(8,128)(2,1)S(1)}, bf16[2,64,1024]{2,1,0:T(8,128)(2,1)S(1)}, u32[]{:S(2)}, u32[]{:S(2)}) collective-permute-start(bf16[2,64,1024]{2,1,0:T(8,128)(2,1)S(1)} %get-tuple-element.70), channel_id=1, source_target_pairs={{0,4},{1,5},{2,6},{3,7},{4,0},{5,1},{6,2},{7,3},{8,12},{9,13},{10,... | collective-permute-start | bytes 786440 | tf_op jit(solution)/shard_map/ppermute | solution.py:507
  247.7 12.2 %collective-permute-start.34 = (bf16[512,512]{1,0:T(8,128)(2,1)S(1)}, bf16[512,512]{1,0:T(8,128)(2,1)S(1)}, u32[]{:S(2)}, u32[]{:S(2)}) collective-permute-start(bf16[512,512]{1,0:T(8,128)(2,1)S(1)} %get-tuple-element.71.refs_3_), channel_id=1, source_target_pairs={{0,8},{8,0},{1,9},{9,1},{2,10},{10,2},{3,11},{11,3},{4,12},{12,4},... | collective-permute-start | bytes 1572872 | tf_op jit(solution)/shard_map/ppermute | solution.py:547
  249.8 12.5 %collective-permute-start.39 = (bf16[2,64,1024]{2,1,0:T(8,128)(2,1)S(1)}, bf16[2,64,1024]{2,1,0:T(8,128)(2,1)S(1)}, u32[]{:S(2)}, u32[]{:S(2)}) collective-permute-start(bf16[2,64,1024]{2,1,0:T(8,128)(2,1)S(1)} %get-tuple-element.77), channel_id=1, source_target_pairs={{0,2},{1,3},{2,4},{3,5},{4,6},{5,7},{6,0},{7,1},{8,10},{9,11},{10,... | collective-permute-start | bytes 786440 | tf_op jit(solution)/shard_map/ppermute | solution.py:507
  249.9 13.9 %collective-permute-start.40 = (bf16[2,64,1024]{2,1,0:T(8,128)(2,1)S(1)}, bf16[2,64,1024]{2,1,0:T(8,128)(2,1)S(1)}, u32[]{:S(2)}, u32[]{:S(2)}) collective-permute-start(bf16[2,64,1024]{2,1,0:T(8,128)(2,1)S(1)} %get-tuple-element.78), channel_id=1, source_target_pairs={{0,6},{1,7},{2,0},{3,1},{4,2},{5,3},{6,4},{7,5},{8,14},{9,15},{10,... | collective-permute-start | bytes 786440 | tf_op jit(solution)/shard_map/ppermute | solution.py:507
  253.7 22.7 %collective-permute-start.41 = (bf16[2,64,1024]{2,1,0:T(8,128)(2,1)S(1)}, bf16[2,64,1024]{2,1,0:T(8,128)(2,1)S(1)}, u32[]{:S(2)}, u32[]{:S(2)}) collective-permute-start(bf16[2,64,1024]{2,1,0:T(8,128)(2,1)S(1)} %get-tuple-element.79), channel_id=1, source_target_pairs={{0,4},{1,5},{2,6},{3,7},{4,0},{5,1},{6,2},{7,3},{8,12},{9,13},{10,... | collective-permute-start | bytes 786440 | tf_op jit(solution)/shard_map/ppermute | solution.py:507
  261.3 16.6 %collective-permute-start.35 = (bf16[2,64,512]{2,1,0:T(8,128)(2,1)S(1)}, bf16[2,64,512]{2,1,0:T(8,128)(2,1)S(1)}, u32[]{:S(2)}, u32[]{:S(2)}) collective-permute-start(bf16[2,64,512]{2,1,0:T(8,128)(2,1)S(1)} %get-tuple-element.73), channel_id=1, source_target_pairs={{0,2},{1,3},{2,4},{3,5},{4,6},{5,7},{6,0},{7,1},{8,10},{9,11},{10,... | collective-permute-start | bytes 393224 | tf_op jit(solution)/shard_map/ppermute | solution.py:507
  262.2 21.7 %collective-permute-start.43 = (bf16[4,64,1024]{2,1,0:T(8,128)(2,1)}, bf16[4,64,1024]{2,1,0:T(8,128)(2,1)S(1)}, u32[]{:S(2)}, u32[]{:S(2)}) collective-permute-start(bf16[4,64,1024]{2,1,0:T(8,128)(2,1)} %pad_maximum_fusion.4), channel_id=1, source_target_pairs={{0,1},{1,0},{2,3},{3,2},{4,5},{5,4},{6,7},{7,6},{8,9},{9,8},{10,11... | collective-permute-start | bytes 1572872 | tf_op jit(solution)/shard_map/ppermute | solution.py:507
  277.0 6.6 %collective-permute-start.36 = (bf16[2,64,512]{2,1,0:T(8,128)(2,1)}, bf16[2,64,512]{2,1,0:T(8,128)(2,1)S(1)}, u32[]{:S(2)}, u32[]{:S(2)}) collective-permute-start(bf16[2,64,512]{2,1,0:T(8,128)(2,1)} %get-tuple-element.74), channel_id=1, source_target_pairs={{0,6},{1,7},{2,0},{3,1},{4,2},{5,3},{6,4},{7,5},{8,14},{9,15},{10,... | collective-permute-start | bytes 393224 | tf_op jit(solution)/shard_map/ppermute | solution.py:507
  277.0 6.6 %collective-permute-start.37 = (bf16[2,64,512]{2,1,0:T(8,128)(2,1)}, bf16[2,64,512]{2,1,0:T(8,128)(2,1)S(1)}, u32[]{:S(2)}, u32[]{:S(2)}) collective-permute-start(bf16[2,64,512]{2,1,0:T(8,128)(2,1)} %get-tuple-element.75), channel_id=1, source_target_pairs={{0,4},{1,5},{2,6},{3,7},{4,0},{5,1},{6,2},{7,3},{8,12},{9,13},{10,... | collective-permute-start | bytes 393224 | tf_op jit(solution)/shard_map/ppermute | solution.py:507
  277.9 7.6 %collective-permute-start.42 = (bf16[4,64,1024]{2,1,0:T(8,128)(2,1)}, bf16[4,64,1024]{2,1,0:T(8,128)(2,1)}, u32[]{:S(2)}, u32[]{:S(2)}) collective-permute-start(bf16[4,64,1024]{2,1,0:T(8,128)(2,1)} %pad_maximum_fusion.3), channel_id=1, source_target_pairs={{0,1},{1,0},{2,3},{3,2},{4,5},{5,4},{6,7},{7,6},{8,9},{9,8},{10,11... | collective-permute-start | bytes 1572872 | tf_op jit(solution)/shard_map/ppermute | solution.py:507
  277.9 14.7 %collective-permute-start.44 = (bf16[4,2,128,256]{3,2,1,0:T(8,128)(2,1)}, bf16[4,2,128,256]{3,2,1,0:T(8,128)(2,1)}, u32[]{:S(2)}, u32[]{:S(2)}) collective-permute-start(bf16[4,2,128,256]{3,2,1,0:T(8,128)(2,1)} %get-tuple-element.81), channel_id=1, source_target_pairs={{0,8},{8,0},{1,9},{9,1},{2,10},{10,2},{3,11},{11,3},{4,12},{12,4},... | collective-permute-start | bytes 1572872 | tf_op jit(solution)/shard_map/ppermute | solution.py:547
  283.7 4.5 %collective-permute-start.38 = (bf16[4,64,512]{2,1,0:T(8,128)(2,1)S(1)}, bf16[4,64,512]{2,1,0:T(8,128)(2,1)S(1)}, u32[]{:S(2)}, u32[]{:S(2)}) collective-permute-start(bf16[4,64,512]{2,1,0:T(8,128)(2,1)S(1)} %pad_maximum_fusion.7), channel_id=1, source_target_pairs={{0,1},{1,0},{2,3},{3,2},{4,5},{5,4},{6,7},{7,6},{8,9},{9,8},{10,11... | collective-permute-start | bytes 786440 | tf_op jit(solution)/shard_map/ppermute | solution.py:507
  (27 other events, 218.9 us)
